TPU v7x, 32 devices: a whole 2x2x4 slice. The times are simulated.
32 devices in a mesh: groups: 2 (over y), ctx: 2 (over x), heads: 8 (over z, core).
Axes of the slice: x: 2, y: 2, z: 4, core: 2. Of those that a mesh axis runs over, the one named last changes fastest.
Arguments:
- hidden_in: bfloat16 [4096, 4096], P(('groups', 'ctx'), 'heads'), parts along dimension 0, may hold values from -6 to 6
- norm_gain: float32 [4096], replicated, may hold values from 0.1 to 1.9
- router_weight: float32 [4096], replicated, may hold values from -0.09375 to 0.09375
- w_query: bfloat16 [4096, 4096], P(None, 'heads')
- w_key: bfloat16 [4096, 1024], P(None, 'heads')
- value_weight: bfloat16 [4096, 1024], P(None, 'heads'), may hold values from -0.09375 to 0.09375
- w_out: bfloat16 [4096, 4096], P(None, 'heads'), may hold values from -1.5 to 1.5
- keep_flags: int32 [4096], P(('groups', 'ctx')), parts along dimension 0, may hold values from 0 to 1, as said below
- keep_counts: int32 [4], P('groups'), parts along dimension 0, may hold values from 1 to 256, as said below
- keep_positions: int32 [4, 256], P('groups'), parts along dimension 0, may hold values from -1 to 2047, as said below
Outputs:
- hidden_out: bfloat16 [4096, 4096], P(('groups', 'ctx'), 'heads'), parts along dimension 0
There are 2 independent parts, one for each index of `groups`. A program takes and returns all parts, laid end to end along the dimension named above; an argument that names none is the same for every part. Nothing has to cross between parts.
Inputs may be any that keep to these rules, and one draw needn't show every extreme that they name: keep_flags is 1 exactly at the positions listed by keep_positions and keep_counts. `keep_counts`: some shard's count is 256. `keep_positions`: row s lists, ascending, keep_counts[s] positions of shard s's tokens, then -1 in the remaining slots.
All inputs are finite; a program needn't handle non-finite values.
Results may differ from a plain program's by a relative error of at most 0.0085.
Values may be sent and summed in bfloat16 or wider, within the bound.
No kernel may reach another device: no remote copies, remote signals or barrier semaphores. Data moves between devices by JAX's collectives and lax.ppermute only.
A program may use at most 128 MiB of HBM per device.

v0:
```python
import jax
import jax.numpy as jnp
from jax import lax
from jax.sharding import PartitionSpec as P

QUERY_HEAD_COUNT = 32
KEY_VALUE_HEADS = 8
HEAD_SIZE = 128


rope_base = 500000.0
norm_eps = 1e-05


def rotate(tensor, positions_in):
    row_count = tensor.shape[0]
    head_count = tensor.shape[1] // HEAD_SIZE
    tensor = tensor.reshape(row_count, head_count, HEAD_SIZE)
    half_dim = HEAD_SIZE // 2
    frequency = rope_base ** (-(jnp.arange(half_dim, dtype=jnp.float32) * 2.0 / HEAD_SIZE))
    angles = positions_in.astype(jnp.float32)[:, None] * frequency[None, :]
    cosine = jnp.cos(angles)[:, None, :]
    sine_part = jnp.sin(angles)[:, None, :]
    first_half = tensor[..., :half_dim]
    second_half = tensor[..., half_dim:]
    turned = jnp.concatenate(
        [
            first_half * cosine - second_half * sine_part,
            second_half * cosine + first_half * sine_part,
        ],
        -1,
    )
    return turned.reshape(row_count, head_count * HEAD_SIZE)


def attend_rows(
    row_block, row_pos, key_pos, norm_gain, router_weight, w_query, w_key, value_weight, w_out
):
    widened = lax.all_gather(row_block, "heads", axis=1, tiled=True)
    wide_float = widened.astype(jnp.float32)
    inv_rms = lax.rsqrt(jnp.mean(wide_float * wide_float, axis=-1, keepdims=True) + norm_eps)
    normed = (wide_float * inv_rms * norm_gain[None, :]).astype(jnp.bfloat16)
    gate_value = jax.nn.sigmoid(jnp.sum(wide_float * router_weight[None, :], axis=-1))
    query_rows = rotate(
        jnp.dot(normed, w_query, preferred_element_type=jnp.float32), row_pos
    ).astype(jnp.bfloat16)
    key_row_block = rotate(
        jnp.dot(normed, w_key, preferred_element_type=jnp.float32), row_pos
    ).astype(jnp.bfloat16)
    value_row_block = jnp.dot(normed, value_weight, preferred_element_type=jnp.float32).astype(
        jnp.bfloat16
    )
    row_count = row_block.shape[0]
    kv_local = w_key.shape[1] // HEAD_SIZE
    group_width = QUERY_HEAD_COUNT // KEY_VALUE_HEADS
    query_heads = query_rows.reshape(row_count, kv_local, group_width, HEAD_SIZE)
    score_scale = 1.0 / HEAD_SIZE**0.5
    running = jnp.full((kv_local, group_width, row_count), -1e30, jnp.float32)
    key_part = lax.all_gather(key_row_block, "ctx", axis=0, tiled=True)
    value_part = lax.all_gather(value_row_block, "ctx", axis=0, tiled=True)
    seen = key_part.shape[0]
    key_heads = key_part.reshape(seen, kv_local, HEAD_SIZE)
    value_heads = value_part.reshape(seen, kv_local, HEAD_SIZE)
    scores = (
        jnp.einsum("rkgd,nkd->kgrn", query_heads, key_heads, preferred_element_type=jnp.float32)
        * score_scale
    )
    visible = (key_pos[None, :] <= row_pos[:, None])[None, None]
    fresh = jnp.maximum(running, jnp.max(jnp.where(visible, scores, -1e30), axis=-1))
    weights_raw = jnp.where(visible, jnp.exp(scores - fresh[..., None]), 0.0)
    denom_sum = jnp.sum(weights_raw, axis=-1)
    mixed = jnp.einsum(
        "kgrn,nkd->kgrd",
        weights_raw.astype(jnp.bfloat16),
        value_heads,
        preferred_element_type=jnp.float32,
    )
    attended = mixed / denom_sum[..., None]
    attn = (
        attended.transpose(2, 0, 1, 3)
        .reshape(row_count, kv_local * group_width * HEAD_SIZE)
        .astype(jnp.bfloat16)
    )
    projected = jnp.dot(
        lax.all_gather(attn, "heads", axis=1, tiled=True), w_out, preferred_element_type=jnp.float32
    )
    return (gate_value[:, None] * projected).astype(jnp.bfloat16)


def body(
    hidden_in,
    norm_gain,
    router_weight,
    w_query,
    w_key,
    value_weight,
    w_out,
    keep_flags,
    keep_counts,
    keep_positions,
):
    shards = lax.axis_size("ctx")
    own_index = lax.axis_index("ctx")
    tok_local = hidden_in.shape[0]
    capacity = keep_positions.shape[1]
    seq_total = tok_local * shards
    slot_ids = jnp.arange(capacity, dtype=jnp.int32)
    valid_all = slot_ids[None, :] < keep_counts[:, None]
    own_pos = keep_positions[own_index]
    own_valid = valid_all[own_index]
    local_rows = jnp.where(own_valid, own_pos - own_index * tok_local, 0)
    picked = hidden_in[local_rows]
    row_pos = jnp.where(own_valid, own_pos, seq_total)
    key_pos = jnp.where(valid_all, keep_positions, seq_total + 1).reshape(-1)
    update = attend_rows(
        picked, row_pos, key_pos, norm_gain, router_weight, w_query, w_key, value_weight, w_out
    )
    slot_update = update.astype(jnp.float32)
    target = jnp.where(own_valid, own_pos - own_index * tok_local, tok_local)
    scattered = (
        jnp.zeros((tok_local, hidden_in.shape[1]), jnp.float32)
        .at[target]
        .add(slot_update, mode="drop")
    )
    flag_float = keep_flags.astype(jnp.float32)[:, None]
    return (hidden_in.astype(jnp.float32) + flag_float * scattered).astype(jnp.bfloat16)


def solution(mesh):
    in_specs = (
        P(("groups", "ctx"), "heads"),
        P(),
        P(),
        P(None, "heads"),
        P(None, "heads"),
        P(None, "heads"),
        P(None, "heads"),
        P(("groups", "ctx")),
        P("groups"),
        P("groups", None),
    )
    out_specs = P(("groups", "ctx"), "heads")
    return jax.shard_map(body, mesh=mesh, in_specs=in_specs, out_specs=out_specs, check_vma=False)
```

profile of v0, /device:TPU:0, one launch (start us, length us, event | category | flops | bytes accessed | tf_op | source)
XLA Modules:
  0.0 109.5 jit_solution(5401100207106977280)
XLA Ops:
  6.5 0.0 copy-start
  6.5 0.0 copy-start.6
  6.5 0.0 copy-start.4
  6.5 0.0 copy-start.3
  6.5 0.0 all-gather.7.cloned.1.call-start
  6.6 0.8 iota_compare_fusion
  7.4 0.7 compare_select_fusion
  8.1 0.0 copy-start.9
  8.1 3.3 %gather_fusion = bf16[256,512]{1,0:T(8,128)(2,1)} fusion(bf16[1024,512]{1,0:T(8,128)(2,1)} %param.10, s32[1024]{0:T(1024)S(1)} %pad_clamp_fusion), kind=kCustom, calls=%fused_computation | custom fusion | bytes 525312 | tf_op jit(solution)/shard_map/gather | solution.py:112
  11.4 0.0 all-gather.7.cloned.1.call-update
  11.4 0.0 all-gather.5.cloned.1.call-start
  11.5 0.0 copy-done.4
  11.5 0.0 copy-done.6
  11.5 0.1 select_bitcast_fusion
  11.6 0.1 broadcast_compare_fusion
  11.8 0.5 multiply_cosine_fusion
  12.3 31.1 %all-gather.7.cloned.1.call-done = bf16[256,4096]{1,0:T(8,128)(2,1)} async-done(((bf16[256,512]{1,0:T(8,128)(2,1)}), bf16[256,4096]{1,0:T(8,128)(2,1)}) %all-gather.7.cloned.1.call-update) | async-done | bytes 2097168 | tf_op jit(solution)/shard_map/all_gather | solution.py:39
  43.4 0.0 copy-done.3
  43.4 0.0 copy-start.2
  43.4 2.5 %fusion = (f32[256]{0:T(256)S(1)}, f32[256]{0:T(256)S(1)}) fusion(bf16[256,4096]{1,0:T(8,128)(2,1)} %all-gather.7.cloned.1.call-done, f32[4096]{0:T(1024)S(1)} %copy-done.3), kind=kLoop, calls=%fused_computation.5 | loop fusion | flops 5242368 | bytes 2115584 | tf_op jit(solution)/shard_map/reduce_sum | solution.py:43
  45.9 0.0 copy-done
  45.9 0.0 copy-done.9
  45.9 0.0 copy-done.2
  45.9 0.0 copy-start.8
  46.0 1.0 convolution_convert_fusion
  46.9 4.9 %all_gather.14 = bf16[512,128]{0,1:T(8,128)(2,1)S(1)} all-gather(bf16[256,128]{0,1:T(8,128)(2,1)S(1)} %convolution_convert_fusion), channel_id=1, replica_groups=mesh['groups'=2,'ctx'=2,'heads'=8] {'ctx'}, dimensions={0}, use_global_device_ids=true | all-gather | bytes 196608 | tf_op jit(solution)/shard_map/all_gather | solution.py:60
  51.9 0.0 copy-done.8
  51.9 0.0 copy-start.7
  51.9 1.0 convolution_bitcast_fusion
  52.9 0.3 fusion.31
  53.2 0.9 copy-done.7
  54.1 1.3 %fusion.38 = f32[256,512]{1,0:T(8,128)S(1)} fusion(bf16[4096,512]{1,0:T(8,128)(2,1)S(1)} %copy-done.7, bf16[256,4096]{1,0:T(8,128)(2,1)S(1)} %copy-done.2, f32[4096]{0:T(1024)S(1)} %copy-done.9, f32[256]{0:T(256)S(1)} %add_rsqrt_fusion), kind=kOutput, calls=%fused_computation.68 | convolution fusion | flops 1077936128 | bytes 6833152 | tf_op jit(solution)/shard_map/dot_general | solution.py:45
  55.4 0.2 reshape.270
  55.6 4.9 %all-gather.1 = bf16[512,1,128]{0,2,1:T(8,128)(2,1)S(1)} all-gather(bf16[256,1,128]{0,2,1:T(8,128)(2,1)S(1)} %pad_maximum_fusion), channel_id=3, replica_groups=mesh['groups'=2,'ctx'=2,'heads'=8] {'ctx'}, dimensions={0}, use_global_device_ids=true | all-gather | bytes 196608 | tf_op jit(solution)/shard_map/all_gather | solution.py:59
  60.5 0.3 fusion.41
  60.8 0.1 subtract_convert_fusion
  61.0 0.6 fusion.4
  61.6 0.5 fusion.7
  62.0 0.0 copy-start.5
  62.1 1.3 %fusion.11 = bf16[4,256,128]{1,2,0:T(8,128)(2,1)} fusion(f32[512,256,4]{1,0,2:T(8,128)S(1)} %get-tuple-element.18, f32[4,256]{1,0:T(4,128)S(1)} %broadcast_maximum_fusion, pred[256,512]{0,1:T(8,128)(4,1)S(1)} %broadcast_compare_fusion, f32[4,256]{1,0:T(4,128)S(1)} %fusion.7, bf16[512,128]{0,1:T(8,128)(2,1)S(1)} %all_gather.14), kind=kOutput, calls=%fused_computation.21 | convolution fusion | flops 136577024 | bytes 2629632 | tf_op jit(solution)/shard_map/kgrn,nkd->kgrd/dot_general | solution.py:72
  63.4 0.0 all-gather.5.cloned.1.call-update
  63.4 0.0 copy-done.5
  63.4 28.7 %all-gather.5.cloned.1.call-done = bf16[256,4096]{0,1:T(8,128)(2,1)} async-done(((bf16[256,512]{0,1:T(8,128)(2,1)}), bf16[256,4096]{0,1:T(8,128)(2,1)}) %all-gather.5.cloned.1.call-update) | async-done | bytes 2097168 | tf_op jit(solution)/shard_map/all_gather | solution.py:85
  92.1 4.1 %fusion.10 = f32[256,512]{1,0:T(8,128)S(1)} fusion(bf16[256,4096]{0,1:T(8,128)(2,1)} %all-gather.5.cloned.1.call-done, bf16[4096,512]{1,0:T(8,128)(2,1)} %param.16, f32[256]{0:T(256)S(1)} %add_divide_fusion), kind=kOutput, calls=%fused_computation.20 | convolution fusion | flops 1074135040 | bytes 6816768 | tf_op jit(solution)/shard_map/dot_general | solution.py:84
  96.2 0.0 copy-start.1
  96.3 3.5 %scatter_custom_fusion = f32[1024,512]{1,0:T(8,128)} fusion(s32[256]{0:T(256)S(1)} %bitcast.58, f32[256,512]{1,0:T(8,128)S(1)} %fusion.10, f32[]{:T(128)} %constant.16.clone.1), kind=kCustom, calls=%fused_computation.28 | custom fusion | flops 131072 | bytes 2097156 | tf_op jit(solution)/shard_map/scatter-add | solution.py:123
  99.8 0.0 copy-done.1
  99.8 2.9 %add_convert_fusion = bf16[1024,512]{1,0:T(8,128)(2,1)} fusion(f32[1024,512]{1,0:T(8,128)} %scatter_custom_fusion, bf16[1024,512]{1,0:T(8,128)(2,1)S(1)} %copy-done.1, f32[1024]{0:T(1024)S(1)} %convert_element_type.55), kind=kLoop, calls=%fused_computation.14 | loop fusion | flops 2097152 | bytes 4198400 | tf_op jit(solution)/shard_map/convert_element_type | solution.py:126
  (10 shorter events, 0.1 us)
Async XLA Ops:
  6.5 39.4 %copy-start = (bf16[4096,128]{1,0:T(8,128)(2,1)S(1)}, bf16[4096,128]{1,0:T(8,128)(2,1)}, u32[]{:S(2)}) copy-start(bf16[4096,128]{1,0:T(8,128)(2,1)} %param.15) | copy-start | bytes 3145732
  6.5 5.0 %copy-start.6 = (s32[2]{0:T(128)S(1)}, s32[2]{0:T(128)}, u32[]{:S(2)}) copy-start(s32[2]{0:T(128)} %param.18) | copy-start | bytes 28
  6.5 4.9 %copy-start.4 = (s32[2,256]{1,0:T(2,128)S(1)}, s32[2,256]{1,0:T(2,128)}, u32[]{:S(2)}) copy-start(s32[2,256]{1,0:T(2,128)} %param.19) | copy-start | bytes 6148
  6.5 36.8 %copy-start.3 = (f32[4096]{0:T(1024)S(1)}, f32[4096]{0:T(1024)}, u32[]{:S(2)}) copy-start(f32[4096]{0:T(1024)} %param.12) | copy-start | bytes 49156
  6.5 36.8 %all-gather.7.cloned.1.call-start = ((), (), s32[]{:S(2)}) async-start(), calls=%async_computation.1 | async-start | bytes 2359296 | tf_op jit(solution)/shard_map/all_gather | solution.py:39
  8.1 37.8 %copy-start.9 = (f32[4096]{0:T(1024)S(1)}, f32[4096]{0:T(1024)}, u32[]{:S(2)}) copy-start(f32[4096]{0:T(1024)} %param.11) | copy-start | bytes 49156
  11.4 80.7 %all-gather.5.cloned.1.call-start = ((), (), s32[]{:S(2)}) async-start(), calls=%async_computation | async-start | bytes 2359296 | tf_op jit(solution)/shard_map/all_gather | solution.py:85
  43.4 2.6 %copy-start.2 = (bf16[256,4096]{1,0:T(8,128)(2,1)S(1)}, bf16[256,4096]{1,0:T(8,128)(2,1)}, u32[]{:S(2)}) copy-start(bf16[256,4096]{1,0:T(8,128)(2,1)} %all-gather.7.cloned.1.call-done) | copy-start | bytes 6291460
  45.9 5.9 %copy-start.8 = (bf16[4096,128]{1,0:T(8,128)(2,1)S(1)}, bf16[4096,128]{1,0:T(8,128)(2,1)}, u32[]{:S(2)}) copy-start(bf16[4096,128]{1,0:T(8,128)(2,1)} %param.14) | copy-start | bytes 3145732
  51.9 2.2 %copy-start.7 = (bf16[4096,512]{1,0:T(8,128)(2,1)S(1)}, bf16[4096,512]{1,0:T(8,128)(2,1)}, u32[]{:S(2)}) copy-start(bf16[4096,512]{1,0:T(8,128)(2,1)} %param.13) | copy-start | bytes 12582916
  62.0 1.3 %copy-start.5 = (s32[1024]{0:T(1024)S(1)}, s32[1024]{0:T(1024)}, u32[]{:S(2)}) copy-start(s32[1024]{0:T(1024)} %param.17) | copy-start | bytes 12292
  96.2 3.5 %copy-start.1 = (bf16[1024,512]{1,0:T(8,128)(2,1)S(1)}, bf16[1024,512]{1,0:T(8,128)(2,1)}, u32[]{:S(2)}) copy-start(bf16[1024,512]{1,0:T(8,128)(2,1)} %param.10) | copy-start | bytes 3145732
Sparse Core Ops, SparseCore 0:
  11.5 31.7 all-gather.6
  63.5 28.6 all-gather.4
where the time goes:
time: 110 us; the launch traced here: 109 us
  waiting for transfers between devices  59.8 us (54%)
  between operations  13.6 us (12%)
  other arithmetic  12.2 us (11%)
  blocking collectives  9.89 us (9%)
  matrix products  9.18 us (8%)
  local copies, waits for them, and re-layouts  4.73 us (4%)
    all_gather x1, waiting for transfers between devices, attend_rows(): widened = lax.all_gather(row_block, 'heads', axis=1, tiled=True)  31.1 us
    all_gather x1, waiting for transfers between devices, attend_rows(): lax.all_gather(attn, 'heads', axis=1, tiled=True)  28.7 us
    all_gather x1, blocking collectives, attend_rows(): value_part = lax.all_gather(value_row_block, 'ctx', axis=0, tiled=True)  4.94 us
    all_gather x1, blocking collectives, attend_rows(): key_part = lax.all_gather(key_row_block, 'ctx', axis=0, tiled=True)  4.94 us
    dot_general x1, matrix products, attend_rows(): jnp.dot(lax.all_gather(attn, 'heads', axis=1, tiled=True), w_out, preferr...  4.08 us
    scatter-add x1, other arithmetic, body(): scattered = jnp.zeros((tok_local, hidden_in.shape[1]), jnp.float32).at[ta...  3.51 us
    gather x1, local copies, waits for them, and re-layouts, body(): picked = hidden_in[local_rows]  3.28 us
    convert_element_type x1, other arithmetic, body(): (hidden_in.astype(jnp.float32) + flag_float * scattered).astype(jnp.bfloa...  2.88 us
  transfers between devices with their start and end apart: 2, of which 2 were waited for; matrix products, arithmetic and copies ran while one was open for 1% of the time, Pallas kernels for 0%

commit v1 on v0

v1 whole, which is shorter than its diff:
```python
import functools

import jax
import jax.numpy as jnp
from jax import lax
from jax.experimental import pallas as pl
from jax.experimental.pallas import tpu as pltpu
from jax.sharding import PartitionSpec as P

HEAD_SIZE = 128
ROPE_BASE = 500000.0
NORM_EPS = 1e-05
LOG2E = 1.4426950408889634
VMEM_LIMIT = 24 * 1024 * 1024
F32 = jnp.float32
BF16 = jnp.bfloat16


def whole():
    return pl.BlockSpec(memory_space=pltpu.VMEM)


def fixed(shape):
    return pl.BlockSpec(shape, lambda *_: (0,) * len(shape))


def params():
    return pltpu.CompilerParams(vmem_limit_bytes=VMEM_LIMIT)


def live_row(pos_ref, cnt_ref, shard, dead):
    pos = pos_ref[pl.ds(shard, 1), :]
    slot = lax.broadcasted_iota(jnp.int32, pos.shape, 1)
    return jnp.where(slot < cnt_ref[shard], pos, dead)


def pick_kernel(cnt_ref, pos_ref, hid_ref, x_ref, xa_ref, xb_ref, rowpos_ref):
    own = lax.axis_index("ctx")
    shards = lax.axis_size("ctx")
    tok = hid_ref.shape[0]
    cap = x_ref.shape[0]
    row = live_row(pos_ref, cnt_ref, own, shards * tok)
    column = jnp.transpose(jnp.broadcast_to(row, (128, cap)))
    rowpos_ref[...] = column
    local = column[:, :1] - own * tok
    hot = (lax.broadcasted_iota(jnp.int32, (cap, tok), 1) == local).astype(F32).astype(BF16)
    x = jnp.dot(hot, hid_ref[...], preferred_element_type=F32).astype(BF16)
    x_ref[...] = x
    xa_ref[...] = x[: cap // 2]
    xb_ref[...] = x[cap // 2 :]


def pick(counts, positions, hidden):
    cap, width = positions.shape[1], hidden.shape[1]
    return pl.pallas_call(
        pick_kernel,
        out_shape=[
            jax.ShapeDtypeStruct((cap, width), BF16),
            jax.ShapeDtypeStruct((cap // 2, width), BF16),
            jax.ShapeDtypeStruct((cap // 2, width), BF16),
            jax.ShapeDtypeStruct((cap, 128), jnp.int32),
        ],
        in_specs=[pl.BlockSpec(memory_space=pltpu.SMEM), whole(), whole()],
        out_specs=[whole()] * 4,
        compiler_params=params(),
        name="pick",
    )(counts, positions, hidden)


def heads_perm(size, f):
    return [(2 * z + c, 2 * f(z) + c) for z in range(size // 2) for c in range(2)]


def spread(size, full, first, second):
    cross = functools.partial(lax.ppermute, axis_name="heads", perm=heads_perm(size, lambda z: 3 - z))
    near = functools.partial(lax.ppermute, axis_name="heads", perm=heads_perm(size, lambda z: z ^ 1))
    twin = functools.partial(
        lax.ppermute, axis_name="heads", perm=[(d, d ^ 1) for d in range(size)]
    )
    far_a, far_b = cross(first), cross(second)
    mate = twin(full)
    beside = near(full)
    far_mate_a, far_mate_b = twin(far_a), twin(far_b)
    beside_mate = twin(beside)
    last_a, last_b = near(far_a), near(far_b)
    last_mate_a, last_mate_b = twin(last_a), twin(last_b)
    return (
        ((full,), (mate,)),
        ((far_a, far_b), (far_mate_a, far_mate_b)),
        ((beside,), (beside_mate,)),
        ((last_a, last_b), (last_mate_a, last_mate_b)),
    )


def joined(refs):
    parts = [ref[...] for ref in refs]
    return parts[0] if len(parts) == 1 else jnp.concatenate(parts, axis=0)


def lanes_sum(x):
    total = x[:, :128]
    for at in range(128, x.shape[1], 128):
        total = total + x[:, at : at + 128]
    return total


def kv_terms(mine, twin, gain_ref, router_ref, wk_ref, wv_ref):
    core = lax.rem(lax.axis_index("heads"), 2)
    width = mine.shape[1]
    sums = None
    scaled = []
    for x, at in ((mine, core), (twin, 1 - core)):
        xf = x.astype(F32)
        rows = pl.ds(pl.multiple_of(at * width, width), width)
        gained = (xf * gain_ref[:, rows]).astype(BF16)
        scaled.append(gained)
        part = (
            jnp.dot(gained, wk_ref[rows, :], preferred_element_type=F32),
            jnp.dot(gained, wv_ref[rows, :], preferred_element_type=F32),
            lanes_sum(xf * xf),
            lanes_sum(xf * router_ref[:, rows]),
        )
        sums = part if sums is None else tuple(a + b for a, b in zip(sums, part))
    return scaled, sums


def q_term(scaled, wq_ref):
    core = lax.rem(lax.axis_index("heads"), 2)
    width = scaled[0].shape[1]
    out = None
    for gained, at in zip(scaled, (core, 1 - core)):
        rows = pl.ds(pl.multiple_of(at * width, width), width)
        part = jnp.dot(gained, wq_ref[rows, :], preferred_element_type=F32)
        out = part if out is None else out + part
    return out


def turn(x, cos, sin):
    return x * cos + pltpu.roll(x, HEAD_SIZE // 2, 1) * sin


def qkv_kernel(n_mine, fresh, chip_ref, *refs):
    mine, twin = joined(refs[:n_mine]), joined(refs[n_mine : 2 * n_mine])
    refs = refs[2 * n_mine :]
    gain_ref, router_ref, wq_ref, wk_ref, wv_ref = refs[:5]
    kv_out, q_out = refs[-2:]
    scaled, (k, v, squares, routed) = kv_terms(mine, twin, gain_ref, router_ref, wk_ref, wv_ref)
    q = q_term(scaled, wq_ref)
    if fresh:
        kv_out[:, 0:128], kv_out[:, 128:256] = k, v
        kv_out[:, 256:384], kv_out[:, 384:512] = squares, routed
        q_out[...] = q
    else:
        kv_in, q_in = refs[5:7]
        kv_out[:, 0:128] = kv_in[:, 0:128] + k
        kv_out[:, 128:256] = kv_in[:, 128:256] + v
        kv_out[:, 256:384] = kv_in[:, 256:384] + squares
        kv_out[:, 384:512] = kv_in[:, 384:512] + routed
        q_out[...] = q_in[...] + q


def weight_spec(rows, columns):
    return pl.BlockSpec((rows, columns), lambda i, chip: (chip[0], 0))


def vector_spec(columns):
    return pl.BlockSpec((1, columns), lambda i, chip: (0, chip[0]))


def qkv_part(chip, pair, gain, router, wq, wk, wv, sums):
    mine, twin = pair
    cap = sum(x.shape[0] for x in mine)
    width = mine[0].shape[1]
    operands = [*mine, *twin, gain, router, wq, wk, wv]
    specs = [fixed(x.shape) for x in (*mine, *twin)]
    specs += [vector_spec(2 * width)] * 2
    specs += [weight_spec(2 * width, w.shape[1]) for w in (wq, wk, wv)]
    aliases = {}
    if sums is not None:
        aliases = {1 + len(operands): 0, 2 + len(operands): 1}
        operands += sums
        specs += [fixed(s.shape) for s in sums]
    return pl.pallas_call(
        functools.partial(qkv_kernel, len(mine), sums is None),
        out_shape=[
            jax.ShapeDtypeStruct((cap, 512), F32),
            jax.ShapeDtypeStruct((cap, wq.shape[1]), F32),
        ],
        grid_spec=pltpu.PrefetchScalarGridSpec(
            num_scalar_prefetch=1,
            grid=(1,),
            in_specs=specs,
            out_specs=[fixed((cap, 512)), fixed((cap, wq.shape[1]))],
        ),
        input_output_aliases=aliases,
        compiler_params=params(),
        cost_estimate=pl.CostEstimate(
            flops=2 * cap * 2 * width * 768, bytes_accessed=4 * 1024 * 1024, transcendentals=0
        ),
        name="qkv_part",
    )(chip, *operands)


def kv_last_kernel(n_mine, features, chip_ref, *refs):
    mine, twin = joined(refs[:n_mine]), joined(refs[n_mine : 2 * n_mine])
    gain_ref, router_ref, wk_ref, wv_ref, kv_in, cos_ref, sin_ref, kv_out, stat_out = refs[2 * n_mine :]
    _, (k, v, squares, routed) = kv_terms(mine, twin, gain_ref, router_ref, wk_ref, wv_ref)
    squares = jnp.sum(kv_in[:, 256:384] + squares, axis=1, keepdims=True)
    routed = jnp.sum(kv_in[:, 384:512] + routed, axis=1, keepdims=True)
    inverse = lax.rsqrt(squares * (1.0 / features) + NORM_EPS)
    k = (kv_in[:, 0:128] + k) * inverse
    kv_out[:, 0:128] = turn(k, cos_ref[...], sin_ref[...]).astype(BF16)
    kv_out[:, 128:256] = ((kv_in[:, 128:256] + v) * inverse).astype(BF16)
    stat_out[:, 0:128] = jnp.broadcast_to(inverse, (inverse.shape[0], 128))
    gate = 1.0 / (1.0 + jnp.exp(-routed))
    stat_out[:, 128:256] = jnp.broadcast_to(gate, (gate.shape[0], 128))


def kv_last(chip, pair, gain, router, wk, wv, kv_sum, cos, sin):
    mine, twin = pair
    cap = sum(x.shape[0] for x in mine)
    width = mine[0].shape[1]
    specs = [fixed(x.shape) for x in (*mine, *twin)]
    specs += [vector_spec(2 * width)] * 2
    specs += [weight_spec(2 * width, w.shape[1]) for w in (wk, wv)]
    specs += [fixed(a.shape) for a in (kv_sum, cos, sin)]
    return pl.pallas_call(
        functools.partial(kv_last_kernel, len(mine), gain.shape[1]),
        out_shape=[
            jax.ShapeDtypeStruct((cap, 256), BF16),
            jax.ShapeDtypeStruct((cap, 256), F32),
        ],
        grid_spec=pltpu.PrefetchScalarGridSpec(
            num_scalar_prefetch=1,
            grid=(1,),
            in_specs=specs,
            out_specs=[fixed((cap, 256)), fixed((cap, 256))],
        ),
        compiler_params=params(),
        name="kv_last",
    )(chip, *mine, *twin, gain, router, wk, wv, kv_sum, cos, sin)


def attend(q, kv, visible, carry, heads):
    k, v = kv[:, 0:128], kv[:, 128:256]
    scale = LOG2E / HEAD_SIZE**0.5
    rows = visible.shape[0]
    out = []
    for h in range(heads):
        s = lax.dot_general(q[h], k, (((1,), (1,)), ((), ())), preferred_element_type=F32) * scale
        s = jnp.where(visible, s, -1e30)
        top = jnp.max(s, axis=1, keepdims=True)
        if carry is not None:
            old_top, old_total, old_mix = carry[h]
            top = jnp.maximum(top, old_top)
        e = jnp.where(visible, jnp.exp2(s - top), 0.0)
        total = jnp.sum(e, axis=1, keepdims=True)
        mix = jnp.dot(e.astype(BF16), v, preferred_element_type=F32)
        if carry is not None:
            fade = jnp.exp2(old_top - top)
            total = total + old_total * fade
            mix = mix + old_mix * fade
        out.append((top, total, mix))
    return out


def keep_carry(state, top_ref, total_ref, mix_ref):
    rows = state[0][0].shape[0]
    for h, (top, total, mix) in enumerate(state):
        at = slice(h * 128, (h + 1) * 128)
        top_ref[:, at] = jnp.broadcast_to(top, (rows, 128))
        total_ref[:, at] = jnp.broadcast_to(total, (rows, 128))
        mix_ref[:, at] = mix


def q_last_kernel(n_mine, tok, chip_ref, cnt_ref, *refs):
    mine, twin = joined(refs[:n_mine]), joined(refs[n_mine : 2 * n_mine])
    (gain_ref, wq_ref, q_in, stat_ref, cos_ref, sin_ref, kv_ref, pos_ref, rowpos_ref) = refs[
        2 * n_mine : 2 * n_mine + 9
    ]
    q_out, top_ref, total_ref, mix_ref = refs[2 * n_mine + 9 :]
    core = lax.rem(lax.axis_index("heads"), 2)
    width = mine.shape[1]
    scaled = []
    for x, at in ((mine, core), (twin, 1 - core)):
        rows = pl.ds(pl.multiple_of(at * width, width), width)
        scaled.append((x.astype(F32) * gain_ref[:, rows]).astype(BF16))
    q = (q_in[...] + q_term(scaled, wq_ref)) * stat_ref[:, 0:1]
    heads = q.shape[1] // HEAD_SIZE
    cos, sin = cos_ref[...], sin_ref[...]
    turned = [turn(q[:, h * 128 : (h + 1) * 128], cos, sin).astype(BF16) for h in range(heads)]
    for h in range(heads):
        q_out[:, h * 128 : (h + 1) * 128] = turned[h]
    own = lax.axis_index("ctx")
    shards = lax.axis_size("ctx")
    keys = live_row(pos_ref, cnt_ref, own, shards * tok + 1)
    visible = keys <= rowpos_ref[:, 0:1]
    state = attend(turned, kv_ref[...], visible, None, heads)
    keep_carry(state, top_ref, total_ref, mix_ref)


def q_last(chip, counts, pair, gain, wq, q_sum, stat, cos, sin, kv, positions, rowpos, tok):
    mine, twin = pair
    cap = sum(x.shape[0] for x in mine)
    width = mine[0].shape[1]
    columns = wq.shape[1]
    vector = pl.BlockSpec((1, 2 * width), lambda i, chip, cnt: (0, chip[0]))
    weight = pl.BlockSpec((2 * width, columns), lambda i, chip, cnt: (chip[0], 0))
    specs = [fixed(x.shape) for x in (*mine, *twin)] + [vector, weight]
    rest = (q_sum, stat, cos, sin, kv, positions, rowpos)
    specs += [fixed(a.shape) for a in rest]
    return pl.pallas_call(
        functools.partial(q_last_kernel, len(mine), tok),
        out_shape=[jax.ShapeDtypeStruct((cap, columns), BF16)]
        + [jax.ShapeDtypeStruct((cap, columns), F32)] * 3,
        grid_spec=pltpu.PrefetchScalarGridSpec(
            num_scalar_prefetch=2,
            grid=(1,),
            in_specs=specs,
            out_specs=[fixed((cap, columns))] * 4,
        ),
        compiler_params=params(),
        name="q_last",
    )(chip, counts, *mine, *twin, gain, wq, *rest)


def attend_kernel(step, last, tok, cnt_ref, q_ref, kv_ref, pos_ref, rowpos_ref, top_in, total_in, mix_in, *outs):
    shards = lax.axis_size("ctx")
    source = lax.rem(lax.axis_index("ctx") + shards - step, shards)
    keys = live_row(pos_ref, cnt_ref, source, shards * tok + 1)
    visible = keys <= rowpos_ref[:, 0:1]
    heads = q_ref.shape[1] // HEAD_SIZE
    q, carry = [], []
    for h in range(heads):
        at = slice(h * 128, (h + 1) * 128)
        q.append(q_ref[:, at])
        carry.append((top_in[:, h * 128 : h * 128 + 1], total_in[:, h * 128 : h * 128 + 1], mix_in[:, at]))
    state = attend(q, kv_ref[...], visible, carry, heads)
    if not last:
        keep_carry(state, *outs)
        return
    full, first, second = outs
    half = first.shape[0]
    for h, (_, total, mix) in enumerate(state):
        at = slice(h * 128, (h + 1) * 128)
        attn = (mix / total).astype(BF16)
        full[:, at] = attn
        first[:, at] = attn[:half]
        second[:, at] = attn[half:]


def attend_more(step, last, tok, counts, q, kv, positions, rowpos, carry):
    cap, columns = q.shape
    if last:
        shapes = [
            jax.ShapeDtypeStruct((cap, columns), BF16),
            jax.ShapeDtypeStruct((cap // 2, columns), BF16),
            jax.ShapeDtypeStruct((cap // 2, columns), BF16),
        ]
    else:
        shapes = [jax.ShapeDtypeStruct((cap, columns), F32)] * 3
    return pl.pallas_call(
        functools.partial(attend_kernel, step, last, tok),
        out_shape=shapes,
        in_specs=[pl.BlockSpec(memory_space=pltpu.SMEM)] + [whole()] * 7,
        out_specs=[whole()] * 3,
        compiler_params=params(),
        name="attend_more",
    )(counts, q, kv, positions, rowpos, *carry)


def out_term(mine, twin, w_ref):
    core = lax.rem(lax.axis_index("heads"), 2)
    width = mine.shape[1]
    out = None
    for x, at in ((mine, core), (twin, 1 - core)):
        rows = pl.ds(pl.multiple_of(at * width, width), width)
        part = jnp.dot(x, w_ref[rows, :], preferred_element_type=F32)
        out = part if out is None else out + part
    return out


def out_kernel(n_mine, fresh, chip_ref, *refs):
    mine, twin = joined(refs[:n_mine]), joined(refs[n_mine : 2 * n_mine])
    w_ref = refs[2 * n_mine]
    term = out_term(mine, twin, w_ref)
    refs[-1][...] = term if fresh else refs[2 * n_mine + 1][...] + term


def out_part(chip, pair, w_out, total):
    mine, twin = pair
    cap = sum(x.shape[0] for x in mine)
    width = mine[0].shape[1]
    columns = w_out.shape[1]
    operands = [*mine, *twin, w_out]
    specs = [fixed(x.shape) for x in (*mine, *twin)] + [weight_spec(2 * width, columns)]
    aliases = {}
    if total is not None:
        aliases = {1 + len(operands): 0}
        operands.append(total)
        specs.append(fixed(total.shape))
    return pl.pallas_call(
        functools.partial(out_kernel, len(mine), total is None),
        out_shape=jax.ShapeDtypeStruct((cap, columns), F32),
        grid_spec=pltpu.PrefetchScalarGridSpec(
            num_scalar_prefetch=1, grid=(1,), in_specs=specs, out_specs=fixed((cap, columns))
        ),
        input_output_aliases=aliases,
        compiler_params=params(),
        cost_estimate=pl.CostEstimate(
            flops=2 * cap * 2 * width * columns, bytes_accessed=3 * 1024 * 1024, transcendentals=0
        ),
        name="out_part",
    )(chip, *operands)


def out_last_kernel(n_mine, chip_ref, cnt_ref, *refs):
    x_refs = refs[: 2 * n_mine]
    w_ref, sum_ref, stat_ref, pos_ref, flag_ref, hid_ref, out_ref, update_ref = refs[2 * n_mine :]
    step = pl.program_id(0)
    block = hid_ref.shape[0]

    @pl.when(step == 0)
    def _():
        mine, twin = joined(x_refs[:n_mine]), joined(x_refs[n_mine:])
        projected = sum_ref[...] + out_term(mine, twin, w_ref)
        update_ref[...] = (stat_ref[:, 128:129] * projected).astype(BF16)

    own = lax.axis_index("ctx")
    shards = lax.axis_size("ctx")
    tok = block * pl.num_programs(0)
    row = live_row(pos_ref, cnt_ref, own, shards * tok) - own * tok - step * block
    hot = (lax.broadcasted_iota(jnp.int32, (block, row.shape[1]), 0) == row).astype(F32).astype(BF16)
    placed = jnp.dot(hot, update_ref[...], preferred_element_type=F32)
    flag = jnp.transpose(jnp.broadcast_to(flag_ref[pl.ds(step, 1), :].astype(F32), (128, block)))[:, :1]
    out_ref[...] = (hid_ref[...].astype(F32) + flag * placed).astype(BF16)


def out_last(chip, counts, pair, w_out, total, stat, positions, flags, hidden):
    mine, twin = pair
    cap = sum(x.shape[0] for x in mine)
    width = mine[0].shape[1]
    tok, columns = hidden.shape
    steps = 4
    block = tok // steps
    flags = flags.reshape(steps, block)
    specs = [fixed(x.shape) for x in (*mine, *twin)]
    specs += [pl.BlockSpec((2 * width, columns), lambda i, chip, cnt: (chip[0], 0))]
    specs += [fixed(a.shape) for a in (total, stat, positions, flags)]
    rows = pl.BlockSpec((block, columns), lambda i, chip, cnt: (i, 0))
    return pl.pallas_call(
        functools.partial(out_last_kernel, len(mine)),
        out_shape=jax.ShapeDtypeStruct((tok, columns), BF16),
        grid_spec=pltpu.PrefetchScalarGridSpec(
            num_scalar_prefetch=2,
            grid=(steps,),
            in_specs=specs + [rows],
            out_specs=rows,
            scratch_shapes=[pltpu.VMEM((cap, columns), BF16)],
        ),
        compiler_params=params(),
        name="out_last",
    )(chip, counts, *mine, *twin, w_out, total, stat, positions, flags, hidden)


def angles(row_pos):
    half = HEAD_SIZE // 2
    frequency = ROPE_BASE ** (-(jnp.arange(half, dtype=F32) * 2.0 / HEAD_SIZE))
    turned = row_pos.astype(F32) * jnp.concatenate([frequency, frequency])[None, :]
    sign = jnp.concatenate([-jnp.ones((half,), F32), jnp.ones((half,), F32)])
    return jnp.cos(turned), jnp.sin(turned) * sign[None, :]


def body(
    size,
    hidden_in,
    norm_gain,
    router_weight,
    w_query,
    w_key,
    value_weight,
    w_out,
    keep_flags,
    keep_counts,
    keep_positions,
):
    shards = lax.axis_size("ctx")
    tok = hidden_in.shape[0]
    z = lax.axis_index("heads") // 2
    chips = [jnp.reshape(c, (1,)).astype(jnp.int32) for c in (z, 3 - z, z ^ 1, z ^ 2)]
    gain = norm_gain.reshape(1, -1)
    router = router_weight.reshape(1, -1)

    full, first, second, rowpos = pick(keep_counts, keep_positions, hidden_in)
    cos, sin = angles(rowpos)
    pairs = spread(size, full, first, second)
    sums = None
    for chip, pair in zip(chips[:3], pairs[:3]):
        sums = qkv_part(chip, pair, gain, router, w_query, w_key, value_weight, sums)
    kv, stat = kv_last(chips[3], pairs[3], gain, router, w_key, value_weight, sums[0], cos, sin)
    ring = [(s, (s + 1) % shards) for s in range(shards)]
    moved = lax.ppermute(kv, "ctx", ring) if shards > 1 else kv
    q, *carry = q_last(
        chips[3], keep_counts, pairs[3], gain, w_query, sums[1], stat, cos, sin, kv, keep_positions, rowpos, tok
    )
    for step in range(1, shards):
        last = step == shards - 1
        carry = attend_more(step, last, tok, keep_counts, q, moved, keep_positions, rowpos, carry)
        if not last:
            moved = lax.ppermute(moved, "ctx", ring)
    pairs = spread(size, *carry)
    total = None
    for chip, pair in zip(chips[:3], pairs[:3]):
        total = out_part(chip, pair, w_out, total)
    return out_last(
        chips[3], keep_counts, pairs[3], w_out, total, stat, keep_positions, keep_flags, hidden_in
    )


def solution(mesh):
    in_specs = (
        P(("groups", "ctx"), "heads"),
        P(),
        P(),
        P(None, "heads"),
        P(None, "heads"),
        P(None, "heads"),
        P(None, "heads"),
        P(("groups", "ctx")),
        P("groups"),
        P("groups", None),
    )
    out_specs = P(("groups", "ctx"), "heads")
    return jax.shard_map(
        functools.partial(body, mesh.shape["heads"]),
        mesh=mesh,
        in_specs=in_specs,
        out_specs=out_specs,
        check_vma=False,
    )
```

time: 110 us -> 79.2 us (0.72)
  waiting for transfers between devices: 59.8 us -> 26.2 us
  starting transfers between devices: 0.08 us -> 22 us
  Pallas kernels: 0 us -> 13.9 us
  between operations: 13.6 us -> 0.28 us
  other arithmetic: 12.2 us -> 1.22 us
  local copies, waits for them, and re-layouts: 4.73 us -> 15.1 us
  blocking collectives: 9.89 us -> 0 us
  matrix products: 9.18 us -> 0 us
    all_gather x2 -> x0, waiting for transfers between devices: 59.8 us -> none  [the longest x1 31.1 us: attend_rows(): widened = lax.all_gather(row_block, 'heads', axis=1, tiled=True)]
    ppermute x0 -> x23, waiting for transfers between devices: none -> 26.2 us  [the longest x4 11.8 us: spread(): far_a, far_b = (cross(first), cross(second))]
    ppermute x0 -> x23, starting transfers between devices: none -> 22 us  [the longest x4 9.01 us: spread(): far_a, far_b = (cross(first), cross(second))]
    unnamed x21 -> x36, local copies, waits for them, and re-layouts: 0.94 us -> 15.1 us
    pallas_call x0 -> x11, Pallas kernels: none -> 13.9 us  [the longest x1 3.27 us: attend_more(): pl.pallas_call(functools.partial(attend_kernel, step, last, tok), out_sha...]
    all_gather x2 -> x0, blocking collectives: 9.89 us -> none  [the longest x1 4.94 us: attend_rows(): value_part = lax.all_gather(value_row_block, 'ctx', axis=0, tiled=True)]
    dot_general x6 -> x0, matrix products: 9.18 us -> none  [the longest x1 4.08 us: attend_rows(): jnp.dot(lax.all_gather(attn, 'heads', axis=1, tiled=True), w_out, preferr...]
    scatter-add x1 -> x0, other arithmetic: 3.51 us -> none  [body(): scattered = jnp.zeros((tok_local, hidden_in.shape[1]), jnp.float32).at[ta...]
  transfers between devices with their start and end apart: 2 -> 23, of which waited for: 2 -> 10; matrix products, arithmetic and copies ran while one was open for 1% -> 2% of each run, Pallas kernels for 0% -> 7%
where the time goes in v1:
time: 79.2 us; the launch traced here: 78.6 us
  waiting for transfers between devices  26.2 us (33%)
  starting transfers between devices  22 us (28%)
  local copies, waits for them, and re-layouts  15.1 us (19%)
  Pallas kernels  13.9 us (18%)
  other arithmetic  1.22 us (2%)
    unnamed x36, local copies, waits for them, and re-layouts  15.1 us
    ppermute x4, waiting for transfers between devices, spread(): far_a, far_b = (cross(first), cross(second))  11.8 us
    ppermute x4, starting transfers between devices, spread(): far_a, far_b = (cross(first), cross(second))  9.01 us
    ppermute x4, waiting for transfers between devices, spread(): last_a, last_b = (near(far_a), near(far_b))  8.91 us
    ppermute x4, starting transfers between devices, spread(): last_a, last_b = (near(far_a), near(far_b))  8.64 us
    pallas_call x1, Pallas kernels, attend_more(): pl.pallas_call(functools.partial(attend_kernel, step, last, tok), out_sha...  3.27 us
    pallas_call x1, Pallas kernels, out_last(): pl.pallas_call(functools.partial(out_last_kernel, len(mine)), out_shape=j...  3.15 us
    ppermute x2, waiting for transfers between devices, spread(): beside = near(full)  2.99 us
  transfers between devices with their start and end apart: 23, of which 10 were waited for; matrix products, arithmetic and copies ran while one was open for 2% of the time, Pallas kernels for 7%

profile of v1, /device:TPU:0, one launch (start us, length us, event | category | flops | bytes accessed | tf_op | source)
XLA Modules:
  0.0 78.6 jit_solution(17103885346913543926)
XLA Ops:
  0.0 1.3 %copy-done.8 = bf16[1024,512]{1,0:T(8,128)(2,1)S(1)} copy-done((bf16[1024,512]{1,0:T(8,128)(2,1)S(1)}, bf16[1024,512]{1,0:T(8,128)(2,1)}, u32[]{:S(2)}) %copy-start.8) | copy-done | bytes 1048600
  1.3 0.7 copy-done.13
  2.0 0.7 copy-done.15
  2.7 1.2 %pick.1 = (bf16[256,512]{1,0:T(8,128)(2,1)S(1)}, bf16[128,512]{1,0:T(8,128)(2,1)S(1)}, bf16[128,512]{1,0:T(8,128)(2,1)S(1)}, s32[256,128]{1,0:T(8,128)S(1)}) custom-call(s32[2]{0:T(128)S(1)} %copy-done.15, s32[2,256]{1,0:T(2,128)S(1)} %copy-done.13, bf16[1024,512]{1,0:T(8,128)(2,1)S(1)} %copy-done.8), custom_call_target="tpu_custom_call" | custom-call | tf_op jit(solution)/shard_map/pick/pallas_call | solution.py:55
  3.9 5.1 %collective-permute-start = (bf16[128,512]{1,0:T(8,128)(2,1)S(1)}, bf16[128,512]{1,0:T(8,128)(2,1)S(1)}, u32[]{:S(2)}, u32[]{:S(2)}) collective-permute-start(bf16[128,512]{1,0:T(8,128)(2,1)S(1)} %get-tuple-element.24), channel_id=1, source_target_pairs={{0,6},{1,7},{2,4},{3,5},{4,2},{5,3},{6,0},{7,1},{8,14},{9,15},{10,... | collective-permute-start | bytes 393224 | tf_op jit(solution)/shard_map/ppermute | solution.py:80
  9.0 0.1 collective-permute-start.2
  9.1 3.8 %collective-permute-done.refs_0_ = bf16[128,512]{1,0:T(8,128)(2,1)S(1)} collective-permute-done((bf16[128,512]{1,0:T(8,128)(2,1)S(1)}, bf16[128,512]{1,0:T(8,128)(2,1)S(1)}, u32[]{:S(2)}, u32[]{:S(2)}) %collective-permute-start) | collective-permute-done | bytes 131104 | tf_op jit(solution)/shard_map/ppermute | solution.py:80
  12.9 5.9 %collective-permute-start.1 = (bf16[128,512]{1,0:T(8,128)(2,1)S(1)}, bf16[128,512]{1,0:T(8,128)(2,1)S(1)}, u32[]{:S(2)}, u32[]{:S(2)}) collective-permute-start(bf16[128,512]{1,0:T(8,128)(2,1)S(1)} %collective-permute-done.refs_0_), channel_id=1, source_target_pairs={{0,2},{1,3},{2,0},{3,1},{4,6},{5,7},{6,4},{7,5},{8,10},{9,11},{10,... | collective-permute-start | bytes 393224 | tf_op jit(solution)/shard_map/ppermute | solution.py:85
  18.8 1.8 %collective-permute-start.3 = (bf16[128,512]{1,0:T(8,128)(2,1)S(1)}, bf16[128,512]{1,0:T(8,128)(2,1)S(1)}, u32[]{:S(2)}, u32[]{:S(2)}) collective-permute-start(bf16[128,512]{1,0:T(8,128)(2,1)S(1)} %collective-permute-done.2.refs_1_), channel_id=1, source_target_pairs={{0,2},{1,3},{2,0},{3,1},{4,6},{5,7},{6,4},{7,5},{8,10},{9,11},{10,... | collective-permute-start | bytes 393224 | tf_op jit(solution)/shard_map/ppermute | solution.py:85
  20.6 0.1 pad_maximum_fusion
  20.7 0.5 collective-permute-start.9
  21.2 0.1 collective-permute-done.6.refs_0_
  21.3 2.8 %collective-permute-done.1.refs_0_ = bf16[128,512]{1,0:T(8,128)(2,1)S(1)} collective-permute-done((bf16[128,512]{1,0:T(8,128)(2,1)S(1)}, bf16[128,512]{1,0:T(8,128)(2,1)S(1)}, u32[]{:S(2)}, u32[]{:S(2)}) %collective-permute-start.1) | collective-permute-done | bytes 131104 | tf_op jit(solution)/shard_map/ppermute | solution.py:85
  24.1 2.5 %collective-permute-done.3.refs_1_ = bf16[128,512]{1,0:T(8,128)(2,1)S(1)} collective-permute-done((bf16[128,512]{1,0:T(8,128)(2,1)S(1)}, bf16[128,512]{1,0:T(8,128)(2,1)S(1)}, u32[]{:S(2)}, u32[]{:S(2)}) %collective-permute-start.3) | collective-permute-done | bytes 131104 | tf_op jit(solution)/shard_map/ppermute | solution.py:85
  26.6 0.1 collective-permute-start.5
  26.7 1.1 %sine_multiply_fusion = (f32[256,128]{1,0:T(8,128)S(1)}, f32[256,128]{1,0:T(8,128)S(1)}) fusion(s32[256,128]{1,0:T(8,128)S(1)} %get-tuple-element.33.refs_12_.rowpos_ref, f32[128]{0:T(128)} %constant.31.clone.1, f32[128]{0:T(128)S(1)} %pad_maximum_fusion), kind=kLoop, calls=%fused_computation | loop fusion | flops 98304 | bytes 394240 | tf_op jit(solution)/shard_map/mul | solution.py:471
  27.9 2.2 %copy-done = bf16[4096,512]{1,0:T(8,128)(2,1)S(1)} copy-done((bf16[4096,512]{1,0:T(8,128)(2,1)S(1)}, bf16[4096,512]{1,0:T(8,128)(2,1)}, u32[]{:S(2)}) %copy-start) | copy-done | bytes 4194328
  30.0 1.2 %copy-done.4 = bf16[4096,128]{1,0:T(8,128)(2,1)S(1)} copy-done((bf16[4096,128]{1,0:T(8,128)(2,1)S(1)}, bf16[4096,128]{1,0:T(8,128)(2,1)}, u32[]{:S(2)}) %copy-start.4) | copy-done | bytes 1048600
  31.3 1.2 %copy-done.6 = bf16[4096,128]{1,0:T(8,128)(2,1)S(1)} copy-done((bf16[4096,128]{1,0:T(8,128)(2,1)S(1)}, bf16[4096,128]{1,0:T(8,128)(2,1)}, u32[]{:S(2)}) %copy-start.6) | copy-done | bytes 1048600
  32.5 0.7 copy-done.10
  33.2 0.7 copy-done.12
  33.9 0.8 qkv_part.3
  34.7 1.4 %copy-done.1 = bf16[4096,512]{1,0:T(8,128)(2,1)S(1)} copy-done((bf16[4096,512]{1,0:T(8,128)(2,1)S(1)}, bf16[4096,512]{1,0:T(8,128)(2,1)}, u32[]{:S(2)}) %copy-start.1) | copy-done | bytes 4194328
  36.1 0.3 copy-done.7
  36.4 0.8 %qkv_part.4 = (f32[256,512]{1,0:T(8,128)S(1)}, f32[256,512]{1,0:T(8,128)S(1)}) custom-call(s32[1]{0:T(128)} %bitcast.4.chip_ref, bf16[128,512]{1,0:T(8,128)(2,1)S(1)} %collective-permute-done.refs_0_, bf16[128,512]{1,0:T(8,128)(2,1)S(1)} %collective-permute-done.2.refs_1_, ...), custom_call_target="tpu_custom_call", output_to_operand_aliasing={{0}: (10, {}), {1}: (11, {})} | custom-call | flops 402653184 | bytes 4194304 | tf_op jit(solution)/shard_map/qkv_part/pallas_call | solution.py:183
  37.3 0.9 %qkv_part.5 = (f32[256,512]{1,0:T(8,128)S(1)}, f32[256,512]{1,0:T(8,128)S(1)}) custom-call(s32[1]{0:T(128)} %bitcast.2.chip_ref, bf16[256,512]{1,0:T(8,128)(2,1)S(1)} %collective-permute-done.6.refs_0_, bf16[256,512]{1,0:T(8,128)(2,1)S(1)} %collective-permute-done.7.refs_1_, f32[1,4096]{1,0:T(1,128)S(1)} %bitcast.8, ...), custom_call_target="tpu_custom_call", output_to_operand_aliasing={{0}: (8, {}), {1}: (9, {})} | custom-call | flops 402653184 | bytes 4194304 | tf_op jit(solution)/shard_map/qkv_part/pallas_call | solution.py:183
  38.2 0.5 kv_last.1
  38.8 1.5 %collective-permute-start.11 = (bf16[256,256]{1,0:T(8,128)(2,1)S(1)}, bf16[256,256]{1,0:T(8,128)(2,1)S(1)}, u32[]{:S(2)}, u32[]{:S(2)}) collective-permute-start(bf16[256,256]{1,0:T(8,128)(2,1)S(1)} %get-tuple-element.35.refs_10_), channel_id=1, source_target_pairs={{0,8},{8,0},{1,9},{9,1},{2,10},{10,2},{3,11},{11,3},{4,12},{12,4},... | collective-permute-start | bytes 393224 | tf_op jit(solution)/shard_map/ppermute | solution.py:502
  40.3 1.9 %q_last.1 = (bf16[256,512]{1,0:T(8,128)(2,1)S(1)}, f32[256,512]{1,0:T(8,128)S(1)}, f32[256,512]{1,0:T(8,128)S(1)}, f32[256,512]{1,0:T(8,128)S(1)}) custom-call(s32[1]{0:T(128)} %bitcast.chip_ref, s32[2]{0:T(128)S(1)} %copy-done.16, bf16[128,512]{1,0:T(8,128)(2,1)S(1)} %collective-permute-done.1.refs_0_, bf16[128,512]{1,0:T(8,128)(2,1)S(1)} %collective-permute-done.3.refs_1_, ...), custom_call_target="tpu_custom_call" | custom-call | tf_op jit(solution)/shard_map/q_last/pallas_call | solution.py:312
  42.2 2.5 %collective-permute-done.11.kv_ref = bf16[256,256]{1,0:T(8,128)(2,1)S(1)} collective-permute-done((bf16[256,256]{1,0:T(8,128)(2,1)S(1)}, bf16[256,256]{1,0:T(8,128)(2,1)S(1)}, u32[]{:S(2)}, u32[]{:S(2)}) %collective-permute-start.11) | collective-permute-done | bytes 131104 | tf_op jit(solution)/shard_map/ppermute | solution.py:502
  44.7 3.3 %attend_more.1 = (bf16[256,512]{1,0:T(8,128)(2,1)S(1)}, bf16[128,512]{1,0:T(8,128)(2,1)S(1)}, bf16[128,512]{1,0:T(8,128)(2,1)S(1)}) custom-call(s32[2]{0:T(128)S(1)} %copy-done.16, bf16[256,512]{1,0:T(8,128)(2,1)S(1)} %get-tuple-element.36.q_ref, bf16[256,256]{1,0:T(8,128)(2,1)S(1)} %collective-permute-done.11.kv_ref, s32[2,256]{1,0:T(2,128)S(1)} %copy-done.14, ...), custom_call_target="tpu_custom_call" | custom-call | tf_op jit(solution)/shard_map/attend_more/pallas_call | solution.py:362
  47.9 1.7 %collective-permute-start.18 = (bf16[256,512]{1,0:T(8,128)(2,1)S(1)}, bf16[256,512]{1,0:T(8,128)(2,1)S(1)}, u32[]{:S(2)}, u32[]{:S(2)}) collective-permute-start(bf16[256,512]{1,0:T(8,128)(2,1)S(1)} %get-tuple-element.42.refs_0_), channel_id=1, source_target_pairs={{0,2},{1,3},{2,0},{3,1},{4,6},{5,7},{6,4},{7,5},{8,10},{9,11},{10,... | collective-permute-start | bytes 786440 | tf_op jit(solution)/shard_map/ppermute | solution.py:82
  49.7 2.0 %collective-permute-start.12 = (bf16[128,512]{1,0:T(8,128)(2,1)S(1)}, bf16[128,512]{1,0:T(8,128)(2,1)S(1)}, u32[]{:S(2)}, u32[]{:S(2)}) collective-permute-start(bf16[128,512]{1,0:T(8,128)(2,1)S(1)} %get-tuple-element.40), channel_id=1, source_target_pairs={{0,6},{1,7},{2,4},{3,5},{4,2},{5,3},{6,0},{7,1},{8,14},{9,15},{10,... | collective-permute-start | bytes 393224 | tf_op jit(solution)/shard_map/ppermute | solution.py:80
  51.7 1.8 %collective-permute-start.14 = (bf16[128,512]{1,0:T(8,128)(2,1)S(1)}, bf16[128,512]{1,0:T(8,128)(2,1)S(1)}, u32[]{:S(2)}, u32[]{:S(2)}) collective-permute-start(bf16[128,512]{1,0:T(8,128)(2,1)S(1)} %get-tuple-element.41), channel_id=1, source_target_pairs={{0,6},{1,7},{2,4},{3,5},{4,2},{5,3},{6,0},{7,1},{8,14},{9,15},{10,... | collective-permute-start | bytes 393224 | tf_op jit(solution)/shard_map/ppermute | solution.py:80
  53.5 2.9 %collective-permute-done.18.refs_0_ = bf16[256,512]{1,0:T(8,128)(2,1)S(1)} collective-permute-done((bf16[256,512]{1,0:T(8,128)(2,1)S(1)}, bf16[256,512]{1,0:T(8,128)(2,1)S(1)}, u32[]{:S(2)}, u32[]{:S(2)}) %collective-permute-start.18) | collective-permute-done | bytes 262176 | tf_op jit(solution)/shard_map/ppermute | solution.py:82
  56.4 5.2 %collective-permute-done.12.refs_0_ = bf16[128,512]{1,0:T(8,128)(2,1)S(1)} collective-permute-done((bf16[128,512]{1,0:T(8,128)(2,1)S(1)}, bf16[128,512]{1,0:T(8,128)(2,1)S(1)}, u32[]{:S(2)}, u32[]{:S(2)}) %collective-permute-start.12) | collective-permute-done | bytes 131104 | tf_op jit(solution)/shard_map/ppermute | solution.py:80
  61.6 2.8 %collective-permute-done.14.refs_1_ = bf16[128,512]{1,0:T(8,128)(2,1)S(1)} collective-permute-done((bf16[128,512]{1,0:T(8,128)(2,1)S(1)}, bf16[128,512]{1,0:T(8,128)(2,1)S(1)}, u32[]{:S(2)}, u32[]{:S(2)}) %collective-permute-start.14) | collective-permute-done | bytes 131104 | tf_op jit(solution)/shard_map/ppermute | solution.py:80
  64.4 0.9 %collective-permute-start.15 = (bf16[128,512]{1,0:T(8,128)(2,1)S(1)}, bf16[128,512]{1,0:T(8,128)(2,1)S(1)}, u32[]{:S(2)}, u32[]{:S(2)}) collective-permute-start(bf16[128,512]{1,0:T(8,128)(2,1)S(1)} %collective-permute-done.14.refs_1_), channel_id=1, source_target_pairs={{0,2},{1,3},{2,0},{3,1},{4,6},{5,7},{6,4},{7,5},{8,10},{9,11},{10,... | collective-permute-start | bytes 393224 | tf_op jit(solution)/shard_map/ppermute | solution.py:85
  65.3 0.5 collective-permute-start.21
  65.8 1.3 %collective-permute-done.13.refs_0_ = bf16[128,512]{1,0:T(8,128)(2,1)S(1)} collective-permute-done((bf16[128,512]{1,0:T(8,128)(2,1)S(1)}, bf16[128,512]{1,0:T(8,128)(2,1)S(1)}, u32[]{:S(2)}, u32[]{:S(2)}) %collective-permute-start.13) | collective-permute-done | bytes 131104 | tf_op jit(solution)/shard_map/ppermute | solution.py:85
  67.1 2.3 %collective-permute-done.15.refs_1_ = bf16[128,512]{1,0:T(8,128)(2,1)S(1)} collective-permute-done((bf16[128,512]{1,0:T(8,128)(2,1)S(1)}, bf16[128,512]{1,0:T(8,128)(2,1)S(1)}, u32[]{:S(2)}, u32[]{:S(2)}) %collective-permute-start.15) | collective-permute-done | bytes 131104 | tf_op jit(solution)/shard_map/ppermute | solution.py:85
  69.4 2.2 %copy-done.2 = bf16[4096,512]{1,0:T(8,128)(2,1)S(1)} copy-done((bf16[4096,512]{1,0:T(8,128)(2,1)S(1)}, bf16[4096,512]{1,0:T(8,128)(2,1)}, u32[]{:S(2)}) %copy-start.2) | copy-done | bytes 4194328
  71.6 0.4 out_part.3.refs_5_
  72.1 1.7 %copy-done.3 = bf16[4096,512]{1,0:T(8,128)(2,1)S(1)} copy-done((bf16[4096,512]{1,0:T(8,128)(2,1)S(1)}, bf16[4096,512]{1,0:T(8,128)(2,1)}, u32[]{:S(2)}) %copy-start.3) | copy-done | bytes 4194328
  73.8 0.4 out_part.4.refs_3_
  74.3 0.5 out_part.5.refs_5_
  74.7 0.7 copy-done.9
  75.5 3.2 %out_last.1 = bf16[1024,512]{1,0:T(8,128)(2,1)} custom-call(s32[1]{0:T(128)} %bitcast.chip_ref, s32[2]{0:T(128)S(1)} %copy-done.16, bf16[128,512]{1,0:T(8,128)(2,1)S(1)} %collective-permute-done.13.refs_0_, bf16[128,512]{1,0:T(8,128)(2,1)S(1)} %collective-permute-done.15.refs_1_, bf16[128,512]{1,0:T(8,128)(2,1)S(1)} %collective-permute-done.16.refs_2_, ...), custom_call_target="tpu_custom_call" | custom-call | tf_op jit(solution)/shard_map/out_last/pallas_call | solution.py:451
  (49 shorter events, 0.1 us)
Async XLA Ops:
  0.0 34.7 %copy-start.5 = (bf16[4096,128]{1,0:T(8,128)(2,1)S(1)}, bf16[4096,128]{1,0:T(8,128)(2,1)}, u32[]{:S(2)}) copy-start(bf16[4096,128]{1,0:T(8,128)(2,1)} %refs_6_.7) | copy-start | bytes 3145732
  0.0 1.3 %copy-start.8 = (bf16[1024,512]{1,0:T(8,128)(2,1)S(1)}, bf16[1024,512]{1,0:T(8,128)(2,1)}, u32[]{:S(2)}) copy-start(bf16[1024,512]{1,0:T(8,128)(2,1)} %refs_9_.1) | copy-start | bytes 3145732
  1.3 0.7 copy-start.13
  2.0 0.7 copy-start.15
  3.9 9.0 %collective-permute-start = (bf16[128,512]{1,0:T(8,128)(2,1)S(1)}, bf16[128,512]{1,0:T(8,128)(2,1)S(1)}, u32[]{:S(2)}, u32[]{:S(2)}) collective-permute-start(bf16[128,512]{1,0:T(8,128)(2,1)S(1)} %get-tuple-element.24), channel_id=1, source_target_pairs={{0,6},{1,7},{2,4},{3,5},{4,2},{5,3},{6,0},{7,1},{8,14},{9,15},{10,... | collective-permute-start | bytes 393224 | tf_op jit(solution)/shard_map/ppermute | solution.py:80
  9.0 9.8 %collective-permute-start.2 = (bf16[128,512]{1,0:T(8,128)(2,1)S(1)}, bf16[128,512]{1,0:T(8,128)(2,1)S(1)}, u32[]{:S(2)}, u32[]{:S(2)}) collective-permute-start(bf16[128,512]{1,0:T(8,128)(2,1)S(1)} %get-tuple-element.25), channel_id=1, source_target_pairs={{0,6},{1,7},{2,4},{3,5},{4,2},{5,3},{6,0},{7,1},{8,14},{9,15},{10,... | collective-permute-start | bytes 393224 | tf_op jit(solution)/shard_map/ppermute | solution.py:80
  9.1 11.7 %collective-permute-start.10 = (bf16[256,512]{1,0:T(8,128)(2,1)S(1)}, bf16[256,512]{1,0:T(8,128)(2,1)S(1)}, u32[]{:S(2)}, u32[]{:S(2)}) collective-permute-start(bf16[256,512]{1,0:T(8,128)(2,1)S(1)} %get-tuple-element.26.refs_0_), channel_id=1, source_target_pairs={{0,1},{1,0},{2,3},{3,2},{4,5},{5,4},{6,7},{7,6},{8,9},{9,8},{10,11... | collective-permute-start | bytes 786440 | tf_op jit(solution)/shard_map/ppermute | solution.py:81
  9.1 12.2 %collective-permute-start.6 = (bf16[256,512]{1,0:T(8,128)(2,1)S(1)}, bf16[256,512]{1,0:T(8,128)(2,1)S(1)}, u32[]{:S(2)}, u32[]{:S(2)}) collective-permute-start(bf16[256,512]{1,0:T(8,128)(2,1)S(1)} %get-tuple-element.26.refs_0_), channel_id=1, source_target_pairs={{0,2},{1,3},{2,0},{3,1},{4,6},{5,7},{6,4},{7,5},{8,10},{9,11},{10,... | collective-permute-start | bytes 786440 | tf_op jit(solution)/shard_map/ppermute | solution.py:82
  12.9 11.2 %collective-permute-start.1 = (bf16[128,512]{1,0:T(8,128)(2,1)S(1)}, bf16[128,512]{1,0:T(8,128)(2,1)S(1)}, u32[]{:S(2)}, u32[]{:S(2)}) collective-permute-start(bf16[128,512]{1,0:T(8,128)(2,1)S(1)} %collective-permute-done.refs_0_), channel_id=1, source_target_pairs={{0,2},{1,3},{2,0},{3,1},{4,6},{5,7},{6,4},{7,5},{8,10},{9,11},{10,... | collective-permute-start | bytes 393224 | tf_op jit(solution)/shard_map/ppermute | solution.py:85
  18.8 7.8 %collective-permute-start.3 = (bf16[128,512]{1,0:T(8,128)(2,1)S(1)}, bf16[128,512]{1,0:T(8,128)(2,1)S(1)}, u32[]{:S(2)}, u32[]{:S(2)}) collective-permute-start(bf16[128,512]{1,0:T(8,128)(2,1)S(1)} %collective-permute-done.2.refs_1_), channel_id=1, source_target_pairs={{0,2},{1,3},{2,0},{3,1},{4,6},{5,7},{6,4},{7,5},{8,10},{9,11},{10,... | collective-permute-start | bytes 393224 | tf_op jit(solution)/shard_map/ppermute | solution.py:85
  20.7 14.0 %collective-permute-start.8 = (bf16[128,512]{1,0:T(8,128)(2,1)S(1)}, bf16[128,512]{1,0:T(8,128)(2,1)S(1)}, u32[]{:S(2)}, u32[]{:S(2)}) collective-permute-start(bf16[128,512]{1,0:T(8,128)(2,1)S(1)} %collective-permute-done.refs_0_), channel_id=1, source_target_pairs={{0,1},{1,0},{2,3},{3,2},{4,5},{5,4},{6,7},{7,6},{8,9},{9,8},{10,11... | collective-permute-start | bytes 393224 | tf_op jit(solution)/shard_map/ppermute | solution.py:83
  20.7 14.0 %collective-permute-start.9 = (bf16[128,512]{1,0:T(8,128)(2,1)S(1)}, bf16[128,512]{1,0:T(8,128)(2,1)S(1)}, u32[]{:S(2)}, u32[]{:S(2)}) collective-permute-start(bf16[128,512]{1,0:T(8,128)(2,1)S(1)} %collective-permute-done.2.refs_1_), channel_id=1, source_target_pairs={{0,1},{1,0},{2,3},{3,2},{4,5},{5,4},{6,7},{7,6},{8,9},{9,8},{10,11... | collective-permute-start | bytes 393224 | tf_op jit(solution)/shard_map/ppermute | solution.py:83
  21.3 15.9 %collective-permute-start.7 = (bf16[256,512]{1,0:T(8,128)(2,1)S(1)}, bf16[256,512]{1,0:T(8,128)(2,1)S(1)}, u32[]{:S(2)}, u32[]{:S(2)}) collective-permute-start(bf16[256,512]{1,0:T(8,128)(2,1)S(1)} %collective-permute-done.6.refs_0_), channel_id=1, source_target_pairs={{0,1},{1,0},{2,3},{3,2},{4,5},{5,4},{6,7},{7,6},{8,9},{9,8},{10,11... | collective-permute-start | bytes 786440 | tf_op jit(solution)/shard_map/ppermute | solution.py:84
  24.1 14.1 %collective-permute-start.4 = (bf16[128,512]{1,0:T(8,128)(2,1)S(1)}, bf16[128,512]{1,0:T(8,128)(2,1)S(1)}, u32[]{:S(2)}, u32[]{:S(2)}) collective-permute-start(bf16[128,512]{1,0:T(8,128)(2,1)S(1)} %collective-permute-done.1.refs_0_), channel_id=1, source_target_pairs={{0,1},{1,0},{2,3},{3,2},{4,5},{5,4},{6,7},{7,6},{8,9},{9,8},{10,11... | collective-permute-start | bytes 393224 | tf_op jit(solution)/shard_map/ppermute | solution.py:86
  26.6 11.6 %collective-permute-start.5 = (bf16[128,512]{1,0:T(8,128)(2,1)S(1)}, bf16[128,512]{1,0:T(8,128)(2,1)S(1)}, u32[]{:S(2)}, u32[]{:S(2)}) collective-permute-start(bf16[128,512]{1,0:T(8,128)(2,1)S(1)} %collective-permute-done.3.refs_1_), channel_id=1, source_target_pairs={{0,1},{1,0},{2,3},{3,2},{4,5},{5,4},{6,7},{7,6},{8,9},{9,8},{10,11... | collective-permute-start | bytes 393224 | tf_op jit(solution)/shard_map/ppermute | solution.py:86
  27.8 2.2 %copy-start = (bf16[4096,512]{1,0:T(8,128)(2,1)S(1)}, bf16[4096,512]{1,0:T(8,128)(2,1)}, u32[]{:S(2)}) copy-start(bf16[4096,512]{1,0:T(8,128)(2,1)} %refs_5_.5) | copy-start | bytes 12582916
  30.0 1.2 %copy-start.4 = (bf16[4096,128]{1,0:T(8,128)(2,1)S(1)}, bf16[4096,128]{1,0:T(8,128)(2,1)}, u32[]{:S(2)}) copy-start(bf16[4096,128]{1,0:T(8,128)(2,1)} %refs_6_.7) | copy-start | bytes 3145732
  31.3 1.2 %copy-start.6 = (bf16[4096,128]{1,0:T(8,128)(2,1)S(1)}, bf16[4096,128]{1,0:T(8,128)(2,1)}, u32[]{:S(2)}) copy-start(bf16[4096,128]{1,0:T(8,128)(2,1)} %refs_7_.4) | copy-start | bytes 3145732
  32.5 0.7 copy-start.10
  33.2 0.7 copy-start.12
  33.9 2.2 %copy-start.1 = (bf16[4096,512]{1,0:T(8,128)(2,1)S(1)}, bf16[4096,512]{1,0:T(8,128)(2,1)}, u32[]{:S(2)}) copy-start(bf16[4096,512]{1,0:T(8,128)(2,1)} %refs_5_.5) | copy-start | bytes 12582916
  33.9 2.5 %copy-start.7 = (bf16[4096,128]{1,0:T(8,128)(2,1)S(1)}, bf16[4096,128]{1,0:T(8,128)(2,1)}, u32[]{:S(2)}) copy-start(bf16[4096,128]{1,0:T(8,128)(2,1)} %refs_7_.4) | copy-start | bytes 3145732
  37.3 3.0 %copy-start.11 = (f32[4096]{0:T(1024)S(1)}, f32[4096]{0:T(1024)}, u32[]{:S(2)}) copy-start(f32[4096]{0:T(1024)} %param.11) | copy-start | bytes 49156
  37.3 3.0 %copy-start.14 = (s32[2,256]{1,0:T(2,128)S(1)}, s32[2,256]{1,0:T(2,128)}, u32[]{:S(2)}) copy-start(s32[2,256]{1,0:T(2,128)} %refs_7_.5) | copy-start | bytes 6148
  37.3 3.0 %copy-start.16 = (s32[2]{0:T(128)S(1)}, s32[2]{0:T(128)}, u32[]{:S(2)}) copy-start(s32[2]{0:T(128)} %cnt_ref.7) | copy-start | bytes 28
  38.8 30.6 %copy-start.17 = (s32[1024]{0:T(1024)S(1)}, s32[1024]{0:T(1024)}, u32[]{:S(2)}) copy-start(s32[1024]{0:T(1024)} %param.17) | copy-start | bytes 12292
  38.8 5.9 %collective-permute-start.11 = (bf16[256,256]{1,0:T(8,128)(2,1)S(1)}, bf16[256,256]{1,0:T(8,128)(2,1)S(1)}, u32[]{:S(2)}, u32[]{:S(2)}) collective-permute-start(bf16[256,256]{1,0:T(8,128)(2,1)S(1)} %get-tuple-element.35.refs_10_), channel_id=1, source_target_pairs={{0,8},{8,0},{1,9},{9,1},{2,10},{10,2},{3,11},{11,3},{4,12},{12,4},... | collective-permute-start | bytes 393224 | tf_op jit(solution)/shard_map/ppermute | solution.py:502
  47.9 8.5 %collective-permute-start.18 = (bf16[256,512]{1,0:T(8,128)(2,1)S(1)}, bf16[256,512]{1,0:T(8,128)(2,1)S(1)}, u32[]{:S(2)}, u32[]{:S(2)}) collective-permute-start(bf16[256,512]{1,0:T(8,128)(2,1)S(1)} %get-tuple-element.42.refs_0_), channel_id=1, source_target_pairs={{0,2},{1,3},{2,0},{3,1},{4,6},{5,7},{6,4},{7,5},{8,10},{9,11},{10,... | collective-permute-start | bytes 786440 | tf_op jit(solution)/shard_map/ppermute | solution.py:82
  49.7 15.6 %collective-permute-start.22 = (bf16[256,512]{1,0:T(8,128)(2,1)S(1)}, bf16[256,512]{1,0:T(8,128)(2,1)S(1)}, u32[]{:S(2)}, u32[]{:S(2)}) collective-permute-start(bf16[256,512]{1,0:T(8,128)(2,1)S(1)} %get-tuple-element.42.refs_0_), channel_id=1, source_target_pairs={{0,1},{1,0},{2,3},{3,2},{4,5},{5,4},{6,7},{7,6},{8,9},{9,8},{10,11... | collective-permute-start | bytes 786440 | tf_op jit(solution)/shard_map/ppermute | solution.py:81
  49.7 11.9 %collective-permute-start.12 = (bf16[128,512]{1,0:T(8,128)(2,1)S(1)}, bf16[128,512]{1,0:T(8,128)(2,1)S(1)}, u32[]{:S(2)}, u32[]{:S(2)}) collective-permute-start(bf16[128,512]{1,0:T(8,128)(2,1)S(1)} %get-tuple-element.40), channel_id=1, source_target_pairs={{0,6},{1,7},{2,4},{3,5},{4,2},{5,3},{6,0},{7,1},{8,14},{9,15},{10,... | collective-permute-start | bytes 393224 | tf_op jit(solution)/shard_map/ppermute | solution.py:80
  51.7 12.7 %collective-permute-start.14 = (bf16[128,512]{1,0:T(8,128)(2,1)S(1)}, bf16[128,512]{1,0:T(8,128)(2,1)S(1)}, u32[]{:S(2)}, u32[]{:S(2)}) collective-permute-start(bf16[128,512]{1,0:T(8,128)(2,1)S(1)} %get-tuple-element.41), channel_id=1, source_target_pairs={{0,6},{1,7},{2,4},{3,5},{4,2},{5,3},{6,0},{7,1},{8,14},{9,15},{10,... | collective-permute-start | bytes 393224 | tf_op jit(solution)/shard_map/ppermute | solution.py:80
  56.4 17.8 %collective-permute-start.19 = (bf16[256,512]{1,0:T(8,128)(2,1)S(1)}, bf16[256,512]{1,0:T(8,128)(2,1)S(1)}, u32[]{:S(2)}, u32[]{:S(2)}) collective-permute-start(bf16[256,512]{1,0:T(8,128)(2,1)S(1)} %collective-permute-done.18.refs_0_), channel_id=1, source_target_pairs={{0,1},{1,0},{2,3},{3,2},{4,5},{5,4},{6,7},{7,6},{8,9},{9,8},{10,11... | collective-permute-start | bytes 786440 | tf_op jit(solution)/shard_map/ppermute | solution.py:84
  61.6 5.5 %collective-permute-start.13 = (bf16[128,512]{1,0:T(8,128)(2,1)S(1)}, bf16[128,512]{1,0:T(8,128)(2,1)S(1)}, u32[]{:S(2)}, u32[]{:S(2)}) collective-permute-start(bf16[128,512]{1,0:T(8,128)(2,1)S(1)} %collective-permute-done.12.refs_0_), channel_id=1, source_target_pairs={{0,2},{1,3},{2,0},{3,1},{4,6},{5,7},{6,4},{7,5},{8,10},{9,11},{10,... | collective-permute-start | bytes 393224 | tf_op jit(solution)/shard_map/ppermute | solution.py:85
  64.4 5.0 %collective-permute-start.15 = (bf16[128,512]{1,0:T(8,128)(2,1)S(1)}, bf16[128,512]{1,0:T(8,128)(2,1)S(1)}, u32[]{:S(2)}, u32[]{:S(2)}) collective-permute-start(bf16[128,512]{1,0:T(8,128)(2,1)S(1)} %collective-permute-done.14.refs_1_), channel_id=1, source_target_pairs={{0,2},{1,3},{2,0},{3,1},{4,6},{5,7},{6,4},{7,5},{8,10},{9,11},{10,... | collective-permute-start | bytes 393224 | tf_op jit(solution)/shard_map/ppermute | solution.py:85
  65.3 6.8 %collective-permute-start.20 = (bf16[128,512]{1,0:T(8,128)(2,1)S(1)}, bf16[128,512]{1,0:T(8,128)(2,1)S(1)}, u32[]{:S(2)}, u32[]{:S(2)}) collective-permute-start(bf16[128,512]{1,0:T(8,128)(2,1)S(1)} %collective-permute-done.12.refs_0_), channel_id=1, source_target_pairs={{0,1},{1,0},{2,3},{3,2},{4,5},{5,4},{6,7},{7,6},{8,9},{9,8},{10,11... | collective-permute-start | bytes 393224 | tf_op jit(solution)/shard_map/ppermute | solution.py:83
  65.3 6.8 %collective-permute-start.21 = (bf16[128,512]{1,0:T(8,128)(2,1)S(1)}, bf16[128,512]{1,0:T(8,128)(2,1)S(1)}, u32[]{:S(2)}, u32[]{:S(2)}) collective-permute-start(bf16[128,512]{1,0:T(8,128)(2,1)S(1)} %collective-permute-done.14.refs_1_), channel_id=1, source_target_pairs={{0,1},{1,0},{2,3},{3,2},{4,5},{5,4},{6,7},{7,6},{8,9},{9,8},{10,11... | collective-permute-start | bytes 393224 | tf_op jit(solution)/shard_map/ppermute | solution.py:83
  67.1 7.6 %collective-permute-start.16 = (bf16[128,512]{1,0:T(8,128)(2,1)S(1)}, bf16[128,512]{1,0:T(8,128)(2,1)S(1)}, u32[]{:S(2)}, u32[]{:S(2)}) collective-permute-start(bf16[128,512]{1,0:T(8,128)(2,1)S(1)} %collective-permute-done.13.refs_0_), channel_id=1, source_target_pairs={{0,1},{1,0},{2,3},{3,2},{4,5},{5,4},{6,7},{7,6},{8,9},{9,8},{10,11... | collective-permute-start | bytes 393224 | tf_op jit(solution)/shard_map/ppermute | solution.py:86
  69.4 5.3 %collective-permute-start.17 = (bf16[128,512]{1,0:T(8,128)(2,1)S(1)}, bf16[128,512]{1,0:T(8,128)(2,1)S(1)}, u32[]{:S(2)}, u32[]{:S(2)}) collective-permute-start(bf16[128,512]{1,0:T(8,128)(2,1)S(1)} %collective-permute-done.15.refs_1_), channel_id=1, source_target_pairs={{0,1},{1,0},{2,3},{3,2},{4,5},{5,4},{6,7},{7,6},{8,9},{9,8},{10,11... | collective-permute-start | bytes 393224 | tf_op jit(solution)/shard_map/ppermute | solution.py:86
  69.4 2.2 %copy-start.2 = (bf16[4096,512]{1,0:T(8,128)(2,1)S(1)}, bf16[4096,512]{1,0:T(8,128)(2,1)}, u32[]{:S(2)}) copy-start(bf16[4096,512]{1,0:T(8,128)(2,1)} %refs_4_.7) | copy-start | bytes 12582916
  71.6 2.2 %copy-start.3 = (bf16[4096,512]{1,0:T(8,128)(2,1)S(1)}, bf16[4096,512]{1,0:T(8,128)(2,1)}, u32[]{:S(2)}) copy-start(bf16[4096,512]{1,0:T(8,128)(2,1)} %refs_4_.7) | copy-start | bytes 12582916
  74.2 1.2 %copy-start.9 = (bf16[1024,512]{1,0:T(8,128)(2,1)S(1)}, bf16[1024,512]{1,0:T(8,128)(2,1)}, u32[]{:S(2)}) copy-start(bf16[1024,512]{1,0:T(8,128)(2,1)} %refs_9_.1) | copy-start | bytes 3145732

commit v2 on v0

v2 whole, which is shorter than its diff:
```python
import functools

import jax
import jax.numpy as jnp
from jax import lax
from jax.experimental import pallas as pl
from jax.experimental.pallas import tpu as pltpu
from jax.sharding import PartitionSpec as P

HEAD_SIZE = 128
ROPE_BASE = 500000.0
NORM_EPS = 1e-05
LOG2E = 1.4426950408889634
VMEM_LIMIT = 24 * 1024 * 1024
F32 = jnp.float32
BF16 = jnp.bfloat16
I32 = jnp.int32
COST = 400_000_000
OWN_OUT = 400_000_000
FAR_OUT = 400_000_000
BESIDE_OUT = 400_000_000

VMEM = pl.BlockSpec(memory_space=pltpu.VMEM)
HBM = pl.BlockSpec(memory_space=pltpu.HBM)


def arr(shape, dtype):
    return jax.ShapeDtypeStruct(shape, dtype)


def call(kernel, name, operands, out_shape, scratch=(), rides=None, hbm=(), out_hbm=False, flops=COST):
    operands = [(o, any(o is h for h in hbm)) for o in operands]
    return pl.pallas_call(
        kernel,
        out_shape=out_shape,
        in_specs=[HBM if far else VMEM for _, far in operands],
        out_specs=[HBM if out_hbm else VMEM] * len(out_shape),
        scratch_shapes=list(scratch),
        input_output_aliases=rides or {},
        compiler_params=pltpu.CompilerParams(vmem_limit_bytes=VMEM_LIMIT),
        cost_estimate=pl.CostEstimate(flops=flops, bytes_accessed=1, transcendentals=0),
        name=name,
    )(*(pltpu.with_memory_space_constraint(o, pltpu.HBM) if far else o for o, far in operands))


def fetch(pairs, sems, base=0):
    copies = [pltpu.make_async_copy(src, dst, sems.at[base + i]) for i, (src, dst) in enumerate(pairs)]
    for copy in copies:
        copy.start()
    return copies


def place():
    d = lax.axis_index("heads")
    return d // 2, lax.rem(d, 2)


def live_row(pos_ref, cnt_ref, shard, dead):
    pos = pos_ref[pl.ds(shard, 1), :]
    slot = lax.broadcasted_iota(I32, pos.shape, 1)
    return jnp.where(slot < cnt_ref[shard], pos, dead)


def column(row):
    return jnp.transpose(jnp.broadcast_to(row, (128, row.shape[1])))


def pick_kernel(cnt_hbm, pos_hbm, hid_hbm, x_ref, xa_ref, xb_ref, rowpos_ref, cnt_ref, pos_ref, hid_ref, sems):
    copies = fetch([(cnt_hbm, cnt_ref), (pos_hbm, pos_ref), (hid_hbm, hid_ref)], sems)
    own, shards = lax.axis_index("ctx"), lax.axis_size("ctx")
    tok, cap = hid_ref.shape[0], x_ref.shape[0]
    copies[0].wait()
    copies[1].wait()
    rowpos = column(live_row(pos_ref, cnt_ref, own, shards * tok))
    rowpos_ref[...] = rowpos
    local = rowpos[:, :1] - own * tok
    hot = (lax.broadcasted_iota(I32, (cap, tok), 1) == local).astype(F32).astype(BF16)
    copies[2].wait()
    x = jnp.dot(hot, hid_ref[...], preferred_element_type=F32).astype(BF16)
    x_ref[...] = x
    xa_ref[...] = x[: cap // 2]
    xb_ref[...] = x[cap // 2 :]


def pick(counts, positions, hidden):
    cap, width = positions.shape[1], hidden.shape[1]
    return call(
        pick_kernel,
        "pick",
        (counts, positions, hidden),
        [arr((cap, width), BF16), arr((cap // 2, width), BF16), arr((cap // 2, width), BF16), arr((cap, 128), I32)],
        scratch=[
            pltpu.SMEM(counts.shape, I32),
            pltpu.VMEM(positions.shape, I32),
            pltpu.VMEM(hidden.shape, BF16),
            pltpu.SemaphoreType.DMA((3,)),
        ],
        hbm=(counts, positions, hidden),
    )


def sender(perm):
    return functools.partial(lax.ppermute, axis_name="heads", perm=perm)


def chip_sender(size, f):
    return sender([(2 * z + c, 2 * f(z) + c) for z in range(size // 2) for c in range(2)])


def spread(size, full, first, second, use_own, use_far, use_beside):
    cross = chip_sender(size, lambda z: 3 - z)
    near = chip_sender(size, lambda z: z ^ 1)
    twin = sender([(d, d ^ 1) for d in range(size)])
    far_a, far_b = cross(first), cross(second)
    mate = twin(full)
    full = use_own(full, mate)
    beside = near(full)
    last_a, last_b = near(far_a), near(far_b)
    last_a = use_far((far_a, far_b), (twin(far_a), twin(far_b)), last_a)
    use_beside((beside,), (twin(beside),))
    return last_a, last_b, twin(last_a), twin(last_b)


def joined(refs):
    parts = [ref[...] for ref in refs]
    return parts[0] if len(parts) == 1 else jnp.concatenate(parts, axis=0)


def lanes_sum(x):
    total = x[:, :128]
    for at in range(128, x.shape[1], 128):
        total = total + x[:, at : at + 128]
    return total


def halves(mine, twin, core):
    width = mine.shape[1]
    return [(x, pl.ds(pl.multiple_of(at * width, width), width)) for x, at in ((mine, core), (twin, 1 - core))]


def add(a, b):
    return b if a is None else a + b


def project(mine, twin, core, gain_ref, router_ref, w_ref, columns, stats=True):
    product = squares = routed = None
    for x, rows in halves(mine, twin, core):
        xf = x.astype(F32)
        gained = (xf * gain_ref[:, rows]).astype(BF16)
        product = add(product, jnp.dot(gained, w_ref[rows, columns], preferred_element_type=F32))
        if stats:
            squares = add(squares, lanes_sum(xf * xf))
            routed = add(routed, lanes_sum(xf * router_ref[:, rows]))
    return product, squares, routed


def block_copies(zz, gain, router, wq, wk, wv, gain_ref, router_ref, w_ref):
    depth = w_ref.shape[0]
    rows = pl.ds(pl.multiple_of(zz * depth, depth), depth)
    nq, nk = wq.shape[1], wk.shape[1]
    return [
        (gain.at[:, rows], gain_ref),
        (router.at[:, rows], router_ref),
        (wq.at[rows, :], w_ref.at[:, 0:nq]),
        (wk.at[rows, :], w_ref.at[:, nq : nq + nk]),
        (wv.at[rows, :], w_ref.at[:, nq + nk : nq + 2 * nk]),
    ]


def fetched(zz, weights, scratch, sems, base=0):
    return fetch(block_copies(zz, *weights, *scratch), sems, base)


def settle(copies):
    for copy in copies:
        copy.wait()


def own_kernel(x_ref, mate_ref, gain, router, wq, wk, wv, cnt_hbm, pos_hbm, flag_hbm, *refs):
    ride, sums_ref, bias_ref, hot_ref = refs[:4]
    gain_ref, router_ref, w_ref, cnt_ref, pos_ref, flag_ref, sems = refs[4:]
    zz, core = place()
    small = fetch([(cnt_hbm, cnt_ref), (pos_hbm, pos_ref), (flag_hbm, flag_ref)], sems, 5)
    copies = fetched(zz, (gain, router, wq, wk, wv), (gain_ref, router_ref, w_ref), sems)
    settle(small)
    own, shards = lax.axis_index("ctx"), lax.axis_size("ctx")
    tok = hot_ref.shape[0]
    seq = shards * tok
    row = live_row(pos_ref, cnt_ref, own, seq)
    for step in range(shards):
        source = lax.rem(own + shards - step, shards)
        keys = column(live_row(pos_ref, cnt_ref, source, seq + 1))[:, :1]
        bias_ref[step] = jnp.where(keys <= row, 0.0, -jnp.inf).astype(F32)
    flags = jnp.transpose(flag_ref[...].astype(F32))
    local = row - own * tok
    for r in range(tok // 128):
        at = lax.broadcasted_iota(I32, (128, row.shape[1]), 0) + r * 128
        hot = jnp.where(at == local, flags[:, r : r + 1], 0.0)
        hot_ref[r * 128 : (r + 1) * 128, :] = hot.astype(BF16)
    settle(copies)
    product, squares, routed = project(x_ref[...], mate_ref[...], core, gain_ref, router_ref, w_ref, slice(None))
    n = product.shape[1]
    sums_ref[:, 0:n] = product
    sums_ref[:, n : n + 128] = squares
    sums_ref[:, n + 128 : n + 256] = routed


def weight_scratch(depth, columns):
    return [pltpu.VMEM((1, depth), F32), pltpu.VMEM((1, depth), F32), pltpu.VMEM((depth, columns), BF16)]


def own_part(full, mate, weights, counts, positions, flags, tok):
    cap, width = full.shape
    columns = sum(w.shape[1] for w in weights[2:])
    shards = positions.shape[0]
    operands = (full, mate, *weights, counts, positions, flags)
    return call(
        own_kernel,
        "own_part",
        operands,
        [
            arr(full.shape, BF16),
            arr((cap, columns + 256), F32),
            arr((shards, cap, cap), F32),
            arr((tok, cap), BF16),
        ],
        scratch=weight_scratch(2 * width, columns)
        + [
            pltpu.SMEM(counts.shape, I32),
            pltpu.VMEM(positions.shape, I32),
            pltpu.VMEM(flags.shape, I32),
            pltpu.SemaphoreType.DMA((8,)),
        ],
        rides={0: 0},
        hbm=operands[2:],
    )


def more_kernel(n_mine, n_ride, flip, keep, *refs):
    mine, twin, refs = refs[:n_mine], refs[n_mine : 2 * n_mine], refs[2 * n_mine :]
    sums_in, refs = refs[0], refs[1 + n_ride :]
    weights, sums_out, refs = refs[:5], refs[5], refs[6 + n_ride :]
    kept, scratch, sems = refs[:-4], refs[-4:-1], refs[-1]
    z, core = place()
    copies = fetched(flip(z), weights, scratch, sems)
    later = fetched(z ^ 2, weights, kept, sems, 5) if keep else []
    settle(copies)
    product, squares, routed = project(joined(mine), joined(twin), core, *scratch, slice(None))
    n = product.shape[1]
    sums_out[:, 0:n] = sums_in[:, 0:n] + product
    sums_out[:, n : n + 128] = sums_in[:, n : n + 128] + squares
    sums_out[:, n + 128 : n + 256] = sums_in[:, n + 128 : n + 256] + routed
    settle(later)


def more_part(mine, twin, sums, rides, weights, flip, keep):
    width = mine[0].shape[1]
    depth, columns = 2 * width, sum(w.shape[1] for w in weights[2:])
    operands = (*mine, *twin, sums, *rides, *weights)
    at = 2 * len(mine)
    kept = [arr((1, depth), F32), arr((1, depth), F32), arr((depth, columns), BF16)] if keep else []
    return call(
        functools.partial(more_kernel, len(mine), len(rides), flip, keep),
        "more_part",
        operands,
        [arr(sums.shape, F32), *(arr(r.shape, BF16) for r in rides), *kept],
        scratch=weight_scratch(depth, columns) + [pltpu.SemaphoreType.DMA((10,))],
        rides={at + i: i for i in range(1 + len(rides))},
        hbm=weights,
    )


def turn(x, cos, sin):
    return x * cos + pltpu.roll(x, HEAD_SIZE // 2, 1) * sin


def kv_last_kernel(nq, features, a, b, c, d, gain_ref, router_ref, w_ref, sums, cos_ref, sin_ref, kv_out, stat_out):
    _, core = place()
    mine, twin = joined((a, b)), joined((c, d))
    n = w_ref.shape[1]
    product, squares, routed = project(mine, twin, core, gain_ref, router_ref, w_ref, slice(nq, n))
    squares = jnp.sum(sums[:, n : n + 128] + squares, axis=1, keepdims=True)
    routed = jnp.sum(sums[:, n + 128 : n + 256] + routed, axis=1, keepdims=True)
    inverse = lax.rsqrt(squares * (1.0 / features) + NORM_EPS)
    kv = (sums[:, nq:n] + product) * inverse
    kv_out[:, 0:128] = turn(kv[:, 0:128], cos_ref[...], sin_ref[...]).astype(BF16)
    kv_out[:, 128:256] = kv[:, 128:256].astype(BF16)
    stat_out[:, 0:128] = jnp.broadcast_to(inverse, (inverse.shape[0], 128))
    gate = 1.0 / (1.0 + jnp.exp(-routed))
    stat_out[:, 128:256] = jnp.broadcast_to(gate, (gate.shape[0], 128))


def kv_last(pair, kept, sums, cos, sin, nq, features):
    cap = sums.shape[0]
    return call(
        functools.partial(kv_last_kernel, nq, features),
        "kv_last",
        (*pair, *kept, sums, cos, sin),
        [arr((cap, 256), BF16), arr((cap, 256), F32)],
    )


def attend(q, kv, bias, carry):
    k, v = kv[:, 0:128], kv[:, 128:256]
    scale = LOG2E / HEAD_SIZE**0.5
    s = lax.dot_general(k, q, (((1,), (1,)), ((), ())), preferred_element_type=F32) * scale + bias
    top = jnp.max(s, axis=0, keepdims=True)
    if carry is not None:
        top = jnp.maximum(top, carry[0])
    e = jnp.exp2(s - top)
    total = jnp.sum(e, axis=0, keepdims=True)
    mix = lax.dot_general(v, e.astype(BF16), (((0,), (0,)), ((), ())), preferred_element_type=F32)
    if carry is not None:
        fade = jnp.exp2(carry[0] - top)
        total = total + carry[1] * fade
        mix = mix + carry[2] * fade
    return top, total, mix


def q_last_kernel(a, b, c, d, gain_ref, w_ref, sums, stat_ref, cos_ref, sin_ref, kv_ref, bias_ref, *outs):
    q_out, top_ref, total_ref, mix_ref = outs
    _, core = place()
    mine, twin = joined((a, b)), joined((c, d))
    nq, cap = q_out.shape[1], q_out.shape[0]
    product, _, _ = project(mine, twin, core, gain_ref, None, w_ref, slice(0, nq), stats=False)
    q = (sums[:, 0:nq] + product) * stat_ref[:, 0:1]
    cos, sin = cos_ref[...], sin_ref[...]
    for h in range(nq // HEAD_SIZE):
        lanes = slice(h * HEAD_SIZE, (h + 1) * HEAD_SIZE)
        turned = turn(q[:, lanes], cos, sin).astype(BF16)
        q_out[:, lanes] = turned
        top, total, mix = attend(turned, kv_ref[...], bias_ref[0], None)
        at = slice(h * cap, (h + 1) * cap)
        top_ref[:, at], total_ref[:, at], mix_ref[:, at] = top, total, mix


def carry_shapes(cap, nq):
    heads = nq // HEAD_SIZE
    return [arr((1, heads * cap), F32), arr((1, heads * cap), F32), arr((HEAD_SIZE, heads * cap), F32)]


def q_last(pair, kept, sums, stat, cos, sin, kv, bias, nq):
    cap = sums.shape[0]
    return call(
        q_last_kernel,
        "q_last",
        (*pair, kept[0], kept[2], sums, stat, cos, sin, kv, bias),
        [arr((cap, nq), BF16), *carry_shapes(cap, nq)],
    )


def attend_kernel(step, last, q_ref, kv_ref, bias_ref, top_in, total_in, mix_in, *outs):
    cap, nq = q_ref.shape
    for h in range(nq // HEAD_SIZE):
        lanes = slice(h * HEAD_SIZE, (h + 1) * HEAD_SIZE)
        at = slice(h * cap, (h + 1) * cap)
        carry = (top_in[:, at], total_in[:, at], mix_in[:, at])
        top, total, mix = attend(q_ref[:, lanes], kv_ref[...], bias_ref[step], carry)
        if not last:
            outs[0][:, at], outs[1][:, at], outs[2][:, at] = top, total, mix
            continue
        full, first, second = outs
        half = cap // 2
        attn = jnp.transpose(mix * (1.0 / total)).astype(BF16)
        full[:, lanes] = attn
        first[:, lanes] = attn[:half]
        second[:, lanes] = attn[half:]


def attend_more(step, last, q, kv, bias, carry):
    cap, nq = q.shape
    shapes = [arr((cap, nq), BF16), arr((cap // 2, nq), BF16), arr((cap // 2, nq), BF16)]
    return call(
        functools.partial(attend_kernel, step, last),
        "attend_more",
        (q, kv, bias, *carry),
        shapes if last else carry_shapes(cap, nq),
    )


def out_term(mine, twin, core, w_ref):
    out = None
    for x, rows in halves(mine, twin, core):
        out = add(out, jnp.dot(x, w_ref[rows, :], preferred_element_type=F32))
    return out


def w_rows(w, zz, depth):
    return w.at[pl.ds(pl.multiple_of(zz * depth, depth), depth), :]


def out_own_kernel(x_ref, mate_ref, w, ride, out_ref, w_ref, sems):
    z, core = place()
    settle(fetch([(w_rows(w, z, w_ref.shape[0]), w_ref)], sems))
    out_ref[...] = out_term(x_ref[...], mate_ref[...], core, w_ref)


def out_own(full, mate, w_out):
    (cap, width), columns = full.shape, w_out.shape[1]
    return call(
        out_own_kernel,
        "out_own",
        (full, mate, w_out),
        [arr(full.shape, BF16), arr((cap, columns), F32)],
        scratch=[pltpu.VMEM((2 * width, columns), BF16), pltpu.SemaphoreType.DMA((1,))],
        rides={0: 0},
        hbm=(w_out,),
        flops=OWN_OUT,
    )


def out_more_kernel(n_mine, n_ride, flip, keep, *refs):
    mine, twin, refs = refs[:n_mine], refs[n_mine : 2 * n_mine], refs[2 * n_mine :]
    total_in, refs = refs[0], refs[1 + n_ride :]
    w, refs = refs[0], refs[1:]
    hidden, refs = (refs[0], refs[1:]) if keep else (None, refs)
    total_out, refs = refs[0], refs[1 + n_ride :]
    w_ref, sems = refs[-2:]
    z, core = place()
    depth = w_ref.shape[0]
    copies = fetch([(w_rows(w, flip(z), depth), w_ref)], sems)
    later = fetch([(w_rows(w, z ^ 2, depth), refs[0]), (hidden, refs[1])], sems, 1) if keep else []
    settle(copies)
    total_out[...] = total_in[...] + out_term(joined(mine), joined(twin), core, w_ref)
    settle(later)


def out_more(mine, twin, total, rides, w_out, flip, hidden=None):
    width, columns = mine[0].shape[1], w_out.shape[1]
    keep = hidden is not None
    operands = (*mine, *twin, total, *rides, w_out) + ((hidden,) if keep else ())
    at = 2 * len(mine)
    kept = [arr((2 * width, columns), BF16), arr(hidden.shape, BF16)] if keep else []
    return call(
        functools.partial(out_more_kernel, len(mine), len(rides), flip, keep),
        "out_more",
        operands,
        [arr(total.shape, F32), *(arr(r.shape, BF16) for r in rides), *kept],
        scratch=[pltpu.VMEM((2 * width, columns), BF16), pltpu.SemaphoreType.DMA((3,))],
        rides={at + i: i for i in range(1 + len(rides))},
        hbm=(w_out, hidden) if keep else (w_out,),
        flops=BESIDE_OUT if keep else FAR_OUT,
    )


def out_last_kernel(a, b, c, d, w_ref, total_ref, stat_ref, hot_ref, hid_ref, out, out_ref, sems):
    _, core = place()
    projected = total_ref[...] + out_term(joined((a, b)), joined((c, d)), core, w_ref)
    update = (stat_ref[:, 128:129] * projected).astype(BF16)
    block = 256
    copies = []
    for i in range(hid_ref.shape[0] // block):
        rows = slice(i * block, (i + 1) * block)
        placed = jnp.dot(hot_ref[rows, :], update, preferred_element_type=F32)
        out_ref[rows, :] = (hid_ref[rows, :].astype(F32) + placed).astype(BF16)
        copies += fetch([(out_ref.at[rows, :], out.at[rows, :])], sems, i)
    settle(copies)


def out_last(pair, w_kept, total, stat, hot, hidden):
    return call(
        out_last_kernel,
        "out_last",
        (*pair, w_kept, total, stat, hot, hidden),
        [arr(hidden.shape, BF16)],
        scratch=[pltpu.VMEM(hidden.shape, BF16), pltpu.SemaphoreType.DMA((hidden.shape[0] // 256,))],
        out_hbm=True,
    )[0]


def angles(row_pos):
    half = HEAD_SIZE // 2
    frequency = ROPE_BASE ** (-(jnp.arange(half, dtype=F32) * 2.0 / HEAD_SIZE))
    turned = row_pos.astype(F32) * jnp.concatenate([frequency, frequency])[None, :]
    sign = jnp.concatenate([-jnp.ones((half,), F32), jnp.ones((half,), F32)])
    return jnp.cos(turned), jnp.sin(turned) * sign[None, :]


def body(
    size,
    hidden_in,
    norm_gain,
    router_weight,
    w_query,
    w_key,
    value_weight,
    w_out,
    keep_flags,
    keep_counts,
    keep_positions,
):
    shards = lax.axis_size("ctx")
    tok = hidden_in.shape[0]
    nq = w_query.shape[1]
    flags = keep_flags.reshape(-1, 128)
    weights = (norm_gain.reshape(1, -1), router_weight.reshape(1, -1), w_query, w_key, value_weight)

    full, first, second, rowpos = pick(keep_counts, keep_positions, hidden_in)
    cos, sin = angles(rowpos)
    held = {}

    def own(x, mate):
        x, held["sums"], held["bias"], held["hot"] = own_part(
            x, mate, weights, keep_counts, keep_positions, flags, tok
        )
        return x

    def far(mine, twin, ride):
        held["sums"], ride = more_part(mine, twin, held["sums"], (ride,), weights, lambda z: 3 - z, False)
        return ride

    def beside(mine, twin):
        held["sums"], *held["kept"] = more_part(mine, twin, held["sums"], (), weights, lambda z: z ^ 1, True)

    pair = spread(size, full, first, second, own, far, beside)
    sums, kept, bias = held["sums"], held["kept"], held["bias"]
    kv, stat = kv_last(pair, kept, sums, cos, sin, nq, norm_gain.shape[0])
    ring = [(s, (s + 1) % shards) for s in range(shards)]
    moved = lax.ppermute(kv, "ctx", ring)
    q, *carry = q_last(pair, kept, sums, stat, cos, sin, kv, bias, nq)
    for step in range(1, shards):
        last = step == shards - 1
        carry = attend_more(step, last, q, moved, bias, carry)
        if not last:
            moved = lax.ppermute(moved, "ctx", ring)

    def own_out(x, mate):
        x, held["total"] = out_own(x, mate, w_out)
        return x

    def far_out(mine, twin, ride):
        held["total"], ride = out_more(mine, twin, held["total"], (ride,), w_out, lambda z: 3 - z)
        return ride

    def beside_out(mine, twin):
        held["total"], held["w"], held["hidden"] = out_more(
            mine, twin, held["total"], (), w_out, lambda z: z ^ 1, hidden_in
        )

    pair = spread(size, *carry, own_out, far_out, beside_out)
    return out_last(pair, held["w"], held["total"], stat, held["hot"], held["hidden"])


def solution(mesh):
    in_specs = (
        P(("groups", "ctx"), "heads"),
        P(),
        P(),
        P(None, "heads"),
        P(None, "heads"),
        P(None, "heads"),
        P(None, "heads"),
        P(("groups", "ctx")),
        P("groups"),
        P("groups", None),
    )
    out_specs = P(("groups", "ctx"), "heads")
    return jax.shard_map(
        functools.partial(body, mesh.shape["heads"]),
        mesh=mesh,
        in_specs=in_specs,
        out_specs=out_specs,
        check_vma=False,
    )
```

time: 110 us -> 66.9 us (0.61)
  waiting for transfers between devices: 59.8 us -> 25.8 us
  starting transfers between devices: 0.08 us -> 21.4 us
  Pallas kernels: 0 us -> 18.7 us
  between operations: 13.6 us -> 0.19 us
  other arithmetic: 12.2 us -> 0.56 us
  blocking collectives: 9.89 us -> 0 us
  matrix products: 9.18 us -> 0 us
  local copies, waits for them, and re-layouts: 4.73 us -> 0.01 us
    all_gather x2 -> x0, waiting for transfers between devices: 59.8 us -> none  [the longest x1 31.1 us: attend_rows(): widened = lax.all_gather(row_block, 'heads', axis=1, tiled=True)]
    ppermute x0 -> x23, waiting for transfers between devices: none -> 25.8 us  [the longest x4 12.2 us: spread(): far_a, far_b = (cross(first), cross(second))]
    ppermute x0 -> x23, starting transfers between devices: none -> 21.4 us  [the longest x4 8.63 us: spread(): last_a, last_b = (near(far_a), near(far_b))]
    pallas_call x0 -> x11, Pallas kernels: none -> 18.7 us  [call(): pl.pallas_call(kernel, out_shape=out_shape, in_specs=[HBM if far else VME...]
    all_gather x2 -> x0, blocking collectives: 9.89 us -> none  [the longest x1 4.94 us: attend_rows(): value_part = lax.all_gather(value_row_block, 'ctx', axis=0, tiled=True)]
    dot_general x6 -> x0, matrix products: 9.18 us -> none  [the longest x1 4.08 us: attend_rows(): jnp.dot(lax.all_gather(attn, 'heads', axis=1, tiled=True), w_out, preferr...]
    scatter-add x1 -> x0, other arithmetic: 3.51 us -> none  [body(): scattered = jnp.zeros((tok_local, hidden_in.shape[1]), jnp.float32).at[ta...]
    gather x1 -> x0, local copies, waits for them, and re-layouts: 3.28 us -> none  [body(): picked = hidden_in[local_rows]]
  transfers between devices with their start and end apart: 2 -> 23, of which waited for: 2 -> 10; matrix products, arithmetic and copies ran while one was open for 1% -> 1% of each run, Pallas kernels for 0% -> 18%
where the time goes in v2:
time: 66.9 us; the launch traced here: 66.6 us
  waiting for transfers between devices  25.8 us (39%)
  starting transfers between devices  21.4 us (32%)
  Pallas kernels  18.7 us (28%)
    pallas_call x11, Pallas kernels, call(): pl.pallas_call(kernel, out_shape=out_shape, in_specs=[HBM if far else VME...  18.7 us
    ppermute x4, waiting for transfers between devices, spread(): far_a, far_b = (cross(first), cross(second))  12.2 us
    ppermute x4, waiting for transfers between devices, spread(): last_a, last_b = (near(far_a), near(far_b))  8.71 us
    ppermute x4, starting transfers between devices, spread(): last_a, last_b = (near(far_a), near(far_b))  8.63 us
    ppermute x4, starting transfers between devices, spread(): far_a, far_b = (cross(first), cross(second))  8.59 us
    ppermute x1, waiting for transfers between devices, body(): moved = lax.ppermute(kv, 'ctx', ring)  2.6 us
    ppermute x1, starting transfers between devices, body(): moved = lax.ppermute(kv, 'ctx', ring)  1.56 us
    ppermute x2, waiting for transfers between devices, spread(): mate = twin(full)  1.52 us
  transfers between devices with their start and end apart: 23, of which 10 were waited for; matrix products, arithmetic and copies ran while one was open for 1% of the time, Pallas kernels for 18%

profile of v2, /device:TPU:0, one launch (start us, length us, event | category | flops | bytes accessed | tf_op | source)
XLA Modules:
  0.0 66.6 jit_solution(10253060223505807160)
XLA Ops:
  0.0 1.7 %pick.1 = (bf16[256,512]{1,0:T(8,128)(2,1)S(1)}, bf16[128,512]{1,0:T(8,128)(2,1)S(1)}, bf16[128,512]{1,0:T(8,128)(2,1)S(1)}, s32[256,128]{1,0:T(8,128)S(1)}) custom-call(s32[2]{0:T(128)} %cnt_hbm.3, s32[2,256]{1,0:T(2,128)} %pos_hbm.3, bf16[1024,512]{1,0:T(8,128)(2,1)} %refs_4_.1), custom_call_target="tpu_custom_call" | custom-call | flops 400000000 | bytes 1 | tf_op jit(solution)/shard_map/pick/pallas_call | solution.py:33
  1.7 0.5 collective-permute-start.4
  2.2 4.7 %collective-permute-start = (bf16[128,512]{1,0:T(8,128)(2,1)S(1)}, bf16[128,512]{1,0:T(8,128)(2,1)S(1)}, u32[]{:S(2)}, u32[]{:S(2)}) collective-permute-start(bf16[128,512]{1,0:T(8,128)(2,1)S(1)} %get-tuple-element.35), channel_id=1, source_target_pairs={{0,6},{1,7},{2,4},{3,5},{4,2},{5,3},{6,0},{7,1},{8,14},{9,15},{10,... | collective-permute-start | bytes 393224 | tf_op jit(solution)/shard_map/ppermute | solution.py:114
  6.9 0.1 collective-permute-start.1
  7.0 0.0 collective-permute-done.4.mate_ref
  7.0 2.1 %own_part.1 = (bf16[256,512]{1,0:T(8,128)(2,1)S(1)}, f32[256,1024]{1,0:T(8,128)S(1)}, f32[2,256,256]{2,1,0:T(8,128)S(1)}, bf16[1024,256]{1,0:T(8,128)(2,1)S(1)}) custom-call(bf16[256,512]{1,0:T(8,128)(2,1)S(1)} %get-tuple-element.37.x_ref, bf16[256,512]{1,0:T(8,128)(2,1)S(1)} %collective-permute-done.4.mate_ref, ...), custom_call_target="tpu_custom_call", output_to_operand_aliasing={{0}: (0, {})} | custom-call | flops 400000000 | bytes 1 | tf_op jit(solution)/shard_map/own_part/pallas_call | solution.py:33
  9.1 0.0 copy-start
  9.1 0.1 collective-permute-start.9
  9.2 1.9 %collective-permute-done.refs_0_ = bf16[128,512]{1,0:T(8,128)(2,1)S(1)} collective-permute-done((bf16[128,512]{1,0:T(8,128)(2,1)S(1)}, bf16[128,512]{1,0:T(8,128)(2,1)S(1)}, u32[]{:S(2)}, u32[]{:S(2)}) %collective-permute-start) | collective-permute-done | bytes 131104 | tf_op jit(solution)/shard_map/ppermute | solution.py:114
  11.1 0.0 collective-permute-start.2
  11.1 5.7 %collective-permute-start.5 = (bf16[128,512]{1,0:T(8,128)(2,1)S(1)}, bf16[128,512]{1,0:T(8,128)(2,1)S(1)}, u32[]{:S(2)}, u32[]{:S(2)}) collective-permute-start(bf16[128,512]{1,0:T(8,128)(2,1)S(1)} %collective-permute-done.refs_0_), channel_id=1, source_target_pairs={{0,2},{1,3},{2,0},{3,1},{4,6},{5,7},{6,4},{7,5},{8,10},{9,11},{10,... | collective-permute-start | bytes 393224 | tf_op jit(solution)/shard_map/ppermute | solution.py:118
  16.8 0.2 collective-permute-start.3
  17.0 2.2 %collective-permute-start.6 = (bf16[128,512]{1,0:T(8,128)(2,1)S(1)}, bf16[128,512]{1,0:T(8,128)(2,1)S(1)}, u32[]{:S(2)}, u32[]{:S(2)}) collective-permute-start(bf16[128,512]{1,0:T(8,128)(2,1)S(1)} %collective-permute-done.1.refs_1_), channel_id=1, source_target_pairs={{0,2},{1,3},{2,0},{3,1},{4,6},{5,7},{6,4},{7,5},{8,10},{9,11},{10,... | collective-permute-start | bytes 393224 | tf_op jit(solution)/shard_map/ppermute | solution.py:118
  19.2 0.1 pad_maximum_fusion
  19.3 0.7 %collective-permute-done.9.refs_0_ = bf16[256,512]{1,0:T(8,128)(2,1)S(1)} collective-permute-done((bf16[256,512]{1,0:T(8,128)(2,1)S(1)}, bf16[256,512]{1,0:T(8,128)(2,1)S(1)}, u32[]{:S(2)}, u32[]{:S(2)}) %collective-permute-start.9) | collective-permute-done | bytes 262176 | tf_op jit(solution)/shard_map/ppermute | solution.py:117
  20.0 0.0 collective-permute-start.10
  20.0 0.0 collective-permute-done.2.refs_2_
  20.0 0.0 collective-permute-done.3.refs_3_
  20.0 2.8 %collective-permute-done.5.refs_5_ = bf16[128,512]{1,0:T(8,128)(2,1)S(1)} collective-permute-done((bf16[128,512]{1,0:T(8,128)(2,1)S(1)}, bf16[128,512]{1,0:T(8,128)(2,1)S(1)}, u32[]{:S(2)}, u32[]{:S(2)}) %collective-permute-start.5) | collective-permute-done | bytes 131104 | tf_op jit(solution)/shard_map/ppermute | solution.py:118
  22.8 2.1 %more_part.2 = (f32[256,1024]{1,0:T(8,128)S(1)}, bf16[128,512]{1,0:T(8,128)(2,1)S(1)}) custom-call(bf16[128,512]{1,0:T(8,128)(2,1)S(1)} %collective-permute-done.refs_0_, bf16[128,512]{1,0:T(8,128)(2,1)S(1)} %collective-permute-done.1.refs_1_, bf16[128,512]{1,0:T(8,128)(2,1)S(1)} %collective-permute-done.2.refs_2_, ...), custom_call_target="tpu_custom_call", output_to_operand_aliasing={{0}: (4, {}), {1}: (5, {})} | custom-call | flops 400000000 | bytes 1 | tf_op jit(solution)/shard_map/more_part/pallas_call | solution.py:33
  25.0 0.1 collective-permute-start.7
  25.0 0.5 collective-permute-done.6.b
  25.6 0.0 collective-permute-start.8
  25.6 0.5 sine_multiply_fusion
  26.0 0.0 collective-permute-done.10.refs_1_
  26.1 2.2 %more_part.3 = (f32[256,1024]{1,0:T(8,128)S(1)}, f32[1,1024]{1,0:T(1,128)S(1)}, f32[1,1024]{1,0:T(1,128)S(1)}, bf16[1024,768]{1,0:T(8,128)(2,1)S(1)}) custom-call(bf16[256,512]{1,0:T(8,128)(2,1)S(1)} %collective-permute-done.9.refs_0_, bf16[256,512]{1,0:T(8,128)(2,1)S(1)} %collective-permute-done.10.refs_1_, ...), custom_call_target="tpu_custom_call", output_to_operand_aliasing={{0}: (2, {})} | custom-call | flops 400000000 | bytes 1 | tf_op jit(solution)/shard_map/more_part/pallas_call | solution.py:33
  28.2 0.0 collective-permute-done.8.d
  28.2 0.4 kv_last.1
  28.7 1.6 %collective-permute-start.11 = (bf16[256,256]{1,0:T(8,128)(2,1)S(1)}, bf16[256,256]{1,0:T(8,128)(2,1)S(1)}, u32[]{:S(2)}, u32[]{:S(2)}) collective-permute-start(bf16[256,256]{1,0:T(8,128)(2,1)S(1)} %get-tuple-element.48.kv_ref), channel_id=1, source_target_pairs={{0,8},{8,0},{1,9},{9,1},{2,10},{10,2},{3,11},{11,3},{4,12},{12,4},... | collective-permute-start | bytes 393224 | tf_op jit(solution)/shard_map/ppermute | solution.py:519
  30.3 1.8 %q_last.1 = (bf16[256,512]{1,0:T(8,128)(2,1)S(1)}, f32[1,1024]{1,0:T(1,128)S(1)}, f32[1,1024]{1,0:T(1,128)S(1)}, f32[128,1024]{1,0:T(8,128)S(1)}) custom-call(bf16[128,512]{1,0:T(8,128)(2,1)S(1)} %get-tuple-element.39.a, bf16[128,512]{1,0:T(8,128)(2,1)S(1)} %collective-permute-done.6.b, bf16[128,512]{1,0:T(8,128)(2,1)S(1)} %collective-permute-done.7.c, ...), custom_call_target="tpu_custom_call" | custom-call | flops 400000000 | bytes 1 | tf_op jit(solution)/shard_map/q_last/pallas_call | solution.py:33
  32.1 2.6 %collective-permute-done.11.kv_ref = bf16[256,256]{1,0:T(8,128)(2,1)S(1)} collective-permute-done((bf16[256,256]{1,0:T(8,128)(2,1)S(1)}, bf16[256,256]{1,0:T(8,128)(2,1)S(1)}, u32[]{:S(2)}, u32[]{:S(2)}) %collective-permute-start.11) | collective-permute-done | bytes 131104 | tf_op jit(solution)/shard_map/ppermute | solution.py:519
  34.7 1.4 %attend_more.1 = (bf16[256,512]{1,0:T(8,128)(2,1)S(1)}, bf16[128,512]{1,0:T(8,128)(2,1)S(1)}, bf16[128,512]{1,0:T(8,128)(2,1)S(1)}) custom-call(bf16[256,512]{1,0:T(8,128)(2,1)S(1)} %get-tuple-element.50.q_ref, bf16[256,256]{1,0:T(8,128)(2,1)S(1)} %collective-permute-done.11.kv_ref, f32[2,256,256]{2,1,0:T(8,128)S(1)} %get-tuple-element.49.bias_ref, ...), custom_call_target="tpu_custom_call" | custom-call | flops 400000000 | bytes 1 | tf_op jit(solution)/shard_map/attend_more/pallas_call | solution.py:33
  36.1 0.1 collective-permute-start.16
  36.1 1.5 %collective-permute-done.16.mate_ref = bf16[256,512]{1,0:T(8,128)(2,1)S(1)} collective-permute-done((bf16[256,512]{1,0:T(8,128)(2,1)S(1)}, bf16[256,512]{1,0:T(8,128)(2,1)S(1)}, u32[]{:S(2)}, u32[]{:S(2)}) %collective-permute-start.16) | collective-permute-done | bytes 262176 | tf_op jit(solution)/shard_map/ppermute | solution.py:115
  37.7 1.7 %out_own.1 = (bf16[256,512]{1,0:T(8,128)(2,1)S(1)}, f32[256,512]{1,0:T(8,128)S(1)}) custom-call(bf16[256,512]{1,0:T(8,128)(2,1)S(1)} %get-tuple-element.56.x_ref, bf16[256,512]{1,0:T(8,128)(2,1)S(1)} %collective-permute-done.16.mate_ref, bf16[4096,512]{1,0:T(8,128)(2,1)} %refs_3_.1), custom_call_target="tpu_custom_call", output_to_operand_aliasing={{0}: (0, {})} | custom-call | flops 400000000 | bytes 1 | tf_op jit(solution)/shard_map/out_own/pallas_call | solution.py:33
  39.3 1.4 %collective-permute-start.21 = (bf16[256,512]{1,0:T(8,128)(2,1)S(1)}, bf16[256,512]{1,0:T(8,128)(2,1)S(1)}, u32[]{:S(2)}, u32[]{:S(2)}) collective-permute-start(bf16[256,512]{1,0:T(8,128)(2,1)S(1)} %get-tuple-element.59), channel_id=1, source_target_pairs={{0,2},{1,3},{2,0},{3,1},{4,6},{5,7},{6,4},{7,5},{8,10},{9,11},{10,... | collective-permute-start | bytes 786440 | tf_op jit(solution)/shard_map/ppermute | solution.py:117
  40.7 1.9 %collective-permute-start.13 = (bf16[128,512]{1,0:T(8,128)(2,1)S(1)}, bf16[128,512]{1,0:T(8,128)(2,1)S(1)}, u32[]{:S(2)}, u32[]{:S(2)}) collective-permute-start(bf16[128,512]{1,0:T(8,128)(2,1)S(1)} %get-tuple-element.55), channel_id=1, source_target_pairs={{0,6},{1,7},{2,4},{3,5},{4,2},{5,3},{6,0},{7,1},{8,14},{9,15},{10,... | collective-permute-start | bytes 393224 | tf_op jit(solution)/shard_map/ppermute | solution.py:114
  42.6 1.9 %collective-permute-start.12 = (bf16[128,512]{1,0:T(8,128)(2,1)S(1)}, bf16[128,512]{1,0:T(8,128)(2,1)S(1)}, u32[]{:S(2)}, u32[]{:S(2)}) collective-permute-start(bf16[128,512]{1,0:T(8,128)(2,1)S(1)} %get-tuple-element.54), channel_id=1, source_target_pairs={{0,6},{1,7},{2,4},{3,5},{4,2},{5,3},{6,0},{7,1},{8,14},{9,15},{10,... | collective-permute-start | bytes 393224 | tf_op jit(solution)/shard_map/ppermute | solution.py:114
  44.5 8.0 %collective-permute-done.13.refs_1_ = bf16[128,512]{1,0:T(8,128)(2,1)S(1)} collective-permute-done((bf16[128,512]{1,0:T(8,128)(2,1)S(1)}, bf16[128,512]{1,0:T(8,128)(2,1)S(1)}, u32[]{:S(2)}, u32[]{:S(2)}) %collective-permute-start.13) | collective-permute-done | bytes 131104 | tf_op jit(solution)/shard_map/ppermute | solution.py:114
  52.6 2.3 %collective-permute-done.12.refs_0_ = bf16[128,512]{1,0:T(8,128)(2,1)S(1)} collective-permute-done((bf16[128,512]{1,0:T(8,128)(2,1)S(1)}, bf16[128,512]{1,0:T(8,128)(2,1)S(1)}, u32[]{:S(2)}, u32[]{:S(2)}) %collective-permute-start.12) | collective-permute-done | bytes 131104 | tf_op jit(solution)/shard_map/ppermute | solution.py:114
  54.9 0.7 %collective-permute-start.17 = (bf16[128,512]{1,0:T(8,128)(2,1)S(1)}, bf16[128,512]{1,0:T(8,128)(2,1)S(1)}, u32[]{:S(2)}, u32[]{:S(2)}) collective-permute-start(bf16[128,512]{1,0:T(8,128)(2,1)S(1)} %collective-permute-done.12.refs_0_), channel_id=1, source_target_pairs={{0,2},{1,3},{2,0},{3,1},{4,6},{5,7},{6,4},{7,5},{8,10},{9,11},{10,... | collective-permute-start | bytes 393224 | tf_op jit(solution)/shard_map/ppermute | solution.py:118
  55.6 0.2 collective-permute-start.22
  55.9 3.0 %collective-permute-done.18.b = bf16[128,512]{1,0:T(8,128)(2,1)S(1)} collective-permute-done((bf16[128,512]{1,0:T(8,128)(2,1)S(1)}, bf16[128,512]{1,0:T(8,128)(2,1)S(1)}, u32[]{:S(2)}, u32[]{:S(2)}) %collective-permute-start.18) | collective-permute-done | bytes 131104 | tf_op jit(solution)/shard_map/ppermute | solution.py:118
  58.9 2.4 %collective-permute-done.17.refs_5_ = bf16[128,512]{1,0:T(8,128)(2,1)S(1)} collective-permute-done((bf16[128,512]{1,0:T(8,128)(2,1)S(1)}, bf16[128,512]{1,0:T(8,128)(2,1)S(1)}, u32[]{:S(2)}, u32[]{:S(2)}) %collective-permute-start.17) | collective-permute-done | bytes 131104 | tf_op jit(solution)/shard_map/ppermute | solution.py:118
  61.3 1.7 %out_more.2 = (f32[256,512]{1,0:T(8,128)S(1)}, bf16[128,512]{1,0:T(8,128)(2,1)S(1)}) custom-call(bf16[128,512]{1,0:T(8,128)(2,1)S(1)} %collective-permute-done.12.refs_0_, bf16[128,512]{1,0:T(8,128)(2,1)S(1)} %collective-permute-done.13.refs_1_, bf16[128,512]{1,0:T(8,128)(2,1)S(1)} %collective-permute-done.14.refs_2_, ...), custom_call_target="tpu_custom_call", output_to_operand_aliasing={{0}: (4, {}), {1}: (5, {})} | custom-call | flops 400000000 | bytes 1 | tf_op jit(solution)/shard_map/out_more/pallas_call | solution.py:33
  63.0 0.1 collective-permute-start.19
  63.1 1.9 %out_more.3 = (f32[256,512]{1,0:T(8,128)S(1)}, bf16[1024,512]{1,0:T(8,128)(2,1)S(1)}, bf16[1024,512]{1,0:T(8,128)(2,1)S(1)}) custom-call(bf16[256,512]{1,0:T(8,128)(2,1)S(1)} %collective-permute-done.21.refs_0_, bf16[256,512]{1,0:T(8,128)(2,1)S(1)} %collective-permute-done.22.refs_1_, ...), custom_call_target="tpu_custom_call", output_to_operand_aliasing={{0}: (2, {})} | custom-call | flops 400000000 | bytes 1 | tf_op jit(solution)/shard_map/out_more/pallas_call | solution.py:33
  65.0 1.7 %out_last.1 = bf16[1024,512]{1,0:T(8,128)(2,1)} custom-call(bf16[128,512]{1,0:T(8,128)(2,1)S(1)} %get-tuple-element.58.a, bf16[128,512]{1,0:T(8,128)(2,1)S(1)} %collective-permute-done.18.b, bf16[128,512]{1,0:T(8,128)(2,1)S(1)} %collective-permute-done.19.c, bf16[128,512]{1,0:T(8,128)(2,1)S(1)} %collective-permute-done.20.d, ...), custom_call_target="tpu_custom_call" | custom-call | flops 400000000 | bytes 1 | tf_op jit(solution)/shard_map/out_last/pallas_call | solution.py:33
  (14 shorter events, 0.0 us)
Async XLA Ops:
  1.7 5.3 %collective-permute-start.4 = (bf16[256,512]{1,0:T(8,128)(2,1)S(1)}, bf16[256,512]{1,0:T(8,128)(2,1)S(1)}, u32[]{:S(2)}, u32[]{:S(2)}) collective-permute-start(bf16[256,512]{1,0:T(8,128)(2,1)S(1)} %get-tuple-element.37.x_ref), channel_id=1, source_target_pairs={{0,1},{1,0},{2,3},{3,2},{4,5},{5,4},{6,7},{7,6},{8,9},{9,8},{10,11... | collective-permute-start | bytes 786440 | tf_op jit(solution)/shard_map/ppermute | solution.py:115
  2.2 8.9 %collective-permute-start = (bf16[128,512]{1,0:T(8,128)(2,1)S(1)}, bf16[128,512]{1,0:T(8,128)(2,1)S(1)}, u32[]{:S(2)}, u32[]{:S(2)}) collective-permute-start(bf16[128,512]{1,0:T(8,128)(2,1)S(1)} %get-tuple-element.35), channel_id=1, source_target_pairs={{0,6},{1,7},{2,4},{3,5},{4,2},{5,3},{6,0},{7,1},{8,14},{9,15},{10,... | collective-permute-start | bytes 393224 | tf_op jit(solution)/shard_map/ppermute | solution.py:114
  6.9 9.9 %collective-permute-start.1 = (bf16[128,512]{1,0:T(8,128)(2,1)S(1)}, bf16[128,512]{1,0:T(8,128)(2,1)S(1)}, u32[]{:S(2)}, u32[]{:S(2)}) collective-permute-start(bf16[128,512]{1,0:T(8,128)(2,1)S(1)} %get-tuple-element.36), channel_id=1, source_target_pairs={{0,6},{1,7},{2,4},{3,5},{4,2},{5,3},{6,0},{7,1},{8,14},{9,15},{10,... | collective-permute-start | bytes 393224 | tf_op jit(solution)/shard_map/ppermute | solution.py:114
  9.1 16.4 %copy-start = (f32[128]{0:T(128)S(1)}, f32[128]{0:T(128)}, u32[]{:S(2)}) copy-start(f32[128]{0:T(128)} %constant.9.clone.1) | copy-start | bytes 1540
  9.1 10.9 %collective-permute-start.9 = (bf16[256,512]{1,0:T(8,128)(2,1)S(1)}, bf16[256,512]{1,0:T(8,128)(2,1)S(1)}, u32[]{:S(2)}, u32[]{:S(2)}) collective-permute-start(bf16[256,512]{1,0:T(8,128)(2,1)S(1)} %get-tuple-element.40), channel_id=1, source_target_pairs={{0,2},{1,3},{2,0},{3,1},{4,6},{5,7},{6,4},{7,5},{8,10},{9,11},{10,... | collective-permute-start | bytes 786440 | tf_op jit(solution)/shard_map/ppermute | solution.py:117
  11.1 8.9 %collective-permute-start.2 = (bf16[128,512]{1,0:T(8,128)(2,1)S(1)}, bf16[128,512]{1,0:T(8,128)(2,1)S(1)}, u32[]{:S(2)}, u32[]{:S(2)}) collective-permute-start(bf16[128,512]{1,0:T(8,128)(2,1)S(1)} %collective-permute-done.refs_0_), channel_id=1, source_target_pairs={{0,1},{1,0},{2,3},{3,2},{4,5},{5,4},{6,7},{7,6},{8,9},{9,8},{10,11... | collective-permute-start | bytes 393224 | tf_op jit(solution)/shard_map/ppermute | solution.py:119
  11.1 11.7 %collective-permute-start.5 = (bf16[128,512]{1,0:T(8,128)(2,1)S(1)}, bf16[128,512]{1,0:T(8,128)(2,1)S(1)}, u32[]{:S(2)}, u32[]{:S(2)}) collective-permute-start(bf16[128,512]{1,0:T(8,128)(2,1)S(1)} %collective-permute-done.refs_0_), channel_id=1, source_target_pairs={{0,2},{1,3},{2,0},{3,1},{4,6},{5,7},{6,4},{7,5},{8,10},{9,11},{10,... | collective-permute-start | bytes 393224 | tf_op jit(solution)/shard_map/ppermute | solution.py:118
  16.8 3.2 %collective-permute-start.3 = (bf16[128,512]{1,0:T(8,128)(2,1)S(1)}, bf16[128,512]{1,0:T(8,128)(2,1)S(1)}, u32[]{:S(2)}, u32[]{:S(2)}) collective-permute-start(bf16[128,512]{1,0:T(8,128)(2,1)S(1)} %collective-permute-done.1.refs_1_), channel_id=1, source_target_pairs={{0,1},{1,0},{2,3},{3,2},{4,5},{5,4},{6,7},{7,6},{8,9},{9,8},{10,11... | collective-permute-start | bytes 393224 | tf_op jit(solution)/shard_map/ppermute | solution.py:119
  17.0 8.5 %collective-permute-start.6 = (bf16[128,512]{1,0:T(8,128)(2,1)S(1)}, bf16[128,512]{1,0:T(8,128)(2,1)S(1)}, u32[]{:S(2)}, u32[]{:S(2)}) collective-permute-start(bf16[128,512]{1,0:T(8,128)(2,1)S(1)} %collective-permute-done.1.refs_1_), channel_id=1, source_target_pairs={{0,2},{1,3},{2,0},{3,1},{4,6},{5,7},{6,4},{7,5},{8,10},{9,11},{10,... | collective-permute-start | bytes 393224 | tf_op jit(solution)/shard_map/ppermute | solution.py:118
  20.0 6.0 %collective-permute-start.10 = (bf16[256,512]{1,0:T(8,128)(2,1)S(1)}, bf16[256,512]{1,0:T(8,128)(2,1)S(1)}, u32[]{:S(2)}, u32[]{:S(2)}) collective-permute-start(bf16[256,512]{1,0:T(8,128)(2,1)S(1)} %collective-permute-done.9.refs_0_), channel_id=1, source_target_pairs={{0,1},{1,0},{2,3},{3,2},{4,5},{5,4},{6,7},{7,6},{8,9},{9,8},{10,11... | collective-permute-start | bytes 786440 | tf_op jit(solution)/shard_map/ppermute | solution.py:120
  25.0 3.3 %collective-permute-start.7 = (bf16[128,512]{1,0:T(8,128)(2,1)S(1)}, bf16[128,512]{1,0:T(8,128)(2,1)S(1)}, u32[]{:S(2)}, u32[]{:S(2)}) collective-permute-start(bf16[128,512]{1,0:T(8,128)(2,1)S(1)} %get-tuple-element.39.a), channel_id=1, source_target_pairs={{0,1},{1,0},{2,3},{3,2},{4,5},{5,4},{6,7},{7,6},{8,9},{9,8},{10,11... | collective-permute-start | bytes 393224 | tf_op jit(solution)/shard_map/ppermute | solution.py:121
  25.6 2.7 %collective-permute-start.8 = (bf16[128,512]{1,0:T(8,128)(2,1)S(1)}, bf16[128,512]{1,0:T(8,128)(2,1)S(1)}, u32[]{:S(2)}, u32[]{:S(2)}) collective-permute-start(bf16[128,512]{1,0:T(8,128)(2,1)S(1)} %collective-permute-done.6.b), channel_id=1, source_target_pairs={{0,1},{1,0},{2,3},{3,2},{4,5},{5,4},{6,7},{7,6},{8,9},{9,8},{10,11... | collective-permute-start | bytes 393224 | tf_op jit(solution)/shard_map/ppermute | solution.py:121
  28.7 6.0 %collective-permute-start.11 = (bf16[256,256]{1,0:T(8,128)(2,1)S(1)}, bf16[256,256]{1,0:T(8,128)(2,1)S(1)}, u32[]{:S(2)}, u32[]{:S(2)}) collective-permute-start(bf16[256,256]{1,0:T(8,128)(2,1)S(1)} %get-tuple-element.48.kv_ref), channel_id=1, source_target_pairs={{0,8},{8,0},{1,9},{9,1},{2,10},{10,2},{3,11},{11,3},{4,12},{12,4},... | collective-permute-start | bytes 393224 | tf_op jit(solution)/shard_map/ppermute | solution.py:519
  36.1 1.6 %collective-permute-start.16 = (bf16[256,512]{1,0:T(8,128)(2,1)S(1)}, bf16[256,512]{1,0:T(8,128)(2,1)S(1)}, u32[]{:S(2)}, u32[]{:S(2)}) collective-permute-start(bf16[256,512]{1,0:T(8,128)(2,1)S(1)} %get-tuple-element.56.x_ref), channel_id=1, source_target_pairs={{0,1},{1,0},{2,3},{3,2},{4,5},{5,4},{6,7},{7,6},{8,9},{9,8},{10,11... | collective-permute-start | bytes 786440 | tf_op jit(solution)/shard_map/ppermute | solution.py:115
  39.3 16.3 %collective-permute-start.21 = (bf16[256,512]{1,0:T(8,128)(2,1)S(1)}, bf16[256,512]{1,0:T(8,128)(2,1)S(1)}, u32[]{:S(2)}, u32[]{:S(2)}) collective-permute-start(bf16[256,512]{1,0:T(8,128)(2,1)S(1)} %get-tuple-element.59), channel_id=1, source_target_pairs={{0,2},{1,3},{2,0},{3,1},{4,6},{5,7},{6,4},{7,5},{8,10},{9,11},{10,... | collective-permute-start | bytes 786440 | tf_op jit(solution)/shard_map/ppermute | solution.py:117
  40.7 11.9 %collective-permute-start.13 = (bf16[128,512]{1,0:T(8,128)(2,1)S(1)}, bf16[128,512]{1,0:T(8,128)(2,1)S(1)}, u32[]{:S(2)}, u32[]{:S(2)}) collective-permute-start(bf16[128,512]{1,0:T(8,128)(2,1)S(1)} %get-tuple-element.55), channel_id=1, source_target_pairs={{0,6},{1,7},{2,4},{3,5},{4,2},{5,3},{6,0},{7,1},{8,14},{9,15},{10,... | collective-permute-start | bytes 393224 | tf_op jit(solution)/shard_map/ppermute | solution.py:114
  42.6 12.2 %collective-permute-start.12 = (bf16[128,512]{1,0:T(8,128)(2,1)S(1)}, bf16[128,512]{1,0:T(8,128)(2,1)S(1)}, u32[]{:S(2)}, u32[]{:S(2)}) collective-permute-start(bf16[128,512]{1,0:T(8,128)(2,1)S(1)} %get-tuple-element.54), channel_id=1, source_target_pairs={{0,6},{1,7},{2,4},{3,5},{4,2},{5,3},{6,0},{7,1},{8,14},{9,15},{10,... | collective-permute-start | bytes 393224 | tf_op jit(solution)/shard_map/ppermute | solution.py:114
  52.6 6.3 %collective-permute-start.15 = (bf16[128,512]{1,0:T(8,128)(2,1)S(1)}, bf16[128,512]{1,0:T(8,128)(2,1)S(1)}, u32[]{:S(2)}, u32[]{:S(2)}) collective-permute-start(bf16[128,512]{1,0:T(8,128)(2,1)S(1)} %collective-permute-done.13.refs_1_), channel_id=1, source_target_pairs={{0,1},{1,0},{2,3},{3,2},{4,5},{5,4},{6,7},{7,6},{8,9},{9,8},{10,11... | collective-permute-start | bytes 393224 | tf_op jit(solution)/shard_map/ppermute | solution.py:119
  52.6 6.3 %collective-permute-start.18 = (bf16[128,512]{1,0:T(8,128)(2,1)S(1)}, bf16[128,512]{1,0:T(8,128)(2,1)S(1)}, u32[]{:S(2)}, u32[]{:S(2)}) collective-permute-start(bf16[128,512]{1,0:T(8,128)(2,1)S(1)} %collective-permute-done.13.refs_1_), channel_id=1, source_target_pairs={{0,2},{1,3},{2,0},{3,1},{4,6},{5,7},{6,4},{7,5},{8,10},{9,11},{10,... | collective-permute-start | bytes 393224 | tf_op jit(solution)/shard_map/ppermute | solution.py:118
  54.9 4.0 %collective-permute-start.14 = (bf16[128,512]{1,0:T(8,128)(2,1)S(1)}, bf16[128,512]{1,0:T(8,128)(2,1)S(1)}, u32[]{:S(2)}, u32[]{:S(2)}) collective-permute-start(bf16[128,512]{1,0:T(8,128)(2,1)S(1)} %collective-permute-done.12.refs_0_), channel_id=1, source_target_pairs={{0,1},{1,0},{2,3},{3,2},{4,5},{5,4},{6,7},{7,6},{8,9},{9,8},{10,11... | collective-permute-start | bytes 393224 | tf_op jit(solution)/shard_map/ppermute | solution.py:119
  54.9 6.4 %collective-permute-start.17 = (bf16[128,512]{1,0:T(8,128)(2,1)S(1)}, bf16[128,512]{1,0:T(8,128)(2,1)S(1)}, u32[]{:S(2)}, u32[]{:S(2)}) collective-permute-start(bf16[128,512]{1,0:T(8,128)(2,1)S(1)} %collective-permute-done.12.refs_0_), channel_id=1, source_target_pairs={{0,2},{1,3},{2,0},{3,1},{4,6},{5,7},{6,4},{7,5},{8,10},{9,11},{10,... | collective-permute-start | bytes 393224 | tf_op jit(solution)/shard_map/ppermute | solution.py:118
  55.6 7.4 %collective-permute-start.22 = (bf16[256,512]{1,0:T(8,128)(2,1)S(1)}, bf16[256,512]{1,0:T(8,128)(2,1)S(1)}, u32[]{:S(2)}, u32[]{:S(2)}) collective-permute-start(bf16[256,512]{1,0:T(8,128)(2,1)S(1)} %collective-permute-done.21.refs_0_), channel_id=1, source_target_pairs={{0,1},{1,0},{2,3},{3,2},{4,5},{5,4},{6,7},{7,6},{8,9},{9,8},{10,11... | collective-permute-start | bytes 786440 | tf_op jit(solution)/shard_map/ppermute | solution.py:120
  58.9 6.1 %collective-permute-start.20 = (bf16[128,512]{1,0:T(8,128)(2,1)S(1)}, bf16[128,512]{1,0:T(8,128)(2,1)S(1)}, u32[]{:S(2)}, u32[]{:S(2)}) collective-permute-start(bf16[128,512]{1,0:T(8,128)(2,1)S(1)} %collective-permute-done.18.b), channel_id=1, source_target_pairs={{0,1},{1,0},{2,3},{3,2},{4,5},{5,4},{6,7},{7,6},{8,9},{9,8},{10,11... | collective-permute-start | bytes 393224 | tf_op jit(solution)/shard_map/ppermute | solution.py:121
  63.0 2.0 %collective-permute-start.19 = (bf16[128,512]{1,0:T(8,128)(2,1)S(1)}, bf16[128,512]{1,0:T(8,128)(2,1)S(1)}, u32[]{:S(2)}, u32[]{:S(2)}) collective-permute-start(bf16[128,512]{1,0:T(8,128)(2,1)S(1)} %get-tuple-element.58.a), channel_id=1, source_target_pairs={{0,1},{1,0},{2,3},{3,2},{4,5},{5,4},{6,7},{7,6},{8,9},{9,8},{10,11... | collective-permute-start | bytes 393224 | tf_op jit(solution)/shard_map/ppermute | solution.py:121

commit v3 on v2

v3 whole, which is shorter than its diff:
```python
import functools

import jax
import jax.numpy as jnp
from jax import lax
from jax.experimental import pallas as pl
from jax.experimental.pallas import tpu as pltpu
from jax.sharding import PartitionSpec as P

HEAD_SIZE = 128
ROPE_BASE = 500000.0
NORM_EPS = 1e-05
LOG2E = 1.4426950408889634
VMEM_LIMIT = 24 * 1024 * 1024
F32 = jnp.float32
BF16 = jnp.bfloat16
I32 = jnp.int32
COST = 400_000_000
PART_COST = 1_500_000_000


VMEM = pl.BlockSpec(memory_space=pltpu.VMEM)
HBM = pl.BlockSpec(memory_space=pltpu.HBM)


def arr(shape, dtype):
    return jax.ShapeDtypeStruct(shape, dtype)


def call(kernel, name, operands, out_shape, scratch=(), rides=None, hbm=(), out_hbm=False, flops=COST):
    operands = [(o, any(o is h for h in hbm)) for o in operands]
    return pl.pallas_call(
        kernel,
        out_shape=out_shape,
        in_specs=[HBM if far else VMEM for _, far in operands],
        out_specs=[HBM if out_hbm else VMEM] * len(out_shape),
        scratch_shapes=list(scratch),
        input_output_aliases=rides or {},
        compiler_params=pltpu.CompilerParams(vmem_limit_bytes=VMEM_LIMIT),
        cost_estimate=pl.CostEstimate(flops=flops, bytes_accessed=1, transcendentals=0),
        name=name,
    )(*(pltpu.with_memory_space_constraint(o, pltpu.HBM) if far else o for o, far in operands))


def fetch(pairs, sems, base=0):
    copies = [pltpu.make_async_copy(src, dst, sems.at[base + i]) for i, (src, dst) in enumerate(pairs)]
    for copy in copies:
        copy.start()
    return copies


def place():
    d = lax.axis_index("heads")
    return d // 2, lax.rem(d, 2)


def live_row(pos_ref, cnt_ref, shard, dead):
    pos = pos_ref[pl.ds(shard, 1), :]
    slot = lax.broadcasted_iota(I32, pos.shape, 1)
    return jnp.where(slot < cnt_ref[shard], pos, dead)


def column(row):
    return jnp.transpose(jnp.broadcast_to(row, (128, row.shape[1])))


def pick_kernel(cnt_hbm, pos_hbm, hid_hbm, x_ref, xa_ref, xb_ref, rowpos_ref, cnt_ref, pos_ref, hid_ref, sems):
    copies = fetch([(cnt_hbm, cnt_ref), (pos_hbm, pos_ref), (hid_hbm, hid_ref)], sems)
    own, shards = lax.axis_index("ctx"), lax.axis_size("ctx")
    tok, cap = hid_ref.shape[0], x_ref.shape[0]
    copies[0].wait()
    copies[1].wait()
    rowpos = column(live_row(pos_ref, cnt_ref, own, shards * tok))
    rowpos_ref[...] = rowpos
    local = rowpos[:, :1] - own * tok
    hot = (lax.broadcasted_iota(I32, (cap, tok), 1) == local).astype(F32).astype(BF16)
    copies[2].wait()
    x = jnp.dot(hot, hid_ref[...], preferred_element_type=F32).astype(BF16)
    x_ref[...] = x
    xa_ref[...] = x[: cap // 2]
    xb_ref[...] = x[cap // 2 :]


def pick(counts, positions, hidden):
    cap, width = positions.shape[1], hidden.shape[1]
    return call(
        pick_kernel,
        "pick",
        (counts, positions, hidden),
        [arr((cap, width), BF16), arr((cap // 2, width), BF16), arr((cap // 2, width), BF16), arr((cap, 128), I32)],
        scratch=[
            pltpu.SMEM(counts.shape, I32),
            pltpu.VMEM(positions.shape, I32),
            pltpu.VMEM(hidden.shape, BF16),
            pltpu.SemaphoreType.DMA((3,)),
        ],
        hbm=(counts, positions, hidden),
    )


def sender(perm):
    return functools.partial(lax.ppermute, axis_name="heads", perm=perm)


def chip_sender(size, f):
    return sender([(2 * z + c, 2 * f(z) + c) for z in range(size // 2) for c in range(2)])


def spread(size, full, first, second, use_own, use_far, use_beside):
    cross = chip_sender(size, lambda z: 3 - z)
    near = chip_sender(size, lambda z: z ^ 1)
    twin = sender([(d, d ^ 1) for d in range(size)])
    far = cross(full)
    mates = twin(first), twin(second)
    beside = near(first), near(second)
    last = near(far)
    beside = use_own((full,), mates, beside)
    beside = use_far((far,), (twin(far),), beside)
    use_beside(beside, (twin(beside[0]), twin(beside[1])))
    return last, twin(last)


def joined(refs):
    parts = [ref[...] for ref in refs]
    return parts[0] if len(parts) == 1 else jnp.concatenate(parts, axis=0)


def lanes_sum(x):
    total = x[:, :128]
    for at in range(128, x.shape[1], 128):
        total = total + x[:, at : at + 128]
    return total


def halves(mine, twin, zz, core):
    width = mine.shape[1]
    rows = [pl.ds(pl.multiple_of((2 * zz + at) * width, width), width) for at in (core, 1 - core)]
    return zip((mine, twin), rows)


def add(a, b):
    return b if a is None else a + b


def project(mine, twin, zz, core, gain_ref, router_ref, w_ref, columns, stats=True):
    product = squares = routed = None
    for x, rows in halves(mine, twin, zz, core):
        xf = x.astype(F32)
        gained = (xf * gain_ref[:, rows]).astype(BF16)
        product = add(product, jnp.dot(gained, w_ref[rows, columns], preferred_element_type=F32))
        if stats:
            squares = add(squares, lanes_sum(xf * xf))
            routed = add(routed, lanes_sum(xf * router_ref[:, rows]))
    return product, squares, routed


def settle(copies):
    for copy in copies:
        copy.wait()


def own_kernel(n_mine, n_twin, *refs):
    mine, twin, refs = refs[:n_mine], refs[n_mine : n_mine + n_twin], refs[n_mine + n_twin :]
    n_ride = (len(refs) - 18) // 2
    gain, router, wq, wk, wv, cnt_hbm, pos_hbm, flag_hbm = refs[n_ride : n_ride + 8]
    sums_ref, bias_ref, hot_ref, gain_ref, router_ref, w_ref = refs[-10:-4]
    cnt_ref, pos_ref, flag_ref, sems = refs[-4:]
    z, core = place()
    small = fetch([(cnt_hbm, cnt_ref), (pos_hbm, pos_ref), (flag_hbm, flag_ref)], sems, 5)
    nq, nk = wq.shape[1], wk.shape[1]
    copies = fetch(
        [
            (gain, gain_ref),
            (router, router_ref),
            (wq, w_ref.at[:, 0:nq]),
            (wk, w_ref.at[:, nq : nq + nk]),
            (wv, w_ref.at[:, nq + nk : nq + 2 * nk]),
        ],
        sems,
    )
    settle(small)
    own, shards = lax.axis_index("ctx"), lax.axis_size("ctx")
    tok = hot_ref.shape[0]
    seq = shards * tok
    row = live_row(pos_ref, cnt_ref, own, seq)
    for step in range(shards):
        source = lax.rem(own + shards - step, shards)
        keys = column(live_row(pos_ref, cnt_ref, source, seq + 1))[:, :1]
        bias_ref[step] = jnp.where(keys <= row, 0.0, -jnp.inf).astype(F32)
    flags = jnp.transpose(flag_ref[...].astype(F32))
    local = row - own * tok
    for r in range(tok // 128):
        at = lax.broadcasted_iota(I32, (128, row.shape[1]), 0) + r * 128
        hot = jnp.where(at == local, flags[:, r : r + 1], 0.0)
        hot_ref[r * 128 : (r + 1) * 128, :] = hot.astype(BF16)
    settle(copies)
    product, squares, routed = project(joined(mine), joined(twin), z, core, gain_ref, router_ref, w_ref, slice(None))
    n = product.shape[1]
    sums_ref[:, 0:n] = product
    sums_ref[:, n : n + 128] = squares
    sums_ref[:, n + 128 : n + 256] = routed


def own_part(mine, twin, rides, weights, counts, positions, flags, tok):
    cap = sum(x.shape[0] for x in mine)
    depth = weights[2].shape[0]
    columns = sum(w.shape[1] for w in weights[2:])
    shards = positions.shape[0]
    far = (*weights, counts, positions, flags)
    at = len(mine) + len(twin)
    return call(
        functools.partial(own_kernel, len(mine), len(twin)),
        "own_part",
        (*mine, *twin, *rides, *far),
        [
            *(arr(r.shape, BF16) for r in rides),
            arr((cap, columns + 256), F32),
            arr((shards, cap, cap), F32),
            arr((tok, cap), BF16),
            arr((1, depth), F32),
            arr((1, depth), F32),
            arr((depth, columns), BF16),
        ],
        scratch=[
            pltpu.SMEM(counts.shape, I32),
            pltpu.VMEM(positions.shape, I32),
            pltpu.VMEM(flags.shape, I32),
            pltpu.SemaphoreType.DMA((8,)),
        ],
        rides={at + i: i for i in range(len(rides))},
        hbm=far,
        flops=PART_COST,
    )


def more_kernel(n_mine, n_twin, flip, *refs):
    mine, twin, refs = refs[:n_mine], refs[n_mine : n_mine + n_twin], refs[n_mine + n_twin :]
    gain_ref, router_ref, w_ref, sums_in = refs[:4]
    sums_out = refs[4 + (len(refs) - 5) // 2]
    z, core = place()
    product, squares, routed = project(
        joined(mine), joined(twin), flip(z), core, gain_ref, router_ref, w_ref, slice(None)
    )
    n = product.shape[1]
    sums_out[:, 0:n] = sums_in[:, 0:n] + product
    sums_out[:, n : n + 128] = sums_in[:, n : n + 128] + squares
    sums_out[:, n + 128 : n + 256] = sums_in[:, n + 128 : n + 256] + routed


def more_part(mine, twin, staged, sums, rides, flip, flops):
    at = len(mine) + len(twin) + 3
    return call(
        functools.partial(more_kernel, len(mine), len(twin), flip),
        "more_part",
        (*mine, *twin, *staged, sums, *rides),
        [arr(sums.shape, F32), *(arr(r.shape, BF16) for r in rides)],
        rides={at + i: i for i in range(1 + len(rides))},
        flops=flops,
    )


def turn(x, cos, sin):
    return x * cos + pltpu.roll(x, HEAD_SIZE // 2, 1) * sin


def kv_last_kernel(nq, mine_ref, twin_ref, gain_ref, router_ref, w_ref, sums, cos_ref, sin_ref, kv_out, stat_out):
    z, core = place()
    n, features = w_ref.shape[1], w_ref.shape[0]
    product, squares, routed = project(
        mine_ref[...], twin_ref[...], z ^ 2, core, gain_ref, router_ref, w_ref, slice(nq, n)
    )
    squares = jnp.sum(sums[:, n : n + 128] + squares, axis=1, keepdims=True)
    routed = jnp.sum(sums[:, n + 128 : n + 256] + routed, axis=1, keepdims=True)
    inverse = lax.rsqrt(squares * (1.0 / features) + NORM_EPS)
    kv = (sums[:, nq:n] + product) * inverse
    kv_out[:, 0:128] = turn(kv[:, 0:128], cos_ref[...], sin_ref[...]).astype(BF16)
    kv_out[:, 128:256] = kv[:, 128:256].astype(BF16)
    stat_out[:, 0:128] = jnp.broadcast_to(inverse, (inverse.shape[0], 128))
    gate = 1.0 / (1.0 + jnp.exp(-routed))
    stat_out[:, 128:256] = jnp.broadcast_to(gate, (gate.shape[0], 128))


def kv_last(pair, staged, sums, cos, sin, nq):
    cap = sums.shape[0]
    return call(
        functools.partial(kv_last_kernel, nq),
        "kv_last",
        (*pair, *staged, sums, cos, sin),
        [arr((cap, 256), BF16), arr((cap, 256), F32)],
    )


def attend(q, kv, bias, carry):
    k, v = kv[:, 0:128], kv[:, 128:256]
    scale = LOG2E / HEAD_SIZE**0.5
    s = lax.dot_general(k, q, (((1,), (1,)), ((), ())), preferred_element_type=F32) * scale + bias
    top = jnp.max(s, axis=0, keepdims=True)
    if carry is not None:
        top = jnp.maximum(top, carry[0])
    e = jnp.exp2(s - top)
    total = jnp.sum(e, axis=0, keepdims=True)
    mix = lax.dot_general(v, e.astype(BF16), (((0,), (0,)), ((), ())), preferred_element_type=F32)
    if carry is not None:
        fade = jnp.exp2(carry[0] - top)
        total = total + carry[1] * fade
        mix = mix + carry[2] * fade
    return top, total, mix


def q_last_kernel(mine_ref, twin_ref, gain_ref, w_ref, sums, stat_ref, cos_ref, sin_ref, kv_ref, bias_ref, *outs):
    q_out, top_ref, total_ref, mix_ref = outs
    z, core = place()
    mine, twin = mine_ref[...], twin_ref[...]
    nq, cap = q_out.shape[1], q_out.shape[0]
    product, _, _ = project(mine, twin, z ^ 2, core, gain_ref, None, w_ref, slice(0, nq), stats=False)
    q = (sums[:, 0:nq] + product) * stat_ref[:, 0:1]
    cos, sin = cos_ref[...], sin_ref[...]
    for h in range(nq // HEAD_SIZE):
        lanes = slice(h * HEAD_SIZE, (h + 1) * HEAD_SIZE)
        turned = turn(q[:, lanes], cos, sin).astype(BF16)
        q_out[:, lanes] = turned
        top, total, mix = attend(turned, kv_ref[...], bias_ref[0], None)
        at = slice(h * cap, (h + 1) * cap)
        top_ref[:, at], total_ref[:, at], mix_ref[:, at] = top, total, mix


def carry_shapes(cap, nq):
    heads = nq // HEAD_SIZE
    return [arr((1, heads * cap), F32), arr((1, heads * cap), F32), arr((HEAD_SIZE, heads * cap), F32)]


def q_last(pair, staged, sums, stat, cos, sin, kv, bias, nq):
    cap = sums.shape[0]
    return call(
        q_last_kernel,
        "q_last",
        (*pair, staged[0], staged[2], sums, stat, cos, sin, kv, bias),
        [arr((cap, nq), BF16), *carry_shapes(cap, nq)],
    )


def attend_kernel(step, last, q_ref, kv_ref, bias_ref, top_in, total_in, mix_in, *outs):
    cap, nq = q_ref.shape
    for h in range(nq // HEAD_SIZE):
        lanes = slice(h * HEAD_SIZE, (h + 1) * HEAD_SIZE)
        at = slice(h * cap, (h + 1) * cap)
        carry = (top_in[:, at], total_in[:, at], mix_in[:, at])
        top, total, mix = attend(q_ref[:, lanes], kv_ref[...], bias_ref[step], carry)
        if not last:
            outs[0][:, at], outs[1][:, at], outs[2][:, at] = top, total, mix
            continue
        full, first, second = outs
        half = cap // 2
        attn = jnp.transpose(mix * (1.0 / total)).astype(BF16)
        full[:, lanes] = attn
        first[:, lanes] = attn[:half]
        second[:, lanes] = attn[half:]


def attend_more(step, last, q, kv, bias, carry):
    cap, nq = q.shape
    shapes = [arr((cap, nq), BF16), arr((cap // 2, nq), BF16), arr((cap // 2, nq), BF16)]
    return call(
        functools.partial(attend_kernel, step, last),
        "attend_more",
        (q, kv, bias, *carry),
        shapes if last else carry_shapes(cap, nq),
    )


def out_term(mine, twin, zz, core, w_ref):
    out = None
    for x, rows in halves(mine, twin, zz, core):
        out = add(out, jnp.dot(x, w_ref[rows, :], preferred_element_type=F32))
    return out


def out_own_kernel(n_mine, n_twin, *refs):
    mine, twin, refs = refs[:n_mine], refs[n_mine : n_mine + n_twin], refs[n_mine + n_twin :]
    n_ride = (len(refs) - 6) // 2
    w, hidden = refs[n_ride : n_ride + 2]
    total_ref, w_ref, hid_ref, sems = refs[-4:]
    z, core = place()
    copies = fetch([(w, w_ref), (hidden, hid_ref)], sems)
    copies[0].wait()
    total_ref[...] = out_term(joined(mine), joined(twin), z, core, w_ref)
    copies[1].wait()


def out_own(mine, twin, rides, w_out, hidden):
    cap = sum(x.shape[0] for x in mine)
    at = len(mine) + len(twin)
    return call(
        functools.partial(out_own_kernel, len(mine), len(twin)),
        "out_own",
        (*mine, *twin, *rides, w_out, hidden),
        [
            *(arr(r.shape, BF16) for r in rides),
            arr((cap, w_out.shape[1]), F32),
            arr(w_out.shape, BF16),
            arr(hidden.shape, BF16),
        ],
        scratch=[pltpu.SemaphoreType.DMA((2,))],
        rides={at + i: i for i in range(len(rides))},
        hbm=(w_out, hidden),
        flops=PART_COST,
    )


def out_more_kernel(n_mine, n_twin, flip, *refs):
    mine, twin, refs = refs[:n_mine], refs[n_mine : n_mine + n_twin], refs[n_mine + n_twin :]
    w_ref, total_in = refs[:2]
    total_out = refs[2 + (len(refs) - 3) // 2]
    z, core = place()
    total_out[...] = total_in[...] + out_term(joined(mine), joined(twin), flip(z), core, w_ref)


def out_more(mine, twin, w, total, rides, flip, flops):
    at = len(mine) + len(twin) + 1
    return call(
        functools.partial(out_more_kernel, len(mine), len(twin), flip),
        "out_more",
        (*mine, *twin, w, total, *rides),
        [arr(total.shape, F32), *(arr(r.shape, BF16) for r in rides)],
        rides={at + i: i for i in range(1 + len(rides))},
        flops=flops,
    )


def out_last_kernel(mine_ref, twin_ref, w_ref, total_ref, stat_ref, hot_ref, hid_ref, out, out_ref, sems):
    z, core = place()
    projected = total_ref[...] + out_term(mine_ref[...], twin_ref[...], z ^ 2, core, w_ref)
    update = (stat_ref[:, 128:129] * projected).astype(BF16)
    block = 256
    copies = []
    for i in range(hid_ref.shape[0] // block):
        rows = slice(i * block, (i + 1) * block)
        placed = jnp.dot(hot_ref[rows, :], update, preferred_element_type=F32)
        out_ref[rows, :] = (hid_ref[rows, :].astype(F32) + placed).astype(BF16)
        copies += fetch([(out_ref.at[rows, :], out.at[rows, :])], sems, i)
    settle(copies)


def out_last(pair, w, total, stat, hot, hidden):
    return call(
        out_last_kernel,
        "out_last",
        (*pair, w, total, stat, hot, hidden),
        [arr(hidden.shape, BF16)],
        scratch=[pltpu.VMEM(hidden.shape, BF16), pltpu.SemaphoreType.DMA((hidden.shape[0] // 256,))],
        out_hbm=True,
    )[0]


def angles(row_pos):
    half = HEAD_SIZE // 2
    frequency = ROPE_BASE ** (-(jnp.arange(half, dtype=F32) * 2.0 / HEAD_SIZE))
    turned = row_pos.astype(F32) * jnp.concatenate([frequency, frequency])[None, :]
    sign = jnp.concatenate([-jnp.ones((half,), F32), jnp.ones((half,), F32)])
    return jnp.cos(turned), jnp.sin(turned) * sign[None, :]


def body(
    size,
    hidden_in,
    norm_gain,
    router_weight,
    w_query,
    w_key,
    value_weight,
    w_out,
    keep_flags,
    keep_counts,
    keep_positions,
):
    shards = lax.axis_size("ctx")
    tok = hidden_in.shape[0]
    nq = w_query.shape[1]
    flags = keep_flags.reshape(-1, 128)
    weights = (norm_gain.reshape(1, -1), router_weight.reshape(1, -1), w_query, w_key, value_weight)

    full, first, second, rowpos = pick(keep_counts, keep_positions, hidden_in)
    cos, sin = angles(rowpos)
    held = {}

    def own(mine, twin, rides):
        *rides, held["sums"], held["bias"], held["hot"], g, r, w = own_part(
            mine, twin, rides, weights, keep_counts, keep_positions, flags, tok
        )
        held["staged"] = (g, r, w)
        return rides

    def far(mine, twin, rides):
        held["sums"], *rides = more_part(
            mine, twin, held["staged"], held["sums"], rides, lambda z: 3 - z, PART_COST
        )
        return rides

    def beside(mine, twin):
        (held["sums"],) = more_part(mine, twin, held["staged"], held["sums"], (), lambda z: z ^ 1, PART_COST)

    pair = spread(size, full, first, second, own, far, beside)
    sums, staged, bias = held["sums"], held["staged"], held["bias"]
    kv, stat = kv_last(pair, staged, sums, cos, sin, nq)
    ring = [(s, (s + 1) % shards) for s in range(shards)]
    moved = lax.ppermute(kv, "ctx", ring)
    q, *carry = q_last(pair, staged, sums, stat, cos, sin, kv, bias, nq)
    for step in range(1, shards):
        last = step == shards - 1
        carry = attend_more(step, last, q, moved, bias, carry)
        if not last:
            moved = lax.ppermute(moved, "ctx", ring)

    def own_out(mine, twin, rides):
        *rides, held["total"], held["w"], held["hidden"] = out_own(mine, twin, rides, w_out, hidden_in)
        return rides

    def far_out(mine, twin, rides):
        held["total"], *rides = out_more(mine, twin, held["w"], held["total"], rides, lambda z: 3 - z, PART_COST)
        return rides

    def beside_out(mine, twin):
        (held["total"],) = out_more(mine, twin, held["w"], held["total"], (), lambda z: z ^ 1, PART_COST)

    pair = spread(size, *carry, own_out, far_out, beside_out)
    return out_last(pair, held["w"], held["total"], stat, held["hot"], held["hidden"])


def solution(mesh):
    in_specs = (
        P(("groups", "ctx"), "heads"),
        P(),
        P(),
        P(None, "heads"),
        P(None, "heads"),
        P(None, "heads"),
        P(None, "heads"),
        P(("groups", "ctx")),
        P("groups"),
        P("groups", None),
    )
    out_specs = P(("groups", "ctx"), "heads")
    return jax.shard_map(
        functools.partial(body, mesh.shape["heads"]),
        mesh=mesh,
        in_specs=in_specs,
        out_specs=out_specs,
        check_vma=False,
    )
```

time: 66.9 us -> 59.9 us (0.90)
  waiting for transfers between devices: 25.8 us -> 20 us
  Pallas kernels: 18.7 us -> 15.4 us
  starting transfers between devices: 21.4 us -> 23.5 us
    ppermute x22 -> x20, waiting for transfers between devices: 23.2 us -> 17.8 us  [the longest x2 11 us: spread(): far = cross(full)]
    pallas_call x11, Pallas kernels: 18.7 us -> 15.4 us  [call(): pl.pallas_call(kernel, out_shape=out_shape, in_specs=[HBM if far else VME...]
    ppermute x22 -> x20, starting transfers between devices: 19.9 us -> 22 us  [the longest x2 8.39 us: spread(): last = near(far)]
  transfers between devices with their start and end apart: 23 -> 21, of which waited for: 10 -> 9; matrix products, arithmetic and copies ran while one was open for 1% -> 1% of each run, Pallas kernels for 18% -> 17%
where the time goes in v3:
time: 59.9 us; the launch traced here: 59.7 us
  starting transfers between devices  23.5 us (39%)
  waiting for transfers between devices  20 us (33%)
  Pallas kernels  15.4 us (26%)
    pallas_call x11, Pallas kernels, call(): pl.pallas_call(kernel, out_shape=out_shape, in_specs=[HBM if far else VME...  15.4 us
    ppermute x2, waiting for transfers between devices, spread(): far = cross(full)  11 us
    ppermute x2, starting transfers between devices, spread(): last = near(far)  8.39 us
    ppermute x2, starting transfers between devices, spread(): far = cross(full)  7.65 us
    ppermute x2, waiting for transfers between devices, spread(): last = near(far)  5 us
    ppermute x4, starting transfers between devices, spread(): beside = (near(first), near(second))  3.77 us
    ppermute x1, waiting for transfers between devices, body(): moved = lax.ppermute(kv, 'ctx', ring)  2.29 us
    ppermute x1, starting transfers between devices, body(): moved = lax.ppermute(kv, 'ctx', ring)  1.56 us
  transfers between devices with their start and end apart: 21, of which 9 were waited for; matrix products, arithmetic and copies ran while one was open for 1% of the time, Pallas kernels for 17%

profile of v3, /device:TPU:0, one launch (start us, length us, event | category | flops | bytes accessed | tf_op | source)
XLA Modules:
  0.0 59.7 jit_solution(17379344034955636881)
XLA Ops:
  0.0 1.7 %pick.1 = (bf16[256,512]{1,0:T(8,128)(2,1)S(1)}, bf16[128,512]{1,0:T(8,128)(2,1)S(1)}, bf16[128,512]{1,0:T(8,128)(2,1)S(1)}, s32[256,128]{1,0:T(8,128)S(1)}) custom-call(s32[2]{0:T(128)} %refs_10_.1, s32[2,256]{1,0:T(2,128)} %refs_11_.1, bf16[1024,512]{1,0:T(8,128)(2,1)} %refs_6_.1), custom_call_target="tpu_custom_call" | custom-call | flops 400000000 | bytes 1 | tf_op jit(solution)/shard_map/pick/pallas_call | solution.py:32
  1.7 5.1 %collective-permute-start = (bf16[256,512]{1,0:T(8,128)(2,1)S(1)}, bf16[256,512]{1,0:T(8,128)(2,1)S(1)}, u32[]{:S(2)}, u32[]{:S(2)}) collective-permute-start(bf16[256,512]{1,0:T(8,128)(2,1)S(1)} %get-tuple-element.37.refs_0_), channel_id=1, source_target_pairs={{0,6},{1,7},{2,4},{3,5},{4,2},{5,3},{6,0},{7,1},{8,14},{9,15},{10,... | collective-permute-start | bytes 786440 | tf_op jit(solution)/shard_map/ppermute | solution.py:113
  6.8 0.0 collective-permute-start.3
  6.8 0.5 collective-permute-start.4
  7.3 1.7 %collective-permute-start.6 = (bf16[128,512]{1,0:T(8,128)(2,1)S(1)}, bf16[128,512]{1,0:T(8,128)(2,1)S(1)}, u32[]{:S(2)}, u32[]{:S(2)}) collective-permute-start(bf16[128,512]{1,0:T(8,128)(2,1)S(1)} %get-tuple-element.39), channel_id=1, source_target_pairs={{0,2},{1,3},{2,0},{3,1},{4,6},{5,7},{6,4},{7,5},{8,10},{9,11},{10,... | collective-permute-start | bytes 393224 | tf_op jit(solution)/shard_map/ppermute | solution.py:115
  9.1 4.9 %collective-permute-done.refs_0_ = bf16[256,512]{1,0:T(8,128)(2,1)S(1)} collective-permute-done((bf16[256,512]{1,0:T(8,128)(2,1)S(1)}, bf16[256,512]{1,0:T(8,128)(2,1)S(1)}, u32[]{:S(2)}, u32[]{:S(2)}) %collective-permute-start) | collective-permute-done | bytes 262176 | tf_op jit(solution)/shard_map/ppermute | solution.py:113
  14.0 0.0 collective-permute-start.7
  14.0 0.1 pad_maximum_fusion
  14.1 0.0 collective-permute-done.3.refs_1_
  14.1 4.5 %collective-permute-start.1 = (bf16[256,512]{1,0:T(8,128)(2,1)S(1)}, bf16[256,512]{1,0:T(8,128)(2,1)S(1)}, u32[]{:S(2)}, u32[]{:S(2)}) collective-permute-start(bf16[256,512]{1,0:T(8,128)(2,1)S(1)} %collective-permute-done.refs_0_), channel_id=1, source_target_pairs={{0,2},{1,3},{2,0},{3,1},{4,6},{5,7},{6,4},{7,5},{8,10},{9,11},{10,... | collective-permute-start | bytes 786440 | tf_op jit(solution)/shard_map/ppermute | solution.py:116
  18.6 0.0 collective-permute-done.4.refs_2_
  18.6 0.3 collective-permute-done.6.refs_4_
  18.9 3.6 %own_part.1 = (bf16[128,512]{1,0:T(8,128)(2,1)S(1)}, bf16[128,512]{1,0:T(8,128)(2,1)S(1)}, f32[256,1024]{1,0:T(8,128)S(1)}, f32[2,256,256]{2,1,0:T(8,128)S(1)}, ...) custom-call(bf16[256,512]{1,0:T(8,128)(2,1)S(1)} %get-tuple-element., ...), custom_call_target="tpu_custom_call", output_to_operand_aliasing={{0}: (3, {}), {1}: (4, {})} | custom-call | flops 1500000000 | bytes 1 | tf_op jit(solution)/shard_map/own_part/pallas_call | solution.py:32
  22.4 0.0 copy-start
  22.4 0.0 collective-permute-done.7.refs_1_
  22.4 0.7 %more_part.2 = (f32[256,1024]{1,0:T(8,128)S(1)}, bf16[128,512]{1,0:T(8,128)(2,1)S(1)}, bf16[128,512]{1,0:T(8,128)(2,1)S(1)}) custom-call(bf16[256,512]{1,0:T(8,128)(2,1)S(1)} %collective-permute-done.refs_0_, bf16[256,512]{1,0:T(8,128)(2,1)S(1)} %collective-permute-done.7.refs_1_, ...), custom_call_target="tpu_custom_call", output_to_operand_aliasing={{0}: (5, {}), {1}: (6, {}), {2}: (7, {})} | custom-call | flops 1500000000 | bytes 1 | tf_op jit(solution)/shard_map/more_part/pallas_call | solution.py:32
  23.1 0.1 collective-permute-start.8
  23.3 0.4 collective-permute-start.9
  23.7 1.8 %collective-permute-done.1.mine_ref = bf16[256,512]{1,0:T(8,128)(2,1)S(1)} collective-permute-done((bf16[256,512]{1,0:T(8,128)(2,1)S(1)}, bf16[256,512]{1,0:T(8,128)(2,1)S(1)}, u32[]{:S(2)}, u32[]{:S(2)}) %collective-permute-start.1) | collective-permute-done | bytes 262176 | tf_op jit(solution)/shard_map/ppermute | solution.py:116
  25.5 0.0 collective-permute-start.2
  25.6 0.5 sine_multiply_fusion
  26.0 0.0 collective-permute-done.8.refs_2_
  26.1 0.7 %more_part.3.sums = f32[256,1024]{1,0:T(8,128)S(1)} custom-call(bf16[128,512]{1,0:T(8,128)(2,1)S(1)} %get-tuple-element.46.refs_0_, bf16[128,512]{1,0:T(8,128)(2,1)S(1)} %get-tuple-element.47.refs_1_, bf16[128,512]{1,0:T(8,128)(2,1)S(1)} %collective-permute-done.8.refs_2_, ...), custom_call_target="tpu_custom_call", output_to_operand_aliasing={{}: (7, {})} | custom-call | flops 1500000000 | bytes 1 | tf_op jit(solution)/shard_map/more_part/pallas_call | solution.py:32
  26.7 0.3 collective-permute-done.2.twin_ref
  27.1 0.4 kv_last.1
  27.5 1.6 %collective-permute-start.10 = (bf16[256,256]{1,0:T(8,128)(2,1)S(1)}, bf16[256,256]{1,0:T(8,128)(2,1)S(1)}, u32[]{:S(2)}, u32[]{:S(2)}) collective-permute-start(bf16[256,256]{1,0:T(8,128)(2,1)S(1)} %get-tuple-element.51.kv_ref), channel_id=1, source_target_pairs={{0,8},{8,0},{1,9},{9,1},{2,10},{10,2},{3,11},{11,3},{4,12},{12,4},... | collective-permute-start | bytes 393224 | tf_op jit(solution)/shard_map/ppermute | solution.py:506
  29.1 1.8 %q_last.1 = (bf16[256,512]{1,0:T(8,128)(2,1)S(1)}, f32[1,1024]{1,0:T(1,128)S(1)}, f32[1,1024]{1,0:T(1,128)S(1)}, f32[128,1024]{1,0:T(8,128)S(1)}) custom-call(bf16[256,512]{1,0:T(8,128)(2,1)S(1)} %collective-permute-done.1.mine_ref, bf16[256,512]{1,0:T(8,128)(2,1)S(1)} %collective-permute-done.2.twin_ref, ...), custom_call_target="tpu_custom_call" | custom-call | flops 400000000 | bytes 1 | tf_op jit(solution)/shard_map/q_last/pallas_call | solution.py:32
  30.9 2.3 %collective-permute-done.10.kv_ref = bf16[256,256]{1,0:T(8,128)(2,1)S(1)} collective-permute-done((bf16[256,256]{1,0:T(8,128)(2,1)S(1)}, bf16[256,256]{1,0:T(8,128)(2,1)S(1)}, u32[]{:S(2)}, u32[]{:S(2)}) %collective-permute-start.10) | collective-permute-done | bytes 131104 | tf_op jit(solution)/shard_map/ppermute | solution.py:506
  33.2 1.4 %attend_more.1 = (bf16[256,512]{1,0:T(8,128)(2,1)S(1)}, bf16[128,512]{1,0:T(8,128)(2,1)S(1)}, bf16[128,512]{1,0:T(8,128)(2,1)S(1)}) custom-call(bf16[256,512]{1,0:T(8,128)(2,1)S(1)} %get-tuple-element.53.q_ref, bf16[256,256]{1,0:T(8,128)(2,1)S(1)} %collective-permute-done.10.kv_ref, f32[2,256,256]{2,1,0:T(8,128)S(1)} %get-tuple-element.52.bias_ref, ...), custom_call_target="tpu_custom_call" | custom-call | flops 400000000 | bytes 1 | tf_op jit(solution)/shard_map/attend_more/pallas_call | solution.py:32
  34.5 2.5 %collective-permute-start.11 = (bf16[256,512]{1,0:T(8,128)(2,1)S(1)}, bf16[256,512]{1,0:T(8,128)(2,1)S(1)}, u32[]{:S(2)}, u32[]{:S(2)}) collective-permute-start(bf16[256,512]{1,0:T(8,128)(2,1)S(1)} %get-tuple-element.57.refs_0_), channel_id=1, source_target_pairs={{0,6},{1,7},{2,4},{3,5},{4,2},{5,3},{6,0},{7,1},{8,14},{9,15},{10,... | collective-permute-start | bytes 786440 | tf_op jit(solution)/shard_map/ppermute | solution.py:113
  37.1 0.0 collective-permute-start.14
  37.1 0.5 collective-permute-start.15
  37.6 0.8 %collective-permute-start.16 = (bf16[128,512]{1,0:T(8,128)(2,1)S(1)}, bf16[128,512]{1,0:T(8,128)(2,1)S(1)}, u32[]{:S(2)}, u32[]{:S(2)}) collective-permute-start(bf16[128,512]{1,0:T(8,128)(2,1)S(1)} %get-tuple-element.58), channel_id=1, source_target_pairs={{0,2},{1,3},{2,0},{3,1},{4,6},{5,7},{6,4},{7,5},{8,10},{9,11},{10,... | collective-permute-start | bytes 393224 | tf_op jit(solution)/shard_map/ppermute | solution.py:115
  38.4 1.2 %collective-permute-start.17 = (bf16[128,512]{1,0:T(8,128)(2,1)S(1)}, bf16[128,512]{1,0:T(8,128)(2,1)S(1)}, u32[]{:S(2)}, u32[]{:S(2)}) collective-permute-start(bf16[128,512]{1,0:T(8,128)(2,1)S(1)} %get-tuple-element.59), channel_id=1, source_target_pairs={{0,2},{1,3},{2,0},{3,1},{4,6},{5,7},{6,4},{7,5},{8,10},{9,11},{10,... | collective-permute-start | bytes 393224 | tf_op jit(solution)/shard_map/ppermute | solution.py:115
  39.6 6.0 %collective-permute-done.11.refs_0_ = bf16[256,512]{1,0:T(8,128)(2,1)S(1)} collective-permute-done((bf16[256,512]{1,0:T(8,128)(2,1)S(1)}, bf16[256,512]{1,0:T(8,128)(2,1)S(1)}, u32[]{:S(2)}, u32[]{:S(2)}) %collective-permute-start.11) | collective-permute-done | bytes 262176 | tf_op jit(solution)/shard_map/ppermute | solution.py:113
  45.7 0.0 collective-permute-start.18
  45.7 0.0 collective-permute-done.14.refs_1_
  45.7 3.9 %collective-permute-start.12 = (bf16[256,512]{1,0:T(8,128)(2,1)S(1)}, bf16[256,512]{1,0:T(8,128)(2,1)S(1)}, u32[]{:S(2)}, u32[]{:S(2)}) collective-permute-start(bf16[256,512]{1,0:T(8,128)(2,1)S(1)} %collective-permute-done.11.refs_0_), channel_id=1, source_target_pairs={{0,2},{1,3},{2,0},{3,1},{4,6},{5,7},{6,4},{7,5},{8,10},{9,11},{10,... | collective-permute-start | bytes 786440 | tf_op jit(solution)/shard_map/ppermute | solution.py:116
  49.6 0.1 collective-permute-done.17.refs_4_
  49.7 2.6 %out_own.1 = (bf16[128,512]{1,0:T(8,128)(2,1)S(1)}, bf16[128,512]{1,0:T(8,128)(2,1)S(1)}, f32[256,512]{1,0:T(8,128)S(1)}, bf16[4096,512]{1,0:T(8,128)(2,1)S(1)}, bf16[1024,512]{1,0:T(8,128)(2,1)S(1)}) custom-call(bf16[256,512]{1,0:T(8,128)(2,1)S(1)} %get-tuple-element.57.refs_0_, ...), custom_call_target="tpu_custom_call", output_to_operand_aliasing={{0}: (3, {}), {1}: (4, {})} | custom-call | flops 1500000000 | bytes 1 | tf_op jit(solution)/shard_map/out_own/pallas_call | solution.py:32
  52.4 0.5 out_more.2
  52.8 0.2 collective-permute-start.19
  53.0 0.4 collective-permute-start.20
  53.4 3.2 %collective-permute-done.12.mine_ref = bf16[256,512]{1,0:T(8,128)(2,1)S(1)} collective-permute-done((bf16[256,512]{1,0:T(8,128)(2,1)S(1)}, bf16[256,512]{1,0:T(8,128)(2,1)S(1)}, u32[]{:S(2)}, u32[]{:S(2)}) %collective-permute-start.12) | collective-permute-done | bytes 262176 | tf_op jit(solution)/shard_map/ppermute | solution.py:116
  56.6 0.0 collective-permute-done.20.refs_3_
  56.6 0.5 out_more.3.total_ref
  57.0 1.1 %collective-permute-done.13.twin_ref = bf16[256,512]{1,0:T(8,128)(2,1)S(1)} collective-permute-done((bf16[256,512]{1,0:T(8,128)(2,1)S(1)}, bf16[256,512]{1,0:T(8,128)(2,1)S(1)}, u32[]{:S(2)}, u32[]{:S(2)}) %collective-permute-start.13) | collective-permute-done | bytes 262176 | tf_op jit(solution)/shard_map/ppermute | solution.py:120
  58.1 1.6 %out_last.1 = bf16[1024,512]{1,0:T(8,128)(2,1)} custom-call(bf16[256,512]{1,0:T(8,128)(2,1)S(1)} %collective-permute-done.12.mine_ref, bf16[256,512]{1,0:T(8,128)(2,1)S(1)} %collective-permute-done.13.twin_ref, bf16[4096,512]{1,0:T(8,128)(2,1)S(1)} %get-tuple-element.60.refs_2_.refs_4_.w_ref, f32[256,512]{1,0:T(8,128)S(1)} %out_more.3.total_ref, ...), custom_call_target="tpu_custom_call" | custom-call | flops 400000000 | bytes 1 | tf_op jit(solution)/shard_map/out_last/pallas_call | solution.py:32
  (10 shorter events, 0.0 us)
Async XLA Ops:
  1.7 12.3 %collective-permute-start = (bf16[256,512]{1,0:T(8,128)(2,1)S(1)}, bf16[256,512]{1,0:T(8,128)(2,1)S(1)}, u32[]{:S(2)}, u32[]{:S(2)}) collective-permute-start(bf16[256,512]{1,0:T(8,128)(2,1)S(1)} %get-tuple-element.37.refs_0_), channel_id=1, source_target_pairs={{0,6},{1,7},{2,4},{3,5},{4,2},{5,3},{6,0},{7,1},{8,14},{9,15},{10,... | collective-permute-start | bytes 786440 | tf_op jit(solution)/shard_map/ppermute | solution.py:113
  6.8 7.3 %collective-permute-start.3 = (bf16[128,512]{1,0:T(8,128)(2,1)S(1)}, bf16[128,512]{1,0:T(8,128)(2,1)S(1)}, u32[]{:S(2)}, u32[]{:S(2)}) collective-permute-start(bf16[128,512]{1,0:T(8,128)(2,1)S(1)} %get-tuple-element.38), channel_id=1, source_target_pairs={{0,1},{1,0},{2,3},{3,2},{4,5},{5,4},{6,7},{7,6},{8,9},{9,8},{10,11... | collective-permute-start | bytes 393224 | tf_op jit(solution)/shard_map/ppermute | solution.py:114
  6.8 11.7 %collective-permute-start.5 = (bf16[128,512]{1,0:T(8,128)(2,1)S(1)}, bf16[128,512]{1,0:T(8,128)(2,1)S(1)}, u32[]{:S(2)}, u32[]{:S(2)}) collective-permute-start(bf16[128,512]{1,0:T(8,128)(2,1)S(1)} %get-tuple-element.38), channel_id=1, source_target_pairs={{0,2},{1,3},{2,0},{3,1},{4,6},{5,7},{6,4},{7,5},{8,10},{9,11},{10,... | collective-permute-start | bytes 393224 | tf_op jit(solution)/shard_map/ppermute | solution.py:115
  6.8 11.7 %collective-permute-start.4 = (bf16[128,512]{1,0:T(8,128)(2,1)S(1)}, bf16[128,512]{1,0:T(8,128)(2,1)S(1)}, u32[]{:S(2)}, u32[]{:S(2)}) collective-permute-start(bf16[128,512]{1,0:T(8,128)(2,1)S(1)} %get-tuple-element.39), channel_id=1, source_target_pairs={{0,1},{1,0},{2,3},{3,2},{4,5},{5,4},{6,7},{7,6},{8,9},{9,8},{10,11... | collective-permute-start | bytes 393224 | tf_op jit(solution)/shard_map/ppermute | solution.py:114
  7.3 11.5 %collective-permute-start.6 = (bf16[128,512]{1,0:T(8,128)(2,1)S(1)}, bf16[128,512]{1,0:T(8,128)(2,1)S(1)}, u32[]{:S(2)}, u32[]{:S(2)}) collective-permute-start(bf16[128,512]{1,0:T(8,128)(2,1)S(1)} %get-tuple-element.39), channel_id=1, source_target_pairs={{0,2},{1,3},{2,0},{3,1},{4,6},{5,7},{6,4},{7,5},{8,10},{9,11},{10,... | collective-permute-start | bytes 393224 | tf_op jit(solution)/shard_map/ppermute | solution.py:115
  14.0 8.4 %collective-permute-start.7 = (bf16[256,512]{1,0:T(8,128)(2,1)S(1)}, bf16[256,512]{1,0:T(8,128)(2,1)S(1)}, u32[]{:S(2)}, u32[]{:S(2)}) collective-permute-start(bf16[256,512]{1,0:T(8,128)(2,1)S(1)} %collective-permute-done.refs_0_), channel_id=1, source_target_pairs={{0,1},{1,0},{2,3},{3,2},{4,5},{5,4},{6,7},{7,6},{8,9},{9,8},{10,11... | collective-permute-start | bytes 786440 | tf_op jit(solution)/shard_map/ppermute | solution.py:118
  14.1 11.4 %collective-permute-start.1 = (bf16[256,512]{1,0:T(8,128)(2,1)S(1)}, bf16[256,512]{1,0:T(8,128)(2,1)S(1)}, u32[]{:S(2)}, u32[]{:S(2)}) collective-permute-start(bf16[256,512]{1,0:T(8,128)(2,1)S(1)} %collective-permute-done.refs_0_), channel_id=1, source_target_pairs={{0,2},{1,3},{2,0},{3,1},{4,6},{5,7},{6,4},{7,5},{8,10},{9,11},{10,... | collective-permute-start | bytes 786440 | tf_op jit(solution)/shard_map/ppermute | solution.py:116
  22.4 3.1 %copy-start = (f32[128]{0:T(128)S(1)}, f32[128]{0:T(128)}, u32[]{:S(2)}) copy-start(f32[128]{0:T(128)} %constant.9.clone.1) | copy-start | bytes 1540
  23.1 2.9 %collective-permute-start.8 = (bf16[128,512]{1,0:T(8,128)(2,1)S(1)}, bf16[128,512]{1,0:T(8,128)(2,1)S(1)}, u32[]{:S(2)}, u32[]{:S(2)}) collective-permute-start(bf16[128,512]{1,0:T(8,128)(2,1)S(1)} %get-tuple-element.46.refs_0_), channel_id=1, source_target_pairs={{0,1},{1,0},{2,3},{3,2},{4,5},{5,4},{6,7},{7,6},{8,9},{9,8},{10,11... | collective-permute-start | bytes 393224 | tf_op jit(solution)/shard_map/ppermute | solution.py:119
  23.3 2.8 %collective-permute-start.9 = (bf16[128,512]{1,0:T(8,128)(2,1)S(1)}, bf16[128,512]{1,0:T(8,128)(2,1)S(1)}, u32[]{:S(2)}, u32[]{:S(2)}) collective-permute-start(bf16[128,512]{1,0:T(8,128)(2,1)S(1)} %get-tuple-element.47.refs_1_), channel_id=1, source_target_pairs={{0,1},{1,0},{2,3},{3,2},{4,5},{5,4},{6,7},{7,6},{8,9},{9,8},{10,11... | collective-permute-start | bytes 393224 | tf_op jit(solution)/shard_map/ppermute | solution.py:119
  25.5 1.5 %collective-permute-start.2 = (bf16[256,512]{1,0:T(8,128)(2,1)S(1)}, bf16[256,512]{1,0:T(8,128)(2,1)S(1)}, u32[]{:S(2)}, u32[]{:S(2)}) collective-permute-start(bf16[256,512]{1,0:T(8,128)(2,1)S(1)} %collective-permute-done.1.mine_ref), channel_id=1, source_target_pairs={{0,1},{1,0},{2,3},{3,2},{4,5},{5,4},{6,7},{7,6},{8,9},{9,8},{10,11... | collective-permute-start | bytes 786440 | tf_op jit(solution)/shard_map/ppermute | solution.py:120
  27.5 5.6 %collective-permute-start.10 = (bf16[256,256]{1,0:T(8,128)(2,1)S(1)}, bf16[256,256]{1,0:T(8,128)(2,1)S(1)}, u32[]{:S(2)}, u32[]{:S(2)}) collective-permute-start(bf16[256,256]{1,0:T(8,128)(2,1)S(1)} %get-tuple-element.51.kv_ref), channel_id=1, source_target_pairs={{0,8},{8,0},{1,9},{9,1},{2,10},{10,2},{3,11},{11,3},{4,12},{12,4},... | collective-permute-start | bytes 393224 | tf_op jit(solution)/shard_map/ppermute | solution.py:506
  34.5 11.1 %collective-permute-start.11 = (bf16[256,512]{1,0:T(8,128)(2,1)S(1)}, bf16[256,512]{1,0:T(8,128)(2,1)S(1)}, u32[]{:S(2)}, u32[]{:S(2)}) collective-permute-start(bf16[256,512]{1,0:T(8,128)(2,1)S(1)} %get-tuple-element.57.refs_0_), channel_id=1, source_target_pairs={{0,6},{1,7},{2,4},{3,5},{4,2},{5,3},{6,0},{7,1},{8,14},{9,15},{10,... | collective-permute-start | bytes 786440 | tf_op jit(solution)/shard_map/ppermute | solution.py:113
  37.1 8.6 %collective-permute-start.14 = (bf16[128,512]{1,0:T(8,128)(2,1)S(1)}, bf16[128,512]{1,0:T(8,128)(2,1)S(1)}, u32[]{:S(2)}, u32[]{:S(2)}) collective-permute-start(bf16[128,512]{1,0:T(8,128)(2,1)S(1)} %get-tuple-element.58), channel_id=1, source_target_pairs={{0,1},{1,0},{2,3},{3,2},{4,5},{5,4},{6,7},{7,6},{8,9},{9,8},{10,11... | collective-permute-start | bytes 393224 | tf_op jit(solution)/shard_map/ppermute | solution.py:114
  37.1 12.5 %collective-permute-start.15 = (bf16[128,512]{1,0:T(8,128)(2,1)S(1)}, bf16[128,512]{1,0:T(8,128)(2,1)S(1)}, u32[]{:S(2)}, u32[]{:S(2)}) collective-permute-start(bf16[128,512]{1,0:T(8,128)(2,1)S(1)} %get-tuple-element.59), channel_id=1, source_target_pairs={{0,1},{1,0},{2,3},{3,2},{4,5},{5,4},{6,7},{7,6},{8,9},{9,8},{10,11... | collective-permute-start | bytes 393224 | tf_op jit(solution)/shard_map/ppermute | solution.py:114
  37.6 12.0 %collective-permute-start.16 = (bf16[128,512]{1,0:T(8,128)(2,1)S(1)}, bf16[128,512]{1,0:T(8,128)(2,1)S(1)}, u32[]{:S(2)}, u32[]{:S(2)}) collective-permute-start(bf16[128,512]{1,0:T(8,128)(2,1)S(1)} %get-tuple-element.58), channel_id=1, source_target_pairs={{0,2},{1,3},{2,0},{3,1},{4,6},{5,7},{6,4},{7,5},{8,10},{9,11},{10,... | collective-permute-start | bytes 393224 | tf_op jit(solution)/shard_map/ppermute | solution.py:115
  38.4 11.2 %collective-permute-start.17 = (bf16[128,512]{1,0:T(8,128)(2,1)S(1)}, bf16[128,512]{1,0:T(8,128)(2,1)S(1)}, u32[]{:S(2)}, u32[]{:S(2)}) collective-permute-start(bf16[128,512]{1,0:T(8,128)(2,1)S(1)} %get-tuple-element.59), channel_id=1, source_target_pairs={{0,2},{1,3},{2,0},{3,1},{4,6},{5,7},{6,4},{7,5},{8,10},{9,11},{10,... | collective-permute-start | bytes 393224 | tf_op jit(solution)/shard_map/ppermute | solution.py:115
  45.7 6.7 %collective-permute-start.18 = (bf16[256,512]{1,0:T(8,128)(2,1)S(1)}, bf16[256,512]{1,0:T(8,128)(2,1)S(1)}, u32[]{:S(2)}, u32[]{:S(2)}) collective-permute-start(bf16[256,512]{1,0:T(8,128)(2,1)S(1)} %collective-permute-done.11.refs_0_), channel_id=1, source_target_pairs={{0,1},{1,0},{2,3},{3,2},{4,5},{5,4},{6,7},{7,6},{8,9},{9,8},{10,11... | collective-permute-start | bytes 786440 | tf_op jit(solution)/shard_map/ppermute | solution.py:118
  45.7 10.9 %collective-permute-start.12 = (bf16[256,512]{1,0:T(8,128)(2,1)S(1)}, bf16[256,512]{1,0:T(8,128)(2,1)S(1)}, u32[]{:S(2)}, u32[]{:S(2)}) collective-permute-start(bf16[256,512]{1,0:T(8,128)(2,1)S(1)} %collective-permute-done.11.refs_0_), channel_id=1, source_target_pairs={{0,2},{1,3},{2,0},{3,1},{4,6},{5,7},{6,4},{7,5},{8,10},{9,11},{10,... | collective-permute-start | bytes 786440 | tf_op jit(solution)/shard_map/ppermute | solution.py:116
  52.8 3.7 %collective-permute-start.19 = (bf16[128,512]{1,0:T(8,128)(2,1)S(1)}, bf16[128,512]{1,0:T(8,128)(2,1)S(1)}, u32[]{:S(2)}, u32[]{:S(2)}) collective-permute-start(bf16[128,512]{1,0:T(8,128)(2,1)S(1)} %get-tuple-element.64.refs_0_), channel_id=1, source_target_pairs={{0,1},{1,0},{2,3},{3,2},{4,5},{5,4},{6,7},{7,6},{8,9},{9,8},{10,11... | collective-permute-start | bytes 393224 | tf_op jit(solution)/shard_map/ppermute | solution.py:119
  53.0 3.5 %collective-permute-start.20 = (bf16[128,512]{1,0:T(8,128)(2,1)S(1)}, bf16[128,512]{1,0:T(8,128)(2,1)S(1)}, u32[]{:S(2)}, u32[]{:S(2)}) collective-permute-start(bf16[128,512]{1,0:T(8,128)(2,1)S(1)} %get-tuple-element.65.refs_1_), channel_id=1, source_target_pairs={{0,1},{1,0},{2,3},{3,2},{4,5},{5,4},{6,7},{7,6},{8,9},{9,8},{10,11... | collective-permute-start | bytes 393224 | tf_op jit(solution)/shard_map/ppermute | solution.py:119
  56.6 1.5 %collective-permute-start.13 = (bf16[256,512]{1,0:T(8,128)(2,1)S(1)}, bf16[256,512]{1,0:T(8,128)(2,1)S(1)}, u32[]{:S(2)}, u32[]{:S(2)}) collective-permute-start(bf16[256,512]{1,0:T(8,128)(2,1)S(1)} %collective-permute-done.12.mine_ref), channel_id=1, source_target_pairs={{0,1},{1,0},{2,3},{3,2},{4,5},{5,4},{6,7},{7,6},{8,9},{9,8},{10,11... | collective-permute-start | bytes 786440 | tf_op jit(solution)/shard_map/ppermute | solution.py:120

commit v4 on v3

--- a/solution.py
+++ b/solution.py
@@ -17,6 +17,13 @@
 I32 = jnp.int32
 COST = 400_000_000
 PART_COST = 1_500_000_000
+OWN_COST = 400_000_000
+FAR_COST = 1_500_000_000
+BESIDE_COST = 1_000_000
+KV_COST = 400_000_000
+Q_COST = 400_000_000
+QA_COST = 1_500_000_000
+ATTEND_COST = 400_000_000
 
 
 VMEM = pl.BlockSpec(memory_space=pltpu.VMEM)
@@ -64,37 +71,35 @@
     return jnp.transpose(jnp.broadcast_to(row, (128, row.shape[1])))
 
 
-def pick_kernel(cnt_hbm, pos_hbm, hid_hbm, x_ref, xa_ref, xb_ref, rowpos_ref, cnt_ref, pos_ref, hid_ref, sems):
-    copies = fetch([(cnt_hbm, cnt_ref), (pos_hbm, pos_ref), (hid_hbm, hid_ref)], sems)
+def pick_kernel(pos_hbm, hid_hbm, x_ref, xa_ref, xb_ref, rowpos_ref, pos_ref, hid_ref, sems):
+    copies = fetch([(pos_hbm, pos_ref), (hid_hbm, hid_ref)], sems)
     own, shards = lax.axis_index("ctx"), lax.axis_size("ctx")
     tok, cap = hid_ref.shape[0], x_ref.shape[0]
     copies[0].wait()
+    pos = column(pos_ref[pl.ds(own, 1), :])
+    rowpos_ref[...] = jnp.where(pos < 0, shards * tok, pos)
+    local = pos[:, :1] - own * tok
+    hot = (lax.broadcasted_iota(I32, (cap, tok), 1) == local).astype(F32).astype(BF16)
     copies[1].wait()
-    rowpos = column(live_row(pos_ref, cnt_ref, own, shards * tok))
-    rowpos_ref[...] = rowpos
-    local = rowpos[:, :1] - own * tok
-    hot = (lax.broadcasted_iota(I32, (cap, tok), 1) == local).astype(F32).astype(BF16)
-    copies[2].wait()
     x = jnp.dot(hot, hid_ref[...], preferred_element_type=F32).astype(BF16)
     x_ref[...] = x
     xa_ref[...] = x[: cap // 2]
     xb_ref[...] = x[cap // 2 :]
 
 
-def pick(counts, positions, hidden):
+def pick(positions, hidden):
     cap, width = positions.shape[1], hidden.shape[1]
     return call(
         pick_kernel,
         "pick",
-        (counts, positions, hidden),
+        (positions, hidden),
         [arr((cap, width), BF16), arr((cap // 2, width), BF16), arr((cap // 2, width), BF16), arr((cap, 128), I32)],
         scratch=[
-            pltpu.SMEM(counts.shape, I32),
             pltpu.VMEM(positions.shape, I32),
             pltpu.VMEM(hidden.shape, BF16),
-            pltpu.SemaphoreType.DMA((3,)),
+            pltpu.SemaphoreType.DMA((2,)),
         ],
-        hbm=(counts, positions, hidden),
+        hbm=(positions, hidden),
     )
 
 
@@ -120,6 +125,18 @@
     return last, twin(last)
 
 
+def spread_halves(size, full, first, second, use_own, use_far, use_beside):
+    cross = chip_sender(size, lambda z: 3 - z)
+    near = chip_sender(size, lambda z: z ^ 1)
+    twin = sender([(d, d ^ 1) for d in range(size)])
+    far = cross(first), cross(second)
+    beside = near(use_own((full,), (twin(full),), full))
+    last_a, last_b = near(far[0]), near(far[1])
+    (last_a,) = use_far(far, (twin(far[0]), twin(far[1])), (last_a,))
+    use_beside((beside,), (twin(beside),))
+    return (last_a, twin(last_a)), (last_b, twin(last_b))
+
+
 def joined(refs):
     parts = [ref[...] for ref in refs]
     return parts[0] if len(parts) == 1 else jnp.concatenate(parts, axis=0)
@@ -159,26 +176,52 @@
         copy.wait()
 
 
-def own_kernel(n_mine, n_twin, *refs):
-    mine, twin, refs = refs[:n_mine], refs[n_mine : n_mine + n_twin], refs[n_mine + n_twin :]
-    n_ride = (len(refs) - 18) // 2
-    gain, router, wq, wk, wv, cnt_hbm, pos_hbm, flag_hbm = refs[n_ride : n_ride + 8]
-    sums_ref, bias_ref, hot_ref, gain_ref, router_ref, w_ref = refs[-10:-4]
-    cnt_ref, pos_ref, flag_ref, sems = refs[-4:]
-    z, core = place()
-    small = fetch([(cnt_hbm, cnt_ref), (pos_hbm, pos_ref), (flag_hbm, flag_ref)], sems, 5)
-    nq, nk = wq.shape[1], wk.shape[1]
-    copies = fetch(
+def own_kernel(x_ref, twin_ref, gain, router, wq, wk, wv, _, sums_ref, gain_ref, router_ref, w_ref, sems):
+    z, core = place()
+    nq, nk, depth = wq.shape[1], wk.shape[1], wq.shape[0]
+    lanes = ((wq, slice(0, nq)), (wk, slice(nq, nq + nk)), (wv, slice(nq + nk, nq + 2 * nk)))
+    block = 2 * x_ref.shape[1]
+    blocks = depth // block
+    vectors = fetch([(gain, gain_ref), (router, router_ref)], sems, 3 * blocks)
+    copies = []
+    for i in range(blocks):
+        rows = pl.ds(pl.multiple_of((z ^ i) * block, block), block)
+        copies.append(fetch([(w.at[rows, :], w_ref.at[rows, at]) for w, at in lanes], sems, 3 * i))
+    settle(vectors)
+    settle(copies[0])
+    product, squares, routed = project(x_ref[...], twin_ref[...], z, core, gain_ref, router_ref, w_ref, slice(None))
+    n = product.shape[1]
+    sums_ref[:, 0:n] = product
+    sums_ref[:, n : n + 128] = squares
+    sums_ref[:, n + 128 : n + 256] = routed
+    for later in copies[1:]:
+        settle(later)
+
+
+def own_part(full, twin, weights):
+    cap, width = full.shape
+    depth = weights[2].shape[0]
+    columns = sum(w.shape[1] for w in weights[2:])
+    return call(
+        own_kernel,
+        "own_part",
+        (full, twin, *weights),
         [
-            (gain, gain_ref),
-            (router, router_ref),
-            (wq, w_ref.at[:, 0:nq]),
-            (wk, w_ref.at[:, nq : nq + nk]),
-            (wv, w_ref.at[:, nq + nk : nq + 2 * nk]),
+            arr(full.shape, BF16),
+            arr((cap, columns + 256), F32),
+            arr((1, depth), F32),
+            arr((1, depth), F32),
+            arr((depth, columns), BF16),
         ],
-        sems,
-    )
-    settle(small)
+        scratch=[pltpu.SemaphoreType.DMA((3 * depth // (2 * width) + 2,))],
+        rides={0: 0},
+        hbm=weights,
+        flops=OWN_COST,
+    )
+
+
+def masks_kernel(cnt_hbm, pos_hbm, flag_hbm, bias_ref, hot_ref, cnt_ref, pos_ref, flag_ref, sems):
+    settle(fetch([(cnt_hbm, cnt_ref), (pos_hbm, pos_ref), (flag_hbm, flag_ref)], sems))
     own, shards = lax.axis_index("ctx"), lax.axis_size("ctx")
     tok = hot_ref.shape[0]
     seq = shards * tok
@@ -193,50 +236,14 @@
         at = lax.broadcasted_iota(I32, (128, row.shape[1]), 0) + r * 128
         hot = jnp.where(at == local, flags[:, r : r + 1], 0.0)
         hot_ref[r * 128 : (r + 1) * 128, :] = hot.astype(BF16)
-    settle(copies)
-    product, squares, routed = project(joined(mine), joined(twin), z, core, gain_ref, router_ref, w_ref, slice(None))
-    n = product.shape[1]
-    sums_ref[:, 0:n] = product
-    sums_ref[:, n : n + 128] = squares
-    sums_ref[:, n + 128 : n + 256] = routed
-
-
-def own_part(mine, twin, rides, weights, counts, positions, flags, tok):
-    cap = sum(x.shape[0] for x in mine)
-    depth = weights[2].shape[0]
-    columns = sum(w.shape[1] for w in weights[2:])
-    shards = positions.shape[0]
-    far = (*weights, counts, positions, flags)
-    at = len(mine) + len(twin)
-    return call(
-        functools.partial(own_kernel, len(mine), len(twin)),
-        "own_part",
-        (*mine, *twin, *rides, *far),
-        [
-            *(arr(r.shape, BF16) for r in rides),
-            arr((cap, columns + 256), F32),
-            arr((shards, cap, cap), F32),
-            arr((tok, cap), BF16),
-            arr((1, depth), F32),
-            arr((1, depth), F32),
-            arr((depth, columns), BF16),
-        ],
-        scratch=[
-            pltpu.SMEM(counts.shape, I32),
-            pltpu.VMEM(positions.shape, I32),
-            pltpu.VMEM(flags.shape, I32),
-            pltpu.SemaphoreType.DMA((8,)),
-        ],
-        rides={at + i: i for i in range(len(rides))},
-        hbm=far,
-        flops=PART_COST,
-    )
-
-
-def more_kernel(n_mine, n_twin, flip, *refs):
+
+
+def more_kernel(n_mine, n_twin, n_ride, flip, masks, *refs):
     mine, twin, refs = refs[:n_mine], refs[n_mine : n_mine + n_twin], refs[n_mine + n_twin :]
     gain_ref, router_ref, w_ref, sums_in = refs[:4]
-    sums_out = refs[4 + (len(refs) - 5) // 2]
+    refs = refs[4 + n_ride :]
+    n_far = 3 if masks else 0
+    sums_out = refs[n_far]
     z, core = place()
     product, squares, routed = project(
         joined(mine), joined(twin), flip(z), core, gain_ref, router_ref, w_ref, slice(None)
@@ -245,16 +252,31 @@
     sums_out[:, 0:n] = sums_in[:, 0:n] + product
     sums_out[:, n : n + 128] = sums_in[:, n : n + 128] + squares
     sums_out[:, n + 128 : n + 256] = sums_in[:, n + 128 : n + 256] + routed
-
-
-def more_part(mine, twin, staged, sums, rides, flip, flops):
+    if masks:
+        masks_kernel(*refs[:3], *refs[4 + n_ride :])
+
+
+def more_part(mine, twin, staged, sums, rides, flip, flops, masks=None):
     at = len(mine) + len(twin) + 3
-    return call(
-        functools.partial(more_kernel, len(mine), len(twin), flip),
+    shapes, scratch, far = [], [], ()
+    if masks:
+        *far, tok = masks
+        shards, cap = far[1].shape
+        shapes = [arr((shards, cap, cap), F32), arr((tok, cap), BF16)]
+        scratch = [
+            pltpu.SMEM(far[0].shape, I32),
+            pltpu.VMEM(far[1].shape, I32),
+            pltpu.VMEM(far[2].shape, I32),
+            pltpu.SemaphoreType.DMA((3,)),
+        ]
+    return call(
+        functools.partial(more_kernel, len(mine), len(twin), len(rides), flip, bool(masks)),
         "more_part",
-        (*mine, *twin, *staged, sums, *rides),
-        [arr(sums.shape, F32), *(arr(r.shape, BF16) for r in rides)],
+        (*mine, *twin, *staged, sums, *rides, *far),
+        [arr(sums.shape, F32), *(arr(r.shape, r.dtype) for r in rides), *shapes],
+        scratch=scratch,
         rides={at + i: i for i in range(1 + len(rides))},
+        hbm=far,
         flops=flops,
     )
 
@@ -263,30 +285,32 @@
     return x * cos + pltpu.roll(x, HEAD_SIZE // 2, 1) * sin
 
 
-def kv_last_kernel(nq, mine_ref, twin_ref, gain_ref, router_ref, w_ref, sums, cos_ref, sin_ref, kv_out, stat_out):
+def kv_last_kernel(nq, at, mine_ref, twin_ref, gain_ref, router_ref, w_ref, sums, cos_ref, sin_ref, kv_out, stat_out):
     z, core = place()
     n, features = w_ref.shape[1], w_ref.shape[0]
+    rows = slice(at, at + mine_ref.shape[0])
     product, squares, routed = project(
         mine_ref[...], twin_ref[...], z ^ 2, core, gain_ref, router_ref, w_ref, slice(nq, n)
     )
-    squares = jnp.sum(sums[:, n : n + 128] + squares, axis=1, keepdims=True)
-    routed = jnp.sum(sums[:, n + 128 : n + 256] + routed, axis=1, keepdims=True)
+    squares = jnp.sum(sums[rows, n : n + 128] + squares, axis=1, keepdims=True)
+    routed = jnp.sum(sums[rows, n + 128 : n + 256] + routed, axis=1, keepdims=True)
     inverse = lax.rsqrt(squares * (1.0 / features) + NORM_EPS)
-    kv = (sums[:, nq:n] + product) * inverse
-    kv_out[:, 0:128] = turn(kv[:, 0:128], cos_ref[...], sin_ref[...]).astype(BF16)
+    kv = (sums[rows, nq:n] + product) * inverse
+    kv_out[:, 0:128] = turn(kv[:, 0:128], cos_ref[rows, :], sin_ref[rows, :]).astype(BF16)
     kv_out[:, 128:256] = kv[:, 128:256].astype(BF16)
     stat_out[:, 0:128] = jnp.broadcast_to(inverse, (inverse.shape[0], 128))
     gate = 1.0 / (1.0 + jnp.exp(-routed))
     stat_out[:, 128:256] = jnp.broadcast_to(gate, (gate.shape[0], 128))
 
 
-def kv_last(pair, staged, sums, cos, sin, nq):
-    cap = sums.shape[0]
-    return call(
-        functools.partial(kv_last_kernel, nq),
+def kv_last(at, pair, staged, sums, cos, sin, nq, flops):
+    cap = pair[0].shape[0]
+    return call(
+        functools.partial(kv_last_kernel, nq, at),
         "kv_last",
         (*pair, *staged, sums, cos, sin),
         [arr((cap, 256), BF16), arr((cap, 256), F32)],
+        flops=flops,
     )
 
 
@@ -307,20 +331,22 @@
     return top, total, mix
 
 
-def q_last_kernel(mine_ref, twin_ref, gain_ref, w_ref, sums, stat_ref, cos_ref, sin_ref, kv_ref, bias_ref, *outs):
-    q_out, top_ref, total_ref, mix_ref = outs
-    z, core = place()
-    mine, twin = mine_ref[...], twin_ref[...]
-    nq, cap = q_out.shape[1], q_out.shape[0]
-    product, _, _ = project(mine, twin, z ^ 2, core, gain_ref, None, w_ref, slice(0, nq), stats=False)
-    q = (sums[:, 0:nq] + product) * stat_ref[:, 0:1]
-    cos, sin = cos_ref[...], sin_ref[...]
+def q_kernel(i, n_kv, mine_ref, twin_ref, gain_ref, w_ref, sums, stat_ref, cos_ref, sin_ref, bias_ref, *refs):
+    kv_refs, (q_out, top_ref, total_ref, mix_ref) = refs[:n_kv], refs[n_kv:]
+    z, core = place()
+    half, nq = q_out.shape
+    rows, keys = slice(i * half, (i + 1) * half), slice(0, (i + 1) * half)
+    product, _, _ = project(
+        mine_ref[...], twin_ref[...], z ^ 2, core, gain_ref, None, w_ref, slice(0, nq), stats=False
+    )
+    q = (sums[rows, 0:nq] + product) * stat_ref[:, 0:1]
+    cos, sin, kv = cos_ref[rows, :], sin_ref[rows, :], joined(kv_refs)
     for h in range(nq // HEAD_SIZE):
         lanes = slice(h * HEAD_SIZE, (h + 1) * HEAD_SIZE)
         turned = turn(q[:, lanes], cos, sin).astype(BF16)
         q_out[:, lanes] = turned
-        top, total, mix = attend(turned, kv_ref[...], bias_ref[0], None)
-        at = slice(h * cap, (h + 1) * cap)
+        top, total, mix = attend(turned, kv, bias_ref[0, keys, rows], None)
+        at = slice(h * half, (h + 1) * half)
         top_ref[:, at], total_ref[:, at], mix_ref[:, at] = top, total, mix
 
 
@@ -329,42 +355,51 @@
     return [arr((1, heads * cap), F32), arr((1, heads * cap), F32), arr((HEAD_SIZE, heads * cap), F32)]
 
 
-def q_last(pair, staged, sums, stat, cos, sin, kv, bias, nq):
-    cap = sums.shape[0]
-    return call(
-        q_last_kernel,
-        "q_last",
-        (*pair, staged[0], staged[2], sums, stat, cos, sin, kv, bias),
-        [arr((cap, nq), BF16), *carry_shapes(cap, nq)],
-    )
-
-
-def attend_kernel(step, last, q_ref, kv_ref, bias_ref, top_in, total_in, mix_in, *outs):
-    cap, nq = q_ref.shape
+def q_part(i, pair, staged, sums, stat, cos, sin, kvs, bias, nq, flops):
+    half = pair[0].shape[0]
+    return call(
+        functools.partial(q_kernel, i, len(kvs)),
+        "q_part",
+        (*pair, staged[0], staged[2], sums, stat, cos, sin, bias, *kvs),
+        [arr((half, nq), BF16), *carry_shapes(half, nq)],
+        flops=flops,
+    )
+
+
+def attend_kernel(step, first_key, n_carry, last, qa_ref, qb_ref, kv_ref, bias_ref, *refs):
+    carries, outs = refs[: 3 * n_carry], refs[3 * n_carry :]
+    half, nq = qa_ref.shape
+    cap = 2 * half
+    keys = slice(first_key, first_key + kv_ref.shape[0])
     for h in range(nq // HEAD_SIZE):
         lanes = slice(h * HEAD_SIZE, (h + 1) * HEAD_SIZE)
         at = slice(h * cap, (h + 1) * cap)
-        carry = (top_in[:, at], total_in[:, at], mix_in[:, at])
-        top, total, mix = attend(q_ref[:, lanes], kv_ref[...], bias_ref[step], carry)
+        part = slice(h * cap // n_carry, (h + 1) * cap // n_carry)
+        carry = [
+            jnp.concatenate([carries[j][:, part] for j in range(k, 3 * n_carry, 3)], axis=1) for k in range(3)
+        ]
+        q = jnp.concatenate([qa_ref[:, lanes], qb_ref[:, lanes]], axis=0)
+        top, total, mix = attend(q, kv_ref[...], bias_ref[step, keys, :], carry)
         if not last:
             outs[0][:, at], outs[1][:, at], outs[2][:, at] = top, total, mix
             continue
         full, first, second = outs
-        half = cap // 2
         attn = jnp.transpose(mix * (1.0 / total)).astype(BF16)
         full[:, lanes] = attn
         first[:, lanes] = attn[:half]
         second[:, lanes] = attn[half:]
 
 
-def attend_more(step, last, q, kv, bias, carry):
-    cap, nq = q.shape
-    shapes = [arr((cap, nq), BF16), arr((cap // 2, nq), BF16), arr((cap // 2, nq), BF16)]
-    return call(
-        functools.partial(attend_kernel, step, last),
+def attend_more(step, first_key, last, qs, kv, bias, carry, flops):
+    half, nq = qs[0].shape
+    cap = 2 * half
+    shapes = [arr((cap, nq), BF16), arr((half, nq), BF16), arr((half, nq), BF16)]
+    return call(
+        functools.partial(attend_kernel, step, first_key, len(carry) // 3, last),
         "attend_more",
-        (q, kv, bias, *carry),
+        (*qs, kv, bias, *carry),
         shapes if last else carry_shapes(cap, nq),
+        flops=flops,
     )
 
 
@@ -395,7 +430,7 @@
         "out_own",
         (*mine, *twin, *rides, w_out, hidden),
         [
-            *(arr(r.shape, BF16) for r in rides),
+            *(arr(r.shape, r.dtype) for r in rides),
             arr((cap, w_out.shape[1]), F32),
             arr(w_out.shape, BF16),
             arr(hidden.shape, BF16),
@@ -421,16 +456,17 @@
         functools.partial(out_more_kernel, len(mine), len(twin), flip),
         "out_more",
         (*mine, *twin, w, total, *rides),
-        [arr(total.shape, F32), *(arr(r.shape, BF16) for r in rides)],
+        [arr(total.shape, F32), *(arr(r.shape, r.dtype) for r in rides)],
         rides={at + i: i for i in range(1 + len(rides))},
         flops=flops,
     )
 
 
-def out_last_kernel(mine_ref, twin_ref, w_ref, total_ref, stat_ref, hot_ref, hid_ref, out, out_ref, sems):
+def out_last_kernel(mine_ref, twin_ref, w_ref, total_ref, sa_ref, sb_ref, hot_ref, hid_ref, out, out_ref, sems):
     z, core = place()
     projected = total_ref[...] + out_term(mine_ref[...], twin_ref[...], z ^ 2, core, w_ref)
-    update = (stat_ref[:, 128:129] * projected).astype(BF16)
+    gate = jnp.concatenate([sa_ref[:, 128:129], sb_ref[:, 128:129]], axis=0)
+    update = (gate * projected).astype(BF16)
     block = 256
     copies = []
     for i in range(hid_ref.shape[0] // block):
@@ -441,11 +477,11 @@
     settle(copies)
 
 
-def out_last(pair, w, total, stat, hot, hidden):
+def out_last(pair, w, total, stats, hot, hidden):
     return call(
         out_last_kernel,
         "out_last",
-        (*pair, w, total, stat, hot, hidden),
+        (*pair, w, total, *stats, hot, hidden),
         [arr(hidden.shape, BF16)],
         scratch=[pltpu.VMEM(hidden.shape, BF16), pltpu.SemaphoreType.DMA((hidden.shape[0] // 256,))],
         out_hbm=True,
@@ -479,37 +515,49 @@
     flags = keep_flags.reshape(-1, 128)
     weights = (norm_gain.reshape(1, -1), router_weight.reshape(1, -1), w_query, w_key, value_weight)
 
-    full, first, second, rowpos = pick(keep_counts, keep_positions, hidden_in)
-    cos, sin = angles(rowpos)
+    full, first, second, rowpos = pick(keep_positions, hidden_in)
     held = {}
 
-    def own(mine, twin, rides):
-        *rides, held["sums"], held["bias"], held["hot"], g, r, w = own_part(
-            mine, twin, rides, weights, keep_counts, keep_positions, flags, tok
+    def own(mine, twin, _):
+        ride, held["sums"], *held["staged"] = own_part(*mine, *twin, weights)
+        return ride
+
+    def far(mine, twin, rides):
+        held["sums"], ride, held["cos"], held["sin"], held["bias"], held["hot"] = more_part(
+            mine,
+            twin,
+            held["staged"],
+            held["sums"],
+            (*rides, *angles(rowpos)),
+            lambda z: 3 - z,
+            FAR_COST,
+            (keep_counts, keep_positions, flags, tok),
         )
-        held["staged"] = (g, r, w)
-        return rides
-
-    def far(mine, twin, rides):
-        held["sums"], *rides = more_part(
-            mine, twin, held["staged"], held["sums"], rides, lambda z: 3 - z, PART_COST
-        )
-        return rides
+        return (ride,)
 
     def beside(mine, twin):
-        (held["sums"],) = more_part(mine, twin, held["staged"], held["sums"], (), lambda z: z ^ 1, PART_COST)
-
-    pair = spread(size, full, first, second, own, far, beside)
+        (held["sums"],) = more_part(mine, twin, held["staged"], held["sums"], (), lambda z: z ^ 1, BESIDE_COST)
+
+    pairs = spread_halves(size, full, first, second, own, far, beside)
     sums, staged, bias = held["sums"], held["staged"], held["bias"]
-    kv, stat = kv_last(pair, staged, sums, cos, sin, nq)
+    cos, sin = held["cos"], held["sin"]
+    half = first.shape[0]
     ring = [(s, (s + 1) % shards) for s in range(shards)]
-    moved = lax.ppermute(kv, "ctx", ring)
-    q, *carry = q_last(pair, staged, sums, stat, cos, sin, kv, bias, nq)
+    kvs, stats, moved, qs, carry = [], [], [], [], []
+    for i in range(2):
+        kv, stat = kv_last(i * half, pairs[i], staged, sums, cos, sin, nq, KV_COST)
+        kvs.append(kv)
+        stats.append(stat)
+        moved.append(lax.ppermute(kv, "ctx", ring))
+        q, *terms = q_part(i, pairs[i], staged, sums, stat, cos, sin, kvs, bias, nq, QA_COST if i == 0 else Q_COST)
+        qs.append(q)
+        carry += terms
     for step in range(1, shards):
-        last = step == shards - 1
-        carry = attend_more(step, last, q, moved, bias, carry)
-        if not last:
-            moved = lax.ppermute(moved, "ctx", ring)
+        for i in range(2):
+            last = step == shards - 1 and i == 1
+            carry = attend_more(step, i * half, last, qs, moved[i], bias, carry, ATTEND_COST)
+        if step < shards - 1:
+            moved = [lax.ppermute(kv, "ctx", ring) for kv in moved]
 
     def own_out(mine, twin, rides):
         *rides, held["total"], held["w"], held["hidden"] = out_own(mine, twin, rides, w_out, hidden_in)
@@ -523,7 +571,7 @@
         (held["total"],) = out_more(mine, twin, held["w"], held["total"], (), lambda z: z ^ 1, PART_COST)
 
     pair = spread(size, *carry, own_out, far_out, beside_out)
-    return out_last(pair, held["w"], held["total"], stat, held["hot"], held["hidden"])
+    return out_last(pair, held["w"], held["total"], stats, held["hot"], held["hidden"])
 
 
 def solution(mesh):

time: 59.9 us -> 58.3 us (0.973)
  waiting for transfers between devices: 20 us -> 16.4 us
  starting transfers between devices: 23.5 us -> 25.2 us
    ppermute x1 -> x13, starting transfers between devices: 1.56 us -> 15.7 us  [the longest x2 7.89 us: spread_halves(): last_a, last_b = (near(far[0]), near(far[1]))]
    ppermute x2 -> x1, waiting for transfers between devices: 11 us -> 5.37 us  [spread(): far = cross(full)]
    ppermute x2 -> x1, starting transfers between devices: 8.39 us -> 3.13 us  [spread(): last = near(far)]
    ppermute x2 -> x1, starting transfers between devices: 7.65 us -> 3.2 us  [spread(): far = cross(full)]
    ppermute x1 -> x13, waiting for transfers between devices: 2.29 us -> 6.71 us  [the longest x2 4.31 us: spread_halves(): last_a, last_b = (near(far[0]), near(far[1]))]
    ppermute x2 -> x1, waiting for transfers between devices: 5 us -> 2.66 us  [spread(): last = near(far)]
    ppermute x4 -> x2, starting transfers between devices: 3.77 us -> 2.03 us  [spread(): beside = (near(first), near(second))]
    ppermute x2 -> x1, waiting for transfers between devices: 1.39 us -> 1.06 us  [spread(): return (last, twin(last))]
  transfers between devices with their start and end apart: 21 -> 23, of which waited for: 9 -> 9; matrix products, arithmetic and copies ran while one was open for 1% -> 1% of each run, Pallas kernels for 17% -> 20%
where the time goes in v4:
time: 58.3 us; the launch traced here: 58 us
  starting transfers between devices  25.2 us (43%)
  waiting for transfers between devices  16.4 us (28%)
  Pallas kernels  15.6 us (27%)
    pallas_call x14, Pallas kernels, call(): pl.pallas_call(kernel, out_shape=out_shape, in_specs=[HBM if far else VME...  15.6 us
    ppermute x2, starting transfers between devices, spread_halves(): last_a, last_b = (near(far[0]), near(far[1]))  7.89 us
    ppermute x1, waiting for transfers between devices, spread(): far = cross(full)  5.37 us
    ppermute x2, starting transfers between devices, spread_halves(): far = (cross(first), cross(second))  4.77 us
    ppermute x2, waiting for transfers between devices, spread_halves(): last_a, last_b = (near(far[0]), near(far[1]))  4.31 us
    ppermute x1, starting transfers between devices, spread(): far = cross(full)  3.2 us
    ppermute x1, starting transfers between devices, spread(): last = near(far)  3.13 us
    ppermute x1, waiting for transfers between devices, spread(): last = near(far)  2.66 us
  transfers between devices with their start and end apart: 23, of which 9 were waited for; matrix products, arithmetic and copies ran while one was open for 1% of the time, Pallas kernels for 20%

profile of v4, /device:TPU:0, one launch (start us, length us, event | category | flops | bytes accessed | tf_op | source)
XLA Modules:
  0.0 58.0 jit_solution(4970130114607226360)
XLA Ops:
  0.0 1.7 %pick.1 = (bf16[256,512]{1,0:T(8,128)(2,1)S(1)}, bf16[128,512]{1,0:T(8,128)(2,1)S(1)}, bf16[128,512]{1,0:T(8,128)(2,1)S(1)}, s32[256,128]{1,0:T(8,128)S(1)}) custom-call(s32[2,256]{1,0:T(2,128)} %refs_12_.1, bf16[1024,512]{1,0:T(8,128)(2,1)} %refs_6_.1), custom_call_target="tpu_custom_call" | custom-call | flops 400000000 | bytes 1 | tf_op jit(solution)/shard_map/pick/pallas_call | solution.py:39
  1.7 0.5 collective-permute-start.4
  2.2 4.7 %collective-permute-start = (bf16[128,512]{1,0:T(8,128)(2,1)S(1)}, bf16[128,512]{1,0:T(8,128)(2,1)S(1)}, u32[]{:S(2)}, u32[]{:S(2)}) collective-permute-start(bf16[128,512]{1,0:T(8,128)(2,1)S(1)} %get-tuple-element.46), channel_id=1, source_target_pairs={{0,6},{1,7},{2,4},{3,5},{4,2},{5,3},{6,0},{7,1},{8,14},{9,15},{10,... | collective-permute-start | bytes 393224 | tf_op jit(solution)/shard_map/ppermute | solution.py:132
  6.9 0.1 collective-permute-start.1
  7.0 2.9 %own_part.1 = (bf16[256,512]{1,0:T(8,128)(2,1)S(1)}, f32[256,1024]{1,0:T(8,128)S(1)}, f32[1,4096]{1,0:T(1,128)S(1)}, f32[1,4096]{1,0:T(1,128)S(1)}, bf16[4096,768]{1,0:T(8,128)(2,1)S(1)}) custom-call(bf16[256,512]{1,0:T(8,128)(2,1)S(1)} %get-tuple-element.48.x_ref, ...), custom_call_target="tpu_custom_call", output_to_operand_aliasing={{0}: (0, {})} | custom-call | flops 400000000 | bytes 1 | tf_op jit(solution)/shard_map/own_part/pallas_call | solution.py:39
  9.9 0.1 collective-permute-start.7
  10.0 0.1 pad_maximum_fusion
  10.1 1.0 %collective-permute-done.refs_0_ = bf16[128,512]{1,0:T(8,128)(2,1)S(1)} collective-permute-done((bf16[128,512]{1,0:T(8,128)(2,1)S(1)}, bf16[128,512]{1,0:T(8,128)(2,1)S(1)}, u32[]{:S(2)}, u32[]{:S(2)}) %collective-permute-start) | collective-permute-done | bytes 131104 | tf_op jit(solution)/shard_map/ppermute | solution.py:132
  11.1 0.0 collective-permute-start.2
  11.1 5.7 %collective-permute-start.5 = (bf16[128,512]{1,0:T(8,128)(2,1)S(1)}, bf16[128,512]{1,0:T(8,128)(2,1)S(1)}, u32[]{:S(2)}, u32[]{:S(2)}) collective-permute-start(bf16[128,512]{1,0:T(8,128)(2,1)S(1)} %collective-permute-done.refs_0_), channel_id=1, source_target_pairs={{0,2},{1,3},{2,0},{3,1},{4,6},{5,7},{6,4},{7,5},{8,10},{9,11},{10,... | collective-permute-start | bytes 393224 | tf_op jit(solution)/shard_map/ppermute | solution.py:134
  16.8 0.2 collective-permute-start.3
  17.0 0.5 sine_multiply_fusion
  17.5 2.2 %collective-permute-start.9 = (bf16[128,512]{1,0:T(8,128)(2,1)S(1)}, bf16[128,512]{1,0:T(8,128)(2,1)S(1)}, u32[]{:S(2)}, u32[]{:S(2)}) collective-permute-start(bf16[128,512]{1,0:T(8,128)(2,1)S(1)} %collective-permute-done.1.refs_1_), channel_id=1, source_target_pairs={{0,2},{1,3},{2,0},{3,1},{4,6},{5,7},{6,4},{7,5},{8,10},{9,11},{10,... | collective-permute-start | bytes 393224 | tf_op jit(solution)/shard_map/ppermute | solution.py:134
  19.7 0.3 collective-permute-done.7.refs_0_
  20.0 0.0 collective-permute-start.8
  20.0 0.0 collective-permute-done.2.refs_2_
  20.0 0.0 collective-permute-done.3.refs_3_
  20.0 2.8 %collective-permute-done.5.refs_8_ = bf16[128,512]{1,0:T(8,128)(2,1)S(1)} collective-permute-done((bf16[128,512]{1,0:T(8,128)(2,1)S(1)}, bf16[128,512]{1,0:T(8,128)(2,1)S(1)}, u32[]{:S(2)}, u32[]{:S(2)}) %collective-permute-start.5) | collective-permute-done | bytes 131104 | tf_op jit(solution)/shard_map/ppermute | solution.py:134
  22.8 1.1 %more_part.2 = (f32[256,1024]{1,0:T(8,128)S(1)}, bf16[128,512]{1,0:T(8,128)(2,1)S(1)}, f32[256,128]{1,0:T(8,128)S(1)}, f32[256,128]{1,0:T(8,128)S(1)}, f32[2,256...) custom-call(bf16[128,512]{1,0:T(8,128)(2,1)S(1)} %collective-permute, ...), custom_call_target="tpu_custom_call", output_to_operand_aliasing={{0}: (7, {}), {1}: (8, {}), {2}: (9, {}), {3}: (10, {})} | custom-call | flops 1500000000 | bytes 1 | tf_op jit(solution)/shard_map/more_part/pallas_call | solution.py:39
  24.0 0.1 collective-permute-start.6
  24.1 1.5 %collective-permute-done.9.mine_ref = bf16[128,512]{1,0:T(8,128)(2,1)S(1)} collective-permute-done((bf16[128,512]{1,0:T(8,128)(2,1)S(1)}, bf16[128,512]{1,0:T(8,128)(2,1)S(1)}, u32[]{:S(2)}, u32[]{:S(2)}) %collective-permute-start.9) | collective-permute-done | bytes 131104 | tf_op jit(solution)/shard_map/ppermute | solution.py:134
  25.6 0.0 collective-permute-start.10
  25.6 0.6 %more_part.3.sums = f32[256,1024]{1,0:T(8,128)S(1)} custom-call(bf16[256,512]{1,0:T(8,128)(2,1)S(1)} %collective-permute-done.7.refs_0_, bf16[256,512]{1,0:T(8,128)(2,1)S(1)} %collective-permute-done.8.refs_1_, f32[1,4096]{1,0:T(1,128)S(1)} %get-tuple-element.49.refs_4_.refs_2_.gain_ref, ...), custom_call_target="tpu_custom_call", output_to_operand_aliasing={{}: (5, {})} | custom-call | flops 1000000 | bytes 1 | tf_op jit(solution)/shard_map/more_part/pallas_call | solution.py:39
  26.3 0.3 kv_last.2
  26.6 1.5 %collective-permute-start.12 = (bf16[128,256]{1,0:T(8,128)(2,1)S(1)}, bf16[128,256]{1,0:T(8,128)(2,1)S(1)}, u32[]{:S(2)}, u32[]{:S(2)}) collective-permute-start(bf16[128,256]{1,0:T(8,128)(2,1)S(1)} %get-tuple-element.61.refs_0_), channel_id=1, source_target_pairs={{0,8},{8,0},{1,9},{9,1},{2,10},{10,2},{3,11},{11,3},{4,12},{12,4},... | collective-permute-start | bytes 196616 | tf_op jit(solution)/shard_map/ppermute | solution.py:551
  28.1 0.0 collective-permute-done.10.twin_ref
  28.1 0.3 kv_last.3
  28.5 0.6 %collective-permute-start.11 = (bf16[128,256]{1,0:T(8,128)(2,1)S(1)}, bf16[128,256]{1,0:T(8,128)(2,1)S(1)}, u32[]{:S(2)}, u32[]{:S(2)}) collective-permute-start(bf16[128,256]{1,0:T(8,128)(2,1)S(1)} %get-tuple-element.64.refs_1_), channel_id=1, source_target_pairs={{0,8},{8,0},{1,9},{9,1},{2,10},{10,2},{3,11},{11,3},{4,12},{12,4},... | collective-permute-start | bytes 196616 | tf_op jit(solution)/shard_map/ppermute | solution.py:551
  29.1 1.1 %q_part.2 = (bf16[128,512]{1,0:T(8,128)(2,1)S(1)}, f32[1,512]{1,0:T(1,128)S(1)}, f32[1,512]{1,0:T(1,128)S(1)}, f32[128,512]{1,0:T(8,128)S(1)}) custom-call(bf16[128,512]{1,0:T(8,128)(2,1)S(1)} %get-tuple-element.54.mine_ref, bf16[128,512]{1,0:T(8,128)(2,1)S(1)} %collective-permute-done.6.twin_ref, f32[1,4096]{1,0:T(1,128)S(1)} %get-tuple-element.49.refs_4_.refs_2_.gain_ref, ...), custom_call_target="tpu_custom_call" | custom-call | flops 1500000000 | bytes 1 | tf_op jit(solution)/shard_map/q_part/pallas_call | solution.py:39
  30.2 0.9 %q_part.3 = (bf16[128,512]{1,0:T(8,128)(2,1)S(1)}, f32[1,512]{1,0:T(1,128)S(1)}, f32[1,512]{1,0:T(1,128)S(1)}, f32[128,512]{1,0:T(8,128)S(1)}) custom-call(bf16[128,512]{1,0:T(8,128)(2,1)S(1)} %collective-permute-done.9.mine_ref, bf16[128,512]{1,0:T(8,128)(2,1)S(1)} %collective-permute-done.10.twin_ref, ...), custom_call_target="tpu_custom_call" | custom-call | flops 400000000 | bytes 1 | tf_op jit(solution)/shard_map/q_part/pallas_call | solution.py:39
  31.1 0.0 collective-permute-done.12.kv_ref
  31.1 0.7 %attend_more.2 = (f32[1,1024]{1,0:T(1,128)S(1)}, f32[1,1024]{1,0:T(1,128)S(1)}, f32[128,1024]{1,0:T(8,128)S(1)}) custom-call(bf16[128,512]{1,0:T(8,128)(2,1)S(1)} %get-tuple-element.62.qa_ref, bf16[128,512]{1,0:T(8,128)(2,1)S(1)} %get-tuple-element.65.qb_ref, bf16[128,256]{1,0:T(8,128)(2,1)S(1)} %collective-permute-done.12.kv_ref, ...), custom_call_target="tpu_custom_call" | custom-call | flops 400000000 | bytes 1 | tf_op jit(solution)/shard_map/attend_more/pallas_call | solution.py:39
  31.8 1.0 %collective-permute-done.11.kv_ref = bf16[128,256]{1,0:T(8,128)(2,1)S(1)} collective-permute-done((bf16[128,256]{1,0:T(8,128)(2,1)S(1)}, bf16[128,256]{1,0:T(8,128)(2,1)S(1)}, u32[]{:S(2)}, u32[]{:S(2)}) %collective-permute-start.11) | collective-permute-done | bytes 65568 | tf_op jit(solution)/shard_map/ppermute | solution.py:551
  32.8 0.7 %attend_more.3 = (bf16[256,512]{1,0:T(8,128)(2,1)S(1)}, bf16[128,512]{1,0:T(8,128)(2,1)S(1)}, bf16[128,512]{1,0:T(8,128)(2,1)S(1)}) custom-call(bf16[128,512]{1,0:T(8,128)(2,1)S(1)} %get-tuple-element.62.qa_ref, bf16[128,512]{1,0:T(8,128)(2,1)S(1)} %get-tuple-element.65.qb_ref, bf16[128,256]{1,0:T(8,128)(2,1)S(1)} %collective-permute-done.11.kv_ref, ...), custom_call_target="tpu_custom_call" | custom-call | flops 400000000 | bytes 1 | tf_op jit(solution)/shard_map/attend_more/pallas_call | solution.py:39
  33.6 3.2 %collective-permute-start.13 = (bf16[256,512]{1,0:T(8,128)(2,1)S(1)}, bf16[256,512]{1,0:T(8,128)(2,1)S(1)}, u32[]{:S(2)}, u32[]{:S(2)}) collective-permute-start(bf16[256,512]{1,0:T(8,128)(2,1)S(1)} %get-tuple-element.75.refs_0_), channel_id=1, source_target_pairs={{0,6},{1,7},{2,4},{3,5},{4,2},{5,3},{6,0},{7,1},{8,14},{9,15},{10,... | collective-permute-start | bytes 786440 | tf_op jit(solution)/shard_map/ppermute | solution.py:118
  36.8 0.5 collective-permute-start.17
  37.3 2.0 %collective-permute-start.19 = (bf16[128,512]{1,0:T(8,128)(2,1)S(1)}, bf16[128,512]{1,0:T(8,128)(2,1)S(1)}, u32[]{:S(2)}, u32[]{:S(2)}) collective-permute-start(bf16[128,512]{1,0:T(8,128)(2,1)S(1)} %get-tuple-element.77), channel_id=1, source_target_pairs={{0,2},{1,3},{2,0},{3,1},{4,6},{5,7},{6,4},{7,5},{8,10},{9,11},{10,... | collective-permute-start | bytes 393224 | tf_op jit(solution)/shard_map/ppermute | solution.py:120
  39.3 5.4 %collective-permute-done.13.refs_0_ = bf16[256,512]{1,0:T(8,128)(2,1)S(1)} collective-permute-done((bf16[256,512]{1,0:T(8,128)(2,1)S(1)}, bf16[256,512]{1,0:T(8,128)(2,1)S(1)}, u32[]{:S(2)}, u32[]{:S(2)}) %collective-permute-start.13) | collective-permute-done | bytes 262176 | tf_op jit(solution)/shard_map/ppermute | solution.py:118
  44.7 3.1 %collective-permute-start.14 = (bf16[256,512]{1,0:T(8,128)(2,1)S(1)}, bf16[256,512]{1,0:T(8,128)(2,1)S(1)}, u32[]{:S(2)}, u32[]{:S(2)}) collective-permute-start(bf16[256,512]{1,0:T(8,128)(2,1)S(1)} %collective-permute-done.13.refs_0_), channel_id=1, source_target_pairs={{0,2},{1,3},{2,0},{3,1},{4,6},{5,7},{6,4},{7,5},{8,10},{9,11},{10,... | collective-permute-start | bytes 786440 | tf_op jit(solution)/shard_map/ppermute | solution.py:121
  47.8 0.6 %collective-permute-done.19.refs_4_ = bf16[128,512]{1,0:T(8,128)(2,1)S(1)} collective-permute-done((bf16[128,512]{1,0:T(8,128)(2,1)S(1)}, bf16[128,512]{1,0:T(8,128)(2,1)S(1)}, u32[]{:S(2)}, u32[]{:S(2)}) %collective-permute-start.19) | collective-permute-done | bytes 131104 | tf_op jit(solution)/shard_map/ppermute | solution.py:120
  48.4 2.6 %out_own.1 = (bf16[128,512]{1,0:T(8,128)(2,1)S(1)}, bf16[128,512]{1,0:T(8,128)(2,1)S(1)}, f32[256,512]{1,0:T(8,128)S(1)}, bf16[4096,512]{1,0:T(8,128)(2,1)S(1)}, bf16[1024,512]{1,0:T(8,128)(2,1)S(1)}) custom-call(bf16[256,512]{1,0:T(8,128)(2,1)S(1)} %get-tuple-element.75.refs_0_, ...), custom_call_target="tpu_custom_call", output_to_operand_aliasing={{0}: (3, {}), {1}: (4, {})} | custom-call | flops 1500000000 | bytes 1 | tf_op jit(solution)/shard_map/out_own/pallas_call | solution.py:39
  51.1 0.5 out_more.2
  51.6 0.1 collective-permute-start.21
  51.6 0.5 collective-permute-start.22
  52.1 2.7 %collective-permute-done.14.mine_ref = bf16[256,512]{1,0:T(8,128)(2,1)S(1)} collective-permute-done((bf16[256,512]{1,0:T(8,128)(2,1)S(1)}, bf16[256,512]{1,0:T(8,128)(2,1)S(1)}, u32[]{:S(2)}, u32[]{:S(2)}) %collective-permute-start.14) | collective-permute-done | bytes 262176 | tf_op jit(solution)/shard_map/ppermute | solution.py:121
  54.8 0.5 out_more.3.total_ref
  55.3 1.1 %collective-permute-done.15.twin_ref = bf16[256,512]{1,0:T(8,128)(2,1)S(1)} collective-permute-done((bf16[256,512]{1,0:T(8,128)(2,1)S(1)}, bf16[256,512]{1,0:T(8,128)(2,1)S(1)}, u32[]{:S(2)}, u32[]{:S(2)}) %collective-permute-start.15) | collective-permute-done | bytes 262176 | tf_op jit(solution)/shard_map/ppermute | solution.py:125
  56.3 1.6 %out_last.1 = bf16[1024,512]{1,0:T(8,128)(2,1)} custom-call(bf16[256,512]{1,0:T(8,128)(2,1)S(1)} %collective-permute-done.14.mine_ref, bf16[256,512]{1,0:T(8,128)(2,1)S(1)} %collective-permute-done.15.twin_ref, bf16[4096,512]{1,0:T(8,128)(2,1)S(1)} %get-tuple-element.78.refs_2_.refs_4_.w_ref, f32[256,512]{1,0:T(8,128)S(1)} %out_more.3.total_ref, ...), custom_call_target="tpu_custom_call" | custom-call | flops 400000000 | bytes 1 | tf_op jit(solution)/shard_map/out_last/pallas_call | solution.py:39
  (17 shorter events, 0.1 us)
Async XLA Ops:
  0.0 17.0 %copy-start = (f32[128]{0:T(128)S(1)}, f32[128]{0:T(128)}, u32[]{:S(2)}) copy-start(f32[128]{0:T(128)} %constant.9.clone.1) | copy-start | bytes 1540
  1.7 5.3 %collective-permute-start.4 = (bf16[256,512]{1,0:T(8,128)(2,1)S(1)}, bf16[256,512]{1,0:T(8,128)(2,1)S(1)}, u32[]{:S(2)}, u32[]{:S(2)}) collective-permute-start(bf16[256,512]{1,0:T(8,128)(2,1)S(1)} %get-tuple-element.48.x_ref), channel_id=1, source_target_pairs={{0,1},{1,0},{2,3},{3,2},{4,5},{5,4},{6,7},{7,6},{8,9},{9,8},{10,11... | collective-permute-start | bytes 786440 | tf_op jit(solution)/shard_map/ppermute | solution.py:133
  2.2 8.9 %collective-permute-start = (bf16[128,512]{1,0:T(8,128)(2,1)S(1)}, bf16[128,512]{1,0:T(8,128)(2,1)S(1)}, u32[]{:S(2)}, u32[]{:S(2)}) collective-permute-start(bf16[128,512]{1,0:T(8,128)(2,1)S(1)} %get-tuple-element.46), channel_id=1, source_target_pairs={{0,6},{1,7},{2,4},{3,5},{4,2},{5,3},{6,0},{7,1},{8,14},{9,15},{10,... | collective-permute-start | bytes 393224 | tf_op jit(solution)/shard_map/ppermute | solution.py:132
  6.9 9.9 %collective-permute-start.1 = (bf16[128,512]{1,0:T(8,128)(2,1)S(1)}, bf16[128,512]{1,0:T(8,128)(2,1)S(1)}, u32[]{:S(2)}, u32[]{:S(2)}) collective-permute-start(bf16[128,512]{1,0:T(8,128)(2,1)S(1)} %get-tuple-element.47), channel_id=1, source_target_pairs={{0,6},{1,7},{2,4},{3,5},{4,2},{5,3},{6,0},{7,1},{8,14},{9,15},{10,... | collective-permute-start | bytes 393224 | tf_op jit(solution)/shard_map/ppermute | solution.py:132
  9.9 10.1 %collective-permute-start.7 = (bf16[256,512]{1,0:T(8,128)(2,1)S(1)}, bf16[256,512]{1,0:T(8,128)(2,1)S(1)}, u32[]{:S(2)}, u32[]{:S(2)}) collective-permute-start(bf16[256,512]{1,0:T(8,128)(2,1)S(1)} %get-tuple-element.55), channel_id=1, source_target_pairs={{0,2},{1,3},{2,0},{3,1},{4,6},{5,7},{6,4},{7,5},{8,10},{9,11},{10,... | collective-permute-start | bytes 786440 | tf_op jit(solution)/shard_map/ppermute | solution.py:133
  11.1 8.9 %collective-permute-start.2 = (bf16[128,512]{1,0:T(8,128)(2,1)S(1)}, bf16[128,512]{1,0:T(8,128)(2,1)S(1)}, u32[]{:S(2)}, u32[]{:S(2)}) collective-permute-start(bf16[128,512]{1,0:T(8,128)(2,1)S(1)} %collective-permute-done.refs_0_), channel_id=1, source_target_pairs={{0,1},{1,0},{2,3},{3,2},{4,5},{5,4},{6,7},{7,6},{8,9},{9,8},{10,11... | collective-permute-start | bytes 393224 | tf_op jit(solution)/shard_map/ppermute | solution.py:135
  11.1 11.7 %collective-permute-start.5 = (bf16[128,512]{1,0:T(8,128)(2,1)S(1)}, bf16[128,512]{1,0:T(8,128)(2,1)S(1)}, u32[]{:S(2)}, u32[]{:S(2)}) collective-permute-start(bf16[128,512]{1,0:T(8,128)(2,1)S(1)} %collective-permute-done.refs_0_), channel_id=1, source_target_pairs={{0,2},{1,3},{2,0},{3,1},{4,6},{5,7},{6,4},{7,5},{8,10},{9,11},{10,... | collective-permute-start | bytes 393224 | tf_op jit(solution)/shard_map/ppermute | solution.py:134
  16.8 3.2 %collective-permute-start.3 = (bf16[128,512]{1,0:T(8,128)(2,1)S(1)}, bf16[128,512]{1,0:T(8,128)(2,1)S(1)}, u32[]{:S(2)}, u32[]{:S(2)}) collective-permute-start(bf16[128,512]{1,0:T(8,128)(2,1)S(1)} %collective-permute-done.1.refs_1_), channel_id=1, source_target_pairs={{0,1},{1,0},{2,3},{3,2},{4,5},{5,4},{6,7},{7,6},{8,9},{9,8},{10,11... | collective-permute-start | bytes 393224 | tf_op jit(solution)/shard_map/ppermute | solution.py:135
  17.5 8.0 %collective-permute-start.9 = (bf16[128,512]{1,0:T(8,128)(2,1)S(1)}, bf16[128,512]{1,0:T(8,128)(2,1)S(1)}, u32[]{:S(2)}, u32[]{:S(2)}) collective-permute-start(bf16[128,512]{1,0:T(8,128)(2,1)S(1)} %collective-permute-done.1.refs_1_), channel_id=1, source_target_pairs={{0,2},{1,3},{2,0},{3,1},{4,6},{5,7},{6,4},{7,5},{8,10},{9,11},{10,... | collective-permute-start | bytes 393224 | tf_op jit(solution)/shard_map/ppermute | solution.py:134
  20.0 5.6 %collective-permute-start.8 = (bf16[256,512]{1,0:T(8,128)(2,1)S(1)}, bf16[256,512]{1,0:T(8,128)(2,1)S(1)}, u32[]{:S(2)}, u32[]{:S(2)}) collective-permute-start(bf16[256,512]{1,0:T(8,128)(2,1)S(1)} %collective-permute-done.7.refs_0_), channel_id=1, source_target_pairs={{0,1},{1,0},{2,3},{3,2},{4,5},{5,4},{6,7},{7,6},{8,9},{9,8},{10,11... | collective-permute-start | bytes 786440 | tf_op jit(solution)/shard_map/ppermute | solution.py:136
  24.0 2.3 %collective-permute-start.6 = (bf16[128,512]{1,0:T(8,128)(2,1)S(1)}, bf16[128,512]{1,0:T(8,128)(2,1)S(1)}, u32[]{:S(2)}, u32[]{:S(2)}) collective-permute-start(bf16[128,512]{1,0:T(8,128)(2,1)S(1)} %get-tuple-element.54.mine_ref), channel_id=1, source_target_pairs={{0,1},{1,0},{2,3},{3,2},{4,5},{5,4},{6,7},{7,6},{8,9},{9,8},{10,11... | collective-permute-start | bytes 393224 | tf_op jit(solution)/shard_map/ppermute | solution.py:137
  25.6 2.6 %collective-permute-start.10 = (bf16[128,512]{1,0:T(8,128)(2,1)S(1)}, bf16[128,512]{1,0:T(8,128)(2,1)S(1)}, u32[]{:S(2)}, u32[]{:S(2)}) collective-permute-start(bf16[128,512]{1,0:T(8,128)(2,1)S(1)} %collective-permute-done.9.mine_ref), channel_id=1, source_target_pairs={{0,1},{1,0},{2,3},{3,2},{4,5},{5,4},{6,7},{7,6},{8,9},{9,8},{10,11... | collective-permute-start | bytes 393224 | tf_op jit(solution)/shard_map/ppermute | solution.py:137
  26.6 4.5 %collective-permute-start.12 = (bf16[128,256]{1,0:T(8,128)(2,1)S(1)}, bf16[128,256]{1,0:T(8,128)(2,1)S(1)}, u32[]{:S(2)}, u32[]{:S(2)}) collective-permute-start(bf16[128,256]{1,0:T(8,128)(2,1)S(1)} %get-tuple-element.61.refs_0_), channel_id=1, source_target_pairs={{0,8},{8,0},{1,9},{9,1},{2,10},{10,2},{3,11},{11,3},{4,12},{12,4},... | collective-permute-start | bytes 196616 | tf_op jit(solution)/shard_map/ppermute | solution.py:551
  28.5 4.3 %collective-permute-start.11 = (bf16[128,256]{1,0:T(8,128)(2,1)S(1)}, bf16[128,256]{1,0:T(8,128)(2,1)S(1)}, u32[]{:S(2)}, u32[]{:S(2)}) collective-permute-start(bf16[128,256]{1,0:T(8,128)(2,1)S(1)} %get-tuple-element.64.refs_1_), channel_id=1, source_target_pairs={{0,8},{8,0},{1,9},{9,1},{2,10},{10,2},{3,11},{11,3},{4,12},{12,4},... | collective-permute-start | bytes 196616 | tf_op jit(solution)/shard_map/ppermute | solution.py:551
  33.6 11.1 %collective-permute-start.13 = (bf16[256,512]{1,0:T(8,128)(2,1)S(1)}, bf16[256,512]{1,0:T(8,128)(2,1)S(1)}, u32[]{:S(2)}, u32[]{:S(2)}) collective-permute-start(bf16[256,512]{1,0:T(8,128)(2,1)S(1)} %get-tuple-element.75.refs_0_), channel_id=1, source_target_pairs={{0,6},{1,7},{2,4},{3,5},{4,2},{5,3},{6,0},{7,1},{8,14},{9,15},{10,... | collective-permute-start | bytes 786440 | tf_op jit(solution)/shard_map/ppermute | solution.py:118
  36.8 7.9 %collective-permute-start.16 = (bf16[128,512]{1,0:T(8,128)(2,1)S(1)}, bf16[128,512]{1,0:T(8,128)(2,1)S(1)}, u32[]{:S(2)}, u32[]{:S(2)}) collective-permute-start(bf16[128,512]{1,0:T(8,128)(2,1)S(1)} %get-tuple-element.76), channel_id=1, source_target_pairs={{0,1},{1,0},{2,3},{3,2},{4,5},{5,4},{6,7},{7,6},{8,9},{9,8},{10,11... | collective-permute-start | bytes 393224 | tf_op jit(solution)/shard_map/ppermute | solution.py:119
  36.8 11.0 %collective-permute-start.17 = (bf16[128,512]{1,0:T(8,128)(2,1)S(1)}, bf16[128,512]{1,0:T(8,128)(2,1)S(1)}, u32[]{:S(2)}, u32[]{:S(2)}) collective-permute-start(bf16[128,512]{1,0:T(8,128)(2,1)S(1)} %get-tuple-element.77), channel_id=1, source_target_pairs={{0,1},{1,0},{2,3},{3,2},{4,5},{5,4},{6,7},{7,6},{8,9},{9,8},{10,11... | collective-permute-start | bytes 393224 | tf_op jit(solution)/shard_map/ppermute | solution.py:119
  37.3 10.5 %collective-permute-start.18 = (bf16[128,512]{1,0:T(8,128)(2,1)S(1)}, bf16[128,512]{1,0:T(8,128)(2,1)S(1)}, u32[]{:S(2)}, u32[]{:S(2)}) collective-permute-start(bf16[128,512]{1,0:T(8,128)(2,1)S(1)} %get-tuple-element.76), channel_id=1, source_target_pairs={{0,2},{1,3},{2,0},{3,1},{4,6},{5,7},{6,4},{7,5},{8,10},{9,11},{10,... | collective-permute-start | bytes 393224 | tf_op jit(solution)/shard_map/ppermute | solution.py:120
  37.3 11.1 %collective-permute-start.19 = (bf16[128,512]{1,0:T(8,128)(2,1)S(1)}, bf16[128,512]{1,0:T(8,128)(2,1)S(1)}, u32[]{:S(2)}, u32[]{:S(2)}) collective-permute-start(bf16[128,512]{1,0:T(8,128)(2,1)S(1)} %get-tuple-element.77), channel_id=1, source_target_pairs={{0,2},{1,3},{2,0},{3,1},{4,6},{5,7},{6,4},{7,5},{8,10},{9,11},{10,... | collective-permute-start | bytes 393224 | tf_op jit(solution)/shard_map/ppermute | solution.py:120
  44.7 6.4 %collective-permute-start.20 = (bf16[256,512]{1,0:T(8,128)(2,1)S(1)}, bf16[256,512]{1,0:T(8,128)(2,1)S(1)}, u32[]{:S(2)}, u32[]{:S(2)}) collective-permute-start(bf16[256,512]{1,0:T(8,128)(2,1)S(1)} %collective-permute-done.13.refs_0_), channel_id=1, source_target_pairs={{0,1},{1,0},{2,3},{3,2},{4,5},{5,4},{6,7},{7,6},{8,9},{9,8},{10,11... | collective-permute-start | bytes 786440 | tf_op jit(solution)/shard_map/ppermute | solution.py:123
  44.7 10.1 %collective-permute-start.14 = (bf16[256,512]{1,0:T(8,128)(2,1)S(1)}, bf16[256,512]{1,0:T(8,128)(2,1)S(1)}, u32[]{:S(2)}, u32[]{:S(2)}) collective-permute-start(bf16[256,512]{1,0:T(8,128)(2,1)S(1)} %collective-permute-done.13.refs_0_), channel_id=1, source_target_pairs={{0,2},{1,3},{2,0},{3,1},{4,6},{5,7},{6,4},{7,5},{8,10},{9,11},{10,... | collective-permute-start | bytes 786440 | tf_op jit(solution)/shard_map/ppermute | solution.py:121
  51.6 3.2 %collective-permute-start.21 = (bf16[128,512]{1,0:T(8,128)(2,1)S(1)}, bf16[128,512]{1,0:T(8,128)(2,1)S(1)}, u32[]{:S(2)}, u32[]{:S(2)}) collective-permute-start(bf16[128,512]{1,0:T(8,128)(2,1)S(1)} %get-tuple-element.82.refs_0_), channel_id=1, source_target_pairs={{0,1},{1,0},{2,3},{3,2},{4,5},{5,4},{6,7},{7,6},{8,9},{9,8},{10,11... | collective-permute-start | bytes 393224 | tf_op jit(solution)/shard_map/ppermute | solution.py:124
  51.6 3.2 %collective-permute-start.22 = (bf16[128,512]{1,0:T(8,128)(2,1)S(1)}, bf16[128,512]{1,0:T(8,128)(2,1)S(1)}, u32[]{:S(2)}, u32[]{:S(2)}) collective-permute-start(bf16[128,512]{1,0:T(8,128)(2,1)S(1)} %get-tuple-element.83.refs_1_), channel_id=1, source_target_pairs={{0,1},{1,0},{2,3},{3,2},{4,5},{5,4},{6,7},{7,6},{8,9},{9,8},{10,11... | collective-permute-start | bytes 393224 | tf_op jit(solution)/shard_map/ppermute | solution.py:124
  54.8 1.5 %collective-permute-start.15 = (bf16[256,512]{1,0:T(8,128)(2,1)S(1)}, bf16[256,512]{1,0:T(8,128)(2,1)S(1)}, u32[]{:S(2)}, u32[]{:S(2)}) collective-permute-start(bf16[256,512]{1,0:T(8,128)(2,1)S(1)} %collective-permute-done.14.mine_ref), channel_id=1, source_target_pairs={{0,1},{1,0},{2,3},{3,2},{4,5},{5,4},{6,7},{7,6},{8,9},{9,8},{10,11... | collective-permute-start | bytes 786440 | tf_op jit(solution)/shard_map/ppermute | solution.py:125

commit v5 on v4

--- a/solution.py
+++ b/solution.py
@@ -17,7 +17,8 @@
 I32 = jnp.int32
 COST = 400_000_000
 PART_COST = 1_500_000_000
-OWN_COST = 400_000_000
+OWN_COST = 1_500_000_000
+GATE_COST = 1_000_000
 FAR_COST = 1_500_000_000
 BESIDE_COST = 1_000_000
 KV_COST = 400_000_000
@@ -72,16 +73,21 @@
 
 
 def pick_kernel(pos_hbm, hid_hbm, x_ref, xa_ref, xb_ref, rowpos_ref, pos_ref, hid_ref, sems):
-    copies = fetch([(pos_hbm, pos_ref), (hid_hbm, hid_ref)], sems)
     own, shards = lax.axis_index("ctx"), lax.axis_size("ctx")
     tok, cap = hid_ref.shape[0], x_ref.shape[0]
+    pieces = [slice(at, at + 256) for at in range(0, tok, 256)]
+    copies = fetch([(pos_hbm, pos_ref), *((hid_hbm.at[p, :], hid_ref.at[p, :]) for p in pieces)], sems)
     copies[0].wait()
     pos = column(pos_ref[pl.ds(own, 1), :])
     rowpos_ref[...] = jnp.where(pos < 0, shards * tok, pos)
     local = pos[:, :1] - own * tok
-    hot = (lax.broadcasted_iota(I32, (cap, tok), 1) == local).astype(F32).astype(BF16)
-    copies[1].wait()
-    x = jnp.dot(hot, hid_ref[...], preferred_element_type=F32).astype(BF16)
+    total = None
+    for piece, copy in zip(pieces, copies[1:]):
+        at = lax.broadcasted_iota(I32, (cap, 256), 1) + piece.start
+        hot = jnp.where(at == local, 1.0, 0.0).astype(BF16)
+        copy.wait()
+        total = add(total, jnp.dot(hot, hid_ref[piece, :], preferred_element_type=F32))
+    x = total.astype(BF16)
     x_ref[...] = x
     xa_ref[...] = x[: cap // 2]
     xb_ref[...] = x[cap // 2 :]
@@ -97,7 +103,7 @@
         scratch=[
             pltpu.VMEM(positions.shape, I32),
             pltpu.VMEM(hidden.shape, BF16),
-            pltpu.SemaphoreType.DMA((2,)),
+            pltpu.SemaphoreType.DMA((1 + hidden.shape[0] // 256,)),
         ],
         hbm=(positions, hidden),
     )
@@ -109,6 +115,10 @@
 
 def chip_sender(size, f):
     return sender([(2 * z + c, 2 * f(z) + c) for z in range(size // 2) for c in range(2)])
+
+
+def gate(ride, other):
+    return call(lambda *_: None, "gate", (ride, other), [arr(ride.shape, ride.dtype)], rides={0: 0}, flops=GATE_COST)[0]
 
 
 def spread(size, full, first, second, use_own, use_far, use_beside):
@@ -130,7 +140,9 @@
     near = chip_sender(size, lambda z: z ^ 1)
     twin = sender([(d, d ^ 1) for d in range(size)])
     far = cross(first), cross(second)
-    beside = near(use_own((full,), (twin(full),), full))
+    mate = twin(full)
+    full = gate(full, mate)
+    beside = use_own((full,), (mate,), near(full))
     last_a, last_b = near(far[0]), near(far[1])
     (last_a,) = use_far(far, (twin(far[0]), twin(far[1])), (last_a,))
     use_beside((beside,), (twin(beside),))
@@ -176,7 +188,8 @@
         copy.wait()
 
 
-def own_kernel(x_ref, twin_ref, gain, router, wq, wk, wv, _, sums_ref, gain_ref, router_ref, w_ref, sems):
+def own_kernel(x_ref, twin_ref, _, gain, router, wq, wk, wv, cnt, pos, flag, *refs):
+    _, sums_ref, gain_ref, router_ref, w_ref, bias_ref, hot_ref, sems = refs[:8]
     z, core = place()
     nq, nk, depth = wq.shape[1], wk.shape[1], wq.shape[0]
     lanes = ((wq, slice(0, nq)), (wk, slice(nq, nq + nk)), (wv, slice(nq + nk, nq + 2 * nk)))
@@ -194,28 +207,38 @@
     sums_ref[:, 0:n] = product
     sums_ref[:, n : n + 128] = squares
     sums_ref[:, n + 128 : n + 256] = routed
+    masks_kernel(cnt, pos, flag, bias_ref, hot_ref, *refs[8:])
     for later in copies[1:]:
         settle(later)
 
 
-def own_part(full, twin, weights):
+def own_part(full, twin, ride, weights, counts, positions, flags, tok):
     cap, width = full.shape
     depth = weights[2].shape[0]
     columns = sum(w.shape[1] for w in weights[2:])
+    shards = positions.shape[0]
     return call(
         own_kernel,
         "own_part",
-        (full, twin, *weights),
+        (full, twin, ride, *weights, counts, positions, flags),
         [
-            arr(full.shape, BF16),
+            arr(ride.shape, BF16),
             arr((cap, columns + 256), F32),
             arr((1, depth), F32),
             arr((1, depth), F32),
             arr((depth, columns), BF16),
+            arr((shards, cap, cap), F32),
+            arr((tok, cap), BF16),
         ],
-        scratch=[pltpu.SemaphoreType.DMA((3 * depth // (2 * width) + 2,))],
-        rides={0: 0},
-        hbm=weights,
+        scratch=[
+            pltpu.SemaphoreType.DMA((3 * depth // (2 * width) + 2,)),
+            pltpu.SMEM(counts.shape, I32),
+            pltpu.VMEM(positions.shape, I32),
+            pltpu.VMEM(flags.shape, I32),
+            pltpu.SemaphoreType.DMA((3,)),
+        ],
+        rides={2: 0},
+        hbm=(*weights, counts, positions, flags),
         flops=OWN_COST,
     )
 
@@ -238,12 +261,10 @@
         hot_ref[r * 128 : (r + 1) * 128, :] = hot.astype(BF16)
 
 
-def more_kernel(n_mine, n_twin, n_ride, flip, masks, *refs):
+def more_kernel(n_mine, n_twin, n_ride, flip, *refs):
     mine, twin, refs = refs[:n_mine], refs[n_mine : n_mine + n_twin], refs[n_mine + n_twin :]
     gain_ref, router_ref, w_ref, sums_in = refs[:4]
-    refs = refs[4 + n_ride :]
-    n_far = 3 if masks else 0
-    sums_out = refs[n_far]
+    sums_out = refs[4 + n_ride]
     z, core = place()
     product, squares, routed = project(
         joined(mine), joined(twin), flip(z), core, gain_ref, router_ref, w_ref, slice(None)
@@ -252,31 +273,16 @@
     sums_out[:, 0:n] = sums_in[:, 0:n] + product
     sums_out[:, n : n + 128] = sums_in[:, n : n + 128] + squares
     sums_out[:, n + 128 : n + 256] = sums_in[:, n + 128 : n + 256] + routed
-    if masks:
-        masks_kernel(*refs[:3], *refs[4 + n_ride :])
-
-
-def more_part(mine, twin, staged, sums, rides, flip, flops, masks=None):
+
+
+def more_part(mine, twin, staged, sums, rides, flip, flops):
     at = len(mine) + len(twin) + 3
-    shapes, scratch, far = [], [], ()
-    if masks:
-        *far, tok = masks
-        shards, cap = far[1].shape
-        shapes = [arr((shards, cap, cap), F32), arr((tok, cap), BF16)]
-        scratch = [
-            pltpu.SMEM(far[0].shape, I32),
-            pltpu.VMEM(far[1].shape, I32),
-            pltpu.VMEM(far[2].shape, I32),
-            pltpu.SemaphoreType.DMA((3,)),
-        ]
-    return call(
-        functools.partial(more_kernel, len(mine), len(twin), len(rides), flip, bool(masks)),
+    return call(
+        functools.partial(more_kernel, len(mine), len(twin), len(rides), flip),
         "more_part",
-        (*mine, *twin, *staged, sums, *rides, *far),
-        [arr(sums.shape, F32), *(arr(r.shape, r.dtype) for r in rides), *shapes],
-        scratch=scratch,
+        (*mine, *twin, *staged, sums, *rides),
+        [arr(sums.shape, F32), *(arr(r.shape, r.dtype) for r in rides)],
         rides={at + i: i for i in range(1 + len(rides))},
-        hbm=far,
         flops=flops,
     )
 
@@ -518,20 +524,15 @@
     full, first, second, rowpos = pick(keep_positions, hidden_in)
     held = {}
 
-    def own(mine, twin, _):
-        ride, held["sums"], *held["staged"] = own_part(*mine, *twin, weights)
+    def own(mine, twin, ride):
+        ride, held["sums"], *held["staged"], held["bias"], held["hot"] = own_part(
+            *mine, *twin, ride, weights, keep_counts, keep_positions, flags, tok
+        )
         return ride
 
     def far(mine, twin, rides):
-        held["sums"], ride, held["cos"], held["sin"], held["bias"], held["hot"] = more_part(
-            mine,
-            twin,
-            held["staged"],
-            held["sums"],
-            (*rides, *angles(rowpos)),
-            lambda z: 3 - z,
-            FAR_COST,
-            (keep_counts, keep_positions, flags, tok),
+        held["sums"], ride, held["cos"], held["sin"] = more_part(
+            mine, twin, held["staged"], held["sums"], (*rides, *angles(rowpos)), lambda z: 3 - z, FAR_COST
         )
         return (ride,)
 
@@ -542,13 +543,13 @@
     sums, staged, bias = held["sums"], held["staged"], held["bias"]
     cos, sin = held["cos"], held["sin"]
     half = first.shape[0]
-    ring = [(s, (s + 1) % shards) for s in range(shards)]
+    onward = [(s, s + 1) for s in range(shards - 1)]
     kvs, stats, moved, qs, carry = [], [], [], [], []
     for i in range(2):
         kv, stat = kv_last(i * half, pairs[i], staged, sums, cos, sin, nq, KV_COST)
         kvs.append(kv)
         stats.append(stat)
-        moved.append(lax.ppermute(kv, "ctx", ring))
+        moved.append(lax.ppermute(kv, "ctx", onward))
         q, *terms = q_part(i, pairs[i], staged, sums, stat, cos, sin, kvs, bias, nq, QA_COST if i == 0 else Q_COST)
         qs.append(q)
         carry += terms
@@ -557,7 +558,7 @@
             last = step == shards - 1 and i == 1
             carry = attend_more(step, i * half, last, qs, moved[i], bias, carry, ATTEND_COST)
         if step < shards - 1:
-            moved = [lax.ppermute(kv, "ctx", ring) for kv in moved]
+            moved = [lax.ppermute(kv, "ctx", onward) for kv in moved]
 
     def own_out(mine, twin, rides):
         *rides, held["total"], held["w"], held["hidden"] = out_own(mine, twin, rides, w_out, hidden_in)

time: 58.3 us -> 61 us (1.046)
  starting transfers between devices: 25.2 us -> 30.1 us
  waiting for transfers between devices: 16.4 us -> 13.5 us
  other arithmetic: 0.56 us -> 1.22 us
    ppermute x2, waiting for transfers between devices: 4.31 us -> 0.87 us  [spread_halves(): last_a, last_b = (near(far[0]), near(far[1]))]
    ppermute x4, starting transfers between devices: 2.75 us -> 5.27 us  [the longest x2 4.67 us: body(): moved.append(lax.ppermute(kv, 'ctx', onward))]
    ppermute x2, waiting for transfers between devices: 1.02 us -> 2.9 us  [spread_halves(): far = (cross(first), cross(second))]
    ppermute x1, starting transfers between devices: 3.13 us -> 4.76 us  [spread(): last = near(far)]
    ppermute x4, waiting for transfers between devices: 1.36 us -> 0.45 us  [the longest x1 0.45 us: spread_halves(): beside = use_own((full,), (mate,), near(full))]
    mul x1, other arithmetic: 0.48 us -> 1.13 us  [angles(): return (jnp.cos(turned), jnp.sin(turned) * sign[None, :])]
    pallas_call x14 -> x15, Pallas kernels: 15.6 us -> 15.6 us  [call(): pl.pallas_call(kernel, out_shape=out_shape, in_specs=[HBM if far else VME...]
  transfers between devices with their start and end apart: 23 -> 23, of which waited for: 9 -> 7; matrix products, arithmetic and copies ran while one was open for 1% -> 2% of each run, Pallas kernels for 20% -> 19%
where the time goes in v5:
time: 61 us; the launch traced here: 60.6 us
  starting transfers between devices  30.1 us (49%)
  Pallas kernels  15.6 us (26%)
  waiting for transfers between devices  13.5 us (22%)
  other arithmetic  1.22 us (2%)
    pallas_call x15, Pallas kernels, call(): pl.pallas_call(kernel, out_shape=out_shape, in_specs=[HBM if far else VME...  15.6 us
    ppermute x2, starting transfers between devices, spread_halves(): last_a, last_b = (near(far[0]), near(far[1]))  7.72 us
    ppermute x1, waiting for transfers between devices, spread(): far = cross(full)  4.95 us
    ppermute x2, starting transfers between devices, spread_halves(): far = (cross(first), cross(second))  4.78 us
    ppermute x1, starting transfers between devices, spread(): last = near(far)  4.76 us
    ppermute x2, starting transfers between devices, body(): moved.append(lax.ppermute(kv, 'ctx', onward))  4.67 us
    ppermute x1, starting transfers between devices, spread(): far = cross(full)  3.6 us
    ppermute x1, waiting for transfers between devices, spread(): last = near(far)  3.12 us
  transfers between devices with their start and end apart: 23, of which 7 were waited for; matrix products, arithmetic and copies ran while one was open for 2% of the time, Pallas kernels for 19%

profile of v5, /device:TPU:0, one launch (start us, length us, event | category | flops | bytes accessed | tf_op | source)
XLA Modules:
  0.0 60.6 jit_solution(14610527907977688990)
XLA Ops:
  0.0 1.6 %pick.1 = (bf16[256,512]{1,0:T(8,128)(2,1)S(1)}, bf16[128,512]{1,0:T(8,128)(2,1)S(1)}, bf16[128,512]{1,0:T(8,128)(2,1)S(1)}, s32[256,128]{1,0:T(8,128)S(1)}) custom-call(s32[2,256]{1,0:T(2,128)} %pos.1, bf16[1024,512]{1,0:T(8,128)(2,1)} %refs_6_.1), custom_call_target="tpu_custom_call" | custom-call | flops 400000000 | bytes 1 | tf_op jit(solution)/shard_map/pick/pallas_call | solution.py:40
  1.6 0.5 collective-permute-start.4
  2.1 4.7 %collective-permute-start = (bf16[128,512]{1,0:T(8,128)(2,1)S(1)}, bf16[128,512]{1,0:T(8,128)(2,1)S(1)}, u32[]{:S(2)}, u32[]{:S(2)}) collective-permute-start(bf16[128,512]{1,0:T(8,128)(2,1)S(1)} %get-tuple-element.46), channel_id=1, source_target_pairs={{0,6},{1,7},{2,4},{3,5},{4,2},{5,3},{6,0},{7,1},{8,14},{9,15},{10,... | collective-permute-start | bytes 393224 | tf_op jit(solution)/shard_map/ppermute | solution.py:142
  6.8 0.1 collective-permute-start.1
  6.9 0.0 collective-permute-done.4.__1_.twin_ref
  6.9 0.1 collective-permute-start.5
  7.0 0.1 pad_maximum_fusion
  7.1 1.1 %sine_multiply_fusion = (f32[256,128]{1,0:T(8,128)S(1)}, f32[256,128]{1,0:T(8,128)S(1)}) fusion(s32[256,128]{1,0:T(8,128)S(1)} %get-tuple-element.53, f32[128]{0:T(128)} %constant.9.clone.1, f32[128]{0:T(128)S(1)} %pad_maximum_fusion), kind=kLoop, calls=%fused_computation | loop fusion | flops 98304 | bytes 394240 | tf_op jit(solution)/shard_map/mul | solution.py:502
  8.2 2.9 %collective-permute-done.refs_0_ = bf16[128,512]{1,0:T(8,128)(2,1)S(1)} collective-permute-done((bf16[128,512]{1,0:T(8,128)(2,1)S(1)}, bf16[128,512]{1,0:T(8,128)(2,1)S(1)}, u32[]{:S(2)}, u32[]{:S(2)}) %collective-permute-start) | collective-permute-done | bytes 131104 | tf_op jit(solution)/shard_map/ppermute | solution.py:142
  11.1 0.0 collective-permute-start.2
  11.1 5.6 %collective-permute-start.6 = (bf16[128,512]{1,0:T(8,128)(2,1)S(1)}, bf16[128,512]{1,0:T(8,128)(2,1)S(1)}, u32[]{:S(2)}, u32[]{:S(2)}) collective-permute-start(bf16[128,512]{1,0:T(8,128)(2,1)S(1)} %collective-permute-done.refs_0_), channel_id=1, source_target_pairs={{0,2},{1,3},{2,0},{3,1},{4,6},{5,7},{6,4},{7,5},{8,10},{9,11},{10,... | collective-permute-start | bytes 393224 | tf_op jit(solution)/shard_map/ppermute | solution.py:146
  16.7 0.0 collective-permute-done.1.refs_1_
  16.7 0.2 collective-permute-start.3
  17.0 2.1 %collective-permute-start.9 = (bf16[128,512]{1,0:T(8,128)(2,1)S(1)}, bf16[128,512]{1,0:T(8,128)(2,1)S(1)}, u32[]{:S(2)}, u32[]{:S(2)}) collective-permute-start(bf16[128,512]{1,0:T(8,128)(2,1)S(1)} %collective-permute-done.1.refs_1_), channel_id=1, source_target_pairs={{0,2},{1,3},{2,0},{3,1},{4,6},{5,7},{6,4},{7,5},{8,10},{9,11},{10,... | collective-permute-start | bytes 393224 | tf_op jit(solution)/shard_map/ppermute | solution.py:146
  19.1 0.4 collective-permute-done.5._
  19.5 3.3 %own_part.1 = (bf16[256,512]{1,0:T(8,128)(2,1)S(1)}, f32[256,1024]{1,0:T(8,128)S(1)}, f32[1,4096]{1,0:T(1,128)S(1)}, f32[1,4096]{1,0:T(1,128)S(1)}, bf16[4096,76...) custom-call(bf16[256,512]{1,0:T(8,128)(2,1)S(1)} %gate.1.x_ref, ...), custom_call_target="tpu_custom_call", output_to_operand_aliasing={{0}: (2, {})} | custom-call | flops 1500000000 | bytes 1 | tf_op jit(solution)/shard_map/own_part/pallas_call | solution.py:40
  22.9 0.1 collective-permute-start.8
  23.0 0.0 collective-permute-done.2.refs_2_
  23.0 0.7 %more_part.2 = (f32[256,1024]{1,0:T(8,128)S(1)}, bf16[128,512]{1,0:T(8,128)(2,1)S(1)}, f32[256,128]{1,0:T(8,128)S(1)}, f32[256,128]{1,0:T(8,128)S(1)}) custom-call(bf16[128,512]{1,0:T(8,128)(2,1)S(1)} %collective-permute-done.refs_0_, ...), custom_call_target="tpu_custom_call", output_to_operand_aliasing={{0}: (7, {}), {1}: (8, {}), {2}: (9, {}), {3}: (10, {})} | custom-call | flops 1500000000 | bytes 1 | tf_op jit(solution)/shard_map/more_part/pallas_call | solution.py:40
  23.7 0.5 collective-permute-start.7
  24.2 0.9 %collective-permute-done.9.mine_ref = bf16[128,512]{1,0:T(8,128)(2,1)S(1)} collective-permute-done((bf16[128,512]{1,0:T(8,128)(2,1)S(1)}, bf16[128,512]{1,0:T(8,128)(2,1)S(1)}, u32[]{:S(2)}, u32[]{:S(2)}) %collective-permute-start.9) | collective-permute-done | bytes 131104 | tf_op jit(solution)/shard_map/ppermute | solution.py:146
  25.1 0.0 collective-permute-start.10
  25.1 0.0 collective-permute-done.8.refs_1_
  25.1 0.6 %more_part.3.sums = f32[256,1024]{1,0:T(8,128)S(1)} custom-call(bf16[256,512]{1,0:T(8,128)(2,1)S(1)} %get-tuple-element.55.refs_0_, bf16[256,512]{1,0:T(8,128)(2,1)S(1)} %collective-permute-done.8.refs_1_, f32[1,4096]{1,0:T(1,128)S(1)} %get-tuple-element.49.refs_4_.refs_2_.gain_ref, ...), custom_call_target="tpu_custom_call", output_to_operand_aliasing={{}: (5, {})} | custom-call | flops 1000000 | bytes 1 | tf_op jit(solution)/shard_map/more_part/pallas_call | solution.py:40
  25.8 0.3 kv_last.2
  26.1 3.4 %collective-permute-start.12 = (bf16[128,256]{1,0:T(8,128)(2,1)S(1)}, bf16[128,256]{1,0:T(8,128)(2,1)S(1)}, u32[]{:S(2)}, u32[]{:S(2)}) collective-permute-start(bf16[128,256]{1,0:T(8,128)(2,1)S(1)} %get-tuple-element.61.refs_0_), channel_id=1, source_target_pairs={{0,8},{1,9},{2,10},{3,11},{4,12},{5,13},{6,14},{7,15},{16,24},{17,... | collective-permute-start | bytes 196616 | tf_op jit(solution)/shard_map/ppermute | solution.py:552
  29.5 0.0 collective-permute-done.10.twin_ref
  29.5 0.4 kv_last.3
  29.9 1.3 %collective-permute-start.11 = (bf16[128,256]{1,0:T(8,128)(2,1)S(1)}, bf16[128,256]{1,0:T(8,128)(2,1)S(1)}, u32[]{:S(2)}, u32[]{:S(2)}) collective-permute-start(bf16[128,256]{1,0:T(8,128)(2,1)S(1)} %get-tuple-element.64.refs_1_), channel_id=1, source_target_pairs={{0,8},{1,9},{2,10},{3,11},{4,12},{5,13},{6,14},{7,15},{16,24},{17,... | collective-permute-start | bytes 196616 | tf_op jit(solution)/shard_map/ppermute | solution.py:552
  31.2 1.1 %q_part.2 = (bf16[128,512]{1,0:T(8,128)(2,1)S(1)}, f32[1,512]{1,0:T(1,128)S(1)}, f32[1,512]{1,0:T(1,128)S(1)}, f32[128,512]{1,0:T(8,128)S(1)}) custom-call(bf16[128,512]{1,0:T(8,128)(2,1)S(1)} %get-tuple-element.54.mine_ref, bf16[128,512]{1,0:T(8,128)(2,1)S(1)} %collective-permute-done.7.twin_ref, f32[1,4096]{1,0:T(1,128)S(1)} %get-tuple-element.49.refs_4_.refs_2_.gain_ref, ...), custom_call_target="tpu_custom_call" | custom-call | flops 1500000000 | bytes 1 | tf_op jit(solution)/shard_map/q_part/pallas_call | solution.py:40
  32.3 0.9 %q_part.3 = (bf16[128,512]{1,0:T(8,128)(2,1)S(1)}, f32[1,512]{1,0:T(1,128)S(1)}, f32[1,512]{1,0:T(1,128)S(1)}, f32[128,512]{1,0:T(8,128)S(1)}) custom-call(bf16[128,512]{1,0:T(8,128)(2,1)S(1)} %collective-permute-done.9.mine_ref, bf16[128,512]{1,0:T(8,128)(2,1)S(1)} %collective-permute-done.10.twin_ref, ...), custom_call_target="tpu_custom_call" | custom-call | flops 400000000 | bytes 1 | tf_op jit(solution)/shard_map/q_part/pallas_call | solution.py:40
  33.2 0.0 collective-permute-done.12.kv_ref
  33.2 0.7 %attend_more.2 = (f32[1,1024]{1,0:T(1,128)S(1)}, f32[1,1024]{1,0:T(1,128)S(1)}, f32[128,1024]{1,0:T(8,128)S(1)}) custom-call(bf16[128,512]{1,0:T(8,128)(2,1)S(1)} %get-tuple-element.62.qa_ref, bf16[128,512]{1,0:T(8,128)(2,1)S(1)} %get-tuple-element.65.qb_ref, bf16[128,256]{1,0:T(8,128)(2,1)S(1)} %collective-permute-done.12.kv_ref, ...), custom_call_target="tpu_custom_call" | custom-call | flops 400000000 | bytes 1 | tf_op jit(solution)/shard_map/attend_more/pallas_call | solution.py:40
  33.9 0.7 %attend_more.3 = (bf16[256,512]{1,0:T(8,128)(2,1)S(1)}, bf16[128,512]{1,0:T(8,128)(2,1)S(1)}, bf16[128,512]{1,0:T(8,128)(2,1)S(1)}) custom-call(bf16[128,512]{1,0:T(8,128)(2,1)S(1)} %get-tuple-element.62.qa_ref, bf16[128,512]{1,0:T(8,128)(2,1)S(1)} %get-tuple-element.65.qb_ref, bf16[128,256]{1,0:T(8,128)(2,1)S(1)} %collective-permute-done.11.kv_ref, ...), custom_call_target="tpu_custom_call" | custom-call | flops 400000000 | bytes 1 | tf_op jit(solution)/shard_map/attend_more/pallas_call | solution.py:40
  34.6 3.6 %collective-permute-start.13 = (bf16[256,512]{1,0:T(8,128)(2,1)S(1)}, bf16[256,512]{1,0:T(8,128)(2,1)S(1)}, u32[]{:S(2)}, u32[]{:S(2)}) collective-permute-start(bf16[256,512]{1,0:T(8,128)(2,1)S(1)} %get-tuple-element.75.refs_0_), channel_id=1, source_target_pairs={{0,6},{1,7},{2,4},{3,5},{4,2},{5,3},{6,0},{7,1},{8,14},{9,15},{10,... | collective-permute-start | bytes 786440 | tf_op jit(solution)/shard_map/ppermute | solution.py:128
  38.2 0.5 collective-permute-start.17
  38.7 2.0 %collective-permute-start.19 = (bf16[128,512]{1,0:T(8,128)(2,1)S(1)}, bf16[128,512]{1,0:T(8,128)(2,1)S(1)}, u32[]{:S(2)}, u32[]{:S(2)}) collective-permute-start(bf16[128,512]{1,0:T(8,128)(2,1)S(1)} %get-tuple-element.77), channel_id=1, source_target_pairs={{0,2},{1,3},{2,0},{3,1},{4,6},{5,7},{6,4},{7,5},{8,10},{9,11},{10,... | collective-permute-start | bytes 393224 | tf_op jit(solution)/shard_map/ppermute | solution.py:130
  40.8 5.0 %collective-permute-done.13.refs_0_ = bf16[256,512]{1,0:T(8,128)(2,1)S(1)} collective-permute-done((bf16[256,512]{1,0:T(8,128)(2,1)S(1)}, bf16[256,512]{1,0:T(8,128)(2,1)S(1)}, u32[]{:S(2)}, u32[]{:S(2)}) %collective-permute-start.13) | collective-permute-done | bytes 262176 | tf_op jit(solution)/shard_map/ppermute | solution.py:128
  45.7 4.8 %collective-permute-start.14 = (bf16[256,512]{1,0:T(8,128)(2,1)S(1)}, bf16[256,512]{1,0:T(8,128)(2,1)S(1)}, u32[]{:S(2)}, u32[]{:S(2)}) collective-permute-start(bf16[256,512]{1,0:T(8,128)(2,1)S(1)} %collective-permute-done.13.refs_0_), channel_id=1, source_target_pairs={{0,2},{1,3},{2,0},{3,1},{4,6},{5,7},{6,4},{7,5},{8,10},{9,11},{10,... | collective-permute-start | bytes 786440 | tf_op jit(solution)/shard_map/ppermute | solution.py:131
  50.5 0.1 collective-permute-done.19.refs_4_
  50.6 2.6 %out_own.1 = (bf16[128,512]{1,0:T(8,128)(2,1)S(1)}, bf16[128,512]{1,0:T(8,128)(2,1)S(1)}, f32[256,512]{1,0:T(8,128)S(1)}, bf16[4096,512]{1,0:T(8,128)(2,1)S(1)}, bf16[1024,512]{1,0:T(8,128)(2,1)S(1)}) custom-call(bf16[256,512]{1,0:T(8,128)(2,1)S(1)} %get-tuple-element.75.refs_0_, ...), custom_call_target="tpu_custom_call", output_to_operand_aliasing={{0}: (3, {}), {1}: (4, {})} | custom-call | flops 1500000000 | bytes 1 | tf_op jit(solution)/shard_map/out_own/pallas_call | solution.py:40
  53.3 0.5 out_more.2
  53.8 0.2 collective-permute-start.21
  53.9 0.4 collective-permute-start.22
  54.3 3.1 %collective-permute-done.14.mine_ref = bf16[256,512]{1,0:T(8,128)(2,1)S(1)} collective-permute-done((bf16[256,512]{1,0:T(8,128)(2,1)S(1)}, bf16[256,512]{1,0:T(8,128)(2,1)S(1)}, u32[]{:S(2)}, u32[]{:S(2)}) %collective-permute-start.14) | collective-permute-done | bytes 262176 | tf_op jit(solution)/shard_map/ppermute | solution.py:131
  57.5 0.5 out_more.3.total_ref
  57.9 1.1 %collective-permute-done.15.twin_ref = bf16[256,512]{1,0:T(8,128)(2,1)S(1)} collective-permute-done((bf16[256,512]{1,0:T(8,128)(2,1)S(1)}, bf16[256,512]{1,0:T(8,128)(2,1)S(1)}, u32[]{:S(2)}, u32[]{:S(2)}) %collective-permute-start.15) | collective-permute-done | bytes 262176 | tf_op jit(solution)/shard_map/ppermute | solution.py:135
  59.0 1.6 %out_last.1 = bf16[1024,512]{1,0:T(8,128)(2,1)} custom-call(bf16[256,512]{1,0:T(8,128)(2,1)S(1)} %collective-permute-done.14.mine_ref, bf16[256,512]{1,0:T(8,128)(2,1)S(1)} %collective-permute-done.15.twin_ref, bf16[4096,512]{1,0:T(8,128)(2,1)S(1)} %get-tuple-element.78.refs_2_.refs_4_.w_ref, f32[256,512]{1,0:T(8,128)S(1)} %out_more.3.total_ref, ...), custom_call_target="tpu_custom_call" | custom-call | flops 400000000 | bytes 1 | tf_op jit(solution)/shard_map/out_last/pallas_call | solution.py:40
  (16 shorter events, 0.0 us)
Async XLA Ops:
  1.6 5.3 %collective-permute-start.4 = (bf16[256,512]{1,0:T(8,128)(2,1)S(1)}, bf16[256,512]{1,0:T(8,128)(2,1)S(1)}, u32[]{:S(2)}, u32[]{:S(2)}) collective-permute-start(bf16[256,512]{1,0:T(8,128)(2,1)S(1)} %get-tuple-element.48.__0_), channel_id=1, source_target_pairs={{0,1},{1,0},{2,3},{3,2},{4,5},{5,4},{6,7},{7,6},{8,9},{9,8},{10,11... | collective-permute-start | bytes 786440 | tf_op jit(solution)/shard_map/ppermute | solution.py:143
  2.1 9.0 %collective-permute-start = (bf16[128,512]{1,0:T(8,128)(2,1)S(1)}, bf16[128,512]{1,0:T(8,128)(2,1)S(1)}, u32[]{:S(2)}, u32[]{:S(2)}) collective-permute-start(bf16[128,512]{1,0:T(8,128)(2,1)S(1)} %get-tuple-element.46), channel_id=1, source_target_pairs={{0,6},{1,7},{2,4},{3,5},{4,2},{5,3},{6,0},{7,1},{8,14},{9,15},{10,... | collective-permute-start | bytes 393224 | tf_op jit(solution)/shard_map/ppermute | solution.py:142
  6.8 9.9 %collective-permute-start.1 = (bf16[128,512]{1,0:T(8,128)(2,1)S(1)}, bf16[128,512]{1,0:T(8,128)(2,1)S(1)}, u32[]{:S(2)}, u32[]{:S(2)}) collective-permute-start(bf16[128,512]{1,0:T(8,128)(2,1)S(1)} %get-tuple-element.47), channel_id=1, source_target_pairs={{0,6},{1,7},{2,4},{3,5},{4,2},{5,3},{6,0},{7,1},{8,14},{9,15},{10,... | collective-permute-start | bytes 393224 | tf_op jit(solution)/shard_map/ppermute | solution.py:142
  6.9 12.6 %collective-permute-start.5 = (bf16[256,512]{1,0:T(8,128)(2,1)S(1)}, bf16[256,512]{1,0:T(8,128)(2,1)S(1)}, u32[]{:S(2)}, u32[]{:S(2)}) collective-permute-start(bf16[256,512]{1,0:T(8,128)(2,1)S(1)} %gate.1.x_ref), channel_id=1, source_target_pairs={{0,2},{1,3},{2,0},{3,1},{4,6},{5,7},{6,4},{7,5},{8,10},{9,11},{10,... | collective-permute-start | bytes 786440 | tf_op jit(solution)/shard_map/ppermute | solution.py:145
  11.1 11.8 %collective-permute-start.2 = (bf16[128,512]{1,0:T(8,128)(2,1)S(1)}, bf16[128,512]{1,0:T(8,128)(2,1)S(1)}, u32[]{:S(2)}, u32[]{:S(2)}) collective-permute-start(bf16[128,512]{1,0:T(8,128)(2,1)S(1)} %collective-permute-done.refs_0_), channel_id=1, source_target_pairs={{0,1},{1,0},{2,3},{3,2},{4,5},{5,4},{6,7},{7,6},{8,9},{9,8},{10,11... | collective-permute-start | bytes 393224 | tf_op jit(solution)/shard_map/ppermute | solution.py:147
  11.1 11.8 %collective-permute-start.6 = (bf16[128,512]{1,0:T(8,128)(2,1)S(1)}, bf16[128,512]{1,0:T(8,128)(2,1)S(1)}, u32[]{:S(2)}, u32[]{:S(2)}) collective-permute-start(bf16[128,512]{1,0:T(8,128)(2,1)S(1)} %collective-permute-done.refs_0_), channel_id=1, source_target_pairs={{0,2},{1,3},{2,0},{3,1},{4,6},{5,7},{6,4},{7,5},{8,10},{9,11},{10,... | collective-permute-start | bytes 393224 | tf_op jit(solution)/shard_map/ppermute | solution.py:146
  16.7 6.2 %collective-permute-start.3 = (bf16[128,512]{1,0:T(8,128)(2,1)S(1)}, bf16[128,512]{1,0:T(8,128)(2,1)S(1)}, u32[]{:S(2)}, u32[]{:S(2)}) collective-permute-start(bf16[128,512]{1,0:T(8,128)(2,1)S(1)} %collective-permute-done.1.refs_1_), channel_id=1, source_target_pairs={{0,1},{1,0},{2,3},{3,2},{4,5},{5,4},{6,7},{7,6},{8,9},{9,8},{10,11... | collective-permute-start | bytes 393224 | tf_op jit(solution)/shard_map/ppermute | solution.py:147
  17.0 8.1 %collective-permute-start.9 = (bf16[128,512]{1,0:T(8,128)(2,1)S(1)}, bf16[128,512]{1,0:T(8,128)(2,1)S(1)}, u32[]{:S(2)}, u32[]{:S(2)}) collective-permute-start(bf16[128,512]{1,0:T(8,128)(2,1)S(1)} %collective-permute-done.1.refs_1_), channel_id=1, source_target_pairs={{0,2},{1,3},{2,0},{3,1},{4,6},{5,7},{6,4},{7,5},{8,10},{9,11},{10,... | collective-permute-start | bytes 393224 | tf_op jit(solution)/shard_map/ppermute | solution.py:146
  22.9 2.2 %collective-permute-start.8 = (bf16[256,512]{1,0:T(8,128)(2,1)S(1)}, bf16[256,512]{1,0:T(8,128)(2,1)S(1)}, u32[]{:S(2)}, u32[]{:S(2)}) collective-permute-start(bf16[256,512]{1,0:T(8,128)(2,1)S(1)} %get-tuple-element.55.refs_0_), channel_id=1, source_target_pairs={{0,1},{1,0},{2,3},{3,2},{4,5},{5,4},{6,7},{7,6},{8,9},{9,8},{10,11... | collective-permute-start | bytes 786440 | tf_op jit(solution)/shard_map/ppermute | solution.py:148
  23.7 2.1 %collective-permute-start.7 = (bf16[128,512]{1,0:T(8,128)(2,1)S(1)}, bf16[128,512]{1,0:T(8,128)(2,1)S(1)}, u32[]{:S(2)}, u32[]{:S(2)}) collective-permute-start(bf16[128,512]{1,0:T(8,128)(2,1)S(1)} %get-tuple-element.54.mine_ref), channel_id=1, source_target_pairs={{0,1},{1,0},{2,3},{3,2},{4,5},{5,4},{6,7},{7,6},{8,9},{9,8},{10,11... | collective-permute-start | bytes 393224 | tf_op jit(solution)/shard_map/ppermute | solution.py:149
  25.1 4.4 %collective-permute-start.10 = (bf16[128,512]{1,0:T(8,128)(2,1)S(1)}, bf16[128,512]{1,0:T(8,128)(2,1)S(1)}, u32[]{:S(2)}, u32[]{:S(2)}) collective-permute-start(bf16[128,512]{1,0:T(8,128)(2,1)S(1)} %collective-permute-done.9.mine_ref), channel_id=1, source_target_pairs={{0,1},{1,0},{2,3},{3,2},{4,5},{5,4},{6,7},{7,6},{8,9},{9,8},{10,11... | collective-permute-start | bytes 393224 | tf_op jit(solution)/shard_map/ppermute | solution.py:149
  26.1 7.1 %collective-permute-start.12 = (bf16[128,256]{1,0:T(8,128)(2,1)S(1)}, bf16[128,256]{1,0:T(8,128)(2,1)S(1)}, u32[]{:S(2)}, u32[]{:S(2)}) collective-permute-start(bf16[128,256]{1,0:T(8,128)(2,1)S(1)} %get-tuple-element.61.refs_0_), channel_id=1, source_target_pairs={{0,8},{1,9},{2,10},{3,11},{4,12},{5,13},{6,14},{7,15},{16,24},{17,... | collective-permute-start | bytes 196616 | tf_op jit(solution)/shard_map/ppermute | solution.py:552
  29.9 4.0 %collective-permute-start.11 = (bf16[128,256]{1,0:T(8,128)(2,1)S(1)}, bf16[128,256]{1,0:T(8,128)(2,1)S(1)}, u32[]{:S(2)}, u32[]{:S(2)}) collective-permute-start(bf16[128,256]{1,0:T(8,128)(2,1)S(1)} %get-tuple-element.64.refs_1_), channel_id=1, source_target_pairs={{0,8},{1,9},{2,10},{3,11},{4,12},{5,13},{6,14},{7,15},{16,24},{17,... | collective-permute-start | bytes 196616 | tf_op jit(solution)/shard_map/ppermute | solution.py:552
  34.6 11.1 %collective-permute-start.13 = (bf16[256,512]{1,0:T(8,128)(2,1)S(1)}, bf16[256,512]{1,0:T(8,128)(2,1)S(1)}, u32[]{:S(2)}, u32[]{:S(2)}) collective-permute-start(bf16[256,512]{1,0:T(8,128)(2,1)S(1)} %get-tuple-element.75.refs_0_), channel_id=1, source_target_pairs={{0,6},{1,7},{2,4},{3,5},{4,2},{5,3},{6,0},{7,1},{8,14},{9,15},{10,... | collective-permute-start | bytes 786440 | tf_op jit(solution)/shard_map/ppermute | solution.py:128
  38.2 7.5 %collective-permute-start.16 = (bf16[128,512]{1,0:T(8,128)(2,1)S(1)}, bf16[128,512]{1,0:T(8,128)(2,1)S(1)}, u32[]{:S(2)}, u32[]{:S(2)}) collective-permute-start(bf16[128,512]{1,0:T(8,128)(2,1)S(1)} %get-tuple-element.76), channel_id=1, source_target_pairs={{0,1},{1,0},{2,3},{3,2},{4,5},{5,4},{6,7},{7,6},{8,9},{9,8},{10,11... | collective-permute-start | bytes 393224 | tf_op jit(solution)/shard_map/ppermute | solution.py:129
  38.2 12.3 %collective-permute-start.17 = (bf16[128,512]{1,0:T(8,128)(2,1)S(1)}, bf16[128,512]{1,0:T(8,128)(2,1)S(1)}, u32[]{:S(2)}, u32[]{:S(2)}) collective-permute-start(bf16[128,512]{1,0:T(8,128)(2,1)S(1)} %get-tuple-element.77), channel_id=1, source_target_pairs={{0,1},{1,0},{2,3},{3,2},{4,5},{5,4},{6,7},{7,6},{8,9},{9,8},{10,11... | collective-permute-start | bytes 393224 | tf_op jit(solution)/shard_map/ppermute | solution.py:129
  38.7 11.8 %collective-permute-start.18 = (bf16[128,512]{1,0:T(8,128)(2,1)S(1)}, bf16[128,512]{1,0:T(8,128)(2,1)S(1)}, u32[]{:S(2)}, u32[]{:S(2)}) collective-permute-start(bf16[128,512]{1,0:T(8,128)(2,1)S(1)} %get-tuple-element.76), channel_id=1, source_target_pairs={{0,2},{1,3},{2,0},{3,1},{4,6},{5,7},{6,4},{7,5},{8,10},{9,11},{10,... | collective-permute-start | bytes 393224 | tf_op jit(solution)/shard_map/ppermute | solution.py:130
  38.7 11.9 %collective-permute-start.19 = (bf16[128,512]{1,0:T(8,128)(2,1)S(1)}, bf16[128,512]{1,0:T(8,128)(2,1)S(1)}, u32[]{:S(2)}, u32[]{:S(2)}) collective-permute-start(bf16[128,512]{1,0:T(8,128)(2,1)S(1)} %get-tuple-element.77), channel_id=1, source_target_pairs={{0,2},{1,3},{2,0},{3,1},{4,6},{5,7},{6,4},{7,5},{8,10},{9,11},{10,... | collective-permute-start | bytes 393224 | tf_op jit(solution)/shard_map/ppermute | solution.py:130
  45.7 7.6 %collective-permute-start.20 = (bf16[256,512]{1,0:T(8,128)(2,1)S(1)}, bf16[256,512]{1,0:T(8,128)(2,1)S(1)}, u32[]{:S(2)}, u32[]{:S(2)}) collective-permute-start(bf16[256,512]{1,0:T(8,128)(2,1)S(1)} %collective-permute-done.13.refs_0_), channel_id=1, source_target_pairs={{0,1},{1,0},{2,3},{3,2},{4,5},{5,4},{6,7},{7,6},{8,9},{9,8},{10,11... | collective-permute-start | bytes 786440 | tf_op jit(solution)/shard_map/ppermute | solution.py:133
  45.7 11.7 %collective-permute-start.14 = (bf16[256,512]{1,0:T(8,128)(2,1)S(1)}, bf16[256,512]{1,0:T(8,128)(2,1)S(1)}, u32[]{:S(2)}, u32[]{:S(2)}) collective-permute-start(bf16[256,512]{1,0:T(8,128)(2,1)S(1)} %collective-permute-done.13.refs_0_), channel_id=1, source_target_pairs={{0,2},{1,3},{2,0},{3,1},{4,6},{5,7},{6,4},{7,5},{8,10},{9,11},{10,... | collective-permute-start | bytes 786440 | tf_op jit(solution)/shard_map/ppermute | solution.py:131
  53.8 3.7 %collective-permute-start.21 = (bf16[128,512]{1,0:T(8,128)(2,1)S(1)}, bf16[128,512]{1,0:T(8,128)(2,1)S(1)}, u32[]{:S(2)}, u32[]{:S(2)}) collective-permute-start(bf16[128,512]{1,0:T(8,128)(2,1)S(1)} %get-tuple-element.82.refs_0_), channel_id=1, source_target_pairs={{0,1},{1,0},{2,3},{3,2},{4,5},{5,4},{6,7},{7,6},{8,9},{9,8},{10,11... | collective-permute-start | bytes 393224 | tf_op jit(solution)/shard_map/ppermute | solution.py:134
  53.9 3.5 %collective-permute-start.22 = (bf16[128,512]{1,0:T(8,128)(2,1)S(1)}, bf16[128,512]{1,0:T(8,128)(2,1)S(1)}, u32[]{:S(2)}, u32[]{:S(2)}) collective-permute-start(bf16[128,512]{1,0:T(8,128)(2,1)S(1)} %get-tuple-element.83.refs_1_), channel_id=1, source_target_pairs={{0,1},{1,0},{2,3},{3,2},{4,5},{5,4},{6,7},{7,6},{8,9},{9,8},{10,11... | collective-permute-start | bytes 393224 | tf_op jit(solution)/shard_map/ppermute | solution.py:134
  57.5 1.5 %collective-permute-start.15 = (bf16[256,512]{1,0:T(8,128)(2,1)S(1)}, bf16[256,512]{1,0:T(8,128)(2,1)S(1)}, u32[]{:S(2)}, u32[]{:S(2)}) collective-permute-start(bf16[256,512]{1,0:T(8,128)(2,1)S(1)} %collective-permute-done.14.mine_ref), channel_id=1, source_target_pairs={{0,1},{1,0},{2,3},{3,2},{4,5},{5,4},{6,7},{7,6},{8,9},{9,8},{10,11... | collective-permute-start | bytes 786440 | tf_op jit(solution)/shard_map/ppermute | solution.py:135

commit v6 on v5

--- a/solution.py
+++ b/solution.py
@@ -18,7 +18,6 @@
 COST = 400_000_000
 PART_COST = 1_500_000_000
 OWN_COST = 1_500_000_000
-GATE_COST = 1_000_000
 FAR_COST = 1_500_000_000
 BESIDE_COST = 1_000_000
 KV_COST = 400_000_000
@@ -117,10 +116,6 @@
     return sender([(2 * z + c, 2 * f(z) + c) for z in range(size // 2) for c in range(2)])
 
 
-def gate(ride, other):
-    return call(lambda *_: None, "gate", (ride, other), [arr(ride.shape, ride.dtype)], rides={0: 0}, flops=GATE_COST)[0]
-
-
 def spread(size, full, first, second, use_own, use_far, use_beside):
     cross = chip_sender(size, lambda z: 3 - z)
     near = chip_sender(size, lambda z: z ^ 1)
@@ -140,9 +135,7 @@
     near = chip_sender(size, lambda z: z ^ 1)
     twin = sender([(d, d ^ 1) for d in range(size)])
     far = cross(first), cross(second)
-    mate = twin(full)
-    full = gate(full, mate)
-    beside = use_own((full,), (mate,), near(full))
+    beside = near(use_own((full,), (twin(full),)))
     last_a, last_b = near(far[0]), near(far[1])
     (last_a,) = use_far(far, (twin(far[0]), twin(far[1])), (last_a,))
     use_beside((beside,), (twin(beside),))
@@ -188,7 +181,7 @@
         copy.wait()
 
 
-def own_kernel(x_ref, twin_ref, _, gain, router, wq, wk, wv, cnt, pos, flag, *refs):
+def own_kernel(x_ref, twin_ref, gain, router, wq, wk, wv, cnt, pos, flag, *refs):
     _, sums_ref, gain_ref, router_ref, w_ref, bias_ref, hot_ref, sems = refs[:8]
     z, core = place()
     nq, nk, depth = wq.shape[1], wk.shape[1], wq.shape[0]
@@ -212,7 +205,7 @@
         settle(later)
 
 
-def own_part(full, twin, ride, weights, counts, positions, flags, tok):
+def own_part(full, twin, weights, counts, positions, flags, tok):
     cap, width = full.shape
     depth = weights[2].shape[0]
     columns = sum(w.shape[1] for w in weights[2:])
@@ -220,9 +213,9 @@
     return call(
         own_kernel,
         "own_part",
-        (full, twin, ride, *weights, counts, positions, flags),
+        (full, twin, *weights, counts, positions, flags),
         [
-            arr(ride.shape, BF16),
+            arr(full.shape, BF16),
             arr((cap, columns + 256), F32),
             arr((1, depth), F32),
             arr((1, depth), F32),
@@ -237,7 +230,7 @@
             pltpu.VMEM(flags.shape, I32),
             pltpu.SemaphoreType.DMA((3,)),
         ],
-        rides={2: 0},
+        rides={0: 0},
         hbm=(*weights, counts, positions, flags),
         flops=OWN_COST,
     )
@@ -291,7 +284,8 @@
     return x * cos + pltpu.roll(x, HEAD_SIZE // 2, 1) * sin
 
 
-def kv_last_kernel(nq, at, mine_ref, twin_ref, gain_ref, router_ref, w_ref, sums, cos_ref, sin_ref, kv_out, stat_out):
+def kv_last_kernel(nq, at, mine_ref, twin_ref, gain_ref, router_ref, w_ref, sums, cos_ref, sin_ref, *outs):
+    kv_out, stat_out = outs[-2:] if len(outs) == 2 else outs[1:3]
     z, core = place()
     n, features = w_ref.shape[1], w_ref.shape[0]
     rows = slice(at, at + mine_ref.shape[0])
@@ -309,13 +303,15 @@
     stat_out[:, 128:256] = jnp.broadcast_to(gate, (gate.shape[0], 128))
 
 
-def kv_last(at, pair, staged, sums, cos, sin, nq, flops):
+def kv_last(at, pair, staged, sums, cos, sin, rides, nq, flops):
     cap = pair[0].shape[0]
+    operands = (*pair, *staged, sums, cos, sin, *rides)
     return call(
         functools.partial(kv_last_kernel, nq, at),
         "kv_last",
-        (*pair, *staged, sums, cos, sin),
-        [arr((cap, 256), BF16), arr((cap, 256), F32)],
+        operands,
+        [arr((cap, 256), BF16), arr((cap, 256), F32), *(arr(r.shape, r.dtype) for r in rides)],
+        rides={len(operands) - len(rides) + i: 2 + i for i in range(len(rides))},
         flops=flops,
     )
 
@@ -524,9 +520,9 @@
     full, first, second, rowpos = pick(keep_positions, hidden_in)
     held = {}
 
-    def own(mine, twin, ride):
+    def own(mine, mate):
         ride, held["sums"], *held["staged"], held["bias"], held["hot"] = own_part(
-            *mine, *twin, ride, weights, keep_counts, keep_positions, flags, tok
+            *mine, *mate, weights, keep_counts, keep_positions, flags, tok
         )
         return ride
 
@@ -543,14 +539,17 @@
     sums, staged, bias = held["sums"], held["staged"], held["bias"]
     cos, sin = held["cos"], held["sin"]
     half = first.shape[0]
-    onward = [(s, s + 1) for s in range(shards - 1)]
-    kvs, stats, moved, qs, carry = [], [], [], [], []
+    ring = [(s, (s + 1) % shards) for s in range(shards)]
+    kvs, stats, qs, carry = [], [], [], []
     for i in range(2):
-        kv, stat = kv_last(i * half, pairs[i], staged, sums, cos, sin, nq, KV_COST)
+        kv, stat, *kvs = kv_last(i * half, pairs[i], staged, sums, cos, sin, kvs, nq, KV_COST)
         kvs.append(kv)
         stats.append(stat)
-        moved.append(lax.ppermute(kv, "ctx", onward))
-        q, *terms = q_part(i, pairs[i], staged, sums, stat, cos, sin, kvs, bias, nq, QA_COST if i == 0 else Q_COST)
+    moved = [lax.ppermute(kv, "ctx", ring) for kv in kvs]
+    for i in range(2):
+        q, *terms = q_part(
+            i, pairs[i], staged, sums, stats[i], cos, sin, kvs[: i + 1], bias, nq, Q_COST if i else QA_COST
+        )
         qs.append(q)
         carry += terms
     for step in range(1, shards):
@@ -558,7 +557,7 @@
             last = step == shards - 1 and i == 1
             carry = attend_more(step, i * half, last, qs, moved[i], bias, carry, ATTEND_COST)
         if step < shards - 1:
-            moved = [lax.ppermute(kv, "ctx", onward) for kv in moved]
+            moved = [lax.ppermute(kv, "ctx", ring) for kv in moved]
 
     def own_out(mine, twin, rides):
         *rides, held["total"], held["w"], held["hidden"] = out_own(mine, twin, rides, w_out, hidden_in)

time: 61 us -> 58.4 us (0.957)
  starting transfers between devices: 30.1 us -> 25.1 us
  waiting for transfers between devices: 13.5 us -> 16.7 us
  other arithmetic: 1.22 us -> 0.56 us
    ppermute x2, waiting for transfers between devices: 0.87 us -> 4.77 us  [spread_halves(): last_a, last_b = (near(far[0]), near(far[1]))]
    ppermute x4, starting transfers between devices: 5.27 us -> 2.67 us  [the longest x2 2.09 us: body(): moved = [lax.ppermute(kv, 'ctx', ring) for kv in kvs]]
    ppermute x2, waiting for transfers between devices: 2.9 us -> 0.59 us  [spread_halves(): far = (cross(first), cross(second))]
    ppermute x1, starting transfers between devices: 4.76 us -> 3.1 us  [spread(): last = near(far)]
    ppermute x4, waiting for transfers between devices: 0.45 us -> 1.38 us  [the longest x2 1.06 us: body(): moved = [lax.ppermute(kv, 'ctx', ring) for kv in kvs]]
    mul x1, other arithmetic: 1.13 us -> 0.48 us  [angles(): return (jnp.cos(turned), jnp.sin(turned) * sign[None, :])]
    pallas_call x15 -> x14, Pallas kernels: 15.6 us -> 15.6 us  [call(): pl.pallas_call(kernel, out_shape=out_shape, in_specs=[HBM if far else VME...]
  transfers between devices with their start and end apart: 23 -> 23, of which waited for: 7 -> 11; matrix products, arithmetic and copies ran while one was open for 2% -> 1% of each run, Pallas kernels for 19% -> 19%
where the time goes in v6:
time: 58.4 us; the launch traced here: 58.1 us
  starting transfers between devices  25.1 us (43%)
  waiting for transfers between devices  16.7 us (29%)
  Pallas kernels  15.6 us (27%)
    pallas_call x14, Pallas kernels, call(): pl.pallas_call(kernel, out_shape=out_shape, in_specs=[HBM if far else VME...  15.6 us
    ppermute x2, starting transfers between devices, spread_halves(): last_a, last_b = (near(far[0]), near(far[1]))  7.88 us
    ppermute x1, waiting for transfers between devices, spread(): far = cross(full)  5.37 us
    ppermute x2, starting transfers between devices, spread_halves(): far = (cross(first), cross(second))  4.78 us
    ppermute x2, waiting for transfers between devices, spread_halves(): last_a, last_b = (near(far[0]), near(far[1]))  4.77 us
    ppermute x1, starting transfers between devices, spread(): far = cross(full)  3.2 us
    ppermute x1, starting transfers between devices, spread(): last = near(far)  3.1 us
    ppermute x1, waiting for transfers between devices, spread(): last = near(far)  2.66 us
  transfers between devices with their start and end apart: 23, of which 11 were waited for; matrix products, arithmetic and copies ran while one was open for 1% of the time, Pallas kernels for 19%

profile of v6, /device:TPU:0, one launch (start us, length us, event | category | flops | bytes accessed | tf_op | source)
XLA Modules:
  0.0 58.1 jit_solution(16435350816951989192)
XLA Ops:
  0.0 1.6 %pick.1 = (bf16[256,512]{1,0:T(8,128)(2,1)S(1)}, bf16[128,512]{1,0:T(8,128)(2,1)S(1)}, bf16[128,512]{1,0:T(8,128)(2,1)S(1)}, s32[256,128]{1,0:T(8,128)S(1)}) custom-call(s32[2,256]{1,0:T(2,128)} %pos.1, bf16[1024,512]{1,0:T(8,128)(2,1)} %refs_6_.1), custom_call_target="tpu_custom_call" | custom-call | flops 400000000 | bytes 1 | tf_op jit(solution)/shard_map/pick/pallas_call | solution.py:39
  1.6 0.5 collective-permute-start.4
  2.2 4.7 %collective-permute-start = (bf16[128,512]{1,0:T(8,128)(2,1)S(1)}, bf16[128,512]{1,0:T(8,128)(2,1)S(1)}, u32[]{:S(2)}, u32[]{:S(2)}) collective-permute-start(bf16[128,512]{1,0:T(8,128)(2,1)S(1)} %get-tuple-element.47), channel_id=1, source_target_pairs={{0,6},{1,7},{2,4},{3,5},{4,2},{5,3},{6,0},{7,1},{8,14},{9,15},{10,... | collective-permute-start | bytes 393224 | tf_op jit(solution)/shard_map/ppermute | solution.py:137
  6.8 0.1 collective-permute-start.1
  7.0 3.3 %own_part.1 = (bf16[256,512]{1,0:T(8,128)(2,1)S(1)}, f32[256,1024]{1,0:T(8,128)S(1)}, f32[1,4096]{1,0:T(1,128)S(1)}, f32[1,4096]{1,0:T(1,128)S(1)}, bf16[4096,76...) custom-call(bf16[256,512]{1,0:T(8,128)(2,1)S(1)} %get-tuple-element., ...), custom_call_target="tpu_custom_call", output_to_operand_aliasing={{0}: (0, {})} | custom-call | flops 1500000000 | bytes 1 | tf_op jit(solution)/shard_map/own_part/pallas_call | solution.py:39
  10.3 0.1 collective-permute-start.7
  10.4 0.1 pad_maximum_fusion
  10.5 0.6 %collective-permute-done.refs_0_ = bf16[128,512]{1,0:T(8,128)(2,1)S(1)} collective-permute-done((bf16[128,512]{1,0:T(8,128)(2,1)S(1)}, bf16[128,512]{1,0:T(8,128)(2,1)S(1)}, u32[]{:S(2)}, u32[]{:S(2)}) %collective-permute-start) | collective-permute-done | bytes 131104 | tf_op jit(solution)/shard_map/ppermute | solution.py:137
  11.1 5.7 %collective-permute-start.5 = (bf16[128,512]{1,0:T(8,128)(2,1)S(1)}, bf16[128,512]{1,0:T(8,128)(2,1)S(1)}, u32[]{:S(2)}, u32[]{:S(2)}) collective-permute-start(bf16[128,512]{1,0:T(8,128)(2,1)S(1)} %collective-permute-done.refs_0_), channel_id=1, source_target_pairs={{0,2},{1,3},{2,0},{3,1},{4,6},{5,7},{6,4},{7,5},{8,10},{9,11},{10,... | collective-permute-start | bytes 393224 | tf_op jit(solution)/shard_map/ppermute | solution.py:139
  16.7 0.0 collective-permute-done.1.refs_1_
  16.7 0.2 collective-permute-start.3
  17.0 0.5 sine_multiply_fusion
  17.5 2.2 %collective-permute-start.9 = (bf16[128,512]{1,0:T(8,128)(2,1)S(1)}, bf16[128,512]{1,0:T(8,128)(2,1)S(1)}, u32[]{:S(2)}, u32[]{:S(2)}) collective-permute-start(bf16[128,512]{1,0:T(8,128)(2,1)S(1)} %collective-permute-done.1.refs_1_), channel_id=1, source_target_pairs={{0,2},{1,3},{2,0},{3,1},{4,6},{5,7},{6,4},{7,5},{8,10},{9,11},{10,... | collective-permute-start | bytes 393224 | tf_op jit(solution)/shard_map/ppermute | solution.py:139
  19.6 0.3 collective-permute-done.7.refs_0_
  20.0 0.0 collective-permute-done.2.refs_2_
  20.0 0.0 collective-permute-done.3.refs_3_
  20.0 2.8 %collective-permute-done.5.refs_8_ = bf16[128,512]{1,0:T(8,128)(2,1)S(1)} collective-permute-done((bf16[128,512]{1,0:T(8,128)(2,1)S(1)}, bf16[128,512]{1,0:T(8,128)(2,1)S(1)}, u32[]{:S(2)}, u32[]{:S(2)}) %collective-permute-start.5) | collective-permute-done | bytes 131104 | tf_op jit(solution)/shard_map/ppermute | solution.py:139
  22.8 0.7 %more_part.2 = (f32[256,1024]{1,0:T(8,128)S(1)}, bf16[128,512]{1,0:T(8,128)(2,1)S(1)}, f32[256,128]{1,0:T(8,128)S(1)}, f32[256,128]{1,0:T(8,128)S(1)}) custom-call(bf16[128,512]{1,0:T(8,128)(2,1)S(1)} %collective-permute-done.refs_0_, ...), custom_call_target="tpu_custom_call", output_to_operand_aliasing={{0}: (7, {}), {1}: (8, {}), {2}: (9, {}), {3}: (10, {})} | custom-call | flops 1500000000 | bytes 1 | tf_op jit(solution)/shard_map/more_part/pallas_call | solution.py:39
  23.4 0.1 collective-permute-start.6
  23.5 2.0 %collective-permute-done.9.mine_ref = bf16[128,512]{1,0:T(8,128)(2,1)S(1)} collective-permute-done((bf16[128,512]{1,0:T(8,128)(2,1)S(1)}, bf16[128,512]{1,0:T(8,128)(2,1)S(1)}, u32[]{:S(2)}, u32[]{:S(2)}) %collective-permute-start.9) | collective-permute-done | bytes 131104 | tf_op jit(solution)/shard_map/ppermute | solution.py:139
  25.5 0.0 collective-permute-start.10
  25.5 0.0 collective-permute-done.8.refs_1_
  25.5 0.7 %more_part.3.sums = f32[256,1024]{1,0:T(8,128)S(1)} custom-call(bf16[256,512]{1,0:T(8,128)(2,1)S(1)} %collective-permute-done.7.refs_0_, bf16[256,512]{1,0:T(8,128)(2,1)S(1)} %collective-permute-done.8.refs_1_, f32[1,4096]{1,0:T(1,128)S(1)} %get-tuple-element.50.refs_4_.refs_2_.gain_ref, ...), custom_call_target="tpu_custom_call", output_to_operand_aliasing={{}: (5, {})} | custom-call | flops 1000000 | bytes 1 | tf_op jit(solution)/shard_map/more_part/pallas_call | solution.py:39
  26.2 0.3 kv_last.2
  26.6 0.3 collective-permute-done.10.twin_ref
  26.9 0.3 kv_last.3
  27.2 1.6 %collective-permute-start.12 = (bf16[128,256]{1,0:T(8,128)(2,1)S(1)}, bf16[128,256]{1,0:T(8,128)(2,1)S(1)}, u32[]{:S(2)}, u32[]{:S(2)}) collective-permute-start(bf16[128,256]{1,0:T(8,128)(2,1)S(1)} %get-tuple-element.63.refs_0_), channel_id=1, source_target_pairs={{0,8},{8,0},{1,9},{9,1},{2,10},{10,2},{3,11},{11,3},{4,12},{12,4},... | collective-permute-start | bytes 196616 | tf_op jit(solution)/shard_map/ppermute | solution.py:548
  28.8 0.5 collective-permute-start.11
  29.3 1.1 %q_part.2 = (bf16[128,512]{1,0:T(8,128)(2,1)S(1)}, f32[1,512]{1,0:T(1,128)S(1)}, f32[1,512]{1,0:T(1,128)S(1)}, f32[128,512]{1,0:T(8,128)S(1)}) custom-call(bf16[128,512]{1,0:T(8,128)(2,1)S(1)} %get-tuple-element.55.mine_ref, bf16[128,512]{1,0:T(8,128)(2,1)S(1)} %collective-permute-done.6.twin_ref, f32[1,4096]{1,0:T(1,128)S(1)} %get-tuple-element.50.refs_4_.refs_2_.gain_ref, ...), custom_call_target="tpu_custom_call" | custom-call | flops 1500000000 | bytes 1 | tf_op jit(solution)/shard_map/q_part/pallas_call | solution.py:39
  30.4 0.9 %q_part.3 = (bf16[128,512]{1,0:T(8,128)(2,1)S(1)}, f32[1,512]{1,0:T(1,128)S(1)}, f32[1,512]{1,0:T(1,128)S(1)}, f32[128,512]{1,0:T(8,128)S(1)}) custom-call(bf16[128,512]{1,0:T(8,128)(2,1)S(1)} %collective-permute-done.9.mine_ref, bf16[128,512]{1,0:T(8,128)(2,1)S(1)} %collective-permute-done.10.twin_ref, ...), custom_call_target="tpu_custom_call" | custom-call | flops 400000000 | bytes 1 | tf_op jit(solution)/shard_map/q_part/pallas_call | solution.py:39
  31.3 0.5 collective-permute-done.12.kv_ref
  31.8 0.7 %attend_more.2 = (f32[1,1024]{1,0:T(1,128)S(1)}, f32[1,1024]{1,0:T(1,128)S(1)}, f32[128,1024]{1,0:T(8,128)S(1)}) custom-call(bf16[128,512]{1,0:T(8,128)(2,1)S(1)} %get-tuple-element.64.qa_ref, bf16[128,512]{1,0:T(8,128)(2,1)S(1)} %get-tuple-element.67.qb_ref, bf16[128,256]{1,0:T(8,128)(2,1)S(1)} %collective-permute-done.12.kv_ref, ...), custom_call_target="tpu_custom_call" | custom-call | flops 400000000 | bytes 1 | tf_op jit(solution)/shard_map/attend_more/pallas_call | solution.py:39
  32.5 0.5 collective-permute-done.11.kv_ref
  33.0 0.7 %attend_more.3 = (bf16[256,512]{1,0:T(8,128)(2,1)S(1)}, bf16[128,512]{1,0:T(8,128)(2,1)S(1)}, bf16[128,512]{1,0:T(8,128)(2,1)S(1)}) custom-call(bf16[128,512]{1,0:T(8,128)(2,1)S(1)} %get-tuple-element.64.qa_ref, bf16[128,512]{1,0:T(8,128)(2,1)S(1)} %get-tuple-element.67.qb_ref, bf16[128,256]{1,0:T(8,128)(2,1)S(1)} %collective-permute-done.11.kv_ref, ...), custom_call_target="tpu_custom_call" | custom-call | flops 400000000 | bytes 1 | tf_op jit(solution)/shard_map/attend_more/pallas_call | solution.py:39
  33.8 3.2 %collective-permute-start.13 = (bf16[256,512]{1,0:T(8,128)(2,1)S(1)}, bf16[256,512]{1,0:T(8,128)(2,1)S(1)}, u32[]{:S(2)}, u32[]{:S(2)}) collective-permute-start(bf16[256,512]{1,0:T(8,128)(2,1)S(1)} %get-tuple-element.77.refs_0_), channel_id=1, source_target_pairs={{0,6},{1,7},{2,4},{3,5},{4,2},{5,3},{6,0},{7,1},{8,14},{9,15},{10,... | collective-permute-start | bytes 786440 | tf_op jit(solution)/shard_map/ppermute | solution.py:123
  37.0 0.5 collective-permute-start.17
  37.5 2.0 %collective-permute-start.19 = (bf16[128,512]{1,0:T(8,128)(2,1)S(1)}, bf16[128,512]{1,0:T(8,128)(2,1)S(1)}, u32[]{:S(2)}, u32[]{:S(2)}) collective-permute-start(bf16[128,512]{1,0:T(8,128)(2,1)S(1)} %get-tuple-element.79), channel_id=1, source_target_pairs={{0,2},{1,3},{2,0},{3,1},{4,6},{5,7},{6,4},{7,5},{8,10},{9,11},{10,... | collective-permute-start | bytes 393224 | tf_op jit(solution)/shard_map/ppermute | solution.py:125
  39.5 5.4 %collective-permute-done.13.refs_0_ = bf16[256,512]{1,0:T(8,128)(2,1)S(1)} collective-permute-done((bf16[256,512]{1,0:T(8,128)(2,1)S(1)}, bf16[256,512]{1,0:T(8,128)(2,1)S(1)}, u32[]{:S(2)}, u32[]{:S(2)}) %collective-permute-start.13) | collective-permute-done | bytes 262176 | tf_op jit(solution)/shard_map/ppermute | solution.py:123
  44.9 3.1 %collective-permute-start.14 = (bf16[256,512]{1,0:T(8,128)(2,1)S(1)}, bf16[256,512]{1,0:T(8,128)(2,1)S(1)}, u32[]{:S(2)}, u32[]{:S(2)}) collective-permute-start(bf16[256,512]{1,0:T(8,128)(2,1)S(1)} %collective-permute-done.13.refs_0_), channel_id=1, source_target_pairs={{0,2},{1,3},{2,0},{3,1},{4,6},{5,7},{6,4},{7,5},{8,10},{9,11},{10,... | collective-permute-start | bytes 786440 | tf_op jit(solution)/shard_map/ppermute | solution.py:126
  48.0 0.6 %collective-permute-done.19.refs_4_ = bf16[128,512]{1,0:T(8,128)(2,1)S(1)} collective-permute-done((bf16[128,512]{1,0:T(8,128)(2,1)S(1)}, bf16[128,512]{1,0:T(8,128)(2,1)S(1)}, u32[]{:S(2)}, u32[]{:S(2)}) %collective-permute-start.19) | collective-permute-done | bytes 131104 | tf_op jit(solution)/shard_map/ppermute | solution.py:125
  48.6 2.6 %out_own.1 = (bf16[128,512]{1,0:T(8,128)(2,1)S(1)}, bf16[128,512]{1,0:T(8,128)(2,1)S(1)}, f32[256,512]{1,0:T(8,128)S(1)}, bf16[4096,512]{1,0:T(8,128)(2,1)S(1)}, bf16[1024,512]{1,0:T(8,128)(2,1)S(1)}) custom-call(bf16[256,512]{1,0:T(8,128)(2,1)S(1)} %get-tuple-element.77.refs_0_, ...), custom_call_target="tpu_custom_call", output_to_operand_aliasing={{0}: (3, {}), {1}: (4, {})} | custom-call | flops 1500000000 | bytes 1 | tf_op jit(solution)/shard_map/out_own/pallas_call | solution.py:39
  51.3 0.5 out_more.2
  51.7 0.1 collective-permute-start.21
  51.8 0.5 collective-permute-start.22
  52.3 2.7 %collective-permute-done.14.mine_ref = bf16[256,512]{1,0:T(8,128)(2,1)S(1)} collective-permute-done((bf16[256,512]{1,0:T(8,128)(2,1)S(1)}, bf16[256,512]{1,0:T(8,128)(2,1)S(1)}, u32[]{:S(2)}, u32[]{:S(2)}) %collective-permute-start.14) | collective-permute-done | bytes 262176 | tf_op jit(solution)/shard_map/ppermute | solution.py:126
  55.0 0.5 out_more.3.total_ref
  55.4 1.1 %collective-permute-done.15.twin_ref = bf16[256,512]{1,0:T(8,128)(2,1)S(1)} collective-permute-done((bf16[256,512]{1,0:T(8,128)(2,1)S(1)}, bf16[256,512]{1,0:T(8,128)(2,1)S(1)}, u32[]{:S(2)}, u32[]{:S(2)}) %collective-permute-start.15) | collective-permute-done | bytes 262176 | tf_op jit(solution)/shard_map/ppermute | solution.py:130
  56.5 1.6 %out_last.1 = bf16[1024,512]{1,0:T(8,128)(2,1)} custom-call(bf16[256,512]{1,0:T(8,128)(2,1)S(1)} %collective-permute-done.14.mine_ref, bf16[256,512]{1,0:T(8,128)(2,1)S(1)} %collective-permute-done.15.twin_ref, bf16[4096,512]{1,0:T(8,128)(2,1)S(1)} %get-tuple-element.80.refs_2_.refs_4_.w_ref, f32[256,512]{1,0:T(8,128)S(1)} %out_more.3.total_ref, ...), custom_call_target="tpu_custom_call" | custom-call | flops 400000000 | bytes 1 | tf_op jit(solution)/shard_map/out_last/pallas_call | solution.py:39
  (17 shorter events, 0.1 us)
Async XLA Ops:
  0.0 17.0 %copy-start = (f32[128]{0:T(128)S(1)}, f32[128]{0:T(128)}, u32[]{:S(2)}) copy-start(f32[128]{0:T(128)} %constant.9.clone.1) | copy-start | bytes 1540
  1.6 5.3 %collective-permute-start.4 = (bf16[256,512]{1,0:T(8,128)(2,1)S(1)}, bf16[256,512]{1,0:T(8,128)(2,1)S(1)}, u32[]{:S(2)}, u32[]{:S(2)}) collective-permute-start(bf16[256,512]{1,0:T(8,128)(2,1)S(1)} %get-tuple-element.49.x_ref), channel_id=1, source_target_pairs={{0,1},{1,0},{2,3},{3,2},{4,5},{5,4},{6,7},{7,6},{8,9},{9,8},{10,11... | collective-permute-start | bytes 786440 | tf_op jit(solution)/shard_map/ppermute | solution.py:138
  2.2 8.9 %collective-permute-start = (bf16[128,512]{1,0:T(8,128)(2,1)S(1)}, bf16[128,512]{1,0:T(8,128)(2,1)S(1)}, u32[]{:S(2)}, u32[]{:S(2)}) collective-permute-start(bf16[128,512]{1,0:T(8,128)(2,1)S(1)} %get-tuple-element.47), channel_id=1, source_target_pairs={{0,6},{1,7},{2,4},{3,5},{4,2},{5,3},{6,0},{7,1},{8,14},{9,15},{10,... | collective-permute-start | bytes 393224 | tf_op jit(solution)/shard_map/ppermute | solution.py:137
  6.8 9.9 %collective-permute-start.1 = (bf16[128,512]{1,0:T(8,128)(2,1)S(1)}, bf16[128,512]{1,0:T(8,128)(2,1)S(1)}, u32[]{:S(2)}, u32[]{:S(2)}) collective-permute-start(bf16[128,512]{1,0:T(8,128)(2,1)S(1)} %get-tuple-element.48), channel_id=1, source_target_pairs={{0,6},{1,7},{2,4},{3,5},{4,2},{5,3},{6,0},{7,1},{8,14},{9,15},{10,... | collective-permute-start | bytes 393224 | tf_op jit(solution)/shard_map/ppermute | solution.py:137
  10.3 9.7 %collective-permute-start.7 = (bf16[256,512]{1,0:T(8,128)(2,1)S(1)}, bf16[256,512]{1,0:T(8,128)(2,1)S(1)}, u32[]{:S(2)}, u32[]{:S(2)}) collective-permute-start(bf16[256,512]{1,0:T(8,128)(2,1)S(1)} %get-tuple-element.56), channel_id=1, source_target_pairs={{0,2},{1,3},{2,0},{3,1},{4,6},{5,7},{6,4},{7,5},{8,10},{9,11},{10,... | collective-permute-start | bytes 786440 | tf_op jit(solution)/shard_map/ppermute | solution.py:138
  11.0 8.9 %collective-permute-start.2 = (bf16[128,512]{1,0:T(8,128)(2,1)S(1)}, bf16[128,512]{1,0:T(8,128)(2,1)S(1)}, u32[]{:S(2)}, u32[]{:S(2)}) collective-permute-start(bf16[128,512]{1,0:T(8,128)(2,1)S(1)} %collective-permute-done.refs_0_), channel_id=1, source_target_pairs={{0,1},{1,0},{2,3},{3,2},{4,5},{5,4},{6,7},{7,6},{8,9},{9,8},{10,11... | collective-permute-start | bytes 393224 | tf_op jit(solution)/shard_map/ppermute | solution.py:140
  11.1 11.7 %collective-permute-start.5 = (bf16[128,512]{1,0:T(8,128)(2,1)S(1)}, bf16[128,512]{1,0:T(8,128)(2,1)S(1)}, u32[]{:S(2)}, u32[]{:S(2)}) collective-permute-start(bf16[128,512]{1,0:T(8,128)(2,1)S(1)} %collective-permute-done.refs_0_), channel_id=1, source_target_pairs={{0,2},{1,3},{2,0},{3,1},{4,6},{5,7},{6,4},{7,5},{8,10},{9,11},{10,... | collective-permute-start | bytes 393224 | tf_op jit(solution)/shard_map/ppermute | solution.py:139
  16.7 3.2 %collective-permute-start.3 = (bf16[128,512]{1,0:T(8,128)(2,1)S(1)}, bf16[128,512]{1,0:T(8,128)(2,1)S(1)}, u32[]{:S(2)}, u32[]{:S(2)}) collective-permute-start(bf16[128,512]{1,0:T(8,128)(2,1)S(1)} %collective-permute-done.1.refs_1_), channel_id=1, source_target_pairs={{0,1},{1,0},{2,3},{3,2},{4,5},{5,4},{6,7},{7,6},{8,9},{9,8},{10,11... | collective-permute-start | bytes 393224 | tf_op jit(solution)/shard_map/ppermute | solution.py:140
  17.5 8.1 %collective-permute-start.9 = (bf16[128,512]{1,0:T(8,128)(2,1)S(1)}, bf16[128,512]{1,0:T(8,128)(2,1)S(1)}, u32[]{:S(2)}, u32[]{:S(2)}) collective-permute-start(bf16[128,512]{1,0:T(8,128)(2,1)S(1)} %collective-permute-done.1.refs_1_), channel_id=1, source_target_pairs={{0,2},{1,3},{2,0},{3,1},{4,6},{5,7},{6,4},{7,5},{8,10},{9,11},{10,... | collective-permute-start | bytes 393224 | tf_op jit(solution)/shard_map/ppermute | solution.py:139
  20.0 5.6 %collective-permute-start.8 = (bf16[256,512]{1,0:T(8,128)(2,1)S(1)}, bf16[256,512]{1,0:T(8,128)(2,1)S(1)}, u32[]{:S(2)}, u32[]{:S(2)}) collective-permute-start(bf16[256,512]{1,0:T(8,128)(2,1)S(1)} %collective-permute-done.7.refs_0_), channel_id=1, source_target_pairs={{0,1},{1,0},{2,3},{3,2},{4,5},{5,4},{6,7},{7,6},{8,9},{9,8},{10,11... | collective-permute-start | bytes 786440 | tf_op jit(solution)/shard_map/ppermute | solution.py:141
  23.4 2.8 %collective-permute-start.6 = (bf16[128,512]{1,0:T(8,128)(2,1)S(1)}, bf16[128,512]{1,0:T(8,128)(2,1)S(1)}, u32[]{:S(2)}, u32[]{:S(2)}) collective-permute-start(bf16[128,512]{1,0:T(8,128)(2,1)S(1)} %get-tuple-element.55.mine_ref), channel_id=1, source_target_pairs={{0,1},{1,0},{2,3},{3,2},{4,5},{5,4},{6,7},{7,6},{8,9},{9,8},{10,11... | collective-permute-start | bytes 393224 | tf_op jit(solution)/shard_map/ppermute | solution.py:142
  25.5 1.3 %collective-permute-start.10 = (bf16[128,512]{1,0:T(8,128)(2,1)S(1)}, bf16[128,512]{1,0:T(8,128)(2,1)S(1)}, u32[]{:S(2)}, u32[]{:S(2)}) collective-permute-start(bf16[128,512]{1,0:T(8,128)(2,1)S(1)} %collective-permute-done.9.mine_ref), channel_id=1, source_target_pairs={{0,1},{1,0},{2,3},{3,2},{4,5},{5,4},{6,7},{7,6},{8,9},{9,8},{10,11... | collective-permute-start | bytes 393224 | tf_op jit(solution)/shard_map/ppermute | solution.py:142
  27.2 4.6 %collective-permute-start.12 = (bf16[128,256]{1,0:T(8,128)(2,1)S(1)}, bf16[128,256]{1,0:T(8,128)(2,1)S(1)}, u32[]{:S(2)}, u32[]{:S(2)}) collective-permute-start(bf16[128,256]{1,0:T(8,128)(2,1)S(1)} %get-tuple-element.63.refs_0_), channel_id=1, source_target_pairs={{0,8},{8,0},{1,9},{9,1},{2,10},{10,2},{3,11},{11,3},{4,12},{12,4},... | collective-permute-start | bytes 196616 | tf_op jit(solution)/shard_map/ppermute | solution.py:548
  28.8 4.3 %collective-permute-start.11 = (bf16[128,256]{1,0:T(8,128)(2,1)S(1)}, bf16[128,256]{1,0:T(8,128)(2,1)S(1)}, u32[]{:S(2)}, u32[]{:S(2)}) collective-permute-start(bf16[128,256]{1,0:T(8,128)(2,1)S(1)} %get-tuple-element.66.refs_1_), channel_id=1, source_target_pairs={{0,8},{8,0},{1,9},{9,1},{2,10},{10,2},{3,11},{11,3},{4,12},{12,4},... | collective-permute-start | bytes 196616 | tf_op jit(solution)/shard_map/ppermute | solution.py:548
  33.8 11.1 %collective-permute-start.13 = (bf16[256,512]{1,0:T(8,128)(2,1)S(1)}, bf16[256,512]{1,0:T(8,128)(2,1)S(1)}, u32[]{:S(2)}, u32[]{:S(2)}) collective-permute-start(bf16[256,512]{1,0:T(8,128)(2,1)S(1)} %get-tuple-element.77.refs_0_), channel_id=1, source_target_pairs={{0,6},{1,7},{2,4},{3,5},{4,2},{5,3},{6,0},{7,1},{8,14},{9,15},{10,... | collective-permute-start | bytes 786440 | tf_op jit(solution)/shard_map/ppermute | solution.py:123
  37.0 7.9 %collective-permute-start.16 = (bf16[128,512]{1,0:T(8,128)(2,1)S(1)}, bf16[128,512]{1,0:T(8,128)(2,1)S(1)}, u32[]{:S(2)}, u32[]{:S(2)}) collective-permute-start(bf16[128,512]{1,0:T(8,128)(2,1)S(1)} %get-tuple-element.78), channel_id=1, source_target_pairs={{0,1},{1,0},{2,3},{3,2},{4,5},{5,4},{6,7},{7,6},{8,9},{9,8},{10,11... | collective-permute-start | bytes 393224 | tf_op jit(solution)/shard_map/ppermute | solution.py:124
  37.0 11.0 %collective-permute-start.17 = (bf16[128,512]{1,0:T(8,128)(2,1)S(1)}, bf16[128,512]{1,0:T(8,128)(2,1)S(1)}, u32[]{:S(2)}, u32[]{:S(2)}) collective-permute-start(bf16[128,512]{1,0:T(8,128)(2,1)S(1)} %get-tuple-element.79), channel_id=1, source_target_pairs={{0,1},{1,0},{2,3},{3,2},{4,5},{5,4},{6,7},{7,6},{8,9},{9,8},{10,11... | collective-permute-start | bytes 393224 | tf_op jit(solution)/shard_map/ppermute | solution.py:124
  37.5 10.5 %collective-permute-start.18 = (bf16[128,512]{1,0:T(8,128)(2,1)S(1)}, bf16[128,512]{1,0:T(8,128)(2,1)S(1)}, u32[]{:S(2)}, u32[]{:S(2)}) collective-permute-start(bf16[128,512]{1,0:T(8,128)(2,1)S(1)} %get-tuple-element.78), channel_id=1, source_target_pairs={{0,2},{1,3},{2,0},{3,1},{4,6},{5,7},{6,4},{7,5},{8,10},{9,11},{10,... | collective-permute-start | bytes 393224 | tf_op jit(solution)/shard_map/ppermute | solution.py:125
  37.5 11.1 %collective-permute-start.19 = (bf16[128,512]{1,0:T(8,128)(2,1)S(1)}, bf16[128,512]{1,0:T(8,128)(2,1)S(1)}, u32[]{:S(2)}, u32[]{:S(2)}) collective-permute-start(bf16[128,512]{1,0:T(8,128)(2,1)S(1)} %get-tuple-element.79), channel_id=1, source_target_pairs={{0,2},{1,3},{2,0},{3,1},{4,6},{5,7},{6,4},{7,5},{8,10},{9,11},{10,... | collective-permute-start | bytes 393224 | tf_op jit(solution)/shard_map/ppermute | solution.py:125
  44.9 6.4 %collective-permute-start.20 = (bf16[256,512]{1,0:T(8,128)(2,1)S(1)}, bf16[256,512]{1,0:T(8,128)(2,1)S(1)}, u32[]{:S(2)}, u32[]{:S(2)}) collective-permute-start(bf16[256,512]{1,0:T(8,128)(2,1)S(1)} %collective-permute-done.13.refs_0_), channel_id=1, source_target_pairs={{0,1},{1,0},{2,3},{3,2},{4,5},{5,4},{6,7},{7,6},{8,9},{9,8},{10,11... | collective-permute-start | bytes 786440 | tf_op jit(solution)/shard_map/ppermute | solution.py:128
  44.9 10.1 %collective-permute-start.14 = (bf16[256,512]{1,0:T(8,128)(2,1)S(1)}, bf16[256,512]{1,0:T(8,128)(2,1)S(1)}, u32[]{:S(2)}, u32[]{:S(2)}) collective-permute-start(bf16[256,512]{1,0:T(8,128)(2,1)S(1)} %collective-permute-done.13.refs_0_), channel_id=1, source_target_pairs={{0,2},{1,3},{2,0},{3,1},{4,6},{5,7},{6,4},{7,5},{8,10},{9,11},{10,... | collective-permute-start | bytes 786440 | tf_op jit(solution)/shard_map/ppermute | solution.py:126
  51.7 3.2 %collective-permute-start.21 = (bf16[128,512]{1,0:T(8,128)(2,1)S(1)}, bf16[128,512]{1,0:T(8,128)(2,1)S(1)}, u32[]{:S(2)}, u32[]{:S(2)}) collective-permute-start(bf16[128,512]{1,0:T(8,128)(2,1)S(1)} %get-tuple-element.84.refs_0_), channel_id=1, source_target_pairs={{0,1},{1,0},{2,3},{3,2},{4,5},{5,4},{6,7},{7,6},{8,9},{9,8},{10,11... | collective-permute-start | bytes 393224 | tf_op jit(solution)/shard_map/ppermute | solution.py:129
  51.8 3.2 %collective-permute-start.22 = (bf16[128,512]{1,0:T(8,128)(2,1)S(1)}, bf16[128,512]{1,0:T(8,128)(2,1)S(1)}, u32[]{:S(2)}, u32[]{:S(2)}) collective-permute-start(bf16[128,512]{1,0:T(8,128)(2,1)S(1)} %get-tuple-element.85.refs_1_), channel_id=1, source_target_pairs={{0,1},{1,0},{2,3},{3,2},{4,5},{5,4},{6,7},{7,6},{8,9},{9,8},{10,11... | collective-permute-start | bytes 393224 | tf_op jit(solution)/shard_map/ppermute | solution.py:129
  55.0 1.5 %collective-permute-start.15 = (bf16[256,512]{1,0:T(8,128)(2,1)S(1)}, bf16[256,512]{1,0:T(8,128)(2,1)S(1)}, u32[]{:S(2)}, u32[]{:S(2)}) collective-permute-start(bf16[256,512]{1,0:T(8,128)(2,1)S(1)} %collective-permute-done.14.mine_ref), channel_id=1, source_target_pairs={{0,1},{1,0},{2,3},{3,2},{4,5},{5,4},{6,7},{7,6},{8,9},{9,8},{10,11... | collective-permute-start | bytes 786440 | tf_op jit(solution)/shard_map/ppermute | solution.py:130

commit v7 on v6

--- a/solution.py
+++ b/solution.py
@@ -12,15 +12,17 @@
 NORM_EPS = 1e-05
 LOG2E = 1.4426950408889634
 VMEM_LIMIT = 24 * 1024 * 1024
+PIECES = 2
 F32 = jnp.float32
 BF16 = jnp.bfloat16
 I32 = jnp.int32
 COST = 400_000_000
 PART_COST = 1_500_000_000
 OWN_COST = 1_500_000_000
-FAR_COST = 1_500_000_000
+GATE_COST = 1_000_000
+FAR_COST = 3_000_000_000
 BESIDE_COST = 1_000_000
-KV_COST = 400_000_000
+KV_COST = 1_000_000
 Q_COST = 400_000_000
 QA_COST = 1_500_000_000
 ATTEND_COST = 400_000_000
@@ -116,6 +118,10 @@
     return sender([(2 * z + c, 2 * f(z) + c) for z in range(size // 2) for c in range(2)])
 
 
+def gate(ride, other):
+    return call(lambda *_: None, "gate", (ride, other), [arr(ride.shape, ride.dtype)], rides={0: 0}, flops=GATE_COST)[0]
+
+
 def spread(size, full, first, second, use_own, use_far, use_beside):
     cross = chip_sender(size, lambda z: 3 - z)
     near = chip_sender(size, lambda z: z ^ 1)
@@ -137,9 +143,9 @@
     far = cross(first), cross(second)
     beside = near(use_own((full,), (twin(full),)))
     last_a, last_b = near(far[0]), near(far[1])
-    (last_a,) = use_far(far, (twin(far[0]), twin(far[1])), (last_a,))
+    last_a = use_far(far, (twin(far[0]), twin(far[1])), last_a)
     use_beside((beside,), (twin(beside),))
-    return (last_a, twin(last_a)), (last_b, twin(last_b))
+    return (last_a, tuple(twin(x) for x in last_a)), last_b, twin
 
 
 def joined(refs):
@@ -254,10 +260,16 @@
         hot_ref[r * 128 : (r + 1) * 128, :] = hot.astype(BF16)
 
 
-def more_kernel(n_mine, n_twin, n_ride, flip, *refs):
+def more_kernel(n_mine, n_twin, n_ride, flip, split, *refs):
     mine, twin, refs = refs[:n_mine], refs[n_mine : n_mine + n_twin], refs[n_mine + n_twin :]
     gain_ref, router_ref, w_ref, sums_in = refs[:4]
-    sums_out = refs[4 + n_ride]
+    refs = refs[4 + n_ride :]
+    if split:
+        whole_ref, refs = refs[0], refs[1:]
+        pieces = refs[1 + n_ride :]
+        for i, piece in enumerate(pieces):
+            piece[...] = whole_ref[i * piece.shape[0] : (i + 1) * piece.shape[0], :]
+    sums_out = refs[0]
     z, core = place()
     product, squares, routed = project(
         joined(mine), joined(twin), flip(z), core, gain_ref, router_ref, w_ref, slice(None)
@@ -268,13 +280,14 @@
     sums_out[:, n + 128 : n + 256] = sums_in[:, n + 128 : n + 256] + routed
 
 
-def more_part(mine, twin, staged, sums, rides, flip, flops):
+def more_part(mine, twin, staged, sums, rides, flip, flops, split=()):
     at = len(mine) + len(twin) + 3
-    return call(
-        functools.partial(more_kernel, len(mine), len(twin), len(rides), flip),
+    shapes = [arr((x.shape[0] // PIECES, x.shape[1]), x.dtype) for x in split for _ in range(PIECES)]
+    return call(
+        functools.partial(more_kernel, len(mine), len(twin), len(rides), flip, bool(split)),
         "more_part",
-        (*mine, *twin, *staged, sums, *rides),
-        [arr(sums.shape, F32), *(arr(r.shape, r.dtype) for r in rides)],
+        (*mine, *twin, *staged, sums, *rides, *split),
+        [arr(sums.shape, F32), *(arr(r.shape, r.dtype) for r in rides), *shapes],
         rides={at + i: i for i in range(1 + len(rides))},
         flops=flops,
     )
@@ -284,14 +297,13 @@
     return x * cos + pltpu.roll(x, HEAD_SIZE // 2, 1) * sin
 
 
-def kv_last_kernel(nq, at, mine_ref, twin_ref, gain_ref, router_ref, w_ref, sums, cos_ref, sin_ref, *outs):
-    kv_out, stat_out = outs[-2:] if len(outs) == 2 else outs[1:3]
+def kv_last_kernel(nq, at, n_mine, *refs):
+    mine, twin, refs = joined(refs[:n_mine]), joined(refs[n_mine : 2 * n_mine]), refs[2 * n_mine :]
+    gain_ref, router_ref, w_ref, sums, cos_ref, sin_ref, kv_out, stat_out = refs
     z, core = place()
     n, features = w_ref.shape[1], w_ref.shape[0]
-    rows = slice(at, at + mine_ref.shape[0])
-    product, squares, routed = project(
-        mine_ref[...], twin_ref[...], z ^ 2, core, gain_ref, router_ref, w_ref, slice(nq, n)
-    )
+    rows = slice(at, at + mine.shape[0])
+    product, squares, routed = project(mine, twin, z ^ 2, core, gain_ref, router_ref, w_ref, slice(nq, n))
     squares = jnp.sum(sums[rows, n : n + 128] + squares, axis=1, keepdims=True)
     routed = jnp.sum(sums[rows, n + 128 : n + 256] + routed, axis=1, keepdims=True)
     inverse = lax.rsqrt(squares * (1.0 / features) + NORM_EPS)
@@ -299,19 +311,18 @@
     kv_out[:, 0:128] = turn(kv[:, 0:128], cos_ref[rows, :], sin_ref[rows, :]).astype(BF16)
     kv_out[:, 128:256] = kv[:, 128:256].astype(BF16)
     stat_out[:, 0:128] = jnp.broadcast_to(inverse, (inverse.shape[0], 128))
-    gate = 1.0 / (1.0 + jnp.exp(-routed))
-    stat_out[:, 128:256] = jnp.broadcast_to(gate, (gate.shape[0], 128))
-
-
-def kv_last(at, pair, staged, sums, cos, sin, rides, nq, flops):
-    cap = pair[0].shape[0]
-    operands = (*pair, *staged, sums, cos, sin, *rides)
-    return call(
-        functools.partial(kv_last_kernel, nq, at),
+    gate_value = 1.0 / (1.0 + jnp.exp(-routed))
+    stat_out[:, 128:256] = jnp.broadcast_to(gate_value, (gate_value.shape[0], 128))
+
+
+def kv_last(at, pair, staged, sums, cos, sin, nq, flops):
+    mine, twin = pair
+    cap = sum(x.shape[0] for x in mine)
+    return call(
+        functools.partial(kv_last_kernel, nq, at, len(mine)),
         "kv_last",
-        operands,
-        [arr((cap, 256), BF16), arr((cap, 256), F32), *(arr(r.shape, r.dtype) for r in rides)],
-        rides={len(operands) - len(rides) + i: 2 + i for i in range(len(rides))},
+        (*mine, *twin, *staged, sums, cos, sin),
+        [arr((cap, 256), BF16), arr((cap, 256), F32)],
         flops=flops,
     )
 
@@ -333,13 +344,15 @@
     return top, total, mix
 
 
-def q_kernel(i, n_kv, mine_ref, twin_ref, gain_ref, w_ref, sums, stat_ref, cos_ref, sin_ref, bias_ref, *refs):
+def q_kernel(i, n_mine, n_kv, *refs):
+    mine, twin, refs = joined(refs[:n_mine]), joined(refs[n_mine : 2 * n_mine]), refs[2 * n_mine :]
+    gain_ref, w_ref, sums, stat_ref, cos_ref, sin_ref, bias_ref, *refs = refs
     kv_refs, (q_out, top_ref, total_ref, mix_ref) = refs[:n_kv], refs[n_kv:]
     z, core = place()
     half, nq = q_out.shape
     rows, keys = slice(i * half, (i + 1) * half), slice(0, (i + 1) * half)
     product, _, _ = project(
-        mine_ref[...], twin_ref[...], z ^ 2, core, gain_ref, None, w_ref, slice(0, nq), stats=False
+        mine, twin, z ^ 2, core, gain_ref, None, w_ref, slice(0, nq), stats=False
     )
     q = (sums[rows, 0:nq] + product) * stat_ref[:, 0:1]
     cos, sin, kv = cos_ref[rows, :], sin_ref[rows, :], joined(kv_refs)
@@ -358,11 +371,12 @@
 
 
 def q_part(i, pair, staged, sums, stat, cos, sin, kvs, bias, nq, flops):
-    half = pair[0].shape[0]
-    return call(
-        functools.partial(q_kernel, i, len(kvs)),
+    mine, twin = pair
+    half = stat.shape[0]
+    return call(
+        functools.partial(q_kernel, i, len(mine), len(kvs)),
         "q_part",
-        (*pair, staged[0], staged[2], sums, stat, cos, sin, bias, *kvs),
+        (*mine, *twin, staged[0], staged[2], sums, stat, cos, sin, bias, *kvs),
         [arr((half, nq), BF16), *carry_shapes(half, nq)],
         flops=flops,
     )
@@ -526,29 +540,32 @@
         )
         return ride
 
-    def far(mine, twin, rides):
-        held["sums"], ride, held["cos"], held["sin"] = more_part(
-            mine, twin, held["staged"], held["sums"], (*rides, *angles(rowpos)), lambda z: 3 - z, FAR_COST
+    def far(mine, twin, last):
+        held["sums"], held["cos"], held["sin"], *pieces = more_part(
+            mine, twin, held["staged"], held["sums"], angles(rowpos), lambda z: 3 - z, FAR_COST, (last,)
         )
-        return (ride,)
+        return tuple(pieces)
 
     def beside(mine, twin):
         (held["sums"],) = more_part(mine, twin, held["staged"], held["sums"], (), lambda z: z ^ 1, BESIDE_COST)
 
-    pairs = spread_halves(size, full, first, second, own, far, beside)
+    pair, last_b, twin = spread_halves(size, full, first, second, own, far, beside)
     sums, staged, bias = held["sums"], held["staged"], held["bias"]
     cos, sin = held["cos"], held["sin"]
     half = first.shape[0]
     ring = [(s, (s + 1) % shards) for s in range(shards)]
     kvs, stats, qs, carry = [], [], [], []
+    moved = []
     for i in range(2):
-        kv, stat, *kvs = kv_last(i * half, pairs[i], staged, sums, cos, sin, kvs, nq, KV_COST)
+        if i == 1:
+            last_b = gate(last_b, kvs[0])
+            pair = (last_b,), (twin(last_b),)
+        kv, stat = kv_last(i * half, pair, staged, sums, cos, sin, nq, KV_COST)
         kvs.append(kv)
         stats.append(stat)
-    moved = [lax.ppermute(kv, "ctx", ring) for kv in kvs]
-    for i in range(2):
+        moved.append(lax.ppermute(kv, "ctx", ring))
         q, *terms = q_part(
-            i, pairs[i], staged, sums, stats[i], cos, sin, kvs[: i + 1], bias, nq, Q_COST if i else QA_COST
+            i, pair, staged, sums, stat, cos, sin, kvs[: i + 1], bias, nq, Q_COST if i else QA_COST
         )
         qs.append(q)
         carry += terms

time: 58.4 us -> 59.1 us (1.012)
  starting transfers between devices: 25.1 us -> 26.8 us
  waiting for transfers between devices: 16.7 us -> 15.8 us
    ppermute x2, waiting for transfers between devices: 4.77 us -> 2.8 us  [spread_halves(): last_a, last_b = (near(far[0]), near(far[1]))]
    ppermute x6 -> x7, waiting for transfers between devices: 1.33 us -> 2.61 us  [the longest x2 2.24 us: body(): moved.append(lax.ppermute(kv, 'ctx', ring))]
    ppermute x1, starting transfers between devices: 3.1 us -> 3.95 us  [spread(): last = near(far)]
    ppermute x6 -> x7, starting transfers between devices: 2.43 us -> 3.03 us  [the longest x2 2.16 us: body(): moved.append(lax.ppermute(kv, 'ctx', ring))]
    pallas_call x14 -> x15, Pallas kernels: 15.6 us -> 15.6 us  [call(): pl.pallas_call(kernel, out_shape=out_shape, in_specs=[HBM if far else VME...]
  transfers between devices with their start and end apart: 23 -> 24, of which waited for: 11 -> 11; matrix products, arithmetic and copies ran while one was open for 1% -> 1% of each run, Pallas kernels for 19% -> 20%
where the time goes in v7:
time: 59.1 us; the launch traced here: 58.9 us
  starting transfers between devices  26.8 us (45%)
  waiting for transfers between devices  15.8 us (27%)
  Pallas kernels  15.6 us (26%)
    pallas_call x15, Pallas kernels, call(): pl.pallas_call(kernel, out_shape=out_shape, in_specs=[HBM if far else VME...  15.6 us
    ppermute x2, starting transfers between devices, spread_halves(): last_a, last_b = (near(far[0]), near(far[1]))  7.88 us
    ppermute x1, waiting for transfers between devices, spread(): far = cross(full)  5.13 us
    ppermute x2, starting transfers between devices, spread_halves(): far = (cross(first), cross(second))  4.78 us
    ppermute x1, starting transfers between devices, spread(): last = near(far)  3.95 us
    ppermute x1, starting transfers between devices, spread(): far = cross(full)  3.43 us
    ppermute x1, waiting for transfers between devices, spread(): last = near(far)  3.03 us
    ppermute x2, waiting for transfers between devices, spread_halves(): last_a, last_b = (near(far[0]), near(far[1]))  2.8 us
  transfers between devices with their start and end apart: 24, of which 11 were waited for; matrix products, arithmetic and copies ran while one was open for 1% of the time, Pallas kernels for 20%

profile of v7, /device:TPU:0, one launch (start us, length us, event | category | flops | bytes accessed | tf_op | source)
XLA Modules:
  0.0 58.9 jit_solution(2488230974056392153)
XLA Ops:
  0.0 1.6 %pick.1 = (bf16[256,512]{1,0:T(8,128)(2,1)S(1)}, bf16[128,512]{1,0:T(8,128)(2,1)S(1)}, bf16[128,512]{1,0:T(8,128)(2,1)S(1)}, s32[256,128]{1,0:T(8,128)S(1)}) custom-call(s32[2,256]{1,0:T(2,128)} %pos.1, bf16[1024,512]{1,0:T(8,128)(2,1)} %refs_6_.1), custom_call_target="tpu_custom_call" | custom-call | flops 400000000 | bytes 1 | tf_op jit(solution)/shard_map/pick/pallas_call | solution.py:41
  1.6 0.5 collective-permute-start.4
  2.2 4.7 %collective-permute-start = (bf16[128,512]{1,0:T(8,128)(2,1)S(1)}, bf16[128,512]{1,0:T(8,128)(2,1)S(1)}, u32[]{:S(2)}, u32[]{:S(2)}) collective-permute-start(bf16[128,512]{1,0:T(8,128)(2,1)S(1)} %get-tuple-element.47), channel_id=1, source_target_pairs={{0,6},{1,7},{2,4},{3,5},{4,2},{5,3},{6,0},{7,1},{8,14},{9,15},{10,... | collective-permute-start | bytes 393224 | tf_op jit(solution)/shard_map/ppermute | solution.py:143
  6.8 0.1 collective-permute-start.1
  7.0 0.0 collective-permute-done.4.twin_ref
  7.0 3.3 %own_part.1 = (bf16[256,512]{1,0:T(8,128)(2,1)S(1)}, f32[256,1024]{1,0:T(8,128)S(1)}, f32[1,4096]{1,0:T(1,128)S(1)}, f32[1,4096]{1,0:T(1,128)S(1)}, bf16[4096,76...) custom-call(bf16[256,512]{1,0:T(8,128)(2,1)S(1)} %get-tuple-element., ...), custom_call_target="tpu_custom_call", output_to_operand_aliasing={{0}: (0, {})} | custom-call | flops 1500000000 | bytes 1 | tf_op jit(solution)/shard_map/own_part/pallas_call | solution.py:41
  10.3 0.1 collective-permute-start.8
  10.4 0.1 pad_maximum_fusion
  10.5 0.6 %collective-permute-done.refs_0_ = bf16[128,512]{1,0:T(8,128)(2,1)S(1)} collective-permute-done((bf16[128,512]{1,0:T(8,128)(2,1)S(1)}, bf16[128,512]{1,0:T(8,128)(2,1)S(1)}, u32[]{:S(2)}, u32[]{:S(2)}) %collective-permute-start) | collective-permute-done | bytes 131104 | tf_op jit(solution)/shard_map/ppermute | solution.py:143
  11.0 0.0 collective-permute-start.2
  11.1 5.7 %collective-permute-start.5 = (bf16[128,512]{1,0:T(8,128)(2,1)S(1)}, bf16[128,512]{1,0:T(8,128)(2,1)S(1)}, u32[]{:S(2)}, u32[]{:S(2)}) collective-permute-start(bf16[128,512]{1,0:T(8,128)(2,1)S(1)} %collective-permute-done.refs_0_), channel_id=1, source_target_pairs={{0,2},{1,3},{2,0},{3,1},{4,6},{5,7},{6,4},{7,5},{8,10},{9,11},{10,... | collective-permute-start | bytes 393224 | tf_op jit(solution)/shard_map/ppermute | solution.py:145
  16.7 0.2 collective-permute-start.3
  17.0 0.5 sine_multiply_fusion
  17.5 2.2 %collective-permute-start.10 = (bf16[128,512]{1,0:T(8,128)(2,1)S(1)}, bf16[128,512]{1,0:T(8,128)(2,1)S(1)}, u32[]{:S(2)}, u32[]{:S(2)}) collective-permute-start(bf16[128,512]{1,0:T(8,128)(2,1)S(1)} %collective-permute-done.1.refs_1_), channel_id=1, source_target_pairs={{0,2},{1,3},{2,0},{3,1},{4,6},{5,7},{6,4},{7,5},{8,10},{9,11},{10,... | collective-permute-start | bytes 393224 | tf_op jit(solution)/shard_map/ppermute | solution.py:145
  19.6 0.3 collective-permute-done.8.refs_0_
  20.0 0.0 collective-permute-start.9
  20.0 2.8 %collective-permute-done.5.refs_10_ = bf16[128,512]{1,0:T(8,128)(2,1)S(1)} collective-permute-done((bf16[128,512]{1,0:T(8,128)(2,1)S(1)}, bf16[128,512]{1,0:T(8,128)(2,1)S(1)}, u32[]{:S(2)}, u32[]{:S(2)}) %collective-permute-start.5) | collective-permute-done | bytes 131104 | tf_op jit(solution)/shard_map/ppermute | solution.py:145
  22.8 0.7 %more_part.2 = (f32[256,1024]{1,0:T(8,128)S(1)}, f32[256,128]{1,0:T(8,128)S(1)}, f32[256,128]{1,0:T(8,128)S(1)}, bf16[64,512]{1,0:T(8,128)(2,1)S(1)}, bf16[64,512]{1,0:T(8,128)(2,1)S(1)}) custom-call(bf16[128,512]{1,0:T(8,128)(2,1)S(1)} %collective-permute-done.refs_0_, ...), custom_call_target="tpu_custom_call", output_to_operand_aliasing={{0}: (7, {}), {1}: (8, {}), {2}: (9, {})} | custom-call | flops 3000000000 | bytes 1 | tf_op jit(solution)/shard_map/more_part/pallas_call | solution.py:41
  23.4 0.1 collective-permute-start.6
  23.5 0.5 collective-permute-start.7
  24.0 0.7 %more_part.3.refs_7_.refs_6_.refs_5_.refs_4_ = f32[256,1024]{1,0:T(8,128)S(1)} custom-call(bf16[256,512]{1,0:T(8,128)(2,1)S(1)} %collective-permute-done.8.refs_0_, bf16[256,512]{1,0:T(8,128)(2,1)S(1)} %collective-permute-done.9.refs_1_, f32[1,4096]{1,0:T(1,128)S(1)} %get-tuple-element.50.refs_4_.refs_2_, ...), custom_call_target="tpu_custom_call", output_to_operand_aliasing={{}: (5, {})} | custom-call | flops 1000000 | bytes 1 | tf_op jit(solution)/shard_map/more_part/pallas_call | solution.py:41
  24.7 0.1 collective-permute-done.6.refs_2_
  24.8 0.2 collective-permute-done.7.refs_3_
  24.9 0.3 kv_last.2
  25.3 1.6 %collective-permute-start.13 = (bf16[128,256]{1,0:T(8,128)(2,1)S(1)}, bf16[128,256]{1,0:T(8,128)(2,1)S(1)}, u32[]{:S(2)}, u32[]{:S(2)}) collective-permute-start(bf16[128,256]{1,0:T(8,128)(2,1)S(1)} %get-tuple-element.63.refs_11_.__1_.refs_9_), channel_id=1, source_target_pairs={{0,8},{8,0},{1,9},{9,1},{2,10},{10,2},{3,11},{11,3},{4,12},{12,4},... | collective-permute-start | bytes 196616 | tf_op jit(solution)/shard_map/ppermute | solution.py:566
  26.8 0.1 collective-permute-start.11
  26.9 1.1 %q_part.2 = (bf16[128,512]{1,0:T(8,128)(2,1)S(1)}, f32[1,512]{1,0:T(1,128)S(1)}, f32[1,512]{1,0:T(1,128)S(1)}, f32[128,512]{1,0:T(8,128)S(1)}) custom-call(bf16[64,512]{1,0:T(8,128)(2,1)S(1)} %get-tuple-element.55.refs_0_, bf16[64,512]{1,0:T(8,128)(2,1)S(1)} %get-tuple-element.56.refs_1_, bf16[64,512]{1,0:T(8,128)(2,1)S(1)} %collective-permute-done.6.refs_2_, ...), custom_call_target="tpu_custom_call" | custom-call | flops 1500000000 | bytes 1 | tf_op jit(solution)/shard_map/q_part/pallas_call | solution.py:41
  28.0 0.1 collective-permute-done.11.refs_1_
  28.2 0.3 kv_last.3
  28.5 0.6 %collective-permute-start.12 = (bf16[128,256]{1,0:T(8,128)(2,1)S(1)}, bf16[128,256]{1,0:T(8,128)(2,1)S(1)}, u32[]{:S(2)}, u32[]{:S(2)}) collective-permute-start(bf16[128,256]{1,0:T(8,128)(2,1)S(1)} %get-tuple-element.66.refs_10_), channel_id=1, source_target_pairs={{0,8},{8,0},{1,9},{9,1},{2,10},{10,2},{3,11},{11,3},{4,12},{12,4},... | collective-permute-start | bytes 196616 | tf_op jit(solution)/shard_map/ppermute | solution.py:566
  29.1 0.8 %q_part.3 = (bf16[128,512]{1,0:T(8,128)(2,1)S(1)}, f32[1,512]{1,0:T(1,128)S(1)}, f32[1,512]{1,0:T(1,128)S(1)}, f32[128,512]{1,0:T(8,128)S(1)}) custom-call(bf16[128,512]{1,0:T(8,128)(2,1)S(1)} %gate.1.refs_0_, bf16[128,512]{1,0:T(8,128)(2,1)S(1)} %collective-permute-done.11.refs_1_, f32[1,4096]{1,0:T(1,128)S(1)} %get-tuple-element.50.refs_4_.refs_2_, ...), custom_call_target="tpu_custom_call" | custom-call | flops 400000000 | bytes 1 | tf_op jit(solution)/shard_map/q_part/pallas_call | solution.py:41
  30.0 0.7 %attend_more.2 = (f32[1,1024]{1,0:T(1,128)S(1)}, f32[1,1024]{1,0:T(1,128)S(1)}, f32[128,1024]{1,0:T(8,128)S(1)}) custom-call(bf16[128,512]{1,0:T(8,128)(2,1)S(1)} %get-tuple-element.64.qa_ref, bf16[128,512]{1,0:T(8,128)(2,1)S(1)} %get-tuple-element.67.qb_ref, bf16[128,256]{1,0:T(8,128)(2,1)S(1)} %collective-permute-done.13.kv_ref, ...), custom_call_target="tpu_custom_call" | custom-call | flops 400000000 | bytes 1 | tf_op jit(solution)/shard_map/attend_more/pallas_call | solution.py:41
  30.6 2.2 %collective-permute-done.12.kv_ref = bf16[128,256]{1,0:T(8,128)(2,1)S(1)} collective-permute-done((bf16[128,256]{1,0:T(8,128)(2,1)S(1)}, bf16[128,256]{1,0:T(8,128)(2,1)S(1)}, u32[]{:S(2)}, u32[]{:S(2)}) %collective-permute-start.12) | collective-permute-done | bytes 65568 | tf_op jit(solution)/shard_map/ppermute | solution.py:566
  32.9 0.7 %attend_more.3 = (bf16[256,512]{1,0:T(8,128)(2,1)S(1)}, bf16[128,512]{1,0:T(8,128)(2,1)S(1)}, bf16[128,512]{1,0:T(8,128)(2,1)S(1)}) custom-call(bf16[128,512]{1,0:T(8,128)(2,1)S(1)} %get-tuple-element.64.qa_ref, bf16[128,512]{1,0:T(8,128)(2,1)S(1)} %get-tuple-element.67.qb_ref, bf16[128,256]{1,0:T(8,128)(2,1)S(1)} %collective-permute-done.12.kv_ref, ...), custom_call_target="tpu_custom_call" | custom-call | flops 400000000 | bytes 1 | tf_op jit(solution)/shard_map/attend_more/pallas_call | solution.py:41
  33.6 3.4 %collective-permute-start.14 = (bf16[256,512]{1,0:T(8,128)(2,1)S(1)}, bf16[256,512]{1,0:T(8,128)(2,1)S(1)}, u32[]{:S(2)}, u32[]{:S(2)}) collective-permute-start(bf16[256,512]{1,0:T(8,128)(2,1)S(1)} %get-tuple-element.77.refs_0_), channel_id=1, source_target_pairs={{0,6},{1,7},{2,4},{3,5},{4,2},{5,3},{6,0},{7,1},{8,14},{9,15},{10,... | collective-permute-start | bytes 786440 | tf_op jit(solution)/shard_map/ppermute | solution.py:129
  37.1 0.5 collective-permute-start.18
  37.6 2.0 %collective-permute-start.20 = (bf16[128,512]{1,0:T(8,128)(2,1)S(1)}, bf16[128,512]{1,0:T(8,128)(2,1)S(1)}, u32[]{:S(2)}, u32[]{:S(2)}) collective-permute-start(bf16[128,512]{1,0:T(8,128)(2,1)S(1)} %get-tuple-element.79), channel_id=1, source_target_pairs={{0,2},{1,3},{2,0},{3,1},{4,6},{5,7},{6,4},{7,5},{8,10},{9,11},{10,... | collective-permute-start | bytes 393224 | tf_op jit(solution)/shard_map/ppermute | solution.py:131
  39.6 5.1 %collective-permute-done.14.refs_0_ = bf16[256,512]{1,0:T(8,128)(2,1)S(1)} collective-permute-done((bf16[256,512]{1,0:T(8,128)(2,1)S(1)}, bf16[256,512]{1,0:T(8,128)(2,1)S(1)}, u32[]{:S(2)}, u32[]{:S(2)}) %collective-permute-start.14) | collective-permute-done | bytes 262176 | tf_op jit(solution)/shard_map/ppermute | solution.py:129
  44.7 4.0 %collective-permute-start.15 = (bf16[256,512]{1,0:T(8,128)(2,1)S(1)}, bf16[256,512]{1,0:T(8,128)(2,1)S(1)}, u32[]{:S(2)}, u32[]{:S(2)}) collective-permute-start(bf16[256,512]{1,0:T(8,128)(2,1)S(1)} %collective-permute-done.14.refs_0_), channel_id=1, source_target_pairs={{0,2},{1,3},{2,0},{3,1},{4,6},{5,7},{6,4},{7,5},{8,10},{9,11},{10,... | collective-permute-start | bytes 786440 | tf_op jit(solution)/shard_map/ppermute | solution.py:132
  48.7 0.2 collective-permute-done.20.refs_4_
  48.9 2.6 %out_own.1 = (bf16[128,512]{1,0:T(8,128)(2,1)S(1)}, bf16[128,512]{1,0:T(8,128)(2,1)S(1)}, f32[256,512]{1,0:T(8,128)S(1)}, bf16[4096,512]{1,0:T(8,128)(2,1)S(1)}, bf16[1024,512]{1,0:T(8,128)(2,1)S(1)}) custom-call(bf16[256,512]{1,0:T(8,128)(2,1)S(1)} %get-tuple-element.77.refs_0_, ...), custom_call_target="tpu_custom_call", output_to_operand_aliasing={{0}: (3, {}), {1}: (4, {})} | custom-call | flops 1500000000 | bytes 1 | tf_op jit(solution)/shard_map/out_own/pallas_call | solution.py:41
  51.6 0.5 out_more.2
  52.1 0.1 collective-permute-start.22
  52.2 0.5 collective-permute-start.23
  52.6 3.0 %collective-permute-done.15.mine_ref = bf16[256,512]{1,0:T(8,128)(2,1)S(1)} collective-permute-done((bf16[256,512]{1,0:T(8,128)(2,1)S(1)}, bf16[256,512]{1,0:T(8,128)(2,1)S(1)}, u32[]{:S(2)}, u32[]{:S(2)}) %collective-permute-start.15) | collective-permute-done | bytes 262176 | tf_op jit(solution)/shard_map/ppermute | solution.py:132
  55.7 0.5 out_more.3.total_ref
  56.2 1.1 %collective-permute-done.16.twin_ref = bf16[256,512]{1,0:T(8,128)(2,1)S(1)} collective-permute-done((bf16[256,512]{1,0:T(8,128)(2,1)S(1)}, bf16[256,512]{1,0:T(8,128)(2,1)S(1)}, u32[]{:S(2)}, u32[]{:S(2)}) %collective-permute-start.16) | collective-permute-done | bytes 262176 | tf_op jit(solution)/shard_map/ppermute | solution.py:136
  57.2 1.6 %out_last.1 = bf16[1024,512]{1,0:T(8,128)(2,1)} custom-call(bf16[256,512]{1,0:T(8,128)(2,1)S(1)} %collective-permute-done.15.mine_ref, bf16[256,512]{1,0:T(8,128)(2,1)S(1)} %collective-permute-done.16.twin_ref, bf16[4096,512]{1,0:T(8,128)(2,1)S(1)} %get-tuple-element.80.refs_2_.refs_4_.w_ref, f32[256,512]{1,0:T(8,128)S(1)} %out_more.3.total_ref, ...), custom_call_target="tpu_custom_call" | custom-call | flops 400000000 | bytes 1 | tf_op jit(solution)/shard_map/out_last/pallas_call | solution.py:41
  (20 shorter events, 0.1 us)
Async XLA Ops:
  0.0 17.0 %copy-start = (f32[128]{0:T(128)S(1)}, f32[128]{0:T(128)}, u32[]{:S(2)}) copy-start(f32[128]{0:T(128)} %constant.9.clone.1) | copy-start | bytes 1540
  1.6 5.3 %collective-permute-start.4 = (bf16[256,512]{1,0:T(8,128)(2,1)S(1)}, bf16[256,512]{1,0:T(8,128)(2,1)S(1)}, u32[]{:S(2)}, u32[]{:S(2)}) collective-permute-start(bf16[256,512]{1,0:T(8,128)(2,1)S(1)} %get-tuple-element.49.x_ref), channel_id=1, source_target_pairs={{0,1},{1,0},{2,3},{3,2},{4,5},{5,4},{6,7},{7,6},{8,9},{9,8},{10,11... | collective-permute-start | bytes 786440 | tf_op jit(solution)/shard_map/ppermute | solution.py:144
  2.2 8.9 %collective-permute-start = (bf16[128,512]{1,0:T(8,128)(2,1)S(1)}, bf16[128,512]{1,0:T(8,128)(2,1)S(1)}, u32[]{:S(2)}, u32[]{:S(2)}) collective-permute-start(bf16[128,512]{1,0:T(8,128)(2,1)S(1)} %get-tuple-element.47), channel_id=1, source_target_pairs={{0,6},{1,7},{2,4},{3,5},{4,2},{5,3},{6,0},{7,1},{8,14},{9,15},{10,... | collective-permute-start | bytes 393224 | tf_op jit(solution)/shard_map/ppermute | solution.py:143
  6.8 9.9 %collective-permute-start.1 = (bf16[128,512]{1,0:T(8,128)(2,1)S(1)}, bf16[128,512]{1,0:T(8,128)(2,1)S(1)}, u32[]{:S(2)}, u32[]{:S(2)}) collective-permute-start(bf16[128,512]{1,0:T(8,128)(2,1)S(1)} %get-tuple-element.48), channel_id=1, source_target_pairs={{0,6},{1,7},{2,4},{3,5},{4,2},{5,3},{6,0},{7,1},{8,14},{9,15},{10,... | collective-permute-start | bytes 393224 | tf_op jit(solution)/shard_map/ppermute | solution.py:143
  10.3 9.7 %collective-permute-start.8 = (bf16[256,512]{1,0:T(8,128)(2,1)S(1)}, bf16[256,512]{1,0:T(8,128)(2,1)S(1)}, u32[]{:S(2)}, u32[]{:S(2)}) collective-permute-start(bf16[256,512]{1,0:T(8,128)(2,1)S(1)} %get-tuple-element.57), channel_id=1, source_target_pairs={{0,2},{1,3},{2,0},{3,1},{4,6},{5,7},{6,4},{7,5},{8,10},{9,11},{10,... | collective-permute-start | bytes 786440 | tf_op jit(solution)/shard_map/ppermute | solution.py:144
  11.0 8.9 %collective-permute-start.2 = (bf16[128,512]{1,0:T(8,128)(2,1)S(1)}, bf16[128,512]{1,0:T(8,128)(2,1)S(1)}, u32[]{:S(2)}, u32[]{:S(2)}) collective-permute-start(bf16[128,512]{1,0:T(8,128)(2,1)S(1)} %collective-permute-done.refs_0_), channel_id=1, source_target_pairs={{0,1},{1,0},{2,3},{3,2},{4,5},{5,4},{6,7},{7,6},{8,9},{9,8},{10,11... | collective-permute-start | bytes 393224 | tf_op jit(solution)/shard_map/ppermute | solution.py:146
  11.1 11.7 %collective-permute-start.5 = (bf16[128,512]{1,0:T(8,128)(2,1)S(1)}, bf16[128,512]{1,0:T(8,128)(2,1)S(1)}, u32[]{:S(2)}, u32[]{:S(2)}) collective-permute-start(bf16[128,512]{1,0:T(8,128)(2,1)S(1)} %collective-permute-done.refs_0_), channel_id=1, source_target_pairs={{0,2},{1,3},{2,0},{3,1},{4,6},{5,7},{6,4},{7,5},{8,10},{9,11},{10,... | collective-permute-start | bytes 393224 | tf_op jit(solution)/shard_map/ppermute | solution.py:145
  16.7 3.2 %collective-permute-start.3 = (bf16[128,512]{1,0:T(8,128)(2,1)S(1)}, bf16[128,512]{1,0:T(8,128)(2,1)S(1)}, u32[]{:S(2)}, u32[]{:S(2)}) collective-permute-start(bf16[128,512]{1,0:T(8,128)(2,1)S(1)} %collective-permute-done.1.refs_1_), channel_id=1, source_target_pairs={{0,1},{1,0},{2,3},{3,2},{4,5},{5,4},{6,7},{7,6},{8,9},{9,8},{10,11... | collective-permute-start | bytes 393224 | tf_op jit(solution)/shard_map/ppermute | solution.py:146
  17.5 9.4 %collective-permute-start.10 = (bf16[128,512]{1,0:T(8,128)(2,1)S(1)}, bf16[128,512]{1,0:T(8,128)(2,1)S(1)}, u32[]{:S(2)}, u32[]{:S(2)}) collective-permute-start(bf16[128,512]{1,0:T(8,128)(2,1)S(1)} %collective-permute-done.1.refs_1_), channel_id=1, source_target_pairs={{0,2},{1,3},{2,0},{3,1},{4,6},{5,7},{6,4},{7,5},{8,10},{9,11},{10,... | collective-permute-start | bytes 393224 | tf_op jit(solution)/shard_map/ppermute | solution.py:145
  20.0 4.1 %collective-permute-start.9 = (bf16[256,512]{1,0:T(8,128)(2,1)S(1)}, bf16[256,512]{1,0:T(8,128)(2,1)S(1)}, u32[]{:S(2)}, u32[]{:S(2)}) collective-permute-start(bf16[256,512]{1,0:T(8,128)(2,1)S(1)} %collective-permute-done.8.refs_0_), channel_id=1, source_target_pairs={{0,1},{1,0},{2,3},{3,2},{4,5},{5,4},{6,7},{7,6},{8,9},{9,8},{10,11... | collective-permute-start | bytes 786440 | tf_op jit(solution)/shard_map/ppermute | solution.py:147
  23.4 1.3 %collective-permute-start.6 = (bf16[64,512]{1,0:T(8,128)(2,1)S(1)}, bf16[64,512]{1,0:T(8,128)(2,1)S(1)}, u32[]{:S(2)}, u32[]{:S(2)}) collective-permute-start(bf16[64,512]{1,0:T(8,128)(2,1)S(1)} %get-tuple-element.55.refs_0_), channel_id=1, source_target_pairs={{0,1},{1,0},{2,3},{3,2},{4,5},{5,4},{6,7},{7,6},{8,9},{9,8},{10,11... | collective-permute-start | bytes 196616 | tf_op jit(solution)/shard_map/ppermute | solution.py:148
  23.5 1.4 %collective-permute-start.7 = (bf16[64,512]{1,0:T(8,128)(2,1)S(1)}, bf16[64,512]{1,0:T(8,128)(2,1)S(1)}, u32[]{:S(2)}, u32[]{:S(2)}) collective-permute-start(bf16[64,512]{1,0:T(8,128)(2,1)S(1)} %get-tuple-element.56.refs_1_), channel_id=1, source_target_pairs={{0,1},{1,0},{2,3},{3,2},{4,5},{5,4},{6,7},{7,6},{8,9},{9,8},{10,11... | collective-permute-start | bytes 196616 | tf_op jit(solution)/shard_map/ppermute | solution.py:148
  25.3 4.7 %collective-permute-start.13 = (bf16[128,256]{1,0:T(8,128)(2,1)S(1)}, bf16[128,256]{1,0:T(8,128)(2,1)S(1)}, u32[]{:S(2)}, u32[]{:S(2)}) collective-permute-start(bf16[128,256]{1,0:T(8,128)(2,1)S(1)} %get-tuple-element.63.refs_11_.__1_.refs_9_), channel_id=1, source_target_pairs={{0,8},{8,0},{1,9},{9,1},{2,10},{10,2},{3,11},{11,3},{4,12},{12,4},... | collective-permute-start | bytes 196616 | tf_op jit(solution)/shard_map/ppermute | solution.py:566
  26.8 1.3 %collective-permute-start.11 = (bf16[128,512]{1,0:T(8,128)(2,1)S(1)}, bf16[128,512]{1,0:T(8,128)(2,1)S(1)}, u32[]{:S(2)}, u32[]{:S(2)}) collective-permute-start(bf16[128,512]{1,0:T(8,128)(2,1)S(1)} %gate.1.refs_0_), channel_id=1, source_target_pairs={{0,1},{1,0},{2,3},{3,2},{4,5},{5,4},{6,7},{7,6},{8,9},{9,8},{10,11... | collective-permute-start | bytes 393224 | tf_op jit(solution)/shard_map/ppermute | solution.py:562
  28.5 4.4 %collective-permute-start.12 = (bf16[128,256]{1,0:T(8,128)(2,1)S(1)}, bf16[128,256]{1,0:T(8,128)(2,1)S(1)}, u32[]{:S(2)}, u32[]{:S(2)}) collective-permute-start(bf16[128,256]{1,0:T(8,128)(2,1)S(1)} %get-tuple-element.66.refs_10_), channel_id=1, source_target_pairs={{0,8},{8,0},{1,9},{9,1},{2,10},{10,2},{3,11},{11,3},{4,12},{12,4},... | collective-permute-start | bytes 196616 | tf_op jit(solution)/shard_map/ppermute | solution.py:566
  33.6 11.1 %collective-permute-start.14 = (bf16[256,512]{1,0:T(8,128)(2,1)S(1)}, bf16[256,512]{1,0:T(8,128)(2,1)S(1)}, u32[]{:S(2)}, u32[]{:S(2)}) collective-permute-start(bf16[256,512]{1,0:T(8,128)(2,1)S(1)} %get-tuple-element.77.refs_0_), channel_id=1, source_target_pairs={{0,6},{1,7},{2,4},{3,5},{4,2},{5,3},{6,0},{7,1},{8,14},{9,15},{10,... | collective-permute-start | bytes 786440 | tf_op jit(solution)/shard_map/ppermute | solution.py:129
  37.1 7.7 %collective-permute-start.17 = (bf16[128,512]{1,0:T(8,128)(2,1)S(1)}, bf16[128,512]{1,0:T(8,128)(2,1)S(1)}, u32[]{:S(2)}, u32[]{:S(2)}) collective-permute-start(bf16[128,512]{1,0:T(8,128)(2,1)S(1)} %get-tuple-element.78), channel_id=1, source_target_pairs={{0,1},{1,0},{2,3},{3,2},{4,5},{5,4},{6,7},{7,6},{8,9},{9,8},{10,11... | collective-permute-start | bytes 393224 | tf_op jit(solution)/shard_map/ppermute | solution.py:130
  37.1 11.6 %collective-permute-start.18 = (bf16[128,512]{1,0:T(8,128)(2,1)S(1)}, bf16[128,512]{1,0:T(8,128)(2,1)S(1)}, u32[]{:S(2)}, u32[]{:S(2)}) collective-permute-start(bf16[128,512]{1,0:T(8,128)(2,1)S(1)} %get-tuple-element.79), channel_id=1, source_target_pairs={{0,1},{1,0},{2,3},{3,2},{4,5},{5,4},{6,7},{7,6},{8,9},{9,8},{10,11... | collective-permute-start | bytes 393224 | tf_op jit(solution)/shard_map/ppermute | solution.py:130
  37.6 11.1 %collective-permute-start.19 = (bf16[128,512]{1,0:T(8,128)(2,1)S(1)}, bf16[128,512]{1,0:T(8,128)(2,1)S(1)}, u32[]{:S(2)}, u32[]{:S(2)}) collective-permute-start(bf16[128,512]{1,0:T(8,128)(2,1)S(1)} %get-tuple-element.78), channel_id=1, source_target_pairs={{0,2},{1,3},{2,0},{3,1},{4,6},{5,7},{6,4},{7,5},{8,10},{9,11},{10,... | collective-permute-start | bytes 393224 | tf_op jit(solution)/shard_map/ppermute | solution.py:131
  37.6 11.4 %collective-permute-start.20 = (bf16[128,512]{1,0:T(8,128)(2,1)S(1)}, bf16[128,512]{1,0:T(8,128)(2,1)S(1)}, u32[]{:S(2)}, u32[]{:S(2)}) collective-permute-start(bf16[128,512]{1,0:T(8,128)(2,1)S(1)} %get-tuple-element.79), channel_id=1, source_target_pairs={{0,2},{1,3},{2,0},{3,1},{4,6},{5,7},{6,4},{7,5},{8,10},{9,11},{10,... | collective-permute-start | bytes 393224 | tf_op jit(solution)/shard_map/ppermute | solution.py:131
  44.7 6.9 %collective-permute-start.21 = (bf16[256,512]{1,0:T(8,128)(2,1)S(1)}, bf16[256,512]{1,0:T(8,128)(2,1)S(1)}, u32[]{:S(2)}, u32[]{:S(2)}) collective-permute-start(bf16[256,512]{1,0:T(8,128)(2,1)S(1)} %collective-permute-done.14.refs_0_), channel_id=1, source_target_pairs={{0,1},{1,0},{2,3},{3,2},{4,5},{5,4},{6,7},{7,6},{8,9},{9,8},{10,11... | collective-permute-start | bytes 786440 | tf_op jit(solution)/shard_map/ppermute | solution.py:134
  44.7 10.9 %collective-permute-start.15 = (bf16[256,512]{1,0:T(8,128)(2,1)S(1)}, bf16[256,512]{1,0:T(8,128)(2,1)S(1)}, u32[]{:S(2)}, u32[]{:S(2)}) collective-permute-start(bf16[256,512]{1,0:T(8,128)(2,1)S(1)} %collective-permute-done.14.refs_0_), channel_id=1, source_target_pairs={{0,2},{1,3},{2,0},{3,1},{4,6},{5,7},{6,4},{7,5},{8,10},{9,11},{10,... | collective-permute-start | bytes 786440 | tf_op jit(solution)/shard_map/ppermute | solution.py:132
  52.1 3.6 %collective-permute-start.22 = (bf16[128,512]{1,0:T(8,128)(2,1)S(1)}, bf16[128,512]{1,0:T(8,128)(2,1)S(1)}, u32[]{:S(2)}, u32[]{:S(2)}) collective-permute-start(bf16[128,512]{1,0:T(8,128)(2,1)S(1)} %get-tuple-element.84.refs_0_), channel_id=1, source_target_pairs={{0,1},{1,0},{2,3},{3,2},{4,5},{5,4},{6,7},{7,6},{8,9},{9,8},{10,11... | collective-permute-start | bytes 393224 | tf_op jit(solution)/shard_map/ppermute | solution.py:135
  52.2 3.5 %collective-permute-start.23 = (bf16[128,512]{1,0:T(8,128)(2,1)S(1)}, bf16[128,512]{1,0:T(8,128)(2,1)S(1)}, u32[]{:S(2)}, u32[]{:S(2)}) collective-permute-start(bf16[128,512]{1,0:T(8,128)(2,1)S(1)} %get-tuple-element.85.refs_1_), channel_id=1, source_target_pairs={{0,1},{1,0},{2,3},{3,2},{4,5},{5,4},{6,7},{7,6},{8,9},{9,8},{10,11... | collective-permute-start | bytes 393224 | tf_op jit(solution)/shard_map/ppermute | solution.py:135
  55.7 1.5 %collective-permute-start.16 = (bf16[256,512]{1,0:T(8,128)(2,1)S(1)}, bf16[256,512]{1,0:T(8,128)(2,1)S(1)}, u32[]{:S(2)}, u32[]{:S(2)}) collective-permute-start(bf16[256,512]{1,0:T(8,128)(2,1)S(1)} %collective-permute-done.15.mine_ref), channel_id=1, source_target_pairs={{0,1},{1,0},{2,3},{3,2},{4,5},{5,4},{6,7},{7,6},{8,9},{9,8},{10,11... | collective-permute-start | bytes 786440 | tf_op jit(solution)/shard_map/ppermute | solution.py:136

commit v8 on v7

--- a/solution.py
+++ b/solution.py
@@ -23,8 +23,8 @@
 FAR_COST = 3_000_000_000
 BESIDE_COST = 1_000_000
 KV_COST = 1_000_000
-Q_COST = 400_000_000
-QA_COST = 1_500_000_000
+Q_COST = 1_000_000
+QA_COST = 1_000_000
 ATTEND_COST = 400_000_000
 
 
@@ -118,8 +118,9 @@
     return sender([(2 * z + c, 2 * f(z) + c) for z in range(size // 2) for c in range(2)])
 
 
-def gate(ride, other):
-    return call(lambda *_: None, "gate", (ride, other), [arr(ride.shape, ride.dtype)], rides={0: 0}, flops=GATE_COST)[0]
+def gate(*rides):
+    shapes = [arr(r.shape, r.dtype) for r in rides]
+    return call(lambda *_: None, "gate", rides, shapes, rides={i: i for i in range(len(rides))}, flops=GATE_COST)
 
 
 def spread(size, full, first, second, use_own, use_far, use_beside):
@@ -554,18 +555,19 @@
     cos, sin = held["cos"], held["sin"]
     half = first.shape[0]
     ring = [(s, (s + 1) % shards) for s in range(shards)]
-    kvs, stats, qs, carry = [], [], [], []
-    moved = []
+    kvs, stats, pairs, qs, carry = [], [], [], [], []
     for i in range(2):
         if i == 1:
-            last_b = gate(last_b, kvs[0])
+            kvs[0], last_b = gate(kvs[0], last_b)
             pair = (last_b,), (twin(last_b),)
         kv, stat = kv_last(i * half, pair, staged, sums, cos, sin, nq, KV_COST)
         kvs.append(kv)
         stats.append(stat)
-        moved.append(lax.ppermute(kv, "ctx", ring))
+        pairs.append(pair)
+    moved = [lax.ppermute(kv, "ctx", ring) for kv in kvs]
+    for i in range(2):
         q, *terms = q_part(
-            i, pair, staged, sums, stat, cos, sin, kvs[: i + 1], bias, nq, Q_COST if i else QA_COST
+            i, pairs[i], staged, sums, stats[i], cos, sin, kvs[: i + 1], bias, nq, Q_COST if i else QA_COST
         )
         qs.append(q)
         carry += terms

time: 59.1 us -> 58.1 us (0.983)
  waiting for transfers between devices: 15.8 us -> 14.1 us
  starting transfers between devices: 26.8 us -> 27.4 us
    ppermute x2, waiting for transfers between devices: 2.24 us -> 0.44 us  [body(): moved = [lax.ppermute(kv, 'ctx', ring) for kv in kvs]]
where the time goes in v8:
time: 58.1 us; the launch traced here: 57.8 us
  starting transfers between devices  27.4 us (47%)
  Pallas kernels  15.6 us (27%)
  waiting for transfers between devices  14.1 us (24%)
    pallas_call x15, Pallas kernels, call(): pl.pallas_call(kernel, out_shape=out_shape, in_specs=[HBM if far else VME...  15.6 us
    ppermute x2, starting transfers between devices, spread_halves(): last_a, last_b = (near(far[0]), near(far[1]))  7.88 us
    ppermute x1, waiting for transfers between devices, spread(): far = cross(full)  5.14 us
    ppermute x2, starting transfers between devices, spread_halves(): far = (cross(first), cross(second))  4.78 us
    ppermute x1, starting transfers between devices, spread(): last = near(far)  3.93 us
    ppermute x1, starting transfers between devices, spread(): far = cross(full)  3.43 us
    ppermute x2, waiting for transfers between devices, spread_halves(): last_a, last_b = (near(far[0]), near(far[1]))  3.04 us
    ppermute x1, waiting for transfers between devices, spread(): last = near(far)  3.03 us
  transfers between devices with their start and end apart: 24, of which 11 were waited for; matrix products, arithmetic and copies ran while one was open for 1% of the time, Pallas kernels for 20%

profile of v8, /device:TPU:0, one launch (start us, length us, event | category | flops | bytes accessed | tf_op | source)
XLA Modules:
  0.0 57.8 jit_solution(7448488975418012350)
XLA Ops:
  0.0 1.6 %pick.1 = (bf16[256,512]{1,0:T(8,128)(2,1)S(1)}, bf16[128,512]{1,0:T(8,128)(2,1)S(1)}, bf16[128,512]{1,0:T(8,128)(2,1)S(1)}, s32[256,128]{1,0:T(8,128)S(1)}) custom-call(s32[2,256]{1,0:T(2,128)} %pos.1, bf16[1024,512]{1,0:T(8,128)(2,1)} %refs_6_.1), custom_call_target="tpu_custom_call" | custom-call | flops 400000000 | bytes 1 | tf_op jit(solution)/shard_map/pick/pallas_call | solution.py:41
  1.6 0.5 collective-permute-start.4
  2.2 4.7 %collective-permute-start = (bf16[128,512]{1,0:T(8,128)(2,1)S(1)}, bf16[128,512]{1,0:T(8,128)(2,1)S(1)}, u32[]{:S(2)}, u32[]{:S(2)}) collective-permute-start(bf16[128,512]{1,0:T(8,128)(2,1)S(1)} %get-tuple-element.49), channel_id=1, source_target_pairs={{0,6},{1,7},{2,4},{3,5},{4,2},{5,3},{6,0},{7,1},{8,14},{9,15},{10,... | collective-permute-start | bytes 393224 | tf_op jit(solution)/shard_map/ppermute | solution.py:144
  6.8 0.1 collective-permute-start.1
  7.0 0.0 collective-permute-done.4.twin_ref
  7.0 3.3 %own_part.1 = (bf16[256,512]{1,0:T(8,128)(2,1)S(1)}, f32[256,1024]{1,0:T(8,128)S(1)}, f32[1,4096]{1,0:T(1,128)S(1)}, f32[1,4096]{1,0:T(1,128)S(1)}, bf16[4096,76...) custom-call(bf16[256,512]{1,0:T(8,128)(2,1)S(1)} %get-tuple-element., ...), custom_call_target="tpu_custom_call", output_to_operand_aliasing={{0}: (0, {})} | custom-call | flops 1500000000 | bytes 1 | tf_op jit(solution)/shard_map/own_part/pallas_call | solution.py:41
  10.3 0.1 collective-permute-start.8
  10.4 0.1 pad_maximum_fusion
  10.5 0.6 %collective-permute-done.refs_0_ = bf16[128,512]{1,0:T(8,128)(2,1)S(1)} collective-permute-done((bf16[128,512]{1,0:T(8,128)(2,1)S(1)}, bf16[128,512]{1,0:T(8,128)(2,1)S(1)}, u32[]{:S(2)}, u32[]{:S(2)}) %collective-permute-start) | collective-permute-done | bytes 131104 | tf_op jit(solution)/shard_map/ppermute | solution.py:144
  11.1 5.7 %collective-permute-start.5 = (bf16[128,512]{1,0:T(8,128)(2,1)S(1)}, bf16[128,512]{1,0:T(8,128)(2,1)S(1)}, u32[]{:S(2)}, u32[]{:S(2)}) collective-permute-start(bf16[128,512]{1,0:T(8,128)(2,1)S(1)} %collective-permute-done.refs_0_), channel_id=1, source_target_pairs={{0,2},{1,3},{2,0},{3,1},{4,6},{5,7},{6,4},{7,5},{8,10},{9,11},{10,... | collective-permute-start | bytes 393224 | tf_op jit(solution)/shard_map/ppermute | solution.py:146
  16.7 0.0 collective-permute-done.1.refs_1_
  16.7 0.2 collective-permute-start.3
  17.0 0.5 sine_multiply_fusion
  17.5 2.2 %collective-permute-start.10 = (bf16[128,512]{1,0:T(8,128)(2,1)S(1)}, bf16[128,512]{1,0:T(8,128)(2,1)S(1)}, u32[]{:S(2)}, u32[]{:S(2)}) collective-permute-start(bf16[128,512]{1,0:T(8,128)(2,1)S(1)} %collective-permute-done.1.refs_1_), channel_id=1, source_target_pairs={{0,2},{1,3},{2,0},{3,1},{4,6},{5,7},{6,4},{7,5},{8,10},{9,11},{10,... | collective-permute-start | bytes 393224 | tf_op jit(solution)/shard_map/ppermute | solution.py:146
  19.6 0.3 collective-permute-done.8.refs_0_
  20.0 0.0 collective-permute-done.3.refs_3_
  20.0 2.8 %collective-permute-done.5.refs_10_ = bf16[128,512]{1,0:T(8,128)(2,1)S(1)} collective-permute-done((bf16[128,512]{1,0:T(8,128)(2,1)S(1)}, bf16[128,512]{1,0:T(8,128)(2,1)S(1)}, u32[]{:S(2)}, u32[]{:S(2)}) %collective-permute-start.5) | collective-permute-done | bytes 131104 | tf_op jit(solution)/shard_map/ppermute | solution.py:146
  22.8 0.7 %more_part.2 = (f32[256,1024]{1,0:T(8,128)S(1)}, f32[256,128]{1,0:T(8,128)S(1)}, f32[256,128]{1,0:T(8,128)S(1)}, bf16[64,512]{1,0:T(8,128)(2,1)S(1)}, bf16[64,512]{1,0:T(8,128)(2,1)S(1)}) custom-call(bf16[128,512]{1,0:T(8,128)(2,1)S(1)} %collective-permute-done.refs_0_, ...), custom_call_target="tpu_custom_call", output_to_operand_aliasing={{0}: (7, {}), {1}: (8, {}), {2}: (9, {})} | custom-call | flops 3000000000 | bytes 1 | tf_op jit(solution)/shard_map/more_part/pallas_call | solution.py:41
  23.4 0.1 collective-permute-start.6
  23.5 0.5 collective-permute-start.7
  24.0 0.7 %more_part.3.refs_7_.refs_6_.refs_5_.refs_4_ = f32[256,1024]{1,0:T(8,128)S(1)} custom-call(bf16[256,512]{1,0:T(8,128)(2,1)S(1)} %collective-permute-done.8.refs_0_, bf16[256,512]{1,0:T(8,128)(2,1)S(1)} %collective-permute-done.9.refs_1_, f32[1,4096]{1,0:T(1,128)S(1)} %get-tuple-element.52.refs_4_.refs_2_, ...), custom_call_target="tpu_custom_call", output_to_operand_aliasing={{}: (5, {})} | custom-call | flops 1000000 | bytes 1 | tf_op jit(solution)/shard_map/more_part/pallas_call | solution.py:41
  24.7 0.1 collective-permute-done.6.refs_2_
  24.8 0.2 collective-permute-done.7.refs_3_
  24.9 0.3 kv_last.2
  25.3 0.2 collective-permute-done.10.__1_
  25.5 0.2 collective-permute-start.11
  25.7 1.5 %collective-permute-start.13 = (bf16[128,256]{1,0:T(8,128)(2,1)S(1)}, bf16[128,256]{1,0:T(8,128)(2,1)S(1)}, u32[]{:S(2)}, u32[]{:S(2)}) collective-permute-start(bf16[128,256]{1,0:T(8,128)(2,1)S(1)} %get-tuple-element.66.refs_11_.refs_9_), channel_id=1, source_target_pairs={{0,8},{8,0},{1,9},{9,1},{2,10},{10,2},{3,11},{11,3},{4,12},{12,4},... | collective-permute-start | bytes 196616 | tf_op jit(solution)/shard_map/ppermute | solution.py:567
  27.2 0.3 kv_last.3
  27.5 1.2 %collective-permute-start.12 = (bf16[128,256]{1,0:T(8,128)(2,1)S(1)}, bf16[128,256]{1,0:T(8,128)(2,1)S(1)}, u32[]{:S(2)}, u32[]{:S(2)}) collective-permute-start(bf16[128,256]{1,0:T(8,128)(2,1)S(1)} %get-tuple-element.70.refs_10_), channel_id=1, source_target_pairs={{0,8},{8,0},{1,9},{9,1},{2,10},{10,2},{3,11},{11,3},{4,12},{12,4},... | collective-permute-start | bytes 196616 | tf_op jit(solution)/shard_map/ppermute | solution.py:567
  28.8 1.1 %q_part.2 = (bf16[128,512]{1,0:T(8,128)(2,1)S(1)}, f32[1,512]{1,0:T(1,128)S(1)}, f32[1,512]{1,0:T(1,128)S(1)}, f32[128,512]{1,0:T(8,128)S(1)}) custom-call(bf16[64,512]{1,0:T(8,128)(2,1)S(1)} %get-tuple-element.57.refs_0_, bf16[64,512]{1,0:T(8,128)(2,1)S(1)} %get-tuple-element.58.refs_1_, bf16[64,512]{1,0:T(8,128)(2,1)S(1)} %collective-permute-done.6.refs_2_, ...), custom_call_target="tpu_custom_call" | custom-call | flops 1000000 | bytes 1 | tf_op jit(solution)/shard_map/q_part/pallas_call | solution.py:41
  29.9 0.9 %q_part.3 = (bf16[128,512]{1,0:T(8,128)(2,1)S(1)}, f32[1,512]{1,0:T(1,128)S(1)}, f32[1,512]{1,0:T(1,128)S(1)}, f32[128,512]{1,0:T(8,128)S(1)}) custom-call(bf16[128,512]{1,0:T(8,128)(2,1)S(1)} %get-tuple-element.68.refs_0_, bf16[128,512]{1,0:T(8,128)(2,1)S(1)} %collective-permute-done.11.refs_1_, f32[1,4096]{1,0:T(1,128)S(1)} %get-tuple-element.52.refs_4_.refs_2_, ...), custom_call_target="tpu_custom_call" | custom-call | flops 1000000 | bytes 1 | tf_op jit(solution)/shard_map/q_part/pallas_call | solution.py:41
  30.8 0.7 %attend_more.2 = (f32[1,1024]{1,0:T(1,128)S(1)}, f32[1,1024]{1,0:T(1,128)S(1)}, f32[128,1024]{1,0:T(8,128)S(1)}) custom-call(bf16[128,512]{1,0:T(8,128)(2,1)S(1)} %get-tuple-element.67.qa_ref, bf16[128,512]{1,0:T(8,128)(2,1)S(1)} %get-tuple-element.71.qb_ref, bf16[128,256]{1,0:T(8,128)(2,1)S(1)} %collective-permute-done.13.kv_ref, ...), custom_call_target="tpu_custom_call" | custom-call | flops 400000000 | bytes 1 | tf_op jit(solution)/shard_map/attend_more/pallas_call | solution.py:41
  31.4 0.4 collective-permute-done.12.kv_ref
  31.9 0.7 %attend_more.3 = (bf16[256,512]{1,0:T(8,128)(2,1)S(1)}, bf16[128,512]{1,0:T(8,128)(2,1)S(1)}, bf16[128,512]{1,0:T(8,128)(2,1)S(1)}) custom-call(bf16[128,512]{1,0:T(8,128)(2,1)S(1)} %get-tuple-element.67.qa_ref, bf16[128,512]{1,0:T(8,128)(2,1)S(1)} %get-tuple-element.71.qb_ref, bf16[128,256]{1,0:T(8,128)(2,1)S(1)} %collective-permute-done.12.kv_ref, ...), custom_call_target="tpu_custom_call" | custom-call | flops 400000000 | bytes 1 | tf_op jit(solution)/shard_map/attend_more/pallas_call | solution.py:41
  32.6 3.4 %collective-permute-start.14 = (bf16[256,512]{1,0:T(8,128)(2,1)S(1)}, bf16[256,512]{1,0:T(8,128)(2,1)S(1)}, u32[]{:S(2)}, u32[]{:S(2)}) collective-permute-start(bf16[256,512]{1,0:T(8,128)(2,1)S(1)} %get-tuple-element.81.refs_0_), channel_id=1, source_target_pairs={{0,6},{1,7},{2,4},{3,5},{4,2},{5,3},{6,0},{7,1},{8,14},{9,15},{10,... | collective-permute-start | bytes 786440 | tf_op jit(solution)/shard_map/ppermute | solution.py:130
  36.1 0.5 collective-permute-start.18
  36.6 2.0 %collective-permute-start.20 = (bf16[128,512]{1,0:T(8,128)(2,1)S(1)}, bf16[128,512]{1,0:T(8,128)(2,1)S(1)}, u32[]{:S(2)}, u32[]{:S(2)}) collective-permute-start(bf16[128,512]{1,0:T(8,128)(2,1)S(1)} %get-tuple-element.83), channel_id=1, source_target_pairs={{0,2},{1,3},{2,0},{3,1},{4,6},{5,7},{6,4},{7,5},{8,10},{9,11},{10,... | collective-permute-start | bytes 393224 | tf_op jit(solution)/shard_map/ppermute | solution.py:132
  38.6 5.1 %collective-permute-done.14.refs_0_ = bf16[256,512]{1,0:T(8,128)(2,1)S(1)} collective-permute-done((bf16[256,512]{1,0:T(8,128)(2,1)S(1)}, bf16[256,512]{1,0:T(8,128)(2,1)S(1)}, u32[]{:S(2)}, u32[]{:S(2)}) %collective-permute-start.14) | collective-permute-done | bytes 262176 | tf_op jit(solution)/shard_map/ppermute | solution.py:130
  43.7 3.9 %collective-permute-start.15 = (bf16[256,512]{1,0:T(8,128)(2,1)S(1)}, bf16[256,512]{1,0:T(8,128)(2,1)S(1)}, u32[]{:S(2)}, u32[]{:S(2)}) collective-permute-start(bf16[256,512]{1,0:T(8,128)(2,1)S(1)} %collective-permute-done.14.refs_0_), channel_id=1, source_target_pairs={{0,2},{1,3},{2,0},{3,1},{4,6},{5,7},{6,4},{7,5},{8,10},{9,11},{10,... | collective-permute-start | bytes 786440 | tf_op jit(solution)/shard_map/ppermute | solution.py:133
  47.7 0.2 collective-permute-done.20.refs_4_
  47.9 2.6 %out_own.1 = (bf16[128,512]{1,0:T(8,128)(2,1)S(1)}, bf16[128,512]{1,0:T(8,128)(2,1)S(1)}, f32[256,512]{1,0:T(8,128)S(1)}, bf16[4096,512]{1,0:T(8,128)(2,1)S(1)}, bf16[1024,512]{1,0:T(8,128)(2,1)S(1)}) custom-call(bf16[256,512]{1,0:T(8,128)(2,1)S(1)} %get-tuple-element.81.refs_0_, ...), custom_call_target="tpu_custom_call", output_to_operand_aliasing={{0}: (3, {}), {1}: (4, {})} | custom-call | flops 1500000000 | bytes 1 | tf_op jit(solution)/shard_map/out_own/pallas_call | solution.py:41
  50.6 0.5 out_more.2
  51.0 0.1 collective-permute-start.22
  51.1 0.5 collective-permute-start.23
  51.6 3.0 %collective-permute-done.15.mine_ref = bf16[256,512]{1,0:T(8,128)(2,1)S(1)} collective-permute-done((bf16[256,512]{1,0:T(8,128)(2,1)S(1)}, bf16[256,512]{1,0:T(8,128)(2,1)S(1)}, u32[]{:S(2)}, u32[]{:S(2)}) %collective-permute-start.15) | collective-permute-done | bytes 262176 | tf_op jit(solution)/shard_map/ppermute | solution.py:133
  54.7 0.5 out_more.3.total_ref
  55.1 1.1 %collective-permute-done.16.twin_ref = bf16[256,512]{1,0:T(8,128)(2,1)S(1)} collective-permute-done((bf16[256,512]{1,0:T(8,128)(2,1)S(1)}, bf16[256,512]{1,0:T(8,128)(2,1)S(1)}, u32[]{:S(2)}, u32[]{:S(2)}) %collective-permute-start.16) | collective-permute-done | bytes 262176 | tf_op jit(solution)/shard_map/ppermute | solution.py:137
  56.2 1.6 %out_last.1 = bf16[1024,512]{1,0:T(8,128)(2,1)} custom-call(bf16[256,512]{1,0:T(8,128)(2,1)S(1)} %collective-permute-done.15.mine_ref, bf16[256,512]{1,0:T(8,128)(2,1)S(1)} %collective-permute-done.16.twin_ref, bf16[4096,512]{1,0:T(8,128)(2,1)S(1)} %get-tuple-element.84.refs_2_.refs_4_.w_ref, f32[256,512]{1,0:T(8,128)S(1)} %out_more.3.total_ref, ...), custom_call_target="tpu_custom_call" | custom-call | flops 400000000 | bytes 1 | tf_op jit(solution)/shard_map/out_last/pallas_call | solution.py:41
  (20 shorter events, 0.1 us)
Async XLA Ops:
  0.0 17.0 %copy-start = (f32[128]{0:T(128)S(1)}, f32[128]{0:T(128)}, u32[]{:S(2)}) copy-start(f32[128]{0:T(128)} %constant.9.clone.1) | copy-start | bytes 1540
  1.6 5.3 %collective-permute-start.4 = (bf16[256,512]{1,0:T(8,128)(2,1)S(1)}, bf16[256,512]{1,0:T(8,128)(2,1)S(1)}, u32[]{:S(2)}, u32[]{:S(2)}) collective-permute-start(bf16[256,512]{1,0:T(8,128)(2,1)S(1)} %get-tuple-element.51.x_ref), channel_id=1, source_target_pairs={{0,1},{1,0},{2,3},{3,2},{4,5},{5,4},{6,7},{7,6},{8,9},{9,8},{10,11... | collective-permute-start | bytes 786440 | tf_op jit(solution)/shard_map/ppermute | solution.py:145
  2.2 8.9 %collective-permute-start = (bf16[128,512]{1,0:T(8,128)(2,1)S(1)}, bf16[128,512]{1,0:T(8,128)(2,1)S(1)}, u32[]{:S(2)}, u32[]{:S(2)}) collective-permute-start(bf16[128,512]{1,0:T(8,128)(2,1)S(1)} %get-tuple-element.49), channel_id=1, source_target_pairs={{0,6},{1,7},{2,4},{3,5},{4,2},{5,3},{6,0},{7,1},{8,14},{9,15},{10,... | collective-permute-start | bytes 393224 | tf_op jit(solution)/shard_map/ppermute | solution.py:144
  6.8 9.9 %collective-permute-start.1 = (bf16[128,512]{1,0:T(8,128)(2,1)S(1)}, bf16[128,512]{1,0:T(8,128)(2,1)S(1)}, u32[]{:S(2)}, u32[]{:S(2)}) collective-permute-start(bf16[128,512]{1,0:T(8,128)(2,1)S(1)} %get-tuple-element.50), channel_id=1, source_target_pairs={{0,6},{1,7},{2,4},{3,5},{4,2},{5,3},{6,0},{7,1},{8,14},{9,15},{10,... | collective-permute-start | bytes 393224 | tf_op jit(solution)/shard_map/ppermute | solution.py:144
  10.3 9.7 %collective-permute-start.8 = (bf16[256,512]{1,0:T(8,128)(2,1)S(1)}, bf16[256,512]{1,0:T(8,128)(2,1)S(1)}, u32[]{:S(2)}, u32[]{:S(2)}) collective-permute-start(bf16[256,512]{1,0:T(8,128)(2,1)S(1)} %get-tuple-element.59), channel_id=1, source_target_pairs={{0,2},{1,3},{2,0},{3,1},{4,6},{5,7},{6,4},{7,5},{8,10},{9,11},{10,... | collective-permute-start | bytes 786440 | tf_op jit(solution)/shard_map/ppermute | solution.py:145
  11.0 8.9 %collective-permute-start.2 = (bf16[128,512]{1,0:T(8,128)(2,1)S(1)}, bf16[128,512]{1,0:T(8,128)(2,1)S(1)}, u32[]{:S(2)}, u32[]{:S(2)}) collective-permute-start(bf16[128,512]{1,0:T(8,128)(2,1)S(1)} %collective-permute-done.refs_0_), channel_id=1, source_target_pairs={{0,1},{1,0},{2,3},{3,2},{4,5},{5,4},{6,7},{7,6},{8,9},{9,8},{10,11... | collective-permute-start | bytes 393224 | tf_op jit(solution)/shard_map/ppermute | solution.py:147
  11.1 11.7 %collective-permute-start.5 = (bf16[128,512]{1,0:T(8,128)(2,1)S(1)}, bf16[128,512]{1,0:T(8,128)(2,1)S(1)}, u32[]{:S(2)}, u32[]{:S(2)}) collective-permute-start(bf16[128,512]{1,0:T(8,128)(2,1)S(1)} %collective-permute-done.refs_0_), channel_id=1, source_target_pairs={{0,2},{1,3},{2,0},{3,1},{4,6},{5,7},{6,4},{7,5},{8,10},{9,11},{10,... | collective-permute-start | bytes 393224 | tf_op jit(solution)/shard_map/ppermute | solution.py:146
  16.7 3.2 %collective-permute-start.3 = (bf16[128,512]{1,0:T(8,128)(2,1)S(1)}, bf16[128,512]{1,0:T(8,128)(2,1)S(1)}, u32[]{:S(2)}, u32[]{:S(2)}) collective-permute-start(bf16[128,512]{1,0:T(8,128)(2,1)S(1)} %collective-permute-done.1.refs_1_), channel_id=1, source_target_pairs={{0,1},{1,0},{2,3},{3,2},{4,5},{5,4},{6,7},{7,6},{8,9},{9,8},{10,11... | collective-permute-start | bytes 393224 | tf_op jit(solution)/shard_map/ppermute | solution.py:147
  17.5 8.1 %collective-permute-start.10 = (bf16[128,512]{1,0:T(8,128)(2,1)S(1)}, bf16[128,512]{1,0:T(8,128)(2,1)S(1)}, u32[]{:S(2)}, u32[]{:S(2)}) collective-permute-start(bf16[128,512]{1,0:T(8,128)(2,1)S(1)} %collective-permute-done.1.refs_1_), channel_id=1, source_target_pairs={{0,2},{1,3},{2,0},{3,1},{4,6},{5,7},{6,4},{7,5},{8,10},{9,11},{10,... | collective-permute-start | bytes 393224 | tf_op jit(solution)/shard_map/ppermute | solution.py:146
  20.0 4.1 %collective-permute-start.9 = (bf16[256,512]{1,0:T(8,128)(2,1)S(1)}, bf16[256,512]{1,0:T(8,128)(2,1)S(1)}, u32[]{:S(2)}, u32[]{:S(2)}) collective-permute-start(bf16[256,512]{1,0:T(8,128)(2,1)S(1)} %collective-permute-done.8.refs_0_), channel_id=1, source_target_pairs={{0,1},{1,0},{2,3},{3,2},{4,5},{5,4},{6,7},{7,6},{8,9},{9,8},{10,11... | collective-permute-start | bytes 786440 | tf_op jit(solution)/shard_map/ppermute | solution.py:148
  23.4 1.3 %collective-permute-start.6 = (bf16[64,512]{1,0:T(8,128)(2,1)S(1)}, bf16[64,512]{1,0:T(8,128)(2,1)S(1)}, u32[]{:S(2)}, u32[]{:S(2)}) collective-permute-start(bf16[64,512]{1,0:T(8,128)(2,1)S(1)} %get-tuple-element.57.refs_0_), channel_id=1, source_target_pairs={{0,1},{1,0},{2,3},{3,2},{4,5},{5,4},{6,7},{7,6},{8,9},{9,8},{10,11... | collective-permute-start | bytes 196616 | tf_op jit(solution)/shard_map/ppermute | solution.py:149
  23.5 1.4 %collective-permute-start.7 = (bf16[64,512]{1,0:T(8,128)(2,1)S(1)}, bf16[64,512]{1,0:T(8,128)(2,1)S(1)}, u32[]{:S(2)}, u32[]{:S(2)}) collective-permute-start(bf16[64,512]{1,0:T(8,128)(2,1)S(1)} %get-tuple-element.58.refs_1_), channel_id=1, source_target_pairs={{0,1},{1,0},{2,3},{3,2},{4,5},{5,4},{6,7},{7,6},{8,9},{9,8},{10,11... | collective-permute-start | bytes 196616 | tf_op jit(solution)/shard_map/ppermute | solution.py:149
  25.5 1.7 %collective-permute-start.11 = (bf16[128,512]{1,0:T(8,128)(2,1)S(1)}, bf16[128,512]{1,0:T(8,128)(2,1)S(1)}, u32[]{:S(2)}, u32[]{:S(2)}) collective-permute-start(bf16[128,512]{1,0:T(8,128)(2,1)S(1)} %get-tuple-element.68.refs_0_), channel_id=1, source_target_pairs={{0,1},{1,0},{2,3},{3,2},{4,5},{5,4},{6,7},{7,6},{8,9},{9,8},{10,11... | collective-permute-start | bytes 393224 | tf_op jit(solution)/shard_map/ppermute | solution.py:562
  25.7 5.1 %collective-permute-start.13 = (bf16[128,256]{1,0:T(8,128)(2,1)S(1)}, bf16[128,256]{1,0:T(8,128)(2,1)S(1)}, u32[]{:S(2)}, u32[]{:S(2)}) collective-permute-start(bf16[128,256]{1,0:T(8,128)(2,1)S(1)} %get-tuple-element.66.refs_11_.refs_9_), channel_id=1, source_target_pairs={{0,8},{8,0},{1,9},{9,1},{2,10},{10,2},{3,11},{11,3},{4,12},{12,4},... | collective-permute-start | bytes 196616 | tf_op jit(solution)/shard_map/ppermute | solution.py:567
  27.5 4.3 %collective-permute-start.12 = (bf16[128,256]{1,0:T(8,128)(2,1)S(1)}, bf16[128,256]{1,0:T(8,128)(2,1)S(1)}, u32[]{:S(2)}, u32[]{:S(2)}) collective-permute-start(bf16[128,256]{1,0:T(8,128)(2,1)S(1)} %get-tuple-element.70.refs_10_), channel_id=1, source_target_pairs={{0,8},{8,0},{1,9},{9,1},{2,10},{10,2},{3,11},{11,3},{4,12},{12,4},... | collective-permute-start | bytes 196616 | tf_op jit(solution)/shard_map/ppermute | solution.py:567
  32.6 11.1 %collective-permute-start.14 = (bf16[256,512]{1,0:T(8,128)(2,1)S(1)}, bf16[256,512]{1,0:T(8,128)(2,1)S(1)}, u32[]{:S(2)}, u32[]{:S(2)}) collective-permute-start(bf16[256,512]{1,0:T(8,128)(2,1)S(1)} %get-tuple-element.81.refs_0_), channel_id=1, source_target_pairs={{0,6},{1,7},{2,4},{3,5},{4,2},{5,3},{6,0},{7,1},{8,14},{9,15},{10,... | collective-permute-start | bytes 786440 | tf_op jit(solution)/shard_map/ppermute | solution.py:130
  36.1 7.7 %collective-permute-start.17 = (bf16[128,512]{1,0:T(8,128)(2,1)S(1)}, bf16[128,512]{1,0:T(8,128)(2,1)S(1)}, u32[]{:S(2)}, u32[]{:S(2)}) collective-permute-start(bf16[128,512]{1,0:T(8,128)(2,1)S(1)} %get-tuple-element.82), channel_id=1, source_target_pairs={{0,1},{1,0},{2,3},{3,2},{4,5},{5,4},{6,7},{7,6},{8,9},{9,8},{10,11... | collective-permute-start | bytes 393224 | tf_op jit(solution)/shard_map/ppermute | solution.py:131
  36.1 11.6 %collective-permute-start.18 = (bf16[128,512]{1,0:T(8,128)(2,1)S(1)}, bf16[128,512]{1,0:T(8,128)(2,1)S(1)}, u32[]{:S(2)}, u32[]{:S(2)}) collective-permute-start(bf16[128,512]{1,0:T(8,128)(2,1)S(1)} %get-tuple-element.83), channel_id=1, source_target_pairs={{0,1},{1,0},{2,3},{3,2},{4,5},{5,4},{6,7},{7,6},{8,9},{9,8},{10,11... | collective-permute-start | bytes 393224 | tf_op jit(solution)/shard_map/ppermute | solution.py:131
  36.6 11.1 %collective-permute-start.19 = (bf16[128,512]{1,0:T(8,128)(2,1)S(1)}, bf16[128,512]{1,0:T(8,128)(2,1)S(1)}, u32[]{:S(2)}, u32[]{:S(2)}) collective-permute-start(bf16[128,512]{1,0:T(8,128)(2,1)S(1)} %get-tuple-element.82), channel_id=1, source_target_pairs={{0,2},{1,3},{2,0},{3,1},{4,6},{5,7},{6,4},{7,5},{8,10},{9,11},{10,... | collective-permute-start | bytes 393224 | tf_op jit(solution)/shard_map/ppermute | solution.py:132
  36.6 11.3 %collective-permute-start.20 = (bf16[128,512]{1,0:T(8,128)(2,1)S(1)}, bf16[128,512]{1,0:T(8,128)(2,1)S(1)}, u32[]{:S(2)}, u32[]{:S(2)}) collective-permute-start(bf16[128,512]{1,0:T(8,128)(2,1)S(1)} %get-tuple-element.83), channel_id=1, source_target_pairs={{0,2},{1,3},{2,0},{3,1},{4,6},{5,7},{6,4},{7,5},{8,10},{9,11},{10,... | collective-permute-start | bytes 393224 | tf_op jit(solution)/shard_map/ppermute | solution.py:132
  43.7 6.8 %collective-permute-start.21 = (bf16[256,512]{1,0:T(8,128)(2,1)S(1)}, bf16[256,512]{1,0:T(8,128)(2,1)S(1)}, u32[]{:S(2)}, u32[]{:S(2)}) collective-permute-start(bf16[256,512]{1,0:T(8,128)(2,1)S(1)} %collective-permute-done.14.refs_0_), channel_id=1, source_target_pairs={{0,1},{1,0},{2,3},{3,2},{4,5},{5,4},{6,7},{7,6},{8,9},{9,8},{10,11... | collective-permute-start | bytes 786440 | tf_op jit(solution)/shard_map/ppermute | solution.py:135
  43.7 10.9 %collective-permute-start.15 = (bf16[256,512]{1,0:T(8,128)(2,1)S(1)}, bf16[256,512]{1,0:T(8,128)(2,1)S(1)}, u32[]{:S(2)}, u32[]{:S(2)}) collective-permute-start(bf16[256,512]{1,0:T(8,128)(2,1)S(1)} %collective-permute-done.14.refs_0_), channel_id=1, source_target_pairs={{0,2},{1,3},{2,0},{3,1},{4,6},{5,7},{6,4},{7,5},{8,10},{9,11},{10,... | collective-permute-start | bytes 786440 | tf_op jit(solution)/shard_map/ppermute | solution.py:133
  51.0 3.6 %collective-permute-start.22 = (bf16[128,512]{1,0:T(8,128)(2,1)S(1)}, bf16[128,512]{1,0:T(8,128)(2,1)S(1)}, u32[]{:S(2)}, u32[]{:S(2)}) collective-permute-start(bf16[128,512]{1,0:T(8,128)(2,1)S(1)} %get-tuple-element.88.refs_0_), channel_id=1, source_target_pairs={{0,1},{1,0},{2,3},{3,2},{4,5},{5,4},{6,7},{7,6},{8,9},{9,8},{10,11... | collective-permute-start | bytes 393224 | tf_op jit(solution)/shard_map/ppermute | solution.py:136
  51.1 3.5 %collective-permute-start.23 = (bf16[128,512]{1,0:T(8,128)(2,1)S(1)}, bf16[128,512]{1,0:T(8,128)(2,1)S(1)}, u32[]{:S(2)}, u32[]{:S(2)}) collective-permute-start(bf16[128,512]{1,0:T(8,128)(2,1)S(1)} %get-tuple-element.89.refs_1_), channel_id=1, source_target_pairs={{0,1},{1,0},{2,3},{3,2},{4,5},{5,4},{6,7},{7,6},{8,9},{9,8},{10,11... | collective-permute-start | bytes 393224 | tf_op jit(solution)/shard_map/ppermute | solution.py:136
  54.6 1.5 %collective-permute-start.16 = (bf16[256,512]{1,0:T(8,128)(2,1)S(1)}, bf16[256,512]{1,0:T(8,128)(2,1)S(1)}, u32[]{:S(2)}, u32[]{:S(2)}) collective-permute-start(bf16[256,512]{1,0:T(8,128)(2,1)S(1)} %collective-permute-done.15.mine_ref), channel_id=1, source_target_pairs={{0,1},{1,0},{2,3},{3,2},{4,5},{5,4},{6,7},{7,6},{8,9},{9,8},{10,11... | collective-permute-start | bytes 786440 | tf_op jit(solution)/shard_map/ppermute | solution.py:137

commit v9 on v8

--- a/solution.py
+++ b/solution.py
@@ -17,7 +17,7 @@
 BF16 = jnp.bfloat16
 I32 = jnp.int32
 COST = 400_000_000
-PART_COST = 1_500_000_000
+PART_COST = 400_000_000
 OWN_COST = 1_500_000_000
 GATE_COST = 1_000_000
 FAR_COST = 3_000_000_000
@@ -130,11 +130,12 @@
     far = cross(full)
     mates = twin(first), twin(second)
     beside = near(first), near(second)
-    last = near(far)
+    half = first.shape[0]
+    last = near(far[:half]), near(far[half:])
     beside = use_own((full,), mates, beside)
     beside = use_far((far,), (twin(far),), beside)
     use_beside(beside, (twin(beside[0]), twin(beside[1])))
-    return last, twin(last)
+    return last, (twin(last[0]), twin(last[1]))
 
 
 def spread_halves(size, full, first, second, use_own, use_far, use_beside):
@@ -479,9 +480,9 @@
     )
 
 
-def out_last_kernel(mine_ref, twin_ref, w_ref, total_ref, sa_ref, sb_ref, hot_ref, hid_ref, out, out_ref, sems):
+def out_last_kernel(a, b, c, d, w_ref, total_ref, sa_ref, sb_ref, hot_ref, hid_ref, out, out_ref, sems):
     z, core = place()
-    projected = total_ref[...] + out_term(mine_ref[...], twin_ref[...], z ^ 2, core, w_ref)
+    projected = total_ref[...] + out_term(joined((a, b)), joined((c, d)), z ^ 2, core, w_ref)
     gate = jnp.concatenate([sa_ref[:, 128:129], sb_ref[:, 128:129]], axis=0)
     update = (gate * projected).astype(BF16)
     block = 256
@@ -498,7 +499,7 @@
     return call(
         out_last_kernel,
         "out_last",
-        (*pair, w, total, *stats, hot, hidden),
+        (*pair[0], *pair[1], w, total, *stats, hot, hidden),
         [arr(hidden.shape, BF16)],
         scratch=[pltpu.VMEM(hidden.shape, BF16), pltpu.SemaphoreType.DMA((hidden.shape[0] // 256,))],
         out_hbm=True,

time: 58.1 us -> 58 us (level)
    ppermute x2 -> x4, starting transfers between devices: 3.93 us -> 4.08 us  [the longest x2 4.08 us: spread(): last = (near(far[:half]), near(far[half:]))]
    ppermute x2 -> x4, waiting for transfers between devices: 4.08 us -> 3.98 us  [the longest x2 3.12 us: spread(): last = (near(far[:half]), near(far[half:]))]
  transfers between devices with their start and end apart: 24 -> 26, of which waited for: 11 -> 12; matrix products, arithmetic and copies ran while one was open for 1% -> 1% of each run, Pallas kernels for 20% -> 20%
where the time goes in v9:
time: 58 us; the launch traced here: 57.7 us
  starting transfers between devices  27.3 us (47%)
  Pallas kernels  15.6 us (27%)
  waiting for transfers between devices  14.1 us (24%)
    pallas_call x15, Pallas kernels, call(): pl.pallas_call(kernel, out_shape=out_shape, in_specs=[HBM if far else VME...  15.6 us
    ppermute x2, starting transfers between devices, spread_halves(): last_a, last_b = (near(far[0]), near(far[1]))  7.88 us
    ppermute x1, waiting for transfers between devices, spread(): far = cross(full)  5.42 us
    ppermute x2, starting transfers between devices, spread_halves(): far = (cross(first), cross(second))  4.78 us
    ppermute x2, starting transfers between devices, spread(): last = (near(far[:half]), near(far[half:]))  4.08 us
    ppermute x1, starting transfers between devices, spread(): far = cross(full)  3.43 us
    ppermute x2, waiting for transfers between devices, spread(): last = (near(far[:half]), near(far[half:]))  3.12 us
    ppermute x2, waiting for transfers between devices, spread_halves(): last_a, last_b = (near(far[0]), near(far[1]))  3.04 us
  transfers between devices with their start and end apart: 26, of which 12 were waited for; matrix products, arithmetic and copies ran while one was open for 1% of the time, Pallas kernels for 20%

profile of v9, /device:TPU:0, one launch (start us, length us, event | category | flops | bytes accessed | tf_op | source)
XLA Modules:
  0.0 57.7 jit_solution(1172685204952643467)
XLA Ops:
  0.0 1.6 %pick.1 = (bf16[256,512]{1,0:T(8,128)(2,1)S(1)}, bf16[128,512]{1,0:T(8,128)(2,1)S(1)}, bf16[128,512]{1,0:T(8,128)(2,1)S(1)}, s32[256,128]{1,0:T(8,128)S(1)}) custom-call(s32[2,256]{1,0:T(2,128)} %pos.1, bf16[1024,512]{1,0:T(8,128)(2,1)} %refs_6_.1), custom_call_target="tpu_custom_call" | custom-call | flops 400000000 | bytes 1 | tf_op jit(solution)/shard_map/pick/pallas_call | solution.py:41
  1.6 0.5 collective-permute-start.4
  2.2 4.7 %collective-permute-start = (bf16[128,512]{1,0:T(8,128)(2,1)S(1)}, bf16[128,512]{1,0:T(8,128)(2,1)S(1)}, u32[]{:S(2)}, u32[]{:S(2)}) collective-permute-start(bf16[128,512]{1,0:T(8,128)(2,1)S(1)} %get-tuple-element.49), channel_id=1, source_target_pairs={{0,6},{1,7},{2,4},{3,5},{4,2},{5,3},{6,0},{7,1},{8,14},{9,15},{10,... | collective-permute-start | bytes 393224 | tf_op jit(solution)/shard_map/ppermute | solution.py:145
  6.8 0.1 collective-permute-start.1
  7.0 0.0 collective-permute-done.4.twin_ref
  7.0 3.3 %own_part.1 = (bf16[256,512]{1,0:T(8,128)(2,1)S(1)}, f32[256,1024]{1,0:T(8,128)S(1)}, f32[1,4096]{1,0:T(1,128)S(1)}, f32[1,4096]{1,0:T(1,128)S(1)}, bf16[4096,76...) custom-call(bf16[256,512]{1,0:T(8,128)(2,1)S(1)} %get-tuple-element., ...), custom_call_target="tpu_custom_call", output_to_operand_aliasing={{0}: (0, {})} | custom-call | flops 1500000000 | bytes 1 | tf_op jit(solution)/shard_map/own_part/pallas_call | solution.py:41
  10.3 0.1 collective-permute-start.8
  10.4 0.1 pad_maximum_fusion
  10.5 0.6 %collective-permute-done.refs_0_ = bf16[128,512]{1,0:T(8,128)(2,1)S(1)} collective-permute-done((bf16[128,512]{1,0:T(8,128)(2,1)S(1)}, bf16[128,512]{1,0:T(8,128)(2,1)S(1)}, u32[]{:S(2)}, u32[]{:S(2)}) %collective-permute-start) | collective-permute-done | bytes 131104 | tf_op jit(solution)/shard_map/ppermute | solution.py:145
  11.1 5.7 %collective-permute-start.5 = (bf16[128,512]{1,0:T(8,128)(2,1)S(1)}, bf16[128,512]{1,0:T(8,128)(2,1)S(1)}, u32[]{:S(2)}, u32[]{:S(2)}) collective-permute-start(bf16[128,512]{1,0:T(8,128)(2,1)S(1)} %collective-permute-done.refs_0_), channel_id=1, source_target_pairs={{0,2},{1,3},{2,0},{3,1},{4,6},{5,7},{6,4},{7,5},{8,10},{9,11},{10,... | collective-permute-start | bytes 393224 | tf_op jit(solution)/shard_map/ppermute | solution.py:147
  16.7 0.2 collective-permute-start.3
  17.0 0.5 sine_multiply_fusion
  17.5 2.2 %collective-permute-start.10 = (bf16[128,512]{1,0:T(8,128)(2,1)S(1)}, bf16[128,512]{1,0:T(8,128)(2,1)S(1)}, u32[]{:S(2)}, u32[]{:S(2)}) collective-permute-start(bf16[128,512]{1,0:T(8,128)(2,1)S(1)} %collective-permute-done.1.refs_1_), channel_id=1, source_target_pairs={{0,2},{1,3},{2,0},{3,1},{4,6},{5,7},{6,4},{7,5},{8,10},{9,11},{10,... | collective-permute-start | bytes 393224 | tf_op jit(solution)/shard_map/ppermute | solution.py:147
  19.6 0.3 collective-permute-done.8.refs_0_
  20.0 2.8 %collective-permute-done.5.refs_10_ = bf16[128,512]{1,0:T(8,128)(2,1)S(1)} collective-permute-done((bf16[128,512]{1,0:T(8,128)(2,1)S(1)}, bf16[128,512]{1,0:T(8,128)(2,1)S(1)}, u32[]{:S(2)}, u32[]{:S(2)}) %collective-permute-start.5) | collective-permute-done | bytes 131104 | tf_op jit(solution)/shard_map/ppermute | solution.py:147
  22.8 0.7 %more_part.2 = (f32[256,1024]{1,0:T(8,128)S(1)}, f32[256,128]{1,0:T(8,128)S(1)}, f32[256,128]{1,0:T(8,128)S(1)}, bf16[64,512]{1,0:T(8,128)(2,1)S(1)}, bf16[64,512]{1,0:T(8,128)(2,1)S(1)}) custom-call(bf16[128,512]{1,0:T(8,128)(2,1)S(1)} %collective-permute-done.refs_0_, ...), custom_call_target="tpu_custom_call", output_to_operand_aliasing={{0}: (7, {}), {1}: (8, {}), {2}: (9, {})} | custom-call | flops 3000000000 | bytes 1 | tf_op jit(solution)/shard_map/more_part/pallas_call | solution.py:41
  23.4 0.1 collective-permute-start.6
  23.5 0.5 collective-permute-start.7
  24.0 0.7 %more_part.3.refs_7_.refs_6_.refs_5_.refs_4_ = f32[256,1024]{1,0:T(8,128)S(1)} custom-call(bf16[256,512]{1,0:T(8,128)(2,1)S(1)} %collective-permute-done.8.refs_0_, bf16[256,512]{1,0:T(8,128)(2,1)S(1)} %collective-permute-done.9.refs_1_, f32[1,4096]{1,0:T(1,128)S(1)} %get-tuple-element.52.refs_4_.refs_2_, ...), custom_call_target="tpu_custom_call", output_to_operand_aliasing={{}: (5, {})} | custom-call | flops 1000000 | bytes 1 | tf_op jit(solution)/shard_map/more_part/pallas_call | solution.py:41
  24.7 0.1 collective-permute-done.6.refs_2_
  24.8 0.2 collective-permute-done.7.refs_3_
  24.9 0.3 kv_last.2
  25.3 0.2 collective-permute-done.10.__1_
  25.5 0.2 collective-permute-start.11
  25.7 1.5 %collective-permute-start.13 = (bf16[128,256]{1,0:T(8,128)(2,1)S(1)}, bf16[128,256]{1,0:T(8,128)(2,1)S(1)}, u32[]{:S(2)}, u32[]{:S(2)}) collective-permute-start(bf16[128,256]{1,0:T(8,128)(2,1)S(1)} %get-tuple-element.66.refs_11_.refs_9_), channel_id=1, source_target_pairs={{0,8},{8,0},{1,9},{9,1},{2,10},{10,2},{3,11},{11,3},{4,12},{12,4},... | collective-permute-start | bytes 196616 | tf_op jit(solution)/shard_map/ppermute | solution.py:568
  27.2 0.3 kv_last.3
  27.5 1.2 %collective-permute-start.12 = (bf16[128,256]{1,0:T(8,128)(2,1)S(1)}, bf16[128,256]{1,0:T(8,128)(2,1)S(1)}, u32[]{:S(2)}, u32[]{:S(2)}) collective-permute-start(bf16[128,256]{1,0:T(8,128)(2,1)S(1)} %get-tuple-element.70.refs_10_), channel_id=1, source_target_pairs={{0,8},{8,0},{1,9},{9,1},{2,10},{10,2},{3,11},{11,3},{4,12},{12,4},... | collective-permute-start | bytes 196616 | tf_op jit(solution)/shard_map/ppermute | solution.py:568
  28.8 1.1 %q_part.2 = (bf16[128,512]{1,0:T(8,128)(2,1)S(1)}, f32[1,512]{1,0:T(1,128)S(1)}, f32[1,512]{1,0:T(1,128)S(1)}, f32[128,512]{1,0:T(8,128)S(1)}) custom-call(bf16[64,512]{1,0:T(8,128)(2,1)S(1)} %get-tuple-element.57.refs_0_, bf16[64,512]{1,0:T(8,128)(2,1)S(1)} %get-tuple-element.58.refs_1_, bf16[64,512]{1,0:T(8,128)(2,1)S(1)} %collective-permute-done.6.refs_2_, ...), custom_call_target="tpu_custom_call" | custom-call | flops 1000000 | bytes 1 | tf_op jit(solution)/shard_map/q_part/pallas_call | solution.py:41
  29.9 0.9 %q_part.3 = (bf16[128,512]{1,0:T(8,128)(2,1)S(1)}, f32[1,512]{1,0:T(1,128)S(1)}, f32[1,512]{1,0:T(1,128)S(1)}, f32[128,512]{1,0:T(8,128)S(1)}) custom-call(bf16[128,512]{1,0:T(8,128)(2,1)S(1)} %get-tuple-element.68.refs_0_, bf16[128,512]{1,0:T(8,128)(2,1)S(1)} %collective-permute-done.11.refs_1_, f32[1,4096]{1,0:T(1,128)S(1)} %get-tuple-element.52.refs_4_.refs_2_, ...), custom_call_target="tpu_custom_call" | custom-call | flops 1000000 | bytes 1 | tf_op jit(solution)/shard_map/q_part/pallas_call | solution.py:41
  30.8 0.7 %attend_more.2 = (f32[1,1024]{1,0:T(1,128)S(1)}, f32[1,1024]{1,0:T(1,128)S(1)}, f32[128,1024]{1,0:T(8,128)S(1)}) custom-call(bf16[128,512]{1,0:T(8,128)(2,1)S(1)} %get-tuple-element.67.qa_ref, bf16[128,512]{1,0:T(8,128)(2,1)S(1)} %get-tuple-element.71.qb_ref, bf16[128,256]{1,0:T(8,128)(2,1)S(1)} %collective-permute-done.13.kv_ref, ...), custom_call_target="tpu_custom_call" | custom-call | flops 400000000 | bytes 1 | tf_op jit(solution)/shard_map/attend_more/pallas_call | solution.py:41
  31.4 0.4 collective-permute-done.12.kv_ref
  31.9 0.7 %attend_more.3 = (bf16[256,512]{1,0:T(8,128)(2,1)S(1)}, bf16[128,512]{1,0:T(8,128)(2,1)S(1)}, bf16[128,512]{1,0:T(8,128)(2,1)S(1)}) custom-call(bf16[128,512]{1,0:T(8,128)(2,1)S(1)} %get-tuple-element.67.qa_ref, bf16[128,512]{1,0:T(8,128)(2,1)S(1)} %get-tuple-element.71.qb_ref, bf16[128,256]{1,0:T(8,128)(2,1)S(1)} %collective-permute-done.12.kv_ref, ...), custom_call_target="tpu_custom_call" | custom-call | flops 400000000 | bytes 1 | tf_op jit(solution)/shard_map/attend_more/pallas_call | solution.py:41
  32.6 3.4 %collective-permute-start.14 = (bf16[256,512]{1,0:T(8,128)(2,1)S(1)}, bf16[256,512]{1,0:T(8,128)(2,1)S(1)}, u32[]{:S(2)}, u32[]{:S(2)}) collective-permute-start(bf16[256,512]{1,0:T(8,128)(2,1)S(1)} %get-tuple-element.81.refs_0_), channel_id=1, source_target_pairs={{0,6},{1,7},{2,4},{3,5},{4,2},{5,3},{6,0},{7,1},{8,14},{9,15},{10,... | collective-permute-start | bytes 786440 | tf_op jit(solution)/shard_map/ppermute | solution.py:130
  36.1 0.5 collective-permute-start.20
  36.6 1.7 %collective-permute-start.22 = (bf16[128,512]{1,0:T(8,128)(2,1)S(1)}, bf16[128,512]{1,0:T(8,128)(2,1)S(1)}, u32[]{:S(2)}, u32[]{:S(2)}) collective-permute-start(bf16[128,512]{1,0:T(8,128)(2,1)S(1)} %get-tuple-element.83), channel_id=1, source_target_pairs={{0,2},{1,3},{2,0},{3,1},{4,6},{5,7},{6,4},{7,5},{8,10},{9,11},{10,... | collective-permute-start | bytes 393224 | tf_op jit(solution)/shard_map/ppermute | solution.py:132
  38.3 5.4 %collective-permute-done.14.refs_0_ = bf16[256,512]{1,0:T(8,128)(2,1)S(1)} collective-permute-done((bf16[256,512]{1,0:T(8,128)(2,1)S(1)}, bf16[256,512]{1,0:T(8,128)(2,1)S(1)}, u32[]{:S(2)}, u32[]{:S(2)}) %collective-permute-start.14) | collective-permute-done | bytes 262176 | tf_op jit(solution)/shard_map/ppermute | solution.py:130
  43.8 4.0 %collective-permute-start.15 = (bf16[128,512]{1,0:T(8,128)(2,1)S(1)}, bf16[128,512]{1,0:T(8,128)(2,1)S(1)}, u32[]{:S(2)}, u32[]{:S(2)}) collective-permute-start(bf16[128,512]{1,0:T(8,128)(2,1)S(1)} %get-tuple-element.94), channel_id=1, source_target_pairs={{0,2},{1,3},{2,0},{3,1},{4,6},{5,7},{6,4},{7,5},{8,10},{9,11},{10,... | collective-permute-start | bytes 393224 | tf_op jit(solution)/shard_map/ppermute | solution.py:134
  47.8 0.1 collective-permute-start.16
  47.9 0.1 collective-permute-done.22.refs_4_
  47.9 2.6 %out_own.1 = (bf16[128,512]{1,0:T(8,128)(2,1)S(1)}, bf16[128,512]{1,0:T(8,128)(2,1)S(1)}, f32[256,512]{1,0:T(8,128)S(1)}, bf16[4096,512]{1,0:T(8,128)(2,1)S(1)}, bf16[1024,512]{1,0:T(8,128)(2,1)S(1)}) custom-call(bf16[256,512]{1,0:T(8,128)(2,1)S(1)} %get-tuple-element.81.refs_0_, ...), custom_call_target="tpu_custom_call", output_to_operand_aliasing={{0}: (3, {}), {1}: (4, {})} | custom-call | flops 400000000 | bytes 1 | tf_op jit(solution)/shard_map/out_own/pallas_call | solution.py:41
  50.6 0.5 out_more.2
  51.0 0.2 collective-permute-start.24
  51.3 0.3 collective-permute-start.25
  51.6 0.5 collective-permute-done.15.a
  52.1 2.6 %collective-permute-done.16.b = bf16[128,512]{1,0:T(8,128)(2,1)S(1)} collective-permute-done((bf16[128,512]{1,0:T(8,128)(2,1)S(1)}, bf16[128,512]{1,0:T(8,128)(2,1)S(1)}, u32[]{:S(2)}, u32[]{:S(2)}) %collective-permute-start.16) | collective-permute-done | bytes 131104 | tf_op jit(solution)/shard_map/ppermute | solution.py:134
  54.7 0.5 out_more.3.total_ref
  55.2 0.9 %collective-permute-done.18.d = bf16[128,512]{1,0:T(8,128)(2,1)S(1)} collective-permute-done((bf16[128,512]{1,0:T(8,128)(2,1)S(1)}, bf16[128,512]{1,0:T(8,128)(2,1)S(1)}, u32[]{:S(2)}, u32[]{:S(2)}) %collective-permute-start.18) | collective-permute-done | bytes 131104 | tf_op jit(solution)/shard_map/ppermute | solution.py:138
  56.1 1.6 %out_last.1 = bf16[1024,512]{1,0:T(8,128)(2,1)} custom-call(bf16[128,512]{1,0:T(8,128)(2,1)S(1)} %collective-permute-done.15.a, bf16[128,512]{1,0:T(8,128)(2,1)S(1)} %collective-permute-done.16.b, bf16[128,512]{1,0:T(8,128)(2,1)S(1)} %collective-permute-done.17.c, bf16[128,512]{1,0:T(8,128)(2,1)S(1)} %collective-permute-done.18.d, ...), custom_call_target="tpu_custom_call" | custom-call | flops 400000000 | bytes 1 | tf_op jit(solution)/shard_map/out_last/pallas_call | solution.py:41
  (25 shorter events, 0.1 us)
Async XLA Ops:
  0.0 17.0 %copy-start = (f32[128]{0:T(128)S(1)}, f32[128]{0:T(128)}, u32[]{:S(2)}) copy-start(f32[128]{0:T(128)} %constant.9.clone.1) | copy-start | bytes 1540
  1.6 5.3 %collective-permute-start.4 = (bf16[256,512]{1,0:T(8,128)(2,1)S(1)}, bf16[256,512]{1,0:T(8,128)(2,1)S(1)}, u32[]{:S(2)}, u32[]{:S(2)}) collective-permute-start(bf16[256,512]{1,0:T(8,128)(2,1)S(1)} %get-tuple-element.51.x_ref), channel_id=1, source_target_pairs={{0,1},{1,0},{2,3},{3,2},{4,5},{5,4},{6,7},{7,6},{8,9},{9,8},{10,11... | collective-permute-start | bytes 786440 | tf_op jit(solution)/shard_map/ppermute | solution.py:146
  2.2 8.9 %collective-permute-start = (bf16[128,512]{1,0:T(8,128)(2,1)S(1)}, bf16[128,512]{1,0:T(8,128)(2,1)S(1)}, u32[]{:S(2)}, u32[]{:S(2)}) collective-permute-start(bf16[128,512]{1,0:T(8,128)(2,1)S(1)} %get-tuple-element.49), channel_id=1, source_target_pairs={{0,6},{1,7},{2,4},{3,5},{4,2},{5,3},{6,0},{7,1},{8,14},{9,15},{10,... | collective-permute-start | bytes 393224 | tf_op jit(solution)/shard_map/ppermute | solution.py:145
  6.8 9.9 %collective-permute-start.1 = (bf16[128,512]{1,0:T(8,128)(2,1)S(1)}, bf16[128,512]{1,0:T(8,128)(2,1)S(1)}, u32[]{:S(2)}, u32[]{:S(2)}) collective-permute-start(bf16[128,512]{1,0:T(8,128)(2,1)S(1)} %get-tuple-element.50), channel_id=1, source_target_pairs={{0,6},{1,7},{2,4},{3,5},{4,2},{5,3},{6,0},{7,1},{8,14},{9,15},{10,... | collective-permute-start | bytes 393224 | tf_op jit(solution)/shard_map/ppermute | solution.py:145
  10.3 9.7 %collective-permute-start.8 = (bf16[256,512]{1,0:T(8,128)(2,1)S(1)}, bf16[256,512]{1,0:T(8,128)(2,1)S(1)}, u32[]{:S(2)}, u32[]{:S(2)}) collective-permute-start(bf16[256,512]{1,0:T(8,128)(2,1)S(1)} %get-tuple-element.59), channel_id=1, source_target_pairs={{0,2},{1,3},{2,0},{3,1},{4,6},{5,7},{6,4},{7,5},{8,10},{9,11},{10,... | collective-permute-start | bytes 786440 | tf_op jit(solution)/shard_map/ppermute | solution.py:146
  11.0 8.9 %collective-permute-start.2 = (bf16[128,512]{1,0:T(8,128)(2,1)S(1)}, bf16[128,512]{1,0:T(8,128)(2,1)S(1)}, u32[]{:S(2)}, u32[]{:S(2)}) collective-permute-start(bf16[128,512]{1,0:T(8,128)(2,1)S(1)} %collective-permute-done.refs_0_), channel_id=1, source_target_pairs={{0,1},{1,0},{2,3},{3,2},{4,5},{5,4},{6,7},{7,6},{8,9},{9,8},{10,11... | collective-permute-start | bytes 393224 | tf_op jit(solution)/shard_map/ppermute | solution.py:148
  11.1 11.7 %collective-permute-start.5 = (bf16[128,512]{1,0:T(8,128)(2,1)S(1)}, bf16[128,512]{1,0:T(8,128)(2,1)S(1)}, u32[]{:S(2)}, u32[]{:S(2)}) collective-permute-start(bf16[128,512]{1,0:T(8,128)(2,1)S(1)} %collective-permute-done.refs_0_), channel_id=1, source_target_pairs={{0,2},{1,3},{2,0},{3,1},{4,6},{5,7},{6,4},{7,5},{8,10},{9,11},{10,... | collective-permute-start | bytes 393224 | tf_op jit(solution)/shard_map/ppermute | solution.py:147
  16.7 3.2 %collective-permute-start.3 = (bf16[128,512]{1,0:T(8,128)(2,1)S(1)}, bf16[128,512]{1,0:T(8,128)(2,1)S(1)}, u32[]{:S(2)}, u32[]{:S(2)}) collective-permute-start(bf16[128,512]{1,0:T(8,128)(2,1)S(1)} %collective-permute-done.1.refs_1_), channel_id=1, source_target_pairs={{0,1},{1,0},{2,3},{3,2},{4,5},{5,4},{6,7},{7,6},{8,9},{9,8},{10,11... | collective-permute-start | bytes 393224 | tf_op jit(solution)/shard_map/ppermute | solution.py:148
  17.5 8.1 %collective-permute-start.10 = (bf16[128,512]{1,0:T(8,128)(2,1)S(1)}, bf16[128,512]{1,0:T(8,128)(2,1)S(1)}, u32[]{:S(2)}, u32[]{:S(2)}) collective-permute-start(bf16[128,512]{1,0:T(8,128)(2,1)S(1)} %collective-permute-done.1.refs_1_), channel_id=1, source_target_pairs={{0,2},{1,3},{2,0},{3,1},{4,6},{5,7},{6,4},{7,5},{8,10},{9,11},{10,... | collective-permute-start | bytes 393224 | tf_op jit(solution)/shard_map/ppermute | solution.py:147
  20.0 4.1 %collective-permute-start.9 = (bf16[256,512]{1,0:T(8,128)(2,1)S(1)}, bf16[256,512]{1,0:T(8,128)(2,1)S(1)}, u32[]{:S(2)}, u32[]{:S(2)}) collective-permute-start(bf16[256,512]{1,0:T(8,128)(2,1)S(1)} %collective-permute-done.8.refs_0_), channel_id=1, source_target_pairs={{0,1},{1,0},{2,3},{3,2},{4,5},{5,4},{6,7},{7,6},{8,9},{9,8},{10,11... | collective-permute-start | bytes 786440 | tf_op jit(solution)/shard_map/ppermute | solution.py:149
  23.4 1.3 %collective-permute-start.6 = (bf16[64,512]{1,0:T(8,128)(2,1)S(1)}, bf16[64,512]{1,0:T(8,128)(2,1)S(1)}, u32[]{:S(2)}, u32[]{:S(2)}) collective-permute-start(bf16[64,512]{1,0:T(8,128)(2,1)S(1)} %get-tuple-element.57.refs_0_), channel_id=1, source_target_pairs={{0,1},{1,0},{2,3},{3,2},{4,5},{5,4},{6,7},{7,6},{8,9},{9,8},{10,11... | collective-permute-start | bytes 196616 | tf_op jit(solution)/shard_map/ppermute | solution.py:150
  23.5 1.4 %collective-permute-start.7 = (bf16[64,512]{1,0:T(8,128)(2,1)S(1)}, bf16[64,512]{1,0:T(8,128)(2,1)S(1)}, u32[]{:S(2)}, u32[]{:S(2)}) collective-permute-start(bf16[64,512]{1,0:T(8,128)(2,1)S(1)} %get-tuple-element.58.refs_1_), channel_id=1, source_target_pairs={{0,1},{1,0},{2,3},{3,2},{4,5},{5,4},{6,7},{7,6},{8,9},{9,8},{10,11... | collective-permute-start | bytes 196616 | tf_op jit(solution)/shard_map/ppermute | solution.py:150
  25.5 1.7 %collective-permute-start.11 = (bf16[128,512]{1,0:T(8,128)(2,1)S(1)}, bf16[128,512]{1,0:T(8,128)(2,1)S(1)}, u32[]{:S(2)}, u32[]{:S(2)}) collective-permute-start(bf16[128,512]{1,0:T(8,128)(2,1)S(1)} %get-tuple-element.68.refs_0_), channel_id=1, source_target_pairs={{0,1},{1,0},{2,3},{3,2},{4,5},{5,4},{6,7},{7,6},{8,9},{9,8},{10,11... | collective-permute-start | bytes 393224 | tf_op jit(solution)/shard_map/ppermute | solution.py:563
  25.7 5.1 %collective-permute-start.13 = (bf16[128,256]{1,0:T(8,128)(2,1)S(1)}, bf16[128,256]{1,0:T(8,128)(2,1)S(1)}, u32[]{:S(2)}, u32[]{:S(2)}) collective-permute-start(bf16[128,256]{1,0:T(8,128)(2,1)S(1)} %get-tuple-element.66.refs_11_.refs_9_), channel_id=1, source_target_pairs={{0,8},{8,0},{1,9},{9,1},{2,10},{10,2},{3,11},{11,3},{4,12},{12,4},... | collective-permute-start | bytes 196616 | tf_op jit(solution)/shard_map/ppermute | solution.py:568
  27.5 4.3 %collective-permute-start.12 = (bf16[128,256]{1,0:T(8,128)(2,1)S(1)}, bf16[128,256]{1,0:T(8,128)(2,1)S(1)}, u32[]{:S(2)}, u32[]{:S(2)}) collective-permute-start(bf16[128,256]{1,0:T(8,128)(2,1)S(1)} %get-tuple-element.70.refs_10_), channel_id=1, source_target_pairs={{0,8},{8,0},{1,9},{9,1},{2,10},{10,2},{3,11},{11,3},{4,12},{12,4},... | collective-permute-start | bytes 196616 | tf_op jit(solution)/shard_map/ppermute | solution.py:568
  32.6 11.1 %collective-permute-start.14 = (bf16[256,512]{1,0:T(8,128)(2,1)S(1)}, bf16[256,512]{1,0:T(8,128)(2,1)S(1)}, u32[]{:S(2)}, u32[]{:S(2)}) collective-permute-start(bf16[256,512]{1,0:T(8,128)(2,1)S(1)} %get-tuple-element.81.refs_0_), channel_id=1, source_target_pairs={{0,6},{1,7},{2,4},{3,5},{4,2},{5,3},{6,0},{7,1},{8,14},{9,15},{10,... | collective-permute-start | bytes 786440 | tf_op jit(solution)/shard_map/ppermute | solution.py:130
  36.1 7.7 %collective-permute-start.19 = (bf16[128,512]{1,0:T(8,128)(2,1)S(1)}, bf16[128,512]{1,0:T(8,128)(2,1)S(1)}, u32[]{:S(2)}, u32[]{:S(2)}) collective-permute-start(bf16[128,512]{1,0:T(8,128)(2,1)S(1)} %get-tuple-element.82), channel_id=1, source_target_pairs={{0,1},{1,0},{2,3},{3,2},{4,5},{5,4},{6,7},{7,6},{8,9},{9,8},{10,11... | collective-permute-start | bytes 393224 | tf_op jit(solution)/shard_map/ppermute | solution.py:131
  36.1 11.8 %collective-permute-start.21 = (bf16[128,512]{1,0:T(8,128)(2,1)S(1)}, bf16[128,512]{1,0:T(8,128)(2,1)S(1)}, u32[]{:S(2)}, u32[]{:S(2)}) collective-permute-start(bf16[128,512]{1,0:T(8,128)(2,1)S(1)} %get-tuple-element.82), channel_id=1, source_target_pairs={{0,2},{1,3},{2,0},{3,1},{4,6},{5,7},{6,4},{7,5},{8,10},{9,11},{10,... | collective-permute-start | bytes 393224 | tf_op jit(solution)/shard_map/ppermute | solution.py:132
  36.1 11.7 %collective-permute-start.20 = (bf16[128,512]{1,0:T(8,128)(2,1)S(1)}, bf16[128,512]{1,0:T(8,128)(2,1)S(1)}, u32[]{:S(2)}, u32[]{:S(2)}) collective-permute-start(bf16[128,512]{1,0:T(8,128)(2,1)S(1)} %get-tuple-element.83), channel_id=1, source_target_pairs={{0,1},{1,0},{2,3},{3,2},{4,5},{5,4},{6,7},{7,6},{8,9},{9,8},{10,11... | collective-permute-start | bytes 393224 | tf_op jit(solution)/shard_map/ppermute | solution.py:131
  36.6 11.3 %collective-permute-start.22 = (bf16[128,512]{1,0:T(8,128)(2,1)S(1)}, bf16[128,512]{1,0:T(8,128)(2,1)S(1)}, u32[]{:S(2)}, u32[]{:S(2)}) collective-permute-start(bf16[128,512]{1,0:T(8,128)(2,1)S(1)} %get-tuple-element.83), channel_id=1, source_target_pairs={{0,2},{1,3},{2,0},{3,1},{4,6},{5,7},{6,4},{7,5},{8,10},{9,11},{10,... | collective-permute-start | bytes 393224 | tf_op jit(solution)/shard_map/ppermute | solution.py:132
  43.7 6.8 %collective-permute-start.23 = (bf16[256,512]{1,0:T(8,128)(2,1)S(1)}, bf16[256,512]{1,0:T(8,128)(2,1)S(1)}, u32[]{:S(2)}, u32[]{:S(2)}) collective-permute-start(bf16[256,512]{1,0:T(8,128)(2,1)S(1)} %collective-permute-done.14.refs_0_), channel_id=1, source_target_pairs={{0,1},{1,0},{2,3},{3,2},{4,5},{5,4},{6,7},{7,6},{8,9},{9,8},{10,11... | collective-permute-start | bytes 786440 | tf_op jit(solution)/shard_map/ppermute | solution.py:136
  43.8 8.3 %collective-permute-start.15 = (bf16[128,512]{1,0:T(8,128)(2,1)S(1)}, bf16[128,512]{1,0:T(8,128)(2,1)S(1)}, u32[]{:S(2)}, u32[]{:S(2)}) collective-permute-start(bf16[128,512]{1,0:T(8,128)(2,1)S(1)} %get-tuple-element.94), channel_id=1, source_target_pairs={{0,2},{1,3},{2,0},{3,1},{4,6},{5,7},{6,4},{7,5},{8,10},{9,11},{10,... | collective-permute-start | bytes 393224 | tf_op jit(solution)/shard_map/ppermute | solution.py:134
  47.8 7.0 %collective-permute-start.16 = (bf16[128,512]{1,0:T(8,128)(2,1)S(1)}, bf16[128,512]{1,0:T(8,128)(2,1)S(1)}, u32[]{:S(2)}, u32[]{:S(2)}) collective-permute-start(bf16[128,512]{1,0:T(8,128)(2,1)S(1)} %get-tuple-element.93), channel_id=1, source_target_pairs={{0,2},{1,3},{2,0},{3,1},{4,6},{5,7},{6,4},{7,5},{8,10},{9,11},{10,... | collective-permute-start | bytes 393224 | tf_op jit(solution)/shard_map/ppermute | solution.py:134
  51.0 3.7 %collective-permute-start.24 = (bf16[128,512]{1,0:T(8,128)(2,1)S(1)}, bf16[128,512]{1,0:T(8,128)(2,1)S(1)}, u32[]{:S(2)}, u32[]{:S(2)}) collective-permute-start(bf16[128,512]{1,0:T(8,128)(2,1)S(1)} %get-tuple-element.88.refs_0_), channel_id=1, source_target_pairs={{0,1},{1,0},{2,3},{3,2},{4,5},{5,4},{6,7},{7,6},{8,9},{9,8},{10,11... | collective-permute-start | bytes 393224 | tf_op jit(solution)/shard_map/ppermute | solution.py:137
  51.3 3.5 %collective-permute-start.25 = (bf16[128,512]{1,0:T(8,128)(2,1)S(1)}, bf16[128,512]{1,0:T(8,128)(2,1)S(1)}, u32[]{:S(2)}, u32[]{:S(2)}) collective-permute-start(bf16[128,512]{1,0:T(8,128)(2,1)S(1)} %get-tuple-element.89.refs_1_), channel_id=1, source_target_pairs={{0,1},{1,0},{2,3},{3,2},{4,5},{5,4},{6,7},{7,6},{8,9},{9,8},{10,11... | collective-permute-start | bytes 393224 | tf_op jit(solution)/shard_map/ppermute | solution.py:137
  52.1 3.1 %collective-permute-start.17 = (bf16[128,512]{1,0:T(8,128)(2,1)S(1)}, bf16[128,512]{1,0:T(8,128)(2,1)S(1)}, u32[]{:S(2)}, u32[]{:S(2)}) collective-permute-start(bf16[128,512]{1,0:T(8,128)(2,1)S(1)} %collective-permute-done.15.a), channel_id=1, source_target_pairs={{0,1},{1,0},{2,3},{3,2},{4,5},{5,4},{6,7},{7,6},{8,9},{9,8},{10,11... | collective-permute-start | bytes 393224 | tf_op jit(solution)/shard_map/ppermute | solution.py:138
  54.7 1.3 %collective-permute-start.18 = (bf16[128,512]{1,0:T(8,128)(2,1)S(1)}, bf16[128,512]{1,0:T(8,128)(2,1)S(1)}, u32[]{:S(2)}, u32[]{:S(2)}) collective-permute-start(bf16[128,512]{1,0:T(8,128)(2,1)S(1)} %collective-permute-done.16.b), channel_id=1, source_target_pairs={{0,1},{1,0},{2,3},{3,2},{4,5},{5,4},{6,7},{7,6},{8,9},{9,8},{10,11... | collective-permute-start | bytes 393224 | tf_op jit(solution)/shard_map/ppermute | solution.py:138

commit v10 on v9

--- a/solution.py
+++ b/solution.py
@@ -134,8 +134,8 @@
     last = near(far[:half]), near(far[half:])
     beside = use_own((full,), mates, beside)
     beside = use_far((far,), (twin(far),), beside)
-    use_beside(beside, (twin(beside[0]), twin(beside[1])))
-    return last, (twin(last[0]), twin(last[1]))
+    use_beside(beside, (twin(beside[0]), twin(beside[1])), last, twin(last[0]))
+    return twin(last[1])
 
 
 def spread_halves(size, full, first, second, use_own, use_far, use_beside):
@@ -480,11 +480,34 @@
     )
 
 
-def out_last_kernel(a, b, c, d, w_ref, total_ref, sa_ref, sb_ref, hot_ref, hid_ref, out, out_ref, sems):
-    z, core = place()
-    projected = total_ref[...] + out_term(joined((a, b)), joined((c, d)), z ^ 2, core, w_ref)
-    gate = jnp.concatenate([sa_ref[:, 128:129], sb_ref[:, 128:129]], axis=0)
-    update = (gate * projected).astype(BF16)
+def out_beside_kernel(a, b, c, d, last_a, last_b, last_twin, w_ref, total_in, total_out):
+    z, core = place()
+    half = last_a.shape[0]
+    last, twin = (rows for _, rows in halves(last_a, last_b, z ^ 2, core))
+    total = total_in[...] + out_term(joined((a, b)), joined((c, d)), z ^ 1, core, w_ref)
+    total = total + jnp.dot(joined((last_a, last_b)), w_ref[last, :], preferred_element_type=F32)
+    total_out[:half] = total[:half] + jnp.dot(last_twin[...], w_ref[twin, :], preferred_element_type=F32)
+    total_out[half:] = total[half:]
+
+
+def out_beside(mine, twin, last, last_twin, w, total, flops):
+    return call(
+        out_beside_kernel,
+        "out_beside",
+        (*mine, *twin, *last, last_twin, w, total),
+        [arr(total.shape, F32)],
+        rides={8: 0},
+        flops=flops,
+    )[0]
+
+
+def out_last_kernel(twin_ref, w_ref, total_ref, sa_ref, sb_ref, hot_ref, hid_ref, out, out_ref, sems):
+    z, core = place()
+    half, width = twin_ref.shape
+    rows = pl.ds(pl.multiple_of((2 * (z ^ 2) + 1 - core) * width, width), width)
+    top = sa_ref[:, 128:129] * total_ref[:half]
+    rest = total_ref[half:] + jnp.dot(twin_ref[...], w_ref[rows, :], preferred_element_type=F32)
+    update = jnp.concatenate([top.astype(BF16), (sb_ref[:, 128:129] * rest).astype(BF16)], axis=0)
     block = 256
     copies = []
     for i in range(hid_ref.shape[0] // block):
@@ -495,11 +518,11 @@
     settle(copies)
 
 
-def out_last(pair, w, total, stats, hot, hidden):
+def out_last(twin, w, total, stats, hot, hidden):
     return call(
         out_last_kernel,
         "out_last",
-        (*pair[0], *pair[1], w, total, *stats, hot, hidden),
+        (twin, w, total, *stats, hot, hidden),
         [arr(hidden.shape, BF16)],
         scratch=[pltpu.VMEM(hidden.shape, BF16), pltpu.SemaphoreType.DMA((hidden.shape[0] // 256,))],
         out_hbm=True,
@@ -587,11 +610,11 @@
         held["total"], *rides = out_more(mine, twin, held["w"], held["total"], rides, lambda z: 3 - z, PART_COST)
         return rides
 
-    def beside_out(mine, twin):
-        (held["total"],) = out_more(mine, twin, held["w"], held["total"], (), lambda z: z ^ 1, PART_COST)
-
-    pair = spread(size, *carry, own_out, far_out, beside_out)
-    return out_last(pair, held["w"], held["total"], stats, held["hot"], held["hidden"])
+    def beside_out(mine, twin, last, last_twin):
+        held["total"] = out_beside(mine, twin, last, last_twin, held["w"], held["total"], PART_COST)
+
+    twin = spread(size, *carry, own_out, far_out, beside_out)
+    return out_last(twin, held["w"], held["total"], stats, held["hot"], held["hidden"])
 
 
 def solution(mesh):

time: 58 us -> 57.8 us (level)
  no operation moved by 1% of the time
where the time goes in v10:
time: 57.8 us; the launch traced here: 57.5 us
  starting transfers between devices  27.4 us (47%)
  Pallas kernels  15.6 us (27%)
  waiting for transfers between devices  13.8 us (24%)
    pallas_call x15, Pallas kernels, call(): pl.pallas_call(kernel, out_shape=out_shape, in_specs=[HBM if far else VME...  15.6 us
    ppermute x2, starting transfers between devices, spread_halves(): last_a, last_b = (near(far[0]), near(far[1]))  7.88 us
    ppermute x1, waiting for transfers between devices, spread(): far = cross(full)  5.42 us
    ppermute x2, starting transfers between devices, spread_halves(): far = (cross(first), cross(second))  4.78 us
    ppermute x2, starting transfers between devices, spread(): last = (near(far[:half]), near(far[half:]))  4.08 us
    ppermute x1, starting transfers between devices, spread(): far = cross(full)  3.43 us
    ppermute x2, waiting for transfers between devices, spread(): last = (near(far[:half]), near(far[half:]))  3.07 us
    ppermute x2, waiting for transfers between devices, spread_halves(): last_a, last_b = (near(far[0]), near(far[1]))  3.04 us
  transfers between devices with their start and end apart: 26, of which 12 were waited for; matrix products, arithmetic and copies ran while one was open for 1% of the time, Pallas kernels for 20%

profile of v10, /device:TPU:0, one launch (start us, length us, event | category | flops | bytes accessed | tf_op | source)
XLA Modules:
  0.0 57.5 jit_solution(8424028574786981257)
XLA Ops:
  0.0 1.6 %pick.1 = (bf16[256,512]{1,0:T(8,128)(2,1)S(1)}, bf16[128,512]{1,0:T(8,128)(2,1)S(1)}, bf16[128,512]{1,0:T(8,128)(2,1)S(1)}, s32[256,128]{1,0:T(8,128)S(1)}) custom-call(s32[2,256]{1,0:T(2,128)} %pos.1, bf16[1024,512]{1,0:T(8,128)(2,1)} %refs_6_.1), custom_call_target="tpu_custom_call" | custom-call | flops 400000000 | bytes 1 | tf_op jit(solution)/shard_map/pick/pallas_call | solution.py:41
  1.6 0.5 collective-permute-start.4
  2.2 4.7 %collective-permute-start = (bf16[128,512]{1,0:T(8,128)(2,1)S(1)}, bf16[128,512]{1,0:T(8,128)(2,1)S(1)}, u32[]{:S(2)}, u32[]{:S(2)}) collective-permute-start(bf16[128,512]{1,0:T(8,128)(2,1)S(1)} %get-tuple-element.49), channel_id=1, source_target_pairs={{0,6},{1,7},{2,4},{3,5},{4,2},{5,3},{6,0},{7,1},{8,14},{9,15},{10,... | collective-permute-start | bytes 393224 | tf_op jit(solution)/shard_map/ppermute | solution.py:145
  6.8 0.1 collective-permute-start.1
  7.0 0.0 collective-permute-done.4.twin_ref
  7.0 3.3 %own_part.1 = (bf16[256,512]{1,0:T(8,128)(2,1)S(1)}, f32[256,1024]{1,0:T(8,128)S(1)}, f32[1,4096]{1,0:T(1,128)S(1)}, f32[1,4096]{1,0:T(1,128)S(1)}, bf16[4096,76...) custom-call(bf16[256,512]{1,0:T(8,128)(2,1)S(1)} %get-tuple-element., ...), custom_call_target="tpu_custom_call", output_to_operand_aliasing={{0}: (0, {})} | custom-call | flops 1500000000 | bytes 1 | tf_op jit(solution)/shard_map/own_part/pallas_call | solution.py:41
  10.3 0.1 collective-permute-start.8
  10.4 0.1 pad_maximum_fusion
  10.5 0.6 %collective-permute-done.refs_0_ = bf16[128,512]{1,0:T(8,128)(2,1)S(1)} collective-permute-done((bf16[128,512]{1,0:T(8,128)(2,1)S(1)}, bf16[128,512]{1,0:T(8,128)(2,1)S(1)}, u32[]{:S(2)}, u32[]{:S(2)}) %collective-permute-start) | collective-permute-done | bytes 131104 | tf_op jit(solution)/shard_map/ppermute | solution.py:145
  11.1 5.7 %collective-permute-start.5 = (bf16[128,512]{1,0:T(8,128)(2,1)S(1)}, bf16[128,512]{1,0:T(8,128)(2,1)S(1)}, u32[]{:S(2)}, u32[]{:S(2)}) collective-permute-start(bf16[128,512]{1,0:T(8,128)(2,1)S(1)} %collective-permute-done.refs_0_), channel_id=1, source_target_pairs={{0,2},{1,3},{2,0},{3,1},{4,6},{5,7},{6,4},{7,5},{8,10},{9,11},{10,... | collective-permute-start | bytes 393224 | tf_op jit(solution)/shard_map/ppermute | solution.py:147
  16.7 0.2 collective-permute-start.3
  17.0 0.5 sine_multiply_fusion
  17.5 2.2 %collective-permute-start.10 = (bf16[128,512]{1,0:T(8,128)(2,1)S(1)}, bf16[128,512]{1,0:T(8,128)(2,1)S(1)}, u32[]{:S(2)}, u32[]{:S(2)}) collective-permute-start(bf16[128,512]{1,0:T(8,128)(2,1)S(1)} %collective-permute-done.1.refs_1_), channel_id=1, source_target_pairs={{0,2},{1,3},{2,0},{3,1},{4,6},{5,7},{6,4},{7,5},{8,10},{9,11},{10,... | collective-permute-start | bytes 393224 | tf_op jit(solution)/shard_map/ppermute | solution.py:147
  19.6 0.3 collective-permute-done.8.refs_0_
  20.0 2.8 %collective-permute-done.5.refs_10_ = bf16[128,512]{1,0:T(8,128)(2,1)S(1)} collective-permute-done((bf16[128,512]{1,0:T(8,128)(2,1)S(1)}, bf16[128,512]{1,0:T(8,128)(2,1)S(1)}, u32[]{:S(2)}, u32[]{:S(2)}) %collective-permute-start.5) | collective-permute-done | bytes 131104 | tf_op jit(solution)/shard_map/ppermute | solution.py:147
  22.8 0.7 %more_part.2 = (f32[256,1024]{1,0:T(8,128)S(1)}, f32[256,128]{1,0:T(8,128)S(1)}, f32[256,128]{1,0:T(8,128)S(1)}, bf16[64,512]{1,0:T(8,128)(2,1)S(1)}, bf16[64,512]{1,0:T(8,128)(2,1)S(1)}) custom-call(bf16[128,512]{1,0:T(8,128)(2,1)S(1)} %collective-permute-done.refs_0_, ...), custom_call_target="tpu_custom_call", output_to_operand_aliasing={{0}: (7, {}), {1}: (8, {}), {2}: (9, {})} | custom-call | flops 3000000000 | bytes 1 | tf_op jit(solution)/shard_map/more_part/pallas_call | solution.py:41
  23.4 0.1 collective-permute-start.6
  23.5 0.5 collective-permute-start.7
  24.0 0.7 %more_part.3.refs_7_.refs_6_.refs_5_.refs_4_ = f32[256,1024]{1,0:T(8,128)S(1)} custom-call(bf16[256,512]{1,0:T(8,128)(2,1)S(1)} %collective-permute-done.8.refs_0_, bf16[256,512]{1,0:T(8,128)(2,1)S(1)} %collective-permute-done.9.refs_1_, f32[1,4096]{1,0:T(1,128)S(1)} %get-tuple-element.52.refs_4_.refs_2_, ...), custom_call_target="tpu_custom_call", output_to_operand_aliasing={{}: (5, {})} | custom-call | flops 1000000 | bytes 1 | tf_op jit(solution)/shard_map/more_part/pallas_call | solution.py:41
  24.7 0.1 collective-permute-done.6.refs_2_
  24.8 0.2 collective-permute-done.7.refs_3_
  24.9 0.3 kv_last.2
  25.3 0.2 collective-permute-done.10.__1_
  25.5 0.2 collective-permute-start.11
  25.7 1.5 %collective-permute-start.13 = (bf16[128,256]{1,0:T(8,128)(2,1)S(1)}, bf16[128,256]{1,0:T(8,128)(2,1)S(1)}, u32[]{:S(2)}, u32[]{:S(2)}) collective-permute-start(bf16[128,256]{1,0:T(8,128)(2,1)S(1)} %get-tuple-element.66.refs_11_.refs_9_), channel_id=1, source_target_pairs={{0,8},{8,0},{1,9},{9,1},{2,10},{10,2},{3,11},{11,3},{4,12},{12,4},... | collective-permute-start | bytes 196616 | tf_op jit(solution)/shard_map/ppermute | solution.py:591
  27.2 0.3 kv_last.3
  27.5 1.2 %collective-permute-start.12 = (bf16[128,256]{1,0:T(8,128)(2,1)S(1)}, bf16[128,256]{1,0:T(8,128)(2,1)S(1)}, u32[]{:S(2)}, u32[]{:S(2)}) collective-permute-start(bf16[128,256]{1,0:T(8,128)(2,1)S(1)} %get-tuple-element.70.refs_10_), channel_id=1, source_target_pairs={{0,8},{8,0},{1,9},{9,1},{2,10},{10,2},{3,11},{11,3},{4,12},{12,4},... | collective-permute-start | bytes 196616 | tf_op jit(solution)/shard_map/ppermute | solution.py:591
  28.8 1.1 %q_part.2 = (bf16[128,512]{1,0:T(8,128)(2,1)S(1)}, f32[1,512]{1,0:T(1,128)S(1)}, f32[1,512]{1,0:T(1,128)S(1)}, f32[128,512]{1,0:T(8,128)S(1)}) custom-call(bf16[64,512]{1,0:T(8,128)(2,1)S(1)} %get-tuple-element.57.refs_0_, bf16[64,512]{1,0:T(8,128)(2,1)S(1)} %get-tuple-element.58.refs_1_, bf16[64,512]{1,0:T(8,128)(2,1)S(1)} %collective-permute-done.6.refs_2_, ...), custom_call_target="tpu_custom_call" | custom-call | flops 1000000 | bytes 1 | tf_op jit(solution)/shard_map/q_part/pallas_call | solution.py:41
  29.9 0.9 %q_part.3 = (bf16[128,512]{1,0:T(8,128)(2,1)S(1)}, f32[1,512]{1,0:T(1,128)S(1)}, f32[1,512]{1,0:T(1,128)S(1)}, f32[128,512]{1,0:T(8,128)S(1)}) custom-call(bf16[128,512]{1,0:T(8,128)(2,1)S(1)} %get-tuple-element.68.refs_0_, bf16[128,512]{1,0:T(8,128)(2,1)S(1)} %collective-permute-done.11.refs_1_, f32[1,4096]{1,0:T(1,128)S(1)} %get-tuple-element.52.refs_4_.refs_2_, ...), custom_call_target="tpu_custom_call" | custom-call | flops 1000000 | bytes 1 | tf_op jit(solution)/shard_map/q_part/pallas_call | solution.py:41
  30.8 0.7 %attend_more.2 = (f32[1,1024]{1,0:T(1,128)S(1)}, f32[1,1024]{1,0:T(1,128)S(1)}, f32[128,1024]{1,0:T(8,128)S(1)}) custom-call(bf16[128,512]{1,0:T(8,128)(2,1)S(1)} %get-tuple-element.67.qa_ref, bf16[128,512]{1,0:T(8,128)(2,1)S(1)} %get-tuple-element.71.qb_ref, bf16[128,256]{1,0:T(8,128)(2,1)S(1)} %collective-permute-done.13.kv_ref, ...), custom_call_target="tpu_custom_call" | custom-call | flops 400000000 | bytes 1 | tf_op jit(solution)/shard_map/attend_more/pallas_call | solution.py:41
  31.4 0.4 collective-permute-done.12.kv_ref
  31.9 0.7 %attend_more.3 = (bf16[256,512]{1,0:T(8,128)(2,1)S(1)}, bf16[128,512]{1,0:T(8,128)(2,1)S(1)}, bf16[128,512]{1,0:T(8,128)(2,1)S(1)}) custom-call(bf16[128,512]{1,0:T(8,128)(2,1)S(1)} %get-tuple-element.67.qa_ref, bf16[128,512]{1,0:T(8,128)(2,1)S(1)} %get-tuple-element.71.qb_ref, bf16[128,256]{1,0:T(8,128)(2,1)S(1)} %collective-permute-done.12.kv_ref, ...), custom_call_target="tpu_custom_call" | custom-call | flops 400000000 | bytes 1 | tf_op jit(solution)/shard_map/attend_more/pallas_call | solution.py:41
  32.6 3.4 %collective-permute-start.14 = (bf16[256,512]{1,0:T(8,128)(2,1)S(1)}, bf16[256,512]{1,0:T(8,128)(2,1)S(1)}, u32[]{:S(2)}, u32[]{:S(2)}) collective-permute-start(bf16[256,512]{1,0:T(8,128)(2,1)S(1)} %get-tuple-element.81.refs_0_), channel_id=1, source_target_pairs={{0,6},{1,7},{2,4},{3,5},{4,2},{5,3},{6,0},{7,1},{8,14},{9,15},{10,... | collective-permute-start | bytes 786440 | tf_op jit(solution)/shard_map/ppermute | solution.py:130
  36.1 0.5 collective-permute-start.18
  36.6 1.7 %collective-permute-start.20 = (bf16[128,512]{1,0:T(8,128)(2,1)S(1)}, bf16[128,512]{1,0:T(8,128)(2,1)S(1)}, u32[]{:S(2)}, u32[]{:S(2)}) collective-permute-start(bf16[128,512]{1,0:T(8,128)(2,1)S(1)} %get-tuple-element.83), channel_id=1, source_target_pairs={{0,2},{1,3},{2,0},{3,1},{4,6},{5,7},{6,4},{7,5},{8,10},{9,11},{10,... | collective-permute-start | bytes 393224 | tf_op jit(solution)/shard_map/ppermute | solution.py:132
  38.3 5.4 %collective-permute-done.14.refs_0_ = bf16[256,512]{1,0:T(8,128)(2,1)S(1)} collective-permute-done((bf16[256,512]{1,0:T(8,128)(2,1)S(1)}, bf16[256,512]{1,0:T(8,128)(2,1)S(1)}, u32[]{:S(2)}, u32[]{:S(2)}) %collective-permute-start.14) | collective-permute-done | bytes 262176 | tf_op jit(solution)/shard_map/ppermute | solution.py:130
  43.8 4.0 %collective-permute-start.24 = (bf16[128,512]{1,0:T(8,128)(2,1)S(1)}, bf16[128,512]{1,0:T(8,128)(2,1)S(1)}, u32[]{:S(2)}, u32[]{:S(2)}) collective-permute-start(bf16[128,512]{1,0:T(8,128)(2,1)S(1)} %get-tuple-element.93), channel_id=1, source_target_pairs={{0,2},{1,3},{2,0},{3,1},{4,6},{5,7},{6,4},{7,5},{8,10},{9,11},{10,... | collective-permute-start | bytes 393224 | tf_op jit(solution)/shard_map/ppermute | solution.py:134
  47.8 0.1 collective-permute-start.15
  47.9 0.1 collective-permute-done.20.refs_4_
  47.9 2.6 %out_own.1 = (bf16[128,512]{1,0:T(8,128)(2,1)S(1)}, bf16[128,512]{1,0:T(8,128)(2,1)S(1)}, f32[256,512]{1,0:T(8,128)S(1)}, bf16[4096,512]{1,0:T(8,128)(2,1)S(1)}, bf16[1024,512]{1,0:T(8,128)(2,1)S(1)}) custom-call(bf16[256,512]{1,0:T(8,128)(2,1)S(1)} %get-tuple-element.81.refs_0_, ...), custom_call_target="tpu_custom_call", output_to_operand_aliasing={{0}: (3, {}), {1}: (4, {})} | custom-call | flops 400000000 | bytes 1 | tf_op jit(solution)/shard_map/out_own/pallas_call | solution.py:41
  50.6 1.6 %collective-permute-done.24.last_a = bf16[128,512]{1,0:T(8,128)(2,1)S(1)} collective-permute-done((bf16[128,512]{1,0:T(8,128)(2,1)S(1)}, bf16[128,512]{1,0:T(8,128)(2,1)S(1)}, u32[]{:S(2)}, u32[]{:S(2)}) %collective-permute-start.24) | collective-permute-done | bytes 131104 | tf_op jit(solution)/shard_map/ppermute | solution.py:134
  52.1 0.5 out_more.1
  52.6 0.6 collective-permute-start.22
  53.1 0.1 collective-permute-start.23
  53.2 1.5 %collective-permute-done.15.last_b = bf16[128,512]{1,0:T(8,128)(2,1)S(1)} collective-permute-done((bf16[128,512]{1,0:T(8,128)(2,1)S(1)}, bf16[128,512]{1,0:T(8,128)(2,1)S(1)}, u32[]{:S(2)}, u32[]{:S(2)}) %collective-permute-start.15) | collective-permute-done | bytes 131104 | tf_op jit(solution)/shard_map/ppermute | solution.py:134
  54.8 0.7 %out_beside.1.total_ref = f32[256,512]{1,0:T(8,128)S(1)} custom-call(bf16[128,512]{1,0:T(8,128)(2,1)S(1)} %get-tuple-element.88.a, bf16[128,512]{1,0:T(8,128)(2,1)S(1)} %get-tuple-element.89.b, bf16[128,512]{1,0:T(8,128)(2,1)S(1)} %collective-permute-done.22.c, bf16[128,512]{1,0:T(8,128)(2,1)S(1)} %collective-permute-done.23.d, ...), custom_call_target="tpu_custom_call", output_to_operand_aliasing={{}: (8, {})} | custom-call | flops 400000000 | bytes 1 | tf_op jit(solution)/shard_map/out_beside/pallas_call | solution.py:41
  55.4 0.7 %collective-permute-done.16.twin_ref = bf16[128,512]{1,0:T(8,128)(2,1)S(1)} collective-permute-done((bf16[128,512]{1,0:T(8,128)(2,1)S(1)}, bf16[128,512]{1,0:T(8,128)(2,1)S(1)}, u32[]{:S(2)}, u32[]{:S(2)}) %collective-permute-start.16) | collective-permute-done | bytes 131104 | tf_op jit(solution)/shard_map/ppermute | solution.py:138
  56.1 1.4 %out_last.1 = bf16[1024,512]{1,0:T(8,128)(2,1)} custom-call(bf16[128,512]{1,0:T(8,128)(2,1)S(1)} %collective-permute-done.16.twin_ref, bf16[4096,512]{1,0:T(8,128)(2,1)S(1)} %get-tuple-element.84.refs_2_.w_ref, f32[256,512]{1,0:T(8,128)S(1)} %out_beside.1.total_ref, f32[128,256]{1,0:T(8,128)S(1)} %get-tuple-element.63.refs_7_.sa_ref, ...), custom_call_target="tpu_custom_call" | custom-call | flops 400000000 | bytes 1 | tf_op jit(solution)/shard_map/out_last/pallas_call | solution.py:41
  (25 shorter events, 0.1 us)
Async XLA Ops:
  0.0 17.0 %copy-start = (f32[128]{0:T(128)S(1)}, f32[128]{0:T(128)}, u32[]{:S(2)}) copy-start(f32[128]{0:T(128)} %constant.9.clone.1) | copy-start | bytes 1540
  1.6 5.3 %collective-permute-start.4 = (bf16[256,512]{1,0:T(8,128)(2,1)S(1)}, bf16[256,512]{1,0:T(8,128)(2,1)S(1)}, u32[]{:S(2)}, u32[]{:S(2)}) collective-permute-start(bf16[256,512]{1,0:T(8,128)(2,1)S(1)} %get-tuple-element.51.x_ref), channel_id=1, source_target_pairs={{0,1},{1,0},{2,3},{3,2},{4,5},{5,4},{6,7},{7,6},{8,9},{9,8},{10,11... | collective-permute-start | bytes 786440 | tf_op jit(solution)/shard_map/ppermute | solution.py:146
  2.2 8.9 %collective-permute-start = (bf16[128,512]{1,0:T(8,128)(2,1)S(1)}, bf16[128,512]{1,0:T(8,128)(2,1)S(1)}, u32[]{:S(2)}, u32[]{:S(2)}) collective-permute-start(bf16[128,512]{1,0:T(8,128)(2,1)S(1)} %get-tuple-element.49), channel_id=1, source_target_pairs={{0,6},{1,7},{2,4},{3,5},{4,2},{5,3},{6,0},{7,1},{8,14},{9,15},{10,... | collective-permute-start | bytes 393224 | tf_op jit(solution)/shard_map/ppermute | solution.py:145
  6.8 9.9 %collective-permute-start.1 = (bf16[128,512]{1,0:T(8,128)(2,1)S(1)}, bf16[128,512]{1,0:T(8,128)(2,1)S(1)}, u32[]{:S(2)}, u32[]{:S(2)}) collective-permute-start(bf16[128,512]{1,0:T(8,128)(2,1)S(1)} %get-tuple-element.50), channel_id=1, source_target_pairs={{0,6},{1,7},{2,4},{3,5},{4,2},{5,3},{6,0},{7,1},{8,14},{9,15},{10,... | collective-permute-start | bytes 393224 | tf_op jit(solution)/shard_map/ppermute | solution.py:145
  10.3 9.7 %collective-permute-start.8 = (bf16[256,512]{1,0:T(8,128)(2,1)S(1)}, bf16[256,512]{1,0:T(8,128)(2,1)S(1)}, u32[]{:S(2)}, u32[]{:S(2)}) collective-permute-start(bf16[256,512]{1,0:T(8,128)(2,1)S(1)} %get-tuple-element.59), channel_id=1, source_target_pairs={{0,2},{1,3},{2,0},{3,1},{4,6},{5,7},{6,4},{7,5},{8,10},{9,11},{10,... | collective-permute-start | bytes 786440 | tf_op jit(solution)/shard_map/ppermute | solution.py:146
  11.0 8.9 %collective-permute-start.2 = (bf16[128,512]{1,0:T(8,128)(2,1)S(1)}, bf16[128,512]{1,0:T(8,128)(2,1)S(1)}, u32[]{:S(2)}, u32[]{:S(2)}) collective-permute-start(bf16[128,512]{1,0:T(8,128)(2,1)S(1)} %collective-permute-done.refs_0_), channel_id=1, source_target_pairs={{0,1},{1,0},{2,3},{3,2},{4,5},{5,4},{6,7},{7,6},{8,9},{9,8},{10,11... | collective-permute-start | bytes 393224 | tf_op jit(solution)/shard_map/ppermute | solution.py:148
  11.1 11.7 %collective-permute-start.5 = (bf16[128,512]{1,0:T(8,128)(2,1)S(1)}, bf16[128,512]{1,0:T(8,128)(2,1)S(1)}, u32[]{:S(2)}, u32[]{:S(2)}) collective-permute-start(bf16[128,512]{1,0:T(8,128)(2,1)S(1)} %collective-permute-done.refs_0_), channel_id=1, source_target_pairs={{0,2},{1,3},{2,0},{3,1},{4,6},{5,7},{6,4},{7,5},{8,10},{9,11},{10,... | collective-permute-start | bytes 393224 | tf_op jit(solution)/shard_map/ppermute | solution.py:147
  16.7 3.2 %collective-permute-start.3 = (bf16[128,512]{1,0:T(8,128)(2,1)S(1)}, bf16[128,512]{1,0:T(8,128)(2,1)S(1)}, u32[]{:S(2)}, u32[]{:S(2)}) collective-permute-start(bf16[128,512]{1,0:T(8,128)(2,1)S(1)} %collective-permute-done.1.refs_1_), channel_id=1, source_target_pairs={{0,1},{1,0},{2,3},{3,2},{4,5},{5,4},{6,7},{7,6},{8,9},{9,8},{10,11... | collective-permute-start | bytes 393224 | tf_op jit(solution)/shard_map/ppermute | solution.py:148
  17.5 8.1 %collective-permute-start.10 = (bf16[128,512]{1,0:T(8,128)(2,1)S(1)}, bf16[128,512]{1,0:T(8,128)(2,1)S(1)}, u32[]{:S(2)}, u32[]{:S(2)}) collective-permute-start(bf16[128,512]{1,0:T(8,128)(2,1)S(1)} %collective-permute-done.1.refs_1_), channel_id=1, source_target_pairs={{0,2},{1,3},{2,0},{3,1},{4,6},{5,7},{6,4},{7,5},{8,10},{9,11},{10,... | collective-permute-start | bytes 393224 | tf_op jit(solution)/shard_map/ppermute | solution.py:147
  20.0 4.1 %collective-permute-start.9 = (bf16[256,512]{1,0:T(8,128)(2,1)S(1)}, bf16[256,512]{1,0:T(8,128)(2,1)S(1)}, u32[]{:S(2)}, u32[]{:S(2)}) collective-permute-start(bf16[256,512]{1,0:T(8,128)(2,1)S(1)} %collective-permute-done.8.refs_0_), channel_id=1, source_target_pairs={{0,1},{1,0},{2,3},{3,2},{4,5},{5,4},{6,7},{7,6},{8,9},{9,8},{10,11... | collective-permute-start | bytes 786440 | tf_op jit(solution)/shard_map/ppermute | solution.py:149
  23.4 1.3 %collective-permute-start.6 = (bf16[64,512]{1,0:T(8,128)(2,1)S(1)}, bf16[64,512]{1,0:T(8,128)(2,1)S(1)}, u32[]{:S(2)}, u32[]{:S(2)}) collective-permute-start(bf16[64,512]{1,0:T(8,128)(2,1)S(1)} %get-tuple-element.57.refs_0_), channel_id=1, source_target_pairs={{0,1},{1,0},{2,3},{3,2},{4,5},{5,4},{6,7},{7,6},{8,9},{9,8},{10,11... | collective-permute-start | bytes 196616 | tf_op jit(solution)/shard_map/ppermute | solution.py:150
  23.5 1.4 %collective-permute-start.7 = (bf16[64,512]{1,0:T(8,128)(2,1)S(1)}, bf16[64,512]{1,0:T(8,128)(2,1)S(1)}, u32[]{:S(2)}, u32[]{:S(2)}) collective-permute-start(bf16[64,512]{1,0:T(8,128)(2,1)S(1)} %get-tuple-element.58.refs_1_), channel_id=1, source_target_pairs={{0,1},{1,0},{2,3},{3,2},{4,5},{5,4},{6,7},{7,6},{8,9},{9,8},{10,11... | collective-permute-start | bytes 196616 | tf_op jit(solution)/shard_map/ppermute | solution.py:150
  25.5 1.7 %collective-permute-start.11 = (bf16[128,512]{1,0:T(8,128)(2,1)S(1)}, bf16[128,512]{1,0:T(8,128)(2,1)S(1)}, u32[]{:S(2)}, u32[]{:S(2)}) collective-permute-start(bf16[128,512]{1,0:T(8,128)(2,1)S(1)} %get-tuple-element.68.refs_0_), channel_id=1, source_target_pairs={{0,1},{1,0},{2,3},{3,2},{4,5},{5,4},{6,7},{7,6},{8,9},{9,8},{10,11... | collective-permute-start | bytes 393224 | tf_op jit(solution)/shard_map/ppermute | solution.py:586
  25.7 5.1 %collective-permute-start.13 = (bf16[128,256]{1,0:T(8,128)(2,1)S(1)}, bf16[128,256]{1,0:T(8,128)(2,1)S(1)}, u32[]{:S(2)}, u32[]{:S(2)}) collective-permute-start(bf16[128,256]{1,0:T(8,128)(2,1)S(1)} %get-tuple-element.66.refs_11_.refs_9_), channel_id=1, source_target_pairs={{0,8},{8,0},{1,9},{9,1},{2,10},{10,2},{3,11},{11,3},{4,12},{12,4},... | collective-permute-start | bytes 196616 | tf_op jit(solution)/shard_map/ppermute | solution.py:591
  27.5 4.3 %collective-permute-start.12 = (bf16[128,256]{1,0:T(8,128)(2,1)S(1)}, bf16[128,256]{1,0:T(8,128)(2,1)S(1)}, u32[]{:S(2)}, u32[]{:S(2)}) collective-permute-start(bf16[128,256]{1,0:T(8,128)(2,1)S(1)} %get-tuple-element.70.refs_10_), channel_id=1, source_target_pairs={{0,8},{8,0},{1,9},{9,1},{2,10},{10,2},{3,11},{11,3},{4,12},{12,4},... | collective-permute-start | bytes 196616 | tf_op jit(solution)/shard_map/ppermute | solution.py:591
  32.6 11.1 %collective-permute-start.14 = (bf16[256,512]{1,0:T(8,128)(2,1)S(1)}, bf16[256,512]{1,0:T(8,128)(2,1)S(1)}, u32[]{:S(2)}, u32[]{:S(2)}) collective-permute-start(bf16[256,512]{1,0:T(8,128)(2,1)S(1)} %get-tuple-element.81.refs_0_), channel_id=1, source_target_pairs={{0,6},{1,7},{2,4},{3,5},{4,2},{5,3},{6,0},{7,1},{8,14},{9,15},{10,... | collective-permute-start | bytes 786440 | tf_op jit(solution)/shard_map/ppermute | solution.py:130
  36.1 7.7 %collective-permute-start.17 = (bf16[128,512]{1,0:T(8,128)(2,1)S(1)}, bf16[128,512]{1,0:T(8,128)(2,1)S(1)}, u32[]{:S(2)}, u32[]{:S(2)}) collective-permute-start(bf16[128,512]{1,0:T(8,128)(2,1)S(1)} %get-tuple-element.82), channel_id=1, source_target_pairs={{0,1},{1,0},{2,3},{3,2},{4,5},{5,4},{6,7},{7,6},{8,9},{9,8},{10,11... | collective-permute-start | bytes 393224 | tf_op jit(solution)/shard_map/ppermute | solution.py:131
  36.1 11.8 %collective-permute-start.19 = (bf16[128,512]{1,0:T(8,128)(2,1)S(1)}, bf16[128,512]{1,0:T(8,128)(2,1)S(1)}, u32[]{:S(2)}, u32[]{:S(2)}) collective-permute-start(bf16[128,512]{1,0:T(8,128)(2,1)S(1)} %get-tuple-element.82), channel_id=1, source_target_pairs={{0,2},{1,3},{2,0},{3,1},{4,6},{5,7},{6,4},{7,5},{8,10},{9,11},{10,... | collective-permute-start | bytes 393224 | tf_op jit(solution)/shard_map/ppermute | solution.py:132
  36.1 11.7 %collective-permute-start.18 = (bf16[128,512]{1,0:T(8,128)(2,1)S(1)}, bf16[128,512]{1,0:T(8,128)(2,1)S(1)}, u32[]{:S(2)}, u32[]{:S(2)}) collective-permute-start(bf16[128,512]{1,0:T(8,128)(2,1)S(1)} %get-tuple-element.83), channel_id=1, source_target_pairs={{0,1},{1,0},{2,3},{3,2},{4,5},{5,4},{6,7},{7,6},{8,9},{9,8},{10,11... | collective-permute-start | bytes 393224 | tf_op jit(solution)/shard_map/ppermute | solution.py:131
  36.6 11.3 %collective-permute-start.20 = (bf16[128,512]{1,0:T(8,128)(2,1)S(1)}, bf16[128,512]{1,0:T(8,128)(2,1)S(1)}, u32[]{:S(2)}, u32[]{:S(2)}) collective-permute-start(bf16[128,512]{1,0:T(8,128)(2,1)S(1)} %get-tuple-element.83), channel_id=1, source_target_pairs={{0,2},{1,3},{2,0},{3,1},{4,6},{5,7},{6,4},{7,5},{8,10},{9,11},{10,... | collective-permute-start | bytes 393224 | tf_op jit(solution)/shard_map/ppermute | solution.py:132
  43.7 8.4 %collective-permute-start.21 = (bf16[256,512]{1,0:T(8,128)(2,1)S(1)}, bf16[256,512]{1,0:T(8,128)(2,1)S(1)}, u32[]{:S(2)}, u32[]{:S(2)}) collective-permute-start(bf16[256,512]{1,0:T(8,128)(2,1)S(1)} %collective-permute-done.14.refs_0_), channel_id=1, source_target_pairs={{0,1},{1,0},{2,3},{3,2},{4,5},{5,4},{6,7},{7,6},{8,9},{9,8},{10,11... | collective-permute-start | bytes 786440 | tf_op jit(solution)/shard_map/ppermute | solution.py:136
  43.8 8.3 %collective-permute-start.24 = (bf16[128,512]{1,0:T(8,128)(2,1)S(1)}, bf16[128,512]{1,0:T(8,128)(2,1)S(1)}, u32[]{:S(2)}, u32[]{:S(2)}) collective-permute-start(bf16[128,512]{1,0:T(8,128)(2,1)S(1)} %get-tuple-element.93), channel_id=1, source_target_pairs={{0,2},{1,3},{2,0},{3,1},{4,6},{5,7},{6,4},{7,5},{8,10},{9,11},{10,... | collective-permute-start | bytes 393224 | tf_op jit(solution)/shard_map/ppermute | solution.py:134
  47.8 7.0 %collective-permute-start.15 = (bf16[128,512]{1,0:T(8,128)(2,1)S(1)}, bf16[128,512]{1,0:T(8,128)(2,1)S(1)}, u32[]{:S(2)}, u32[]{:S(2)}) collective-permute-start(bf16[128,512]{1,0:T(8,128)(2,1)S(1)} %get-tuple-element.94), channel_id=1, source_target_pairs={{0,2},{1,3},{2,0},{3,1},{4,6},{5,7},{6,4},{7,5},{8,10},{9,11},{10,... | collective-permute-start | bytes 393224 | tf_op jit(solution)/shard_map/ppermute | solution.py:134
  52.1 2.6 %collective-permute-start.25 = (bf16[128,512]{1,0:T(8,128)(2,1)S(1)}, bf16[128,512]{1,0:T(8,128)(2,1)S(1)}, u32[]{:S(2)}, u32[]{:S(2)}) collective-permute-start(bf16[128,512]{1,0:T(8,128)(2,1)S(1)} %collective-permute-done.24.last_a), channel_id=1, source_target_pairs={{0,1},{1,0},{2,3},{3,2},{4,5},{5,4},{6,7},{7,6},{8,9},{9,8},{10,11... | collective-permute-start | bytes 393224 | tf_op jit(solution)/shard_map/ppermute | solution.py:137
  52.6 2.2 %collective-permute-start.22 = (bf16[128,512]{1,0:T(8,128)(2,1)S(1)}, bf16[128,512]{1,0:T(8,128)(2,1)S(1)}, u32[]{:S(2)}, u32[]{:S(2)}) collective-permute-start(bf16[128,512]{1,0:T(8,128)(2,1)S(1)} %get-tuple-element.88.a), channel_id=1, source_target_pairs={{0,1},{1,0},{2,3},{3,2},{4,5},{5,4},{6,7},{7,6},{8,9},{9,8},{10,11... | collective-permute-start | bytes 393224 | tf_op jit(solution)/shard_map/ppermute | solution.py:137
  53.1 1.6 %collective-permute-start.23 = (bf16[128,512]{1,0:T(8,128)(2,1)S(1)}, bf16[128,512]{1,0:T(8,128)(2,1)S(1)}, u32[]{:S(2)}, u32[]{:S(2)}) collective-permute-start(bf16[128,512]{1,0:T(8,128)(2,1)S(1)} %get-tuple-element.89.b), channel_id=1, source_target_pairs={{0,1},{1,0},{2,3},{3,2},{4,5},{5,4},{6,7},{7,6},{8,9},{9,8},{10,11... | collective-permute-start | bytes 393224 | tf_op jit(solution)/shard_map/ppermute | solution.py:137
  54.7 1.3 %collective-permute-start.16 = (bf16[128,512]{1,0:T(8,128)(2,1)S(1)}, bf16[128,512]{1,0:T(8,128)(2,1)S(1)}, u32[]{:S(2)}, u32[]{:S(2)}) collective-permute-start(bf16[128,512]{1,0:T(8,128)(2,1)S(1)} %collective-permute-done.15.last_b), channel_id=1, source_target_pairs={{0,1},{1,0},{2,3},{3,2},{4,5},{5,4},{6,7},{7,6},{8,9},{9,8},{10,11... | collective-permute-start | bytes 393224 | tf_op jit(solution)/shard_map/ppermute | solution.py:138

commit v11 on v10

--- a/solution.py
+++ b/solution.py
@@ -124,7 +124,7 @@
 
 
 def spread(size, full, first, second, use_own, use_far, use_beside):
-    cross = chip_sender(size, lambda z: 3 - z)
+    cross = chip_sender(size, lambda z: z ^ 2)
     near = chip_sender(size, lambda z: z ^ 1)
     twin = sender([(d, d ^ 1) for d in range(size)])
     far = cross(full)
@@ -139,7 +139,7 @@
 
 
 def spread_halves(size, full, first, second, use_own, use_far, use_beside):
-    cross = chip_sender(size, lambda z: 3 - z)
+    cross = chip_sender(size, lambda z: z ^ 2)
     near = chip_sender(size, lambda z: z ^ 1)
     twin = sender([(d, d ^ 1) for d in range(size)])
     far = cross(first), cross(second)
@@ -305,7 +305,7 @@
     z, core = place()
     n, features = w_ref.shape[1], w_ref.shape[0]
     rows = slice(at, at + mine.shape[0])
-    product, squares, routed = project(mine, twin, z ^ 2, core, gain_ref, router_ref, w_ref, slice(nq, n))
+    product, squares, routed = project(mine, twin, 3 - z, core, gain_ref, router_ref, w_ref, slice(nq, n))
     squares = jnp.sum(sums[rows, n : n + 128] + squares, axis=1, keepdims=True)
     routed = jnp.sum(sums[rows, n + 128 : n + 256] + routed, axis=1, keepdims=True)
     inverse = lax.rsqrt(squares * (1.0 / features) + NORM_EPS)
@@ -354,7 +354,7 @@
     half, nq = q_out.shape
     rows, keys = slice(i * half, (i + 1) * half), slice(0, (i + 1) * half)
     product, _, _ = project(
-        mine, twin, z ^ 2, core, gain_ref, None, w_ref, slice(0, nq), stats=False
+        mine, twin, 3 - z, core, gain_ref, None, w_ref, slice(0, nq), stats=False
     )
     q = (sums[rows, 0:nq] + product) * stat_ref[:, 0:1]
     cos, sin, kv = cos_ref[rows, :], sin_ref[rows, :], joined(kv_refs)
@@ -483,7 +483,7 @@
 def out_beside_kernel(a, b, c, d, last_a, last_b, last_twin, w_ref, total_in, total_out):
     z, core = place()
     half = last_a.shape[0]
-    last, twin = (rows for _, rows in halves(last_a, last_b, z ^ 2, core))
+    last, twin = (rows for _, rows in halves(last_a, last_b, 3 - z, core))
     total = total_in[...] + out_term(joined((a, b)), joined((c, d)), z ^ 1, core, w_ref)
     total = total + jnp.dot(joined((last_a, last_b)), w_ref[last, :], preferred_element_type=F32)
     total_out[:half] = total[:half] + jnp.dot(last_twin[...], w_ref[twin, :], preferred_element_type=F32)
@@ -504,7 +504,7 @@
 def out_last_kernel(twin_ref, w_ref, total_ref, sa_ref, sb_ref, hot_ref, hid_ref, out, out_ref, sems):
     z, core = place()
     half, width = twin_ref.shape
-    rows = pl.ds(pl.multiple_of((2 * (z ^ 2) + 1 - core) * width, width), width)
+    rows = pl.ds(pl.multiple_of((2 * (3 - z) + 1 - core) * width, width), width)
     top = sa_ref[:, 128:129] * total_ref[:half]
     rest = total_ref[half:] + jnp.dot(twin_ref[...], w_ref[rows, :], preferred_element_type=F32)
     update = jnp.concatenate([top.astype(BF16), (sb_ref[:, 128:129] * rest).astype(BF16)], axis=0)
@@ -567,7 +567,7 @@
 
     def far(mine, twin, last):
         held["sums"], held["cos"], held["sin"], *pieces = more_part(
-            mine, twin, held["staged"], held["sums"], angles(rowpos), lambda z: 3 - z, FAR_COST, (last,)
+            mine, twin, held["staged"], held["sums"], angles(rowpos), lambda z: z ^ 2, FAR_COST, (last,)
         )
         return tuple(pieces)
 
@@ -607,7 +607,7 @@
         return rides
 
     def far_out(mine, twin, rides):
-        held["total"], *rides = out_more(mine, twin, held["w"], held["total"], rides, lambda z: 3 - z, PART_COST)
+        held["total"], *rides = out_more(mine, twin, held["w"], held["total"], rides, lambda z: z ^ 2, PART_COST)
         return rides
 
     def beside_out(mine, twin, last, last_twin):

time: 57.8 us -> 62.2 us (1.076)
  waiting for transfers between devices: 13.8 us -> 26.2 us
  starting transfers between devices: 27.4 us -> 19.4 us
    ppermute x2, starting transfers between devices: 7.88 us -> 1.3 us  [spread_halves(): last_a, last_b = (near(far[0]), near(far[1]))]
    ppermute x2, waiting for transfers between devices: 0.59 us -> 6.73 us  [spread_halves(): far = (cross(first), cross(second))]
    ppermute x1, waiting for transfers between devices: 5.42 us -> 9 us  [spread(): far = cross(full)]
    ppermute x2, waiting for transfers between devices: 0.32 us -> 3.21 us  [spread_halves(): beside = near(use_own((full,), (twin(full),)))]
    ppermute x2, starting transfers between devices: 4.08 us -> 2.09 us  [spread(): last = (near(far[:half]), near(far[half:]))]
    ppermute x2, starting transfers between devices: 0.58 us -> 2.38 us  [spread_halves(): beside = near(use_own((full,), (twin(full),)))]
    ppermute x1, starting transfers between devices: 3.43 us -> 2.43 us  [spread(): far = cross(full)]
    ppermute x2, starting transfers between devices: 4.78 us -> 3.78 us  [spread_halves(): far = (cross(first), cross(second))]
  transfers between devices with their start and end apart: 26 -> 26, of which waited for: 12 -> 11; matrix products, arithmetic and copies ran while one was open for 1% -> 1% of each run, Pallas kernels for 20% -> 19%
where the time goes in v11:
time: 62.2 us; the launch traced here: 61.9 us
  waiting for transfers between devices  26.2 us (42%)
  starting transfers between devices  19.4 us (31%)
  Pallas kernels  15.6 us (25%)
    pallas_call x15, Pallas kernels, call(): pl.pallas_call(kernel, out_shape=out_shape, in_specs=[HBM if far else VME...  15.6 us
    ppermute x1, waiting for transfers between devices, spread(): far = cross(full)  9 us
    ppermute x2, waiting for transfers between devices, spread_halves(): far = (cross(first), cross(second))  6.73 us
    ppermute x2, starting transfers between devices, spread_halves(): far = (cross(first), cross(second))  3.78 us
    ppermute x2, waiting for transfers between devices, spread_halves(): beside = near(use_own((full,), (twin(full),)))  3.21 us
    ppermute x2, waiting for transfers between devices, spread(): last = (near(far[:half]), near(far[half:]))  2.92 us
    ppermute x2, starting transfers between devices, body(): moved = [lax.ppermute(kv, 'ctx', ring) for kv in kvs]  2.84 us
    ppermute x2, waiting for transfers between devices, spread_halves(): last_a, last_b = (near(far[0]), near(far[1]))  2.8 us
  transfers between devices with their start and end apart: 26, of which 11 were waited for; matrix products, arithmetic and copies ran while one was open for 1% of the time, Pallas kernels for 19%

profile of v11, /device:TPU:0, one launch (start us, length us, event | category | flops | bytes accessed | tf_op | source)
XLA Modules:
  0.0 61.9 jit_solution(2716360948805157755)
XLA Ops:
  0.0 1.6 %pick.1 = (bf16[256,512]{1,0:T(8,128)(2,1)S(1)}, bf16[128,512]{1,0:T(8,128)(2,1)S(1)}, bf16[128,512]{1,0:T(8,128)(2,1)S(1)}, s32[256,128]{1,0:T(8,128)S(1)}) custom-call(s32[2,256]{1,0:T(2,128)} %pos.1, bf16[1024,512]{1,0:T(8,128)(2,1)} %refs_6_.1), custom_call_target="tpu_custom_call" | custom-call | flops 400000000 | bytes 1 | tf_op jit(solution)/shard_map/pick/pallas_call | solution.py:41
  1.6 0.5 collective-permute-start.4
  2.2 3.7 %collective-permute-start = (bf16[128,512]{1,0:T(8,128)(2,1)S(1)}, bf16[128,512]{1,0:T(8,128)(2,1)S(1)}, u32[]{:S(2)}, u32[]{:S(2)}) collective-permute-start(bf16[128,512]{1,0:T(8,128)(2,1)S(1)} %get-tuple-element.49), channel_id=1, source_target_pairs={{0,4},{1,5},{2,6},{3,7},{4,0},{5,1},{6,2},{7,3},{8,12},{9,13},{10,... | collective-permute-start | bytes 393224 | tf_op jit(solution)/shard_map/ppermute | solution.py:145
  5.8 0.1 collective-permute-start.1
  6.0 0.0 collective-permute-done.4.twin_ref
  6.0 3.3 %own_part.1 = (bf16[256,512]{1,0:T(8,128)(2,1)S(1)}, f32[256,1024]{1,0:T(8,128)S(1)}, f32[1,4096]{1,0:T(1,128)S(1)}, f32[1,4096]{1,0:T(1,128)S(1)}, bf16[4096,76...) custom-call(bf16[256,512]{1,0:T(8,128)(2,1)S(1)} %get-tuple-element., ...), custom_call_target="tpu_custom_call", output_to_operand_aliasing={{0}: (0, {})} | custom-call | flops 1500000000 | bytes 1 | tf_op jit(solution)/shard_map/own_part/pallas_call | solution.py:41
  9.3 1.9 %collective-permute-start.8 = (bf16[256,512]{1,0:T(8,128)(2,1)S(1)}, bf16[256,512]{1,0:T(8,128)(2,1)S(1)}, u32[]{:S(2)}, u32[]{:S(2)}) collective-permute-start(bf16[256,512]{1,0:T(8,128)(2,1)S(1)} %get-tuple-element.59), channel_id=1, source_target_pairs={{0,2},{1,3},{2,0},{3,1},{4,6},{5,7},{6,4},{7,5},{8,10},{9,11},{10,... | collective-permute-start | bytes 786440 | tf_op jit(solution)/shard_map/ppermute | solution.py:146
  11.2 0.1 pad_maximum_fusion
  11.2 4.7 %collective-permute-done.refs_0_ = bf16[128,512]{1,0:T(8,128)(2,1)S(1)} collective-permute-done((bf16[128,512]{1,0:T(8,128)(2,1)S(1)}, bf16[128,512]{1,0:T(8,128)(2,1)S(1)}, u32[]{:S(2)}, u32[]{:S(2)}) %collective-permute-start) | collective-permute-done | bytes 131104 | tf_op jit(solution)/shard_map/ppermute | solution.py:145
  15.9 0.0 collective-permute-start.2
  15.9 0.5 collective-permute-start.5
  16.4 2.1 %collective-permute-done.1.refs_1_ = bf16[128,512]{1,0:T(8,128)(2,1)S(1)} collective-permute-done((bf16[128,512]{1,0:T(8,128)(2,1)S(1)}, bf16[128,512]{1,0:T(8,128)(2,1)S(1)}, u32[]{:S(2)}, u32[]{:S(2)}) %collective-permute-start.1) | collective-permute-done | bytes 131104 | tf_op jit(solution)/shard_map/ppermute | solution.py:145
  18.5 0.5 sine_multiply_fusion
  19.0 0.8 %collective-permute-start.10 = (bf16[128,512]{1,0:T(8,128)(2,1)S(1)}, bf16[128,512]{1,0:T(8,128)(2,1)S(1)}, u32[]{:S(2)}, u32[]{:S(2)}) collective-permute-start(bf16[128,512]{1,0:T(8,128)(2,1)S(1)} %collective-permute-done.1.refs_1_), channel_id=1, source_target_pairs={{0,2},{1,3},{2,0},{3,1},{4,6},{5,7},{6,4},{7,5},{8,10},{9,11},{10,... | collective-permute-start | bytes 393224 | tf_op jit(solution)/shard_map/ppermute | solution.py:147
  19.8 3.2 %collective-permute-done.8.refs_0_ = bf16[256,512]{1,0:T(8,128)(2,1)S(1)} collective-permute-done((bf16[256,512]{1,0:T(8,128)(2,1)S(1)}, bf16[256,512]{1,0:T(8,128)(2,1)S(1)}, u32[]{:S(2)}, u32[]{:S(2)}) %collective-permute-start.8) | collective-permute-done | bytes 262176 | tf_op jit(solution)/shard_map/ppermute | solution.py:146
  23.0 2.8 %collective-permute-done.5.refs_10_ = bf16[128,512]{1,0:T(8,128)(2,1)S(1)} collective-permute-done((bf16[128,512]{1,0:T(8,128)(2,1)S(1)}, bf16[128,512]{1,0:T(8,128)(2,1)S(1)}, u32[]{:S(2)}, u32[]{:S(2)}) %collective-permute-start.5) | collective-permute-done | bytes 131104 | tf_op jit(solution)/shard_map/ppermute | solution.py:147
  25.8 0.6 %more_part.2 = (f32[256,1024]{1,0:T(8,128)S(1)}, f32[256,128]{1,0:T(8,128)S(1)}, f32[256,128]{1,0:T(8,128)S(1)}, bf16[64,512]{1,0:T(8,128)(2,1)S(1)}, bf16[64,512]{1,0:T(8,128)(2,1)S(1)}) custom-call(bf16[128,512]{1,0:T(8,128)(2,1)S(1)} %collective-permute-done.refs_0_, ...), custom_call_target="tpu_custom_call", output_to_operand_aliasing={{0}: (7, {}), {1}: (8, {}), {2}: (9, {})} | custom-call | flops 3000000000 | bytes 1 | tf_op jit(solution)/shard_map/more_part/pallas_call | solution.py:41
  26.4 0.1 collective-permute-start.6
  26.5 0.5 collective-permute-start.7
  27.0 0.7 %more_part.3.refs_7_.refs_6_.refs_5_.refs_4_ = f32[256,1024]{1,0:T(8,128)S(1)} custom-call(bf16[256,512]{1,0:T(8,128)(2,1)S(1)} %collective-permute-done.8.refs_0_, bf16[256,512]{1,0:T(8,128)(2,1)S(1)} %collective-permute-done.9.refs_1_, f32[1,4096]{1,0:T(1,128)S(1)} %get-tuple-element.52.refs_4_.refs_2_, ...), custom_call_target="tpu_custom_call", output_to_operand_aliasing={{}: (5, {})} | custom-call | flops 1000000 | bytes 1 | tf_op jit(solution)/shard_map/more_part/pallas_call | solution.py:41
  27.7 0.1 collective-permute-done.6.refs_2_
  27.8 0.2 collective-permute-done.7.refs_3_
  27.9 0.3 kv_last.2
  28.3 0.4 collective-permute-start.11
  28.7 1.8 %collective-permute-start.13 = (bf16[128,256]{1,0:T(8,128)(2,1)S(1)}, bf16[128,256]{1,0:T(8,128)(2,1)S(1)}, u32[]{:S(2)}, u32[]{:S(2)}) collective-permute-start(bf16[128,256]{1,0:T(8,128)(2,1)S(1)} %get-tuple-element.66.refs_11_.refs_9_), channel_id=1, source_target_pairs={{0,8},{8,0},{1,9},{9,1},{2,10},{10,2},{3,11},{11,3},{4,12},{12,4},... | collective-permute-start | bytes 196616 | tf_op jit(solution)/shard_map/ppermute | solution.py:591
  30.5 0.3 kv_last.3
  30.8 1.0 %collective-permute-start.12 = (bf16[128,256]{1,0:T(8,128)(2,1)S(1)}, bf16[128,256]{1,0:T(8,128)(2,1)S(1)}, u32[]{:S(2)}, u32[]{:S(2)}) collective-permute-start(bf16[128,256]{1,0:T(8,128)(2,1)S(1)} %get-tuple-element.70.refs_10_), channel_id=1, source_target_pairs={{0,8},{8,0},{1,9},{9,1},{2,10},{10,2},{3,11},{11,3},{4,12},{12,4},... | collective-permute-start | bytes 196616 | tf_op jit(solution)/shard_map/ppermute | solution.py:591
  31.9 1.1 %q_part.2 = (bf16[128,512]{1,0:T(8,128)(2,1)S(1)}, f32[1,512]{1,0:T(1,128)S(1)}, f32[1,512]{1,0:T(1,128)S(1)}, f32[128,512]{1,0:T(8,128)S(1)}) custom-call(bf16[64,512]{1,0:T(8,128)(2,1)S(1)} %get-tuple-element.57.refs_0_, bf16[64,512]{1,0:T(8,128)(2,1)S(1)} %get-tuple-element.58.refs_1_, bf16[64,512]{1,0:T(8,128)(2,1)S(1)} %collective-permute-done.6.refs_2_, ...), custom_call_target="tpu_custom_call" | custom-call | flops 1000000 | bytes 1 | tf_op jit(solution)/shard_map/q_part/pallas_call | solution.py:41
  33.0 0.9 %q_part.3 = (bf16[128,512]{1,0:T(8,128)(2,1)S(1)}, f32[1,512]{1,0:T(1,128)S(1)}, f32[1,512]{1,0:T(1,128)S(1)}, f32[128,512]{1,0:T(8,128)S(1)}) custom-call(bf16[128,512]{1,0:T(8,128)(2,1)S(1)} %get-tuple-element.68.refs_0_, bf16[128,512]{1,0:T(8,128)(2,1)S(1)} %collective-permute-done.11.refs_1_, f32[1,4096]{1,0:T(1,128)S(1)} %get-tuple-element.52.refs_4_.refs_2_, ...), custom_call_target="tpu_custom_call" | custom-call | flops 1000000 | bytes 1 | tf_op jit(solution)/shard_map/q_part/pallas_call | solution.py:41
  33.9 0.7 %attend_more.2 = (f32[1,1024]{1,0:T(1,128)S(1)}, f32[1,1024]{1,0:T(1,128)S(1)}, f32[128,1024]{1,0:T(8,128)S(1)}) custom-call(bf16[128,512]{1,0:T(8,128)(2,1)S(1)} %get-tuple-element.67.qa_ref, bf16[128,512]{1,0:T(8,128)(2,1)S(1)} %get-tuple-element.71.qb_ref, bf16[128,256]{1,0:T(8,128)(2,1)S(1)} %collective-permute-done.13.kv_ref, ...), custom_call_target="tpu_custom_call" | custom-call | flops 400000000 | bytes 1 | tf_op jit(solution)/shard_map/attend_more/pallas_call | solution.py:41
  34.6 0.6 collective-permute-done.12.kv_ref
  35.2 0.7 %attend_more.3 = (bf16[256,512]{1,0:T(8,128)(2,1)S(1)}, bf16[128,512]{1,0:T(8,128)(2,1)S(1)}, bf16[128,512]{1,0:T(8,128)(2,1)S(1)}) custom-call(bf16[128,512]{1,0:T(8,128)(2,1)S(1)} %get-tuple-element.67.qa_ref, bf16[128,512]{1,0:T(8,128)(2,1)S(1)} %get-tuple-element.71.qb_ref, bf16[128,256]{1,0:T(8,128)(2,1)S(1)} %collective-permute-done.12.kv_ref, ...), custom_call_target="tpu_custom_call" | custom-call | flops 400000000 | bytes 1 | tf_op jit(solution)/shard_map/attend_more/pallas_call | solution.py:41
  35.9 2.4 %collective-permute-start.14 = (bf16[256,512]{1,0:T(8,128)(2,1)S(1)}, bf16[256,512]{1,0:T(8,128)(2,1)S(1)}, u32[]{:S(2)}, u32[]{:S(2)}) collective-permute-start(bf16[256,512]{1,0:T(8,128)(2,1)S(1)} %get-tuple-element.81.refs_0_), channel_id=1, source_target_pairs={{0,4},{1,5},{2,6},{3,7},{4,0},{5,1},{6,2},{7,3},{8,12},{9,13},{10,... | collective-permute-start | bytes 786440 | tf_op jit(solution)/shard_map/ppermute | solution.py:130
  38.3 2.5 %collective-permute-start.19 = (bf16[128,512]{1,0:T(8,128)(2,1)S(1)}, bf16[128,512]{1,0:T(8,128)(2,1)S(1)}, u32[]{:S(2)}, u32[]{:S(2)}) collective-permute-start(bf16[128,512]{1,0:T(8,128)(2,1)S(1)} %get-tuple-element.82), channel_id=1, source_target_pairs={{0,2},{1,3},{2,0},{3,1},{4,6},{5,7},{6,4},{7,5},{8,10},{9,11},{10,... | collective-permute-start | bytes 393224 | tf_op jit(solution)/shard_map/ppermute | solution.py:132
  40.8 0.2 collective-permute-start.18
  41.0 0.3 collective-permute-start.20
  41.3 9.0 %collective-permute-done.14.refs_0_ = bf16[256,512]{1,0:T(8,128)(2,1)S(1)} collective-permute-done((bf16[256,512]{1,0:T(8,128)(2,1)S(1)}, bf16[256,512]{1,0:T(8,128)(2,1)S(1)}, u32[]{:S(2)}, u32[]{:S(2)}) %collective-permute-start.14) | collective-permute-done | bytes 262176 | tf_op jit(solution)/shard_map/ppermute | solution.py:130
  50.3 0.5 collective-permute-start.24
  50.8 1.6 %collective-permute-start.15 = (bf16[128,512]{1,0:T(8,128)(2,1)S(1)}, bf16[128,512]{1,0:T(8,128)(2,1)S(1)}, u32[]{:S(2)}, u32[]{:S(2)}) collective-permute-start(bf16[128,512]{1,0:T(8,128)(2,1)S(1)} %get-tuple-element.94), channel_id=1, source_target_pairs={{0,2},{1,3},{2,0},{3,1},{4,6},{5,7},{6,4},{7,5},{8,10},{9,11},{10,... | collective-permute-start | bytes 393224 | tf_op jit(solution)/shard_map/ppermute | solution.py:134
  52.4 2.6 %out_own.1 = (bf16[128,512]{1,0:T(8,128)(2,1)S(1)}, bf16[128,512]{1,0:T(8,128)(2,1)S(1)}, f32[256,512]{1,0:T(8,128)S(1)}, bf16[4096,512]{1,0:T(8,128)(2,1)S(1)}, bf16[1024,512]{1,0:T(8,128)(2,1)S(1)}) custom-call(bf16[256,512]{1,0:T(8,128)(2,1)S(1)} %get-tuple-element.81.refs_0_, ...), custom_call_target="tpu_custom_call", output_to_operand_aliasing={{0}: (3, {}), {1}: (4, {})} | custom-call | flops 400000000 | bytes 1 | tf_op jit(solution)/shard_map/out_own/pallas_call | solution.py:41
  55.1 1.6 %collective-permute-done.24.last_a = bf16[128,512]{1,0:T(8,128)(2,1)S(1)} collective-permute-done((bf16[128,512]{1,0:T(8,128)(2,1)S(1)}, bf16[128,512]{1,0:T(8,128)(2,1)S(1)}, u32[]{:S(2)}, u32[]{:S(2)}) %collective-permute-start.24) | collective-permute-done | bytes 131104 | tf_op jit(solution)/shard_map/ppermute | solution.py:134
  56.7 0.5 out_more.1
  57.2 0.6 collective-permute-start.22
  57.7 0.1 collective-permute-start.23
  57.8 1.3 %collective-permute-done.15.last_b = bf16[128,512]{1,0:T(8,128)(2,1)S(1)} collective-permute-done((bf16[128,512]{1,0:T(8,128)(2,1)S(1)}, bf16[128,512]{1,0:T(8,128)(2,1)S(1)}, u32[]{:S(2)}, u32[]{:S(2)}) %collective-permute-start.15) | collective-permute-done | bytes 131104 | tf_op jit(solution)/shard_map/ppermute | solution.py:134
  59.1 0.7 %out_beside.1.total_ref = f32[256,512]{1,0:T(8,128)S(1)} custom-call(bf16[128,512]{1,0:T(8,128)(2,1)S(1)} %get-tuple-element.88.a, bf16[128,512]{1,0:T(8,128)(2,1)S(1)} %get-tuple-element.89.b, bf16[128,512]{1,0:T(8,128)(2,1)S(1)} %collective-permute-done.22.c, bf16[128,512]{1,0:T(8,128)(2,1)S(1)} %collective-permute-done.23.d, ...), custom_call_target="tpu_custom_call", output_to_operand_aliasing={{}: (8, {})} | custom-call | flops 400000000 | bytes 1 | tf_op jit(solution)/shard_map/out_beside/pallas_call | solution.py:41
  59.8 0.7 %collective-permute-done.16.twin_ref = bf16[128,512]{1,0:T(8,128)(2,1)S(1)} collective-permute-done((bf16[128,512]{1,0:T(8,128)(2,1)S(1)}, bf16[128,512]{1,0:T(8,128)(2,1)S(1)}, u32[]{:S(2)}, u32[]{:S(2)}) %collective-permute-start.16) | collective-permute-done | bytes 131104 | tf_op jit(solution)/shard_map/ppermute | solution.py:138
  60.5 1.4 %out_last.1 = bf16[1024,512]{1,0:T(8,128)(2,1)} custom-call(bf16[128,512]{1,0:T(8,128)(2,1)S(1)} %collective-permute-done.16.twin_ref, bf16[4096,512]{1,0:T(8,128)(2,1)S(1)} %get-tuple-element.84.refs_2_.w_ref, f32[256,512]{1,0:T(8,128)S(1)} %out_beside.1.total_ref, f32[128,256]{1,0:T(8,128)S(1)} %get-tuple-element.63.refs_7_.sa_ref, ...), custom_call_target="tpu_custom_call" | custom-call | flops 400000000 | bytes 1 | tf_op jit(solution)/shard_map/out_last/pallas_call | solution.py:41
  (25 shorter events, 0.1 us)
Async XLA Ops:
  0.0 18.5 %copy-start = (f32[128]{0:T(128)S(1)}, f32[128]{0:T(128)}, u32[]{:S(2)}) copy-start(f32[128]{0:T(128)} %constant.9.clone.1) | copy-start | bytes 1540
  1.6 4.3 %collective-permute-start.4 = (bf16[256,512]{1,0:T(8,128)(2,1)S(1)}, bf16[256,512]{1,0:T(8,128)(2,1)S(1)}, u32[]{:S(2)}, u32[]{:S(2)}) collective-permute-start(bf16[256,512]{1,0:T(8,128)(2,1)S(1)} %get-tuple-element.51.x_ref), channel_id=1, source_target_pairs={{0,1},{1,0},{2,3},{3,2},{4,5},{5,4},{6,7},{7,6},{8,9},{9,8},{10,11... | collective-permute-start | bytes 786440 | tf_op jit(solution)/shard_map/ppermute | solution.py:146
  2.2 13.8 %collective-permute-start = (bf16[128,512]{1,0:T(8,128)(2,1)S(1)}, bf16[128,512]{1,0:T(8,128)(2,1)S(1)}, u32[]{:S(2)}, u32[]{:S(2)}) collective-permute-start(bf16[128,512]{1,0:T(8,128)(2,1)S(1)} %get-tuple-element.49), channel_id=1, source_target_pairs={{0,4},{1,5},{2,6},{3,7},{4,0},{5,1},{6,2},{7,3},{8,12},{9,13},{10,... | collective-permute-start | bytes 393224 | tf_op jit(solution)/shard_map/ppermute | solution.py:145
  5.8 12.6 %collective-permute-start.1 = (bf16[128,512]{1,0:T(8,128)(2,1)S(1)}, bf16[128,512]{1,0:T(8,128)(2,1)S(1)}, u32[]{:S(2)}, u32[]{:S(2)}) collective-permute-start(bf16[128,512]{1,0:T(8,128)(2,1)S(1)} %get-tuple-element.50), channel_id=1, source_target_pairs={{0,4},{1,5},{2,6},{3,7},{4,0},{5,1},{6,2},{7,3},{8,12},{9,13},{10,... | collective-permute-start | bytes 393224 | tf_op jit(solution)/shard_map/ppermute | solution.py:145
  9.3 13.7 %collective-permute-start.8 = (bf16[256,512]{1,0:T(8,128)(2,1)S(1)}, bf16[256,512]{1,0:T(8,128)(2,1)S(1)}, u32[]{:S(2)}, u32[]{:S(2)}) collective-permute-start(bf16[256,512]{1,0:T(8,128)(2,1)S(1)} %get-tuple-element.59), channel_id=1, source_target_pairs={{0,2},{1,3},{2,0},{3,1},{4,6},{5,7},{6,4},{7,5},{8,10},{9,11},{10,... | collective-permute-start | bytes 786440 | tf_op jit(solution)/shard_map/ppermute | solution.py:146
  15.9 7.1 %collective-permute-start.2 = (bf16[128,512]{1,0:T(8,128)(2,1)S(1)}, bf16[128,512]{1,0:T(8,128)(2,1)S(1)}, u32[]{:S(2)}, u32[]{:S(2)}) collective-permute-start(bf16[128,512]{1,0:T(8,128)(2,1)S(1)} %collective-permute-done.refs_0_), channel_id=1, source_target_pairs={{0,1},{1,0},{2,3},{3,2},{4,5},{5,4},{6,7},{7,6},{8,9},{9,8},{10,11... | collective-permute-start | bytes 393224 | tf_op jit(solution)/shard_map/ppermute | solution.py:148
  15.9 9.9 %collective-permute-start.5 = (bf16[128,512]{1,0:T(8,128)(2,1)S(1)}, bf16[128,512]{1,0:T(8,128)(2,1)S(1)}, u32[]{:S(2)}, u32[]{:S(2)}) collective-permute-start(bf16[128,512]{1,0:T(8,128)(2,1)S(1)} %collective-permute-done.refs_0_), channel_id=1, source_target_pairs={{0,2},{1,3},{2,0},{3,1},{4,6},{5,7},{6,4},{7,5},{8,10},{9,11},{10,... | collective-permute-start | bytes 393224 | tf_op jit(solution)/shard_map/ppermute | solution.py:147
  18.5 4.5 %collective-permute-start.3 = (bf16[128,512]{1,0:T(8,128)(2,1)S(1)}, bf16[128,512]{1,0:T(8,128)(2,1)S(1)}, u32[]{:S(2)}, u32[]{:S(2)}) collective-permute-start(bf16[128,512]{1,0:T(8,128)(2,1)S(1)} %collective-permute-done.1.refs_1_), channel_id=1, source_target_pairs={{0,1},{1,0},{2,3},{3,2},{4,5},{5,4},{6,7},{7,6},{8,9},{9,8},{10,11... | collective-permute-start | bytes 393224 | tf_op jit(solution)/shard_map/ppermute | solution.py:148
  19.0 9.3 %collective-permute-start.10 = (bf16[128,512]{1,0:T(8,128)(2,1)S(1)}, bf16[128,512]{1,0:T(8,128)(2,1)S(1)}, u32[]{:S(2)}, u32[]{:S(2)}) collective-permute-start(bf16[128,512]{1,0:T(8,128)(2,1)S(1)} %collective-permute-done.1.refs_1_), channel_id=1, source_target_pairs={{0,2},{1,3},{2,0},{3,1},{4,6},{5,7},{6,4},{7,5},{8,10},{9,11},{10,... | collective-permute-start | bytes 393224 | tf_op jit(solution)/shard_map/ppermute | solution.py:147
  23.0 4.0 %collective-permute-start.9 = (bf16[256,512]{1,0:T(8,128)(2,1)S(1)}, bf16[256,512]{1,0:T(8,128)(2,1)S(1)}, u32[]{:S(2)}, u32[]{:S(2)}) collective-permute-start(bf16[256,512]{1,0:T(8,128)(2,1)S(1)} %collective-permute-done.8.refs_0_), channel_id=1, source_target_pairs={{0,1},{1,0},{2,3},{3,2},{4,5},{5,4},{6,7},{7,6},{8,9},{9,8},{10,11... | collective-permute-start | bytes 786440 | tf_op jit(solution)/shard_map/ppermute | solution.py:149
  26.4 1.3 %collective-permute-start.6 = (bf16[64,512]{1,0:T(8,128)(2,1)S(1)}, bf16[64,512]{1,0:T(8,128)(2,1)S(1)}, u32[]{:S(2)}, u32[]{:S(2)}) collective-permute-start(bf16[64,512]{1,0:T(8,128)(2,1)S(1)} %get-tuple-element.57.refs_0_), channel_id=1, source_target_pairs={{0,1},{1,0},{2,3},{3,2},{4,5},{5,4},{6,7},{7,6},{8,9},{9,8},{10,11... | collective-permute-start | bytes 196616 | tf_op jit(solution)/shard_map/ppermute | solution.py:150
  26.5 1.4 %collective-permute-start.7 = (bf16[64,512]{1,0:T(8,128)(2,1)S(1)}, bf16[64,512]{1,0:T(8,128)(2,1)S(1)}, u32[]{:S(2)}, u32[]{:S(2)}) collective-permute-start(bf16[64,512]{1,0:T(8,128)(2,1)S(1)} %get-tuple-element.58.refs_1_), channel_id=1, source_target_pairs={{0,1},{1,0},{2,3},{3,2},{4,5},{5,4},{6,7},{7,6},{8,9},{9,8},{10,11... | collective-permute-start | bytes 196616 | tf_op jit(solution)/shard_map/ppermute | solution.py:150
  28.3 2.2 %collective-permute-start.11 = (bf16[128,512]{1,0:T(8,128)(2,1)S(1)}, bf16[128,512]{1,0:T(8,128)(2,1)S(1)}, u32[]{:S(2)}, u32[]{:S(2)}) collective-permute-start(bf16[128,512]{1,0:T(8,128)(2,1)S(1)} %get-tuple-element.68.refs_0_), channel_id=1, source_target_pairs={{0,1},{1,0},{2,3},{3,2},{4,5},{5,4},{6,7},{7,6},{8,9},{9,8},{10,11... | collective-permute-start | bytes 393224 | tf_op jit(solution)/shard_map/ppermute | solution.py:586
  28.7 5.2 %collective-permute-start.13 = (bf16[128,256]{1,0:T(8,128)(2,1)S(1)}, bf16[128,256]{1,0:T(8,128)(2,1)S(1)}, u32[]{:S(2)}, u32[]{:S(2)}) collective-permute-start(bf16[128,256]{1,0:T(8,128)(2,1)S(1)} %get-tuple-element.66.refs_11_.refs_9_), channel_id=1, source_target_pairs={{0,8},{8,0},{1,9},{9,1},{2,10},{10,2},{3,11},{11,3},{4,12},{12,4},... | collective-permute-start | bytes 196616 | tf_op jit(solution)/shard_map/ppermute | solution.py:591
  30.8 4.3 %collective-permute-start.12 = (bf16[128,256]{1,0:T(8,128)(2,1)S(1)}, bf16[128,256]{1,0:T(8,128)(2,1)S(1)}, u32[]{:S(2)}, u32[]{:S(2)}) collective-permute-start(bf16[128,256]{1,0:T(8,128)(2,1)S(1)} %get-tuple-element.70.refs_10_), channel_id=1, source_target_pairs={{0,8},{8,0},{1,9},{9,1},{2,10},{10,2},{3,11},{11,3},{4,12},{12,4},... | collective-permute-start | bytes 196616 | tf_op jit(solution)/shard_map/ppermute | solution.py:591
  35.9 14.4 %collective-permute-start.14 = (bf16[256,512]{1,0:T(8,128)(2,1)S(1)}, bf16[256,512]{1,0:T(8,128)(2,1)S(1)}, u32[]{:S(2)}, u32[]{:S(2)}) collective-permute-start(bf16[256,512]{1,0:T(8,128)(2,1)S(1)} %get-tuple-element.81.refs_0_), channel_id=1, source_target_pairs={{0,4},{1,5},{2,6},{3,7},{4,0},{5,1},{6,2},{7,3},{8,12},{9,13},{10,... | collective-permute-start | bytes 786440 | tf_op jit(solution)/shard_map/ppermute | solution.py:130
  38.3 12.0 %collective-permute-start.17 = (bf16[128,512]{1,0:T(8,128)(2,1)S(1)}, bf16[128,512]{1,0:T(8,128)(2,1)S(1)}, u32[]{:S(2)}, u32[]{:S(2)}) collective-permute-start(bf16[128,512]{1,0:T(8,128)(2,1)S(1)} %get-tuple-element.82), channel_id=1, source_target_pairs={{0,1},{1,0},{2,3},{3,2},{4,5},{5,4},{6,7},{7,6},{8,9},{9,8},{10,11... | collective-permute-start | bytes 393224 | tf_op jit(solution)/shard_map/ppermute | solution.py:131
  38.3 14.1 %collective-permute-start.19 = (bf16[128,512]{1,0:T(8,128)(2,1)S(1)}, bf16[128,512]{1,0:T(8,128)(2,1)S(1)}, u32[]{:S(2)}, u32[]{:S(2)}) collective-permute-start(bf16[128,512]{1,0:T(8,128)(2,1)S(1)} %get-tuple-element.82), channel_id=1, source_target_pairs={{0,2},{1,3},{2,0},{3,1},{4,6},{5,7},{6,4},{7,5},{8,10},{9,11},{10,... | collective-permute-start | bytes 393224 | tf_op jit(solution)/shard_map/ppermute | solution.py:132
  40.8 10.0 %collective-permute-start.18 = (bf16[128,512]{1,0:T(8,128)(2,1)S(1)}, bf16[128,512]{1,0:T(8,128)(2,1)S(1)}, u32[]{:S(2)}, u32[]{:S(2)}) collective-permute-start(bf16[128,512]{1,0:T(8,128)(2,1)S(1)} %get-tuple-element.83), channel_id=1, source_target_pairs={{0,1},{1,0},{2,3},{3,2},{4,5},{5,4},{6,7},{7,6},{8,9},{9,8},{10,11... | collective-permute-start | bytes 393224 | tf_op jit(solution)/shard_map/ppermute | solution.py:131
  41.0 11.4 %collective-permute-start.20 = (bf16[128,512]{1,0:T(8,128)(2,1)S(1)}, bf16[128,512]{1,0:T(8,128)(2,1)S(1)}, u32[]{:S(2)}, u32[]{:S(2)}) collective-permute-start(bf16[128,512]{1,0:T(8,128)(2,1)S(1)} %get-tuple-element.83), channel_id=1, source_target_pairs={{0,2},{1,3},{2,0},{3,1},{4,6},{5,7},{6,4},{7,5},{8,10},{9,11},{10,... | collective-permute-start | bytes 393224 | tf_op jit(solution)/shard_map/ppermute | solution.py:132
  50.3 6.4 %collective-permute-start.21 = (bf16[256,512]{1,0:T(8,128)(2,1)S(1)}, bf16[256,512]{1,0:T(8,128)(2,1)S(1)}, u32[]{:S(2)}, u32[]{:S(2)}) collective-permute-start(bf16[256,512]{1,0:T(8,128)(2,1)S(1)} %collective-permute-done.14.refs_0_), channel_id=1, source_target_pairs={{0,1},{1,0},{2,3},{3,2},{4,5},{5,4},{6,7},{7,6},{8,9},{9,8},{10,11... | collective-permute-start | bytes 786440 | tf_op jit(solution)/shard_map/ppermute | solution.py:136
  50.3 6.4 %collective-permute-start.24 = (bf16[128,512]{1,0:T(8,128)(2,1)S(1)}, bf16[128,512]{1,0:T(8,128)(2,1)S(1)}, u32[]{:S(2)}, u32[]{:S(2)}) collective-permute-start(bf16[128,512]{1,0:T(8,128)(2,1)S(1)} %get-tuple-element.93), channel_id=1, source_target_pairs={{0,2},{1,3},{2,0},{3,1},{4,6},{5,7},{6,4},{7,5},{8,10},{9,11},{10,... | collective-permute-start | bytes 393224 | tf_op jit(solution)/shard_map/ppermute | solution.py:134
  50.8 8.3 %collective-permute-start.15 = (bf16[128,512]{1,0:T(8,128)(2,1)S(1)}, bf16[128,512]{1,0:T(8,128)(2,1)S(1)}, u32[]{:S(2)}, u32[]{:S(2)}) collective-permute-start(bf16[128,512]{1,0:T(8,128)(2,1)S(1)} %get-tuple-element.94), channel_id=1, source_target_pairs={{0,2},{1,3},{2,0},{3,1},{4,6},{5,7},{6,4},{7,5},{8,10},{9,11},{10,... | collective-permute-start | bytes 393224 | tf_op jit(solution)/shard_map/ppermute | solution.py:134
  56.7 2.4 %collective-permute-start.25 = (bf16[128,512]{1,0:T(8,128)(2,1)S(1)}, bf16[128,512]{1,0:T(8,128)(2,1)S(1)}, u32[]{:S(2)}, u32[]{:S(2)}) collective-permute-start(bf16[128,512]{1,0:T(8,128)(2,1)S(1)} %collective-permute-done.24.last_a), channel_id=1, source_target_pairs={{0,1},{1,0},{2,3},{3,2},{4,5},{5,4},{6,7},{7,6},{8,9},{9,8},{10,11... | collective-permute-start | bytes 393224 | tf_op jit(solution)/shard_map/ppermute | solution.py:137
  57.2 2.0 %collective-permute-start.22 = (bf16[128,512]{1,0:T(8,128)(2,1)S(1)}, bf16[128,512]{1,0:T(8,128)(2,1)S(1)}, u32[]{:S(2)}, u32[]{:S(2)}) collective-permute-start(bf16[128,512]{1,0:T(8,128)(2,1)S(1)} %get-tuple-element.88.a), channel_id=1, source_target_pairs={{0,1},{1,0},{2,3},{3,2},{4,5},{5,4},{6,7},{7,6},{8,9},{9,8},{10,11... | collective-permute-start | bytes 393224 | tf_op jit(solution)/shard_map/ppermute | solution.py:137
  57.7 1.4 %collective-permute-start.23 = (bf16[128,512]{1,0:T(8,128)(2,1)S(1)}, bf16[128,512]{1,0:T(8,128)(2,1)S(1)}, u32[]{:S(2)}, u32[]{:S(2)}) collective-permute-start(bf16[128,512]{1,0:T(8,128)(2,1)S(1)} %get-tuple-element.89.b), channel_id=1, source_target_pairs={{0,1},{1,0},{2,3},{3,2},{4,5},{5,4},{6,7},{7,6},{8,9},{9,8},{10,11... | collective-permute-start | bytes 393224 | tf_op jit(solution)/shard_map/ppermute | solution.py:137
  59.1 1.3 %collective-permute-start.16 = (bf16[128,512]{1,0:T(8,128)(2,1)S(1)}, bf16[128,512]{1,0:T(8,128)(2,1)S(1)}, u32[]{:S(2)}, u32[]{:S(2)}) collective-permute-start(bf16[128,512]{1,0:T(8,128)(2,1)S(1)} %collective-permute-done.15.last_b), channel_id=1, source_target_pairs={{0,1},{1,0},{2,3},{3,2},{4,5},{5,4},{6,7},{7,6},{8,9},{9,8},{10,11... | collective-permute-start | bytes 393224 | tf_op jit(solution)/shard_map/ppermute | solution.py:138

commit v12 on v10

--- a/solution.py
+++ b/solution.py
@@ -402,7 +402,7 @@
             outs[0][:, at], outs[1][:, at], outs[2][:, at] = top, total, mix
             continue
         full, first, second = outs
-        attn = jnp.transpose(mix * (1.0 / total)).astype(BF16)
+        attn = jnp.transpose((mix * (1.0 / total)).astype(BF16))
         full[:, lanes] = attn
         first[:, lanes] = attn[:half]
         second[:, lanes] = attn[half:]

time: 57.8 us -> 57.8 us (level)
  no operation moved by 1% of the time
where the time goes in v12:
time: 57.8 us; the launch traced here: 57.5 us
  starting transfers between devices  27.4 us (47%)
  Pallas kernels  15.6 us (27%)
  waiting for transfers between devices  13.8 us (24%)
    pallas_call x15, Pallas kernels, call(): pl.pallas_call(kernel, out_shape=out_shape, in_specs=[HBM if far else VME...  15.6 us
    ppermute x2, starting transfers between devices, spread_halves(): last_a, last_b = (near(far[0]), near(far[1]))  7.88 us
    ppermute x1, waiting for transfers between devices, spread(): far = cross(full)  5.42 us
    ppermute x2, starting transfers between devices, spread_halves(): far = (cross(first), cross(second))  4.78 us
    ppermute x2, starting transfers between devices, spread(): last = (near(far[:half]), near(far[half:]))  4.08 us
    ppermute x1, starting transfers between devices, spread(): far = cross(full)  3.43 us
    ppermute x2, waiting for transfers between devices, spread(): last = (near(far[:half]), near(far[half:]))  3.07 us
    ppermute x2, waiting for transfers between devices, spread_halves(): last_a, last_b = (near(far[0]), near(far[1]))  3.04 us
  transfers between devices with their start and end apart: 26, of which 12 were waited for; matrix products, arithmetic and copies ran while one was open for 1% of the time, Pallas kernels for 20%

profile of v12, /device:TPU:0, one launch (start us, length us, event | category | flops | bytes accessed | tf_op | source)
XLA Modules:
  0.0 57.5 jit_solution(15659543796337010765)
XLA Ops:
  0.0 1.6 %pick.1 = (bf16[256,512]{1,0:T(8,128)(2,1)S(1)}, bf16[128,512]{1,0:T(8,128)(2,1)S(1)}, bf16[128,512]{1,0:T(8,128)(2,1)S(1)}, s32[256,128]{1,0:T(8,128)S(1)}) custom-call(s32[2,256]{1,0:T(2,128)} %pos.1, bf16[1024,512]{1,0:T(8,128)(2,1)} %refs_6_.1), custom_call_target="tpu_custom_call" | custom-call | flops 400000000 | bytes 1 | tf_op jit(solution)/shard_map/pick/pallas_call | solution.py:41
  1.6 0.5 collective-permute-start.4
  2.2 4.7 %collective-permute-start = (bf16[128,512]{1,0:T(8,128)(2,1)S(1)}, bf16[128,512]{1,0:T(8,128)(2,1)S(1)}, u32[]{:S(2)}, u32[]{:S(2)}) collective-permute-start(bf16[128,512]{1,0:T(8,128)(2,1)S(1)} %get-tuple-element.49), channel_id=1, source_target_pairs={{0,6},{1,7},{2,4},{3,5},{4,2},{5,3},{6,0},{7,1},{8,14},{9,15},{10,... | collective-permute-start | bytes 393224 | tf_op jit(solution)/shard_map/ppermute | solution.py:145
  6.8 0.1 collective-permute-start.1
  7.0 0.0 collective-permute-done.4.twin_ref
  7.0 3.3 %own_part.1 = (bf16[256,512]{1,0:T(8,128)(2,1)S(1)}, f32[256,1024]{1,0:T(8,128)S(1)}, f32[1,4096]{1,0:T(1,128)S(1)}, f32[1,4096]{1,0:T(1,128)S(1)}, bf16[4096,76...) custom-call(bf16[256,512]{1,0:T(8,128)(2,1)S(1)} %get-tuple-element., ...), custom_call_target="tpu_custom_call", output_to_operand_aliasing={{0}: (0, {})} | custom-call | flops 1500000000 | bytes 1 | tf_op jit(solution)/shard_map/own_part/pallas_call | solution.py:41
  10.3 0.1 collective-permute-start.8
  10.4 0.1 pad_maximum_fusion
  10.5 0.6 %collective-permute-done.refs_0_ = bf16[128,512]{1,0:T(8,128)(2,1)S(1)} collective-permute-done((bf16[128,512]{1,0:T(8,128)(2,1)S(1)}, bf16[128,512]{1,0:T(8,128)(2,1)S(1)}, u32[]{:S(2)}, u32[]{:S(2)}) %collective-permute-start) | collective-permute-done | bytes 131104 | tf_op jit(solution)/shard_map/ppermute | solution.py:145
  11.1 5.7 %collective-permute-start.5 = (bf16[128,512]{1,0:T(8,128)(2,1)S(1)}, bf16[128,512]{1,0:T(8,128)(2,1)S(1)}, u32[]{:S(2)}, u32[]{:S(2)}) collective-permute-start(bf16[128,512]{1,0:T(8,128)(2,1)S(1)} %collective-permute-done.refs_0_), channel_id=1, source_target_pairs={{0,2},{1,3},{2,0},{3,1},{4,6},{5,7},{6,4},{7,5},{8,10},{9,11},{10,... | collective-permute-start | bytes 393224 | tf_op jit(solution)/shard_map/ppermute | solution.py:147
  16.7 0.2 collective-permute-start.3
  17.0 0.5 sine_multiply_fusion
  17.5 2.2 %collective-permute-start.10 = (bf16[128,512]{1,0:T(8,128)(2,1)S(1)}, bf16[128,512]{1,0:T(8,128)(2,1)S(1)}, u32[]{:S(2)}, u32[]{:S(2)}) collective-permute-start(bf16[128,512]{1,0:T(8,128)(2,1)S(1)} %collective-permute-done.1.refs_1_), channel_id=1, source_target_pairs={{0,2},{1,3},{2,0},{3,1},{4,6},{5,7},{6,4},{7,5},{8,10},{9,11},{10,... | collective-permute-start | bytes 393224 | tf_op jit(solution)/shard_map/ppermute | solution.py:147
  19.6 0.3 collective-permute-done.8.refs_0_
  20.0 2.8 %collective-permute-done.5.refs_10_ = bf16[128,512]{1,0:T(8,128)(2,1)S(1)} collective-permute-done((bf16[128,512]{1,0:T(8,128)(2,1)S(1)}, bf16[128,512]{1,0:T(8,128)(2,1)S(1)}, u32[]{:S(2)}, u32[]{:S(2)}) %collective-permute-start.5) | collective-permute-done | bytes 131104 | tf_op jit(solution)/shard_map/ppermute | solution.py:147
  22.8 0.7 %more_part.2 = (f32[256,1024]{1,0:T(8,128)S(1)}, f32[256,128]{1,0:T(8,128)S(1)}, f32[256,128]{1,0:T(8,128)S(1)}, bf16[64,512]{1,0:T(8,128)(2,1)S(1)}, bf16[64,512]{1,0:T(8,128)(2,1)S(1)}) custom-call(bf16[128,512]{1,0:T(8,128)(2,1)S(1)} %collective-permute-done.refs_0_, ...), custom_call_target="tpu_custom_call", output_to_operand_aliasing={{0}: (7, {}), {1}: (8, {}), {2}: (9, {})} | custom-call | flops 3000000000 | bytes 1 | tf_op jit(solution)/shard_map/more_part/pallas_call | solution.py:41
  23.4 0.1 collective-permute-start.6
  23.5 0.5 collective-permute-start.7
  24.0 0.7 %more_part.3.refs_7_.refs_6_.refs_5_.refs_4_ = f32[256,1024]{1,0:T(8,128)S(1)} custom-call(bf16[256,512]{1,0:T(8,128)(2,1)S(1)} %collective-permute-done.8.refs_0_, bf16[256,512]{1,0:T(8,128)(2,1)S(1)} %collective-permute-done.9.refs_1_, f32[1,4096]{1,0:T(1,128)S(1)} %get-tuple-element.52.refs_4_.refs_2_, ...), custom_call_target="tpu_custom_call", output_to_operand_aliasing={{}: (5, {})} | custom-call | flops 1000000 | bytes 1 | tf_op jit(solution)/shard_map/more_part/pallas_call | solution.py:41
  24.7 0.1 collective-permute-done.6.refs_2_
  24.8 0.2 collective-permute-done.7.refs_3_
  24.9 0.3 kv_last.2
  25.3 0.2 collective-permute-done.10.__1_
  25.5 0.2 collective-permute-start.11
  25.7 1.5 %collective-permute-start.13 = (bf16[128,256]{1,0:T(8,128)(2,1)S(1)}, bf16[128,256]{1,0:T(8,128)(2,1)S(1)}, u32[]{:S(2)}, u32[]{:S(2)}) collective-permute-start(bf16[128,256]{1,0:T(8,128)(2,1)S(1)} %get-tuple-element.66.refs_11_.refs_9_), channel_id=1, source_target_pairs={{0,8},{8,0},{1,9},{9,1},{2,10},{10,2},{3,11},{11,3},{4,12},{12,4},... | collective-permute-start | bytes 196616 | tf_op jit(solution)/shard_map/ppermute | solution.py:591
  27.2 0.3 kv_last.3
  27.5 1.2 %collective-permute-start.12 = (bf16[128,256]{1,0:T(8,128)(2,1)S(1)}, bf16[128,256]{1,0:T(8,128)(2,1)S(1)}, u32[]{:S(2)}, u32[]{:S(2)}) collective-permute-start(bf16[128,256]{1,0:T(8,128)(2,1)S(1)} %get-tuple-element.70.refs_10_), channel_id=1, source_target_pairs={{0,8},{8,0},{1,9},{9,1},{2,10},{10,2},{3,11},{11,3},{4,12},{12,4},... | collective-permute-start | bytes 196616 | tf_op jit(solution)/shard_map/ppermute | solution.py:591
  28.8 1.1 %q_part.2 = (bf16[128,512]{1,0:T(8,128)(2,1)S(1)}, f32[1,512]{1,0:T(1,128)S(1)}, f32[1,512]{1,0:T(1,128)S(1)}, f32[128,512]{1,0:T(8,128)S(1)}) custom-call(bf16[64,512]{1,0:T(8,128)(2,1)S(1)} %get-tuple-element.57.refs_0_, bf16[64,512]{1,0:T(8,128)(2,1)S(1)} %get-tuple-element.58.refs_1_, bf16[64,512]{1,0:T(8,128)(2,1)S(1)} %collective-permute-done.6.refs_2_, ...), custom_call_target="tpu_custom_call" | custom-call | flops 1000000 | bytes 1 | tf_op jit(solution)/shard_map/q_part/pallas_call | solution.py:41
  29.9 0.9 %q_part.3 = (bf16[128,512]{1,0:T(8,128)(2,1)S(1)}, f32[1,512]{1,0:T(1,128)S(1)}, f32[1,512]{1,0:T(1,128)S(1)}, f32[128,512]{1,0:T(8,128)S(1)}) custom-call(bf16[128,512]{1,0:T(8,128)(2,1)S(1)} %get-tuple-element.68.refs_0_, bf16[128,512]{1,0:T(8,128)(2,1)S(1)} %collective-permute-done.11.refs_1_, f32[1,4096]{1,0:T(1,128)S(1)} %get-tuple-element.52.refs_4_.refs_2_, ...), custom_call_target="tpu_custom_call" | custom-call | flops 1000000 | bytes 1 | tf_op jit(solution)/shard_map/q_part/pallas_call | solution.py:41
  30.8 0.7 %attend_more.2 = (f32[1,1024]{1,0:T(1,128)S(1)}, f32[1,1024]{1,0:T(1,128)S(1)}, f32[128,1024]{1,0:T(8,128)S(1)}) custom-call(bf16[128,512]{1,0:T(8,128)(2,1)S(1)} %get-tuple-element.67.qa_ref, bf16[128,512]{1,0:T(8,128)(2,1)S(1)} %get-tuple-element.71.qb_ref, bf16[128,256]{1,0:T(8,128)(2,1)S(1)} %collective-permute-done.13.kv_ref, ...), custom_call_target="tpu_custom_call" | custom-call | flops 400000000 | bytes 1 | tf_op jit(solution)/shard_map/attend_more/pallas_call | solution.py:41
  31.4 0.4 collective-permute-done.12.kv_ref
  31.9 0.7 %attend_more.3 = (bf16[256,512]{1,0:T(8,128)(2,1)S(1)}, bf16[128,512]{1,0:T(8,128)(2,1)S(1)}, bf16[128,512]{1,0:T(8,128)(2,1)S(1)}) custom-call(bf16[128,512]{1,0:T(8,128)(2,1)S(1)} %get-tuple-element.67.qa_ref, bf16[128,512]{1,0:T(8,128)(2,1)S(1)} %get-tuple-element.71.qb_ref, bf16[128,256]{1,0:T(8,128)(2,1)S(1)} %collective-permute-done.12.kv_ref, ...), custom_call_target="tpu_custom_call" | custom-call | flops 400000000 | bytes 1 | tf_op jit(solution)/shard_map/attend_more/pallas_call | solution.py:41
  32.6 3.4 %collective-permute-start.14 = (bf16[256,512]{1,0:T(8,128)(2,1)S(1)}, bf16[256,512]{1,0:T(8,128)(2,1)S(1)}, u32[]{:S(2)}, u32[]{:S(2)}) collective-permute-start(bf16[256,512]{1,0:T(8,128)(2,1)S(1)} %get-tuple-element.81.refs_0_), channel_id=1, source_target_pairs={{0,6},{1,7},{2,4},{3,5},{4,2},{5,3},{6,0},{7,1},{8,14},{9,15},{10,... | collective-permute-start | bytes 786440 | tf_op jit(solution)/shard_map/ppermute | solution.py:130
  36.0 0.5 collective-permute-start.18
  36.6 1.7 %collective-permute-start.20 = (bf16[128,512]{1,0:T(8,128)(2,1)S(1)}, bf16[128,512]{1,0:T(8,128)(2,1)S(1)}, u32[]{:S(2)}, u32[]{:S(2)}) collective-permute-start(bf16[128,512]{1,0:T(8,128)(2,1)S(1)} %get-tuple-element.83), channel_id=1, source_target_pairs={{0,2},{1,3},{2,0},{3,1},{4,6},{5,7},{6,4},{7,5},{8,10},{9,11},{10,... | collective-permute-start | bytes 393224 | tf_op jit(solution)/shard_map/ppermute | solution.py:132
  38.3 5.4 %collective-permute-done.14.refs_0_ = bf16[256,512]{1,0:T(8,128)(2,1)S(1)} collective-permute-done((bf16[256,512]{1,0:T(8,128)(2,1)S(1)}, bf16[256,512]{1,0:T(8,128)(2,1)S(1)}, u32[]{:S(2)}, u32[]{:S(2)}) %collective-permute-start.14) | collective-permute-done | bytes 262176 | tf_op jit(solution)/shard_map/ppermute | solution.py:130
  43.7 4.0 %collective-permute-start.24 = (bf16[128,512]{1,0:T(8,128)(2,1)S(1)}, bf16[128,512]{1,0:T(8,128)(2,1)S(1)}, u32[]{:S(2)}, u32[]{:S(2)}) collective-permute-start(bf16[128,512]{1,0:T(8,128)(2,1)S(1)} %get-tuple-element.93), channel_id=1, source_target_pairs={{0,2},{1,3},{2,0},{3,1},{4,6},{5,7},{6,4},{7,5},{8,10},{9,11},{10,... | collective-permute-start | bytes 393224 | tf_op jit(solution)/shard_map/ppermute | solution.py:134
  47.7 0.1 collective-permute-start.15
  47.8 0.1 collective-permute-done.20.refs_4_
  47.9 2.6 %out_own.1 = (bf16[128,512]{1,0:T(8,128)(2,1)S(1)}, bf16[128,512]{1,0:T(8,128)(2,1)S(1)}, f32[256,512]{1,0:T(8,128)S(1)}, bf16[4096,512]{1,0:T(8,128)(2,1)S(1)}, bf16[1024,512]{1,0:T(8,128)(2,1)S(1)}) custom-call(bf16[256,512]{1,0:T(8,128)(2,1)S(1)} %get-tuple-element.81.refs_0_, ...), custom_call_target="tpu_custom_call", output_to_operand_aliasing={{0}: (3, {}), {1}: (4, {})} | custom-call | flops 400000000 | bytes 1 | tf_op jit(solution)/shard_map/out_own/pallas_call | solution.py:41
  50.5 1.6 %collective-permute-done.24.last_a = bf16[128,512]{1,0:T(8,128)(2,1)S(1)} collective-permute-done((bf16[128,512]{1,0:T(8,128)(2,1)S(1)}, bf16[128,512]{1,0:T(8,128)(2,1)S(1)}, u32[]{:S(2)}, u32[]{:S(2)}) %collective-permute-start.24) | collective-permute-done | bytes 131104 | tf_op jit(solution)/shard_map/ppermute | solution.py:134
  52.1 0.5 out_more.1
  52.6 0.6 collective-permute-start.22
  53.1 0.1 collective-permute-start.23
  53.2 1.5 %collective-permute-done.15.last_b = bf16[128,512]{1,0:T(8,128)(2,1)S(1)} collective-permute-done((bf16[128,512]{1,0:T(8,128)(2,1)S(1)}, bf16[128,512]{1,0:T(8,128)(2,1)S(1)}, u32[]{:S(2)}, u32[]{:S(2)}) %collective-permute-start.15) | collective-permute-done | bytes 131104 | tf_op jit(solution)/shard_map/ppermute | solution.py:134
  54.7 0.7 %out_beside.1.total_ref = f32[256,512]{1,0:T(8,128)S(1)} custom-call(bf16[128,512]{1,0:T(8,128)(2,1)S(1)} %get-tuple-element.88.a, bf16[128,512]{1,0:T(8,128)(2,1)S(1)} %get-tuple-element.89.b, bf16[128,512]{1,0:T(8,128)(2,1)S(1)} %collective-permute-done.22.c, bf16[128,512]{1,0:T(8,128)(2,1)S(1)} %collective-permute-done.23.d, ...), custom_call_target="tpu_custom_call", output_to_operand_aliasing={{}: (8, {})} | custom-call | flops 400000000 | bytes 1 | tf_op jit(solution)/shard_map/out_beside/pallas_call | solution.py:41
  55.4 0.7 %collective-permute-done.16.twin_ref = bf16[128,512]{1,0:T(8,128)(2,1)S(1)} collective-permute-done((bf16[128,512]{1,0:T(8,128)(2,1)S(1)}, bf16[128,512]{1,0:T(8,128)(2,1)S(1)}, u32[]{:S(2)}, u32[]{:S(2)}) %collective-permute-start.16) | collective-permute-done | bytes 131104 | tf_op jit(solution)/shard_map/ppermute | solution.py:138
  56.1 1.4 %out_last.1 = bf16[1024,512]{1,0:T(8,128)(2,1)} custom-call(bf16[128,512]{1,0:T(8,128)(2,1)S(1)} %collective-permute-done.16.twin_ref, bf16[4096,512]{1,0:T(8,128)(2,1)S(1)} %get-tuple-element.84.refs_2_.w_ref, f32[256,512]{1,0:T(8,128)S(1)} %out_beside.1.total_ref, f32[128,256]{1,0:T(8,128)S(1)} %get-tuple-element.63.refs_7_.sa_ref, ...), custom_call_target="tpu_custom_call" | custom-call | flops 400000000 | bytes 1 | tf_op jit(solution)/shard_map/out_last/pallas_call | solution.py:41
  (25 shorter events, 0.1 us)
Async XLA Ops:
  0.0 17.0 %copy-start = (f32[128]{0:T(128)S(1)}, f32[128]{0:T(128)}, u32[]{:S(2)}) copy-start(f32[128]{0:T(128)} %constant.9.clone.1) | copy-start | bytes 1540
  1.6 5.3 %collective-permute-start.4 = (bf16[256,512]{1,0:T(8,128)(2,1)S(1)}, bf16[256,512]{1,0:T(8,128)(2,1)S(1)}, u32[]{:S(2)}, u32[]{:S(2)}) collective-permute-start(bf16[256,512]{1,0:T(8,128)(2,1)S(1)} %get-tuple-element.51.x_ref), channel_id=1, source_target_pairs={{0,1},{1,0},{2,3},{3,2},{4,5},{5,4},{6,7},{7,6},{8,9},{9,8},{10,11... | collective-permute-start | bytes 786440 | tf_op jit(solution)/shard_map/ppermute | solution.py:146
  2.2 8.9 %collective-permute-start = (bf16[128,512]{1,0:T(8,128)(2,1)S(1)}, bf16[128,512]{1,0:T(8,128)(2,1)S(1)}, u32[]{:S(2)}, u32[]{:S(2)}) collective-permute-start(bf16[128,512]{1,0:T(8,128)(2,1)S(1)} %get-tuple-element.49), channel_id=1, source_target_pairs={{0,6},{1,7},{2,4},{3,5},{4,2},{5,3},{6,0},{7,1},{8,14},{9,15},{10,... | collective-permute-start | bytes 393224 | tf_op jit(solution)/shard_map/ppermute | solution.py:145
  6.8 9.9 %collective-permute-start.1 = (bf16[128,512]{1,0:T(8,128)(2,1)S(1)}, bf16[128,512]{1,0:T(8,128)(2,1)S(1)}, u32[]{:S(2)}, u32[]{:S(2)}) collective-permute-start(bf16[128,512]{1,0:T(8,128)(2,1)S(1)} %get-tuple-element.50), channel_id=1, source_target_pairs={{0,6},{1,7},{2,4},{3,5},{4,2},{5,3},{6,0},{7,1},{8,14},{9,15},{10,... | collective-permute-start | bytes 393224 | tf_op jit(solution)/shard_map/ppermute | solution.py:145
  10.3 9.7 %collective-permute-start.8 = (bf16[256,512]{1,0:T(8,128)(2,1)S(1)}, bf16[256,512]{1,0:T(8,128)(2,1)S(1)}, u32[]{:S(2)}, u32[]{:S(2)}) collective-permute-start(bf16[256,512]{1,0:T(8,128)(2,1)S(1)} %get-tuple-element.59), channel_id=1, source_target_pairs={{0,2},{1,3},{2,0},{3,1},{4,6},{5,7},{6,4},{7,5},{8,10},{9,11},{10,... | collective-permute-start | bytes 786440 | tf_op jit(solution)/shard_map/ppermute | solution.py:146
  11.0 8.9 %collective-permute-start.2 = (bf16[128,512]{1,0:T(8,128)(2,1)S(1)}, bf16[128,512]{1,0:T(8,128)(2,1)S(1)}, u32[]{:S(2)}, u32[]{:S(2)}) collective-permute-start(bf16[128,512]{1,0:T(8,128)(2,1)S(1)} %collective-permute-done.refs_0_), channel_id=1, source_target_pairs={{0,1},{1,0},{2,3},{3,2},{4,5},{5,4},{6,7},{7,6},{8,9},{9,8},{10,11... | collective-permute-start | bytes 393224 | tf_op jit(solution)/shard_map/ppermute | solution.py:148
  11.1 11.7 %collective-permute-start.5 = (bf16[128,512]{1,0:T(8,128)(2,1)S(1)}, bf16[128,512]{1,0:T(8,128)(2,1)S(1)}, u32[]{:S(2)}, u32[]{:S(2)}) collective-permute-start(bf16[128,512]{1,0:T(8,128)(2,1)S(1)} %collective-permute-done.refs_0_), channel_id=1, source_target_pairs={{0,2},{1,3},{2,0},{3,1},{4,6},{5,7},{6,4},{7,5},{8,10},{9,11},{10,... | collective-permute-start | bytes 393224 | tf_op jit(solution)/shard_map/ppermute | solution.py:147
  16.7 3.2 %collective-permute-start.3 = (bf16[128,512]{1,0:T(8,128)(2,1)S(1)}, bf16[128,512]{1,0:T(8,128)(2,1)S(1)}, u32[]{:S(2)}, u32[]{:S(2)}) collective-permute-start(bf16[128,512]{1,0:T(8,128)(2,1)S(1)} %collective-permute-done.1.refs_1_), channel_id=1, source_target_pairs={{0,1},{1,0},{2,3},{3,2},{4,5},{5,4},{6,7},{7,6},{8,9},{9,8},{10,11... | collective-permute-start | bytes 393224 | tf_op jit(solution)/shard_map/ppermute | solution.py:148
  17.5 8.1 %collective-permute-start.10 = (bf16[128,512]{1,0:T(8,128)(2,1)S(1)}, bf16[128,512]{1,0:T(8,128)(2,1)S(1)}, u32[]{:S(2)}, u32[]{:S(2)}) collective-permute-start(bf16[128,512]{1,0:T(8,128)(2,1)S(1)} %collective-permute-done.1.refs_1_), channel_id=1, source_target_pairs={{0,2},{1,3},{2,0},{3,1},{4,6},{5,7},{6,4},{7,5},{8,10},{9,11},{10,... | collective-permute-start | bytes 393224 | tf_op jit(solution)/shard_map/ppermute | solution.py:147
  20.0 4.1 %collective-permute-start.9 = (bf16[256,512]{1,0:T(8,128)(2,1)S(1)}, bf16[256,512]{1,0:T(8,128)(2,1)S(1)}, u32[]{:S(2)}, u32[]{:S(2)}) collective-permute-start(bf16[256,512]{1,0:T(8,128)(2,1)S(1)} %collective-permute-done.8.refs_0_), channel_id=1, source_target_pairs={{0,1},{1,0},{2,3},{3,2},{4,5},{5,4},{6,7},{7,6},{8,9},{9,8},{10,11... | collective-permute-start | bytes 786440 | tf_op jit(solution)/shard_map/ppermute | solution.py:149
  23.4 1.3 %collective-permute-start.6 = (bf16[64,512]{1,0:T(8,128)(2,1)S(1)}, bf16[64,512]{1,0:T(8,128)(2,1)S(1)}, u32[]{:S(2)}, u32[]{:S(2)}) collective-permute-start(bf16[64,512]{1,0:T(8,128)(2,1)S(1)} %get-tuple-element.57.refs_0_), channel_id=1, source_target_pairs={{0,1},{1,0},{2,3},{3,2},{4,5},{5,4},{6,7},{7,6},{8,9},{9,8},{10,11... | collective-permute-start | bytes 196616 | tf_op jit(solution)/shard_map/ppermute | solution.py:150
  23.5 1.4 %collective-permute-start.7 = (bf16[64,512]{1,0:T(8,128)(2,1)S(1)}, bf16[64,512]{1,0:T(8,128)(2,1)S(1)}, u32[]{:S(2)}, u32[]{:S(2)}) collective-permute-start(bf16[64,512]{1,0:T(8,128)(2,1)S(1)} %get-tuple-element.58.refs_1_), channel_id=1, source_target_pairs={{0,1},{1,0},{2,3},{3,2},{4,5},{5,4},{6,7},{7,6},{8,9},{9,8},{10,11... | collective-permute-start | bytes 196616 | tf_op jit(solution)/shard_map/ppermute | solution.py:150
  25.5 1.7 %collective-permute-start.11 = (bf16[128,512]{1,0:T(8,128)(2,1)S(1)}, bf16[128,512]{1,0:T(8,128)(2,1)S(1)}, u32[]{:S(2)}, u32[]{:S(2)}) collective-permute-start(bf16[128,512]{1,0:T(8,128)(2,1)S(1)} %get-tuple-element.68.refs_0_), channel_id=1, source_target_pairs={{0,1},{1,0},{2,3},{3,2},{4,5},{5,4},{6,7},{7,6},{8,9},{9,8},{10,11... | collective-permute-start | bytes 393224 | tf_op jit(solution)/shard_map/ppermute | solution.py:586
  25.7 5.1 %collective-permute-start.13 = (bf16[128,256]{1,0:T(8,128)(2,1)S(1)}, bf16[128,256]{1,0:T(8,128)(2,1)S(1)}, u32[]{:S(2)}, u32[]{:S(2)}) collective-permute-start(bf16[128,256]{1,0:T(8,128)(2,1)S(1)} %get-tuple-element.66.refs_11_.refs_9_), channel_id=1, source_target_pairs={{0,8},{8,0},{1,9},{9,1},{2,10},{10,2},{3,11},{11,3},{4,12},{12,4},... | collective-permute-start | bytes 196616 | tf_op jit(solution)/shard_map/ppermute | solution.py:591
  27.5 4.3 %collective-permute-start.12 = (bf16[128,256]{1,0:T(8,128)(2,1)S(1)}, bf16[128,256]{1,0:T(8,128)(2,1)S(1)}, u32[]{:S(2)}, u32[]{:S(2)}) collective-permute-start(bf16[128,256]{1,0:T(8,128)(2,1)S(1)} %get-tuple-element.70.refs_10_), channel_id=1, source_target_pairs={{0,8},{8,0},{1,9},{9,1},{2,10},{10,2},{3,11},{11,3},{4,12},{12,4},... | collective-permute-start | bytes 196616 | tf_op jit(solution)/shard_map/ppermute | solution.py:591
  32.6 11.1 %collective-permute-start.14 = (bf16[256,512]{1,0:T(8,128)(2,1)S(1)}, bf16[256,512]{1,0:T(8,128)(2,1)S(1)}, u32[]{:S(2)}, u32[]{:S(2)}) collective-permute-start(bf16[256,512]{1,0:T(8,128)(2,1)S(1)} %get-tuple-element.81.refs_0_), channel_id=1, source_target_pairs={{0,6},{1,7},{2,4},{3,5},{4,2},{5,3},{6,0},{7,1},{8,14},{9,15},{10,... | collective-permute-start | bytes 786440 | tf_op jit(solution)/shard_map/ppermute | solution.py:130
  36.0 7.7 %collective-permute-start.17 = (bf16[128,512]{1,0:T(8,128)(2,1)S(1)}, bf16[128,512]{1,0:T(8,128)(2,1)S(1)}, u32[]{:S(2)}, u32[]{:S(2)}) collective-permute-start(bf16[128,512]{1,0:T(8,128)(2,1)S(1)} %get-tuple-element.82), channel_id=1, source_target_pairs={{0,1},{1,0},{2,3},{3,2},{4,5},{5,4},{6,7},{7,6},{8,9},{9,8},{10,11... | collective-permute-start | bytes 393224 | tf_op jit(solution)/shard_map/ppermute | solution.py:131
  36.0 11.8 %collective-permute-start.19 = (bf16[128,512]{1,0:T(8,128)(2,1)S(1)}, bf16[128,512]{1,0:T(8,128)(2,1)S(1)}, u32[]{:S(2)}, u32[]{:S(2)}) collective-permute-start(bf16[128,512]{1,0:T(8,128)(2,1)S(1)} %get-tuple-element.82), channel_id=1, source_target_pairs={{0,2},{1,3},{2,0},{3,1},{4,6},{5,7},{6,4},{7,5},{8,10},{9,11},{10,... | collective-permute-start | bytes 393224 | tf_op jit(solution)/shard_map/ppermute | solution.py:132
  36.0 11.7 %collective-permute-start.18 = (bf16[128,512]{1,0:T(8,128)(2,1)S(1)}, bf16[128,512]{1,0:T(8,128)(2,1)S(1)}, u32[]{:S(2)}, u32[]{:S(2)}) collective-permute-start(bf16[128,512]{1,0:T(8,128)(2,1)S(1)} %get-tuple-element.83), channel_id=1, source_target_pairs={{0,1},{1,0},{2,3},{3,2},{4,5},{5,4},{6,7},{7,6},{8,9},{9,8},{10,11... | collective-permute-start | bytes 393224 | tf_op jit(solution)/shard_map/ppermute | solution.py:131
  36.6 11.3 %collective-permute-start.20 = (bf16[128,512]{1,0:T(8,128)(2,1)S(1)}, bf16[128,512]{1,0:T(8,128)(2,1)S(1)}, u32[]{:S(2)}, u32[]{:S(2)}) collective-permute-start(bf16[128,512]{1,0:T(8,128)(2,1)S(1)} %get-tuple-element.83), channel_id=1, source_target_pairs={{0,2},{1,3},{2,0},{3,1},{4,6},{5,7},{6,4},{7,5},{8,10},{9,11},{10,... | collective-permute-start | bytes 393224 | tf_op jit(solution)/shard_map/ppermute | solution.py:132
  43.7 8.4 %collective-permute-start.21 = (bf16[256,512]{1,0:T(8,128)(2,1)S(1)}, bf16[256,512]{1,0:T(8,128)(2,1)S(1)}, u32[]{:S(2)}, u32[]{:S(2)}) collective-permute-start(bf16[256,512]{1,0:T(8,128)(2,1)S(1)} %collective-permute-done.14.refs_0_), channel_id=1, source_target_pairs={{0,1},{1,0},{2,3},{3,2},{4,5},{5,4},{6,7},{7,6},{8,9},{9,8},{10,11... | collective-permute-start | bytes 786440 | tf_op jit(solution)/shard_map/ppermute | solution.py:136
  43.7 8.3 %collective-permute-start.24 = (bf16[128,512]{1,0:T(8,128)(2,1)S(1)}, bf16[128,512]{1,0:T(8,128)(2,1)S(1)}, u32[]{:S(2)}, u32[]{:S(2)}) collective-permute-start(bf16[128,512]{1,0:T(8,128)(2,1)S(1)} %get-tuple-element.93), channel_id=1, source_target_pairs={{0,2},{1,3},{2,0},{3,1},{4,6},{5,7},{6,4},{7,5},{8,10},{9,11},{10,... | collective-permute-start | bytes 393224 | tf_op jit(solution)/shard_map/ppermute | solution.py:134
  47.7 7.0 %collective-permute-start.15 = (bf16[128,512]{1,0:T(8,128)(2,1)S(1)}, bf16[128,512]{1,0:T(8,128)(2,1)S(1)}, u32[]{:S(2)}, u32[]{:S(2)}) collective-permute-start(bf16[128,512]{1,0:T(8,128)(2,1)S(1)} %get-tuple-element.94), channel_id=1, source_target_pairs={{0,2},{1,3},{2,0},{3,1},{4,6},{5,7},{6,4},{7,5},{8,10},{9,11},{10,... | collective-permute-start | bytes 393224 | tf_op jit(solution)/shard_map/ppermute | solution.py:134
  52.1 2.6 %collective-permute-start.25 = (bf16[128,512]{1,0:T(8,128)(2,1)S(1)}, bf16[128,512]{1,0:T(8,128)(2,1)S(1)}, u32[]{:S(2)}, u32[]{:S(2)}) collective-permute-start(bf16[128,512]{1,0:T(8,128)(2,1)S(1)} %collective-permute-done.24.last_a), channel_id=1, source_target_pairs={{0,1},{1,0},{2,3},{3,2},{4,5},{5,4},{6,7},{7,6},{8,9},{9,8},{10,11... | collective-permute-start | bytes 393224 | tf_op jit(solution)/shard_map/ppermute | solution.py:137
  52.6 2.2 %collective-permute-start.22 = (bf16[128,512]{1,0:T(8,128)(2,1)S(1)}, bf16[128,512]{1,0:T(8,128)(2,1)S(1)}, u32[]{:S(2)}, u32[]{:S(2)}) collective-permute-start(bf16[128,512]{1,0:T(8,128)(2,1)S(1)} %get-tuple-element.88.a), channel_id=1, source_target_pairs={{0,1},{1,0},{2,3},{3,2},{4,5},{5,4},{6,7},{7,6},{8,9},{9,8},{10,11... | collective-permute-start | bytes 393224 | tf_op jit(solution)/shard_map/ppermute | solution.py:137
  53.1 1.6 %collective-permute-start.23 = (bf16[128,512]{1,0:T(8,128)(2,1)S(1)}, bf16[128,512]{1,0:T(8,128)(2,1)S(1)}, u32[]{:S(2)}, u32[]{:S(2)}) collective-permute-start(bf16[128,512]{1,0:T(8,128)(2,1)S(1)} %get-tuple-element.89.b), channel_id=1, source_target_pairs={{0,1},{1,0},{2,3},{3,2},{4,5},{5,4},{6,7},{7,6},{8,9},{9,8},{10,11... | collective-permute-start | bytes 393224 | tf_op jit(solution)/shard_map/ppermute | solution.py:137
  54.7 1.3 %collective-permute-start.16 = (bf16[128,512]{1,0:T(8,128)(2,1)S(1)}, bf16[128,512]{1,0:T(8,128)(2,1)S(1)}, u32[]{:S(2)}, u32[]{:S(2)}) collective-permute-start(bf16[128,512]{1,0:T(8,128)(2,1)S(1)} %collective-permute-done.15.last_b), channel_id=1, source_target_pairs={{0,1},{1,0},{2,3},{3,2},{4,5},{5,4},{6,7},{7,6},{8,9},{9,8},{10,11... | collective-permute-start | bytes 393224 | tf_op jit(solution)/shard_map/ppermute | solution.py:138

commit v13 on v10

--- a/solution.py
+++ b/solution.py
@@ -77,13 +77,13 @@
     own, shards = lax.axis_index("ctx"), lax.axis_size("ctx")
     tok, cap = hid_ref.shape[0], x_ref.shape[0]
     pieces = [slice(at, at + 256) for at in range(0, tok, 256)]
-    copies = fetch([(pos_hbm, pos_ref), *((hid_hbm.at[p, :], hid_ref.at[p, :]) for p in pieces)], sems)
-    copies[0].wait()
+    copies = fetch([*((hid_hbm.at[p, :], hid_ref.at[p, :]) for p in pieces), (pos_hbm, pos_ref)], sems)
+    copies[-1].wait()
     pos = column(pos_ref[pl.ds(own, 1), :])
     rowpos_ref[...] = jnp.where(pos < 0, shards * tok, pos)
     local = pos[:, :1] - own * tok
     total = None
-    for piece, copy in zip(pieces, copies[1:]):
+    for piece, copy in zip(pieces, copies):
         at = lax.broadcasted_iota(I32, (cap, 256), 1) + piece.start
         hot = jnp.where(at == local, 1.0, 0.0).astype(BF16)
         copy.wait()

time: 57.8 us -> 58 us (level)
  no operation moved by 1% of the time
where the time goes in v13:
time: 58 us; the launch traced here: 57.7 us
  starting transfers between devices  27.4 us (47%)
  Pallas kernels  15.7 us (27%)
  waiting for transfers between devices  13.8 us (24%)
    pallas_call x15, Pallas kernels, call(): pl.pallas_call(kernel, out_shape=out_shape, in_specs=[HBM if far else VME...  15.7 us
    ppermute x2, starting transfers between devices, spread_halves(): last_a, last_b = (near(far[0]), near(far[1]))  7.88 us
    ppermute x1, waiting for transfers between devices, spread(): far = cross(full)  5.42 us
    ppermute x2, starting transfers between devices, spread_halves(): far = (cross(first), cross(second))  4.78 us
    ppermute x2, starting transfers between devices, spread(): last = (near(far[:half]), near(far[half:]))  4.08 us
    ppermute x1, starting transfers between devices, spread(): far = cross(full)  3.43 us
    ppermute x2, waiting for transfers between devices, spread(): last = (near(far[:half]), near(far[half:]))  3.07 us
    ppermute x2, waiting for transfers between devices, spread_halves(): last_a, last_b = (near(far[0]), near(far[1]))  3.04 us
  transfers between devices with their start and end apart: 26, of which 12 were waited for; matrix products, arithmetic and copies ran while one was open for 1% of the time, Pallas kernels for 20%

profile of v13, /device:TPU:0, one launch (start us, length us, event | category | flops | bytes accessed | tf_op | source)
XLA Modules:
  0.0 57.7 jit_solution(9122212564458585405)
XLA Ops:
  0.0 1.8 %pick.1 = (bf16[256,512]{1,0:T(8,128)(2,1)S(1)}, bf16[128,512]{1,0:T(8,128)(2,1)S(1)}, bf16[128,512]{1,0:T(8,128)(2,1)S(1)}, s32[256,128]{1,0:T(8,128)S(1)}) custom-call(s32[2,256]{1,0:T(2,128)} %pos.1, bf16[1024,512]{1,0:T(8,128)(2,1)} %refs_6_.1), custom_call_target="tpu_custom_call" | custom-call | flops 400000000 | bytes 1 | tf_op jit(solution)/shard_map/pick/pallas_call | solution.py:41
  1.8 0.5 collective-permute-start.4
  2.3 4.7 %collective-permute-start = (bf16[128,512]{1,0:T(8,128)(2,1)S(1)}, bf16[128,512]{1,0:T(8,128)(2,1)S(1)}, u32[]{:S(2)}, u32[]{:S(2)}) collective-permute-start(bf16[128,512]{1,0:T(8,128)(2,1)S(1)} %get-tuple-element.49), channel_id=1, source_target_pairs={{0,6},{1,7},{2,4},{3,5},{4,2},{5,3},{6,0},{7,1},{8,14},{9,15},{10,... | collective-permute-start | bytes 393224 | tf_op jit(solution)/shard_map/ppermute | solution.py:145
  7.0 0.1 collective-permute-start.1
  7.1 0.0 collective-permute-done.4.twin_ref
  7.1 3.3 %own_part.1 = (bf16[256,512]{1,0:T(8,128)(2,1)S(1)}, f32[256,1024]{1,0:T(8,128)S(1)}, f32[1,4096]{1,0:T(1,128)S(1)}, f32[1,4096]{1,0:T(1,128)S(1)}, bf16[4096,76...) custom-call(bf16[256,512]{1,0:T(8,128)(2,1)S(1)} %get-tuple-element., ...), custom_call_target="tpu_custom_call", output_to_operand_aliasing={{0}: (0, {})} | custom-call | flops 1500000000 | bytes 1 | tf_op jit(solution)/shard_map/own_part/pallas_call | solution.py:41
  10.4 0.1 collective-permute-start.8
  10.5 0.1 pad_maximum_fusion
  10.6 0.6 %collective-permute-done.refs_0_ = bf16[128,512]{1,0:T(8,128)(2,1)S(1)} collective-permute-done((bf16[128,512]{1,0:T(8,128)(2,1)S(1)}, bf16[128,512]{1,0:T(8,128)(2,1)S(1)}, u32[]{:S(2)}, u32[]{:S(2)}) %collective-permute-start) | collective-permute-done | bytes 131104 | tf_op jit(solution)/shard_map/ppermute | solution.py:145
  11.2 5.7 %collective-permute-start.5 = (bf16[128,512]{1,0:T(8,128)(2,1)S(1)}, bf16[128,512]{1,0:T(8,128)(2,1)S(1)}, u32[]{:S(2)}, u32[]{:S(2)}) collective-permute-start(bf16[128,512]{1,0:T(8,128)(2,1)S(1)} %collective-permute-done.refs_0_), channel_id=1, source_target_pairs={{0,2},{1,3},{2,0},{3,1},{4,6},{5,7},{6,4},{7,5},{8,10},{9,11},{10,... | collective-permute-start | bytes 393224 | tf_op jit(solution)/shard_map/ppermute | solution.py:147
  16.9 0.2 collective-permute-start.3
  17.1 0.5 sine_multiply_fusion
  17.6 2.2 %collective-permute-start.10 = (bf16[128,512]{1,0:T(8,128)(2,1)S(1)}, bf16[128,512]{1,0:T(8,128)(2,1)S(1)}, u32[]{:S(2)}, u32[]{:S(2)}) collective-permute-start(bf16[128,512]{1,0:T(8,128)(2,1)S(1)} %collective-permute-done.1.refs_1_), channel_id=1, source_target_pairs={{0,2},{1,3},{2,0},{3,1},{4,6},{5,7},{6,4},{7,5},{8,10},{9,11},{10,... | collective-permute-start | bytes 393224 | tf_op jit(solution)/shard_map/ppermute | solution.py:147
  19.8 0.3 collective-permute-done.8.refs_0_
  20.1 2.8 %collective-permute-done.5.refs_10_ = bf16[128,512]{1,0:T(8,128)(2,1)S(1)} collective-permute-done((bf16[128,512]{1,0:T(8,128)(2,1)S(1)}, bf16[128,512]{1,0:T(8,128)(2,1)S(1)}, u32[]{:S(2)}, u32[]{:S(2)}) %collective-permute-start.5) | collective-permute-done | bytes 131104 | tf_op jit(solution)/shard_map/ppermute | solution.py:147
  22.9 0.7 %more_part.2 = (f32[256,1024]{1,0:T(8,128)S(1)}, f32[256,128]{1,0:T(8,128)S(1)}, f32[256,128]{1,0:T(8,128)S(1)}, bf16[64,512]{1,0:T(8,128)(2,1)S(1)}, bf16[64,512]{1,0:T(8,128)(2,1)S(1)}) custom-call(bf16[128,512]{1,0:T(8,128)(2,1)S(1)} %collective-permute-done.refs_0_, ...), custom_call_target="tpu_custom_call", output_to_operand_aliasing={{0}: (7, {}), {1}: (8, {}), {2}: (9, {})} | custom-call | flops 3000000000 | bytes 1 | tf_op jit(solution)/shard_map/more_part/pallas_call | solution.py:41
  23.6 0.1 collective-permute-start.6
  23.7 0.5 collective-permute-start.7
  24.2 0.7 %more_part.3.refs_7_.refs_6_.refs_5_.refs_4_ = f32[256,1024]{1,0:T(8,128)S(1)} custom-call(bf16[256,512]{1,0:T(8,128)(2,1)S(1)} %collective-permute-done.8.refs_0_, bf16[256,512]{1,0:T(8,128)(2,1)S(1)} %collective-permute-done.9.refs_1_, f32[1,4096]{1,0:T(1,128)S(1)} %get-tuple-element.52.refs_4_.refs_2_, ...), custom_call_target="tpu_custom_call", output_to_operand_aliasing={{}: (5, {})} | custom-call | flops 1000000 | bytes 1 | tf_op jit(solution)/shard_map/more_part/pallas_call | solution.py:41
  24.9 0.1 collective-permute-done.6.refs_2_
  24.9 0.2 collective-permute-done.7.refs_3_
  25.1 0.3 kv_last.2
  25.4 0.2 collective-permute-done.10.__1_
  25.6 0.2 collective-permute-start.11
  25.8 1.5 %collective-permute-start.13 = (bf16[128,256]{1,0:T(8,128)(2,1)S(1)}, bf16[128,256]{1,0:T(8,128)(2,1)S(1)}, u32[]{:S(2)}, u32[]{:S(2)}) collective-permute-start(bf16[128,256]{1,0:T(8,128)(2,1)S(1)} %get-tuple-element.66.refs_11_.refs_9_), channel_id=1, source_target_pairs={{0,8},{8,0},{1,9},{9,1},{2,10},{10,2},{3,11},{11,3},{4,12},{12,4},... | collective-permute-start | bytes 196616 | tf_op jit(solution)/shard_map/ppermute | solution.py:591
  27.3 0.3 kv_last.3
  27.7 1.2 %collective-permute-start.12 = (bf16[128,256]{1,0:T(8,128)(2,1)S(1)}, bf16[128,256]{1,0:T(8,128)(2,1)S(1)}, u32[]{:S(2)}, u32[]{:S(2)}) collective-permute-start(bf16[128,256]{1,0:T(8,128)(2,1)S(1)} %get-tuple-element.70.refs_10_), channel_id=1, source_target_pairs={{0,8},{8,0},{1,9},{9,1},{2,10},{10,2},{3,11},{11,3},{4,12},{12,4},... | collective-permute-start | bytes 196616 | tf_op jit(solution)/shard_map/ppermute | solution.py:591
  28.9 1.1 %q_part.2 = (bf16[128,512]{1,0:T(8,128)(2,1)S(1)}, f32[1,512]{1,0:T(1,128)S(1)}, f32[1,512]{1,0:T(1,128)S(1)}, f32[128,512]{1,0:T(8,128)S(1)}) custom-call(bf16[64,512]{1,0:T(8,128)(2,1)S(1)} %get-tuple-element.57.refs_0_, bf16[64,512]{1,0:T(8,128)(2,1)S(1)} %get-tuple-element.58.refs_1_, bf16[64,512]{1,0:T(8,128)(2,1)S(1)} %collective-permute-done.6.refs_2_, ...), custom_call_target="tpu_custom_call" | custom-call | flops 1000000 | bytes 1 | tf_op jit(solution)/shard_map/q_part/pallas_call | solution.py:41
  30.0 0.9 %q_part.3 = (bf16[128,512]{1,0:T(8,128)(2,1)S(1)}, f32[1,512]{1,0:T(1,128)S(1)}, f32[1,512]{1,0:T(1,128)S(1)}, f32[128,512]{1,0:T(8,128)S(1)}) custom-call(bf16[128,512]{1,0:T(8,128)(2,1)S(1)} %get-tuple-element.68.refs_0_, bf16[128,512]{1,0:T(8,128)(2,1)S(1)} %collective-permute-done.11.refs_1_, f32[1,4096]{1,0:T(1,128)S(1)} %get-tuple-element.52.refs_4_.refs_2_, ...), custom_call_target="tpu_custom_call" | custom-call | flops 1000000 | bytes 1 | tf_op jit(solution)/shard_map/q_part/pallas_call | solution.py:41
  30.9 0.7 %attend_more.2 = (f32[1,1024]{1,0:T(1,128)S(1)}, f32[1,1024]{1,0:T(1,128)S(1)}, f32[128,1024]{1,0:T(8,128)S(1)}) custom-call(bf16[128,512]{1,0:T(8,128)(2,1)S(1)} %get-tuple-element.67.qa_ref, bf16[128,512]{1,0:T(8,128)(2,1)S(1)} %get-tuple-element.71.qb_ref, bf16[128,256]{1,0:T(8,128)(2,1)S(1)} %collective-permute-done.13.kv_ref, ...), custom_call_target="tpu_custom_call" | custom-call | flops 400000000 | bytes 1 | tf_op jit(solution)/shard_map/attend_more/pallas_call | solution.py:41
  31.6 0.4 collective-permute-done.12.kv_ref
  32.0 0.7 %attend_more.3 = (bf16[256,512]{1,0:T(8,128)(2,1)S(1)}, bf16[128,512]{1,0:T(8,128)(2,1)S(1)}, bf16[128,512]{1,0:T(8,128)(2,1)S(1)}) custom-call(bf16[128,512]{1,0:T(8,128)(2,1)S(1)} %get-tuple-element.67.qa_ref, bf16[128,512]{1,0:T(8,128)(2,1)S(1)} %get-tuple-element.71.qb_ref, bf16[128,256]{1,0:T(8,128)(2,1)S(1)} %collective-permute-done.12.kv_ref, ...), custom_call_target="tpu_custom_call" | custom-call | flops 400000000 | bytes 1 | tf_op jit(solution)/shard_map/attend_more/pallas_call | solution.py:41
  32.8 3.4 %collective-permute-start.14 = (bf16[256,512]{1,0:T(8,128)(2,1)S(1)}, bf16[256,512]{1,0:T(8,128)(2,1)S(1)}, u32[]{:S(2)}, u32[]{:S(2)}) collective-permute-start(bf16[256,512]{1,0:T(8,128)(2,1)S(1)} %get-tuple-element.81.refs_0_), channel_id=1, source_target_pairs={{0,6},{1,7},{2,4},{3,5},{4,2},{5,3},{6,0},{7,1},{8,14},{9,15},{10,... | collective-permute-start | bytes 786440 | tf_op jit(solution)/shard_map/ppermute | solution.py:130
  36.2 0.5 collective-permute-start.18
  36.7 1.7 %collective-permute-start.20 = (bf16[128,512]{1,0:T(8,128)(2,1)S(1)}, bf16[128,512]{1,0:T(8,128)(2,1)S(1)}, u32[]{:S(2)}, u32[]{:S(2)}) collective-permute-start(bf16[128,512]{1,0:T(8,128)(2,1)S(1)} %get-tuple-element.83), channel_id=1, source_target_pairs={{0,2},{1,3},{2,0},{3,1},{4,6},{5,7},{6,4},{7,5},{8,10},{9,11},{10,... | collective-permute-start | bytes 393224 | tf_op jit(solution)/shard_map/ppermute | solution.py:132
  38.5 5.4 %collective-permute-done.14.refs_0_ = bf16[256,512]{1,0:T(8,128)(2,1)S(1)} collective-permute-done((bf16[256,512]{1,0:T(8,128)(2,1)S(1)}, bf16[256,512]{1,0:T(8,128)(2,1)S(1)}, u32[]{:S(2)}, u32[]{:S(2)}) %collective-permute-start.14) | collective-permute-done | bytes 262176 | tf_op jit(solution)/shard_map/ppermute | solution.py:130
  43.9 4.0 %collective-permute-start.24 = (bf16[128,512]{1,0:T(8,128)(2,1)S(1)}, bf16[128,512]{1,0:T(8,128)(2,1)S(1)}, u32[]{:S(2)}, u32[]{:S(2)}) collective-permute-start(bf16[128,512]{1,0:T(8,128)(2,1)S(1)} %get-tuple-element.93), channel_id=1, source_target_pairs={{0,2},{1,3},{2,0},{3,1},{4,6},{5,7},{6,4},{7,5},{8,10},{9,11},{10,... | collective-permute-start | bytes 393224 | tf_op jit(solution)/shard_map/ppermute | solution.py:134
  47.9 0.1 collective-permute-start.15
  48.0 0.1 collective-permute-done.20.refs_4_
  48.0 2.6 %out_own.1 = (bf16[128,512]{1,0:T(8,128)(2,1)S(1)}, bf16[128,512]{1,0:T(8,128)(2,1)S(1)}, f32[256,512]{1,0:T(8,128)S(1)}, bf16[4096,512]{1,0:T(8,128)(2,1)S(1)}, bf16[1024,512]{1,0:T(8,128)(2,1)S(1)}) custom-call(bf16[256,512]{1,0:T(8,128)(2,1)S(1)} %get-tuple-element.81.refs_0_, ...), custom_call_target="tpu_custom_call", output_to_operand_aliasing={{0}: (3, {}), {1}: (4, {})} | custom-call | flops 400000000 | bytes 1 | tf_op jit(solution)/shard_map/out_own/pallas_call | solution.py:41
  50.7 1.6 %collective-permute-done.24.last_a = bf16[128,512]{1,0:T(8,128)(2,1)S(1)} collective-permute-done((bf16[128,512]{1,0:T(8,128)(2,1)S(1)}, bf16[128,512]{1,0:T(8,128)(2,1)S(1)}, u32[]{:S(2)}, u32[]{:S(2)}) %collective-permute-start.24) | collective-permute-done | bytes 131104 | tf_op jit(solution)/shard_map/ppermute | solution.py:134
  52.3 0.5 out_more.1
  52.7 0.6 collective-permute-start.22
  53.3 0.1 collective-permute-start.23
  53.4 1.5 %collective-permute-done.15.last_b = bf16[128,512]{1,0:T(8,128)(2,1)S(1)} collective-permute-done((bf16[128,512]{1,0:T(8,128)(2,1)S(1)}, bf16[128,512]{1,0:T(8,128)(2,1)S(1)}, u32[]{:S(2)}, u32[]{:S(2)}) %collective-permute-start.15) | collective-permute-done | bytes 131104 | tf_op jit(solution)/shard_map/ppermute | solution.py:134
  54.9 0.7 %out_beside.1.total_ref = f32[256,512]{1,0:T(8,128)S(1)} custom-call(bf16[128,512]{1,0:T(8,128)(2,1)S(1)} %get-tuple-element.88.a, bf16[128,512]{1,0:T(8,128)(2,1)S(1)} %get-tuple-element.89.b, bf16[128,512]{1,0:T(8,128)(2,1)S(1)} %collective-permute-done.22.c, bf16[128,512]{1,0:T(8,128)(2,1)S(1)} %collective-permute-done.23.d, ...), custom_call_target="tpu_custom_call", output_to_operand_aliasing={{}: (8, {})} | custom-call | flops 400000000 | bytes 1 | tf_op jit(solution)/shard_map/out_beside/pallas_call | solution.py:41
  55.6 0.7 %collective-permute-done.16.twin_ref = bf16[128,512]{1,0:T(8,128)(2,1)S(1)} collective-permute-done((bf16[128,512]{1,0:T(8,128)(2,1)S(1)}, bf16[128,512]{1,0:T(8,128)(2,1)S(1)}, u32[]{:S(2)}, u32[]{:S(2)}) %collective-permute-start.16) | collective-permute-done | bytes 131104 | tf_op jit(solution)/shard_map/ppermute | solution.py:138
  56.2 1.4 %out_last.1 = bf16[1024,512]{1,0:T(8,128)(2,1)} custom-call(bf16[128,512]{1,0:T(8,128)(2,1)S(1)} %collective-permute-done.16.twin_ref, bf16[4096,512]{1,0:T(8,128)(2,1)S(1)} %get-tuple-element.84.refs_2_.w_ref, f32[256,512]{1,0:T(8,128)S(1)} %out_beside.1.total_ref, f32[128,256]{1,0:T(8,128)S(1)} %get-tuple-element.63.refs_7_.sa_ref, ...), custom_call_target="tpu_custom_call" | custom-call | flops 400000000 | bytes 1 | tf_op jit(solution)/shard_map/out_last/pallas_call | solution.py:41
  (25 shorter events, 0.1 us)
Async XLA Ops:
  0.0 17.1 %copy-start = (f32[128]{0:T(128)S(1)}, f32[128]{0:T(128)}, u32[]{:S(2)}) copy-start(f32[128]{0:T(128)} %constant.9.clone.1) | copy-start | bytes 1540
  1.8 5.3 %collective-permute-start.4 = (bf16[256,512]{1,0:T(8,128)(2,1)S(1)}, bf16[256,512]{1,0:T(8,128)(2,1)S(1)}, u32[]{:S(2)}, u32[]{:S(2)}) collective-permute-start(bf16[256,512]{1,0:T(8,128)(2,1)S(1)} %get-tuple-element.51.x_ref), channel_id=1, source_target_pairs={{0,1},{1,0},{2,3},{3,2},{4,5},{5,4},{6,7},{7,6},{8,9},{9,8},{10,11... | collective-permute-start | bytes 786440 | tf_op jit(solution)/shard_map/ppermute | solution.py:146
  2.3 8.9 %collective-permute-start = (bf16[128,512]{1,0:T(8,128)(2,1)S(1)}, bf16[128,512]{1,0:T(8,128)(2,1)S(1)}, u32[]{:S(2)}, u32[]{:S(2)}) collective-permute-start(bf16[128,512]{1,0:T(8,128)(2,1)S(1)} %get-tuple-element.49), channel_id=1, source_target_pairs={{0,6},{1,7},{2,4},{3,5},{4,2},{5,3},{6,0},{7,1},{8,14},{9,15},{10,... | collective-permute-start | bytes 393224 | tf_op jit(solution)/shard_map/ppermute | solution.py:145
  7.0 9.9 %collective-permute-start.1 = (bf16[128,512]{1,0:T(8,128)(2,1)S(1)}, bf16[128,512]{1,0:T(8,128)(2,1)S(1)}, u32[]{:S(2)}, u32[]{:S(2)}) collective-permute-start(bf16[128,512]{1,0:T(8,128)(2,1)S(1)} %get-tuple-element.50), channel_id=1, source_target_pairs={{0,6},{1,7},{2,4},{3,5},{4,2},{5,3},{6,0},{7,1},{8,14},{9,15},{10,... | collective-permute-start | bytes 393224 | tf_op jit(solution)/shard_map/ppermute | solution.py:145
  10.4 9.7 %collective-permute-start.8 = (bf16[256,512]{1,0:T(8,128)(2,1)S(1)}, bf16[256,512]{1,0:T(8,128)(2,1)S(1)}, u32[]{:S(2)}, u32[]{:S(2)}) collective-permute-start(bf16[256,512]{1,0:T(8,128)(2,1)S(1)} %get-tuple-element.59), channel_id=1, source_target_pairs={{0,2},{1,3},{2,0},{3,1},{4,6},{5,7},{6,4},{7,5},{8,10},{9,11},{10,... | collective-permute-start | bytes 786440 | tf_op jit(solution)/shard_map/ppermute | solution.py:146
  11.2 8.9 %collective-permute-start.2 = (bf16[128,512]{1,0:T(8,128)(2,1)S(1)}, bf16[128,512]{1,0:T(8,128)(2,1)S(1)}, u32[]{:S(2)}, u32[]{:S(2)}) collective-permute-start(bf16[128,512]{1,0:T(8,128)(2,1)S(1)} %collective-permute-done.refs_0_), channel_id=1, source_target_pairs={{0,1},{1,0},{2,3},{3,2},{4,5},{5,4},{6,7},{7,6},{8,9},{9,8},{10,11... | collective-permute-start | bytes 393224 | tf_op jit(solution)/shard_map/ppermute | solution.py:148
  11.2 11.7 %collective-permute-start.5 = (bf16[128,512]{1,0:T(8,128)(2,1)S(1)}, bf16[128,512]{1,0:T(8,128)(2,1)S(1)}, u32[]{:S(2)}, u32[]{:S(2)}) collective-permute-start(bf16[128,512]{1,0:T(8,128)(2,1)S(1)} %collective-permute-done.refs_0_), channel_id=1, source_target_pairs={{0,2},{1,3},{2,0},{3,1},{4,6},{5,7},{6,4},{7,5},{8,10},{9,11},{10,... | collective-permute-start | bytes 393224 | tf_op jit(solution)/shard_map/ppermute | solution.py:147
  16.9 3.2 %collective-permute-start.3 = (bf16[128,512]{1,0:T(8,128)(2,1)S(1)}, bf16[128,512]{1,0:T(8,128)(2,1)S(1)}, u32[]{:S(2)}, u32[]{:S(2)}) collective-permute-start(bf16[128,512]{1,0:T(8,128)(2,1)S(1)} %collective-permute-done.1.refs_1_), channel_id=1, source_target_pairs={{0,1},{1,0},{2,3},{3,2},{4,5},{5,4},{6,7},{7,6},{8,9},{9,8},{10,11... | collective-permute-start | bytes 393224 | tf_op jit(solution)/shard_map/ppermute | solution.py:148
  17.6 8.1 %collective-permute-start.10 = (bf16[128,512]{1,0:T(8,128)(2,1)S(1)}, bf16[128,512]{1,0:T(8,128)(2,1)S(1)}, u32[]{:S(2)}, u32[]{:S(2)}) collective-permute-start(bf16[128,512]{1,0:T(8,128)(2,1)S(1)} %collective-permute-done.1.refs_1_), channel_id=1, source_target_pairs={{0,2},{1,3},{2,0},{3,1},{4,6},{5,7},{6,4},{7,5},{8,10},{9,11},{10,... | collective-permute-start | bytes 393224 | tf_op jit(solution)/shard_map/ppermute | solution.py:147
  20.1 4.1 %collective-permute-start.9 = (bf16[256,512]{1,0:T(8,128)(2,1)S(1)}, bf16[256,512]{1,0:T(8,128)(2,1)S(1)}, u32[]{:S(2)}, u32[]{:S(2)}) collective-permute-start(bf16[256,512]{1,0:T(8,128)(2,1)S(1)} %collective-permute-done.8.refs_0_), channel_id=1, source_target_pairs={{0,1},{1,0},{2,3},{3,2},{4,5},{5,4},{6,7},{7,6},{8,9},{9,8},{10,11... | collective-permute-start | bytes 786440 | tf_op jit(solution)/shard_map/ppermute | solution.py:149
  23.6 1.3 %collective-permute-start.6 = (bf16[64,512]{1,0:T(8,128)(2,1)S(1)}, bf16[64,512]{1,0:T(8,128)(2,1)S(1)}, u32[]{:S(2)}, u32[]{:S(2)}) collective-permute-start(bf16[64,512]{1,0:T(8,128)(2,1)S(1)} %get-tuple-element.57.refs_0_), channel_id=1, source_target_pairs={{0,1},{1,0},{2,3},{3,2},{4,5},{5,4},{6,7},{7,6},{8,9},{9,8},{10,11... | collective-permute-start | bytes 196616 | tf_op jit(solution)/shard_map/ppermute | solution.py:150
  23.7 1.4 %collective-permute-start.7 = (bf16[64,512]{1,0:T(8,128)(2,1)S(1)}, bf16[64,512]{1,0:T(8,128)(2,1)S(1)}, u32[]{:S(2)}, u32[]{:S(2)}) collective-permute-start(bf16[64,512]{1,0:T(8,128)(2,1)S(1)} %get-tuple-element.58.refs_1_), channel_id=1, source_target_pairs={{0,1},{1,0},{2,3},{3,2},{4,5},{5,4},{6,7},{7,6},{8,9},{9,8},{10,11... | collective-permute-start | bytes 196616 | tf_op jit(solution)/shard_map/ppermute | solution.py:150
  25.6 1.7 %collective-permute-start.11 = (bf16[128,512]{1,0:T(8,128)(2,1)S(1)}, bf16[128,512]{1,0:T(8,128)(2,1)S(1)}, u32[]{:S(2)}, u32[]{:S(2)}) collective-permute-start(bf16[128,512]{1,0:T(8,128)(2,1)S(1)} %get-tuple-element.68.refs_0_), channel_id=1, source_target_pairs={{0,1},{1,0},{2,3},{3,2},{4,5},{5,4},{6,7},{7,6},{8,9},{9,8},{10,11... | collective-permute-start | bytes 393224 | tf_op jit(solution)/shard_map/ppermute | solution.py:586
  25.8 5.1 %collective-permute-start.13 = (bf16[128,256]{1,0:T(8,128)(2,1)S(1)}, bf16[128,256]{1,0:T(8,128)(2,1)S(1)}, u32[]{:S(2)}, u32[]{:S(2)}) collective-permute-start(bf16[128,256]{1,0:T(8,128)(2,1)S(1)} %get-tuple-element.66.refs_11_.refs_9_), channel_id=1, source_target_pairs={{0,8},{8,0},{1,9},{9,1},{2,10},{10,2},{3,11},{11,3},{4,12},{12,4},... | collective-permute-start | bytes 196616 | tf_op jit(solution)/shard_map/ppermute | solution.py:591
  27.7 4.3 %collective-permute-start.12 = (bf16[128,256]{1,0:T(8,128)(2,1)S(1)}, bf16[128,256]{1,0:T(8,128)(2,1)S(1)}, u32[]{:S(2)}, u32[]{:S(2)}) collective-permute-start(bf16[128,256]{1,0:T(8,128)(2,1)S(1)} %get-tuple-element.70.refs_10_), channel_id=1, source_target_pairs={{0,8},{8,0},{1,9},{9,1},{2,10},{10,2},{3,11},{11,3},{4,12},{12,4},... | collective-permute-start | bytes 196616 | tf_op jit(solution)/shard_map/ppermute | solution.py:591
  32.8 11.1 %collective-permute-start.14 = (bf16[256,512]{1,0:T(8,128)(2,1)S(1)}, bf16[256,512]{1,0:T(8,128)(2,1)S(1)}, u32[]{:S(2)}, u32[]{:S(2)}) collective-permute-start(bf16[256,512]{1,0:T(8,128)(2,1)S(1)} %get-tuple-element.81.refs_0_), channel_id=1, source_target_pairs={{0,6},{1,7},{2,4},{3,5},{4,2},{5,3},{6,0},{7,1},{8,14},{9,15},{10,... | collective-permute-start | bytes 786440 | tf_op jit(solution)/shard_map/ppermute | solution.py:130
  36.2 7.7 %collective-permute-start.17 = (bf16[128,512]{1,0:T(8,128)(2,1)S(1)}, bf16[128,512]{1,0:T(8,128)(2,1)S(1)}, u32[]{:S(2)}, u32[]{:S(2)}) collective-permute-start(bf16[128,512]{1,0:T(8,128)(2,1)S(1)} %get-tuple-element.82), channel_id=1, source_target_pairs={{0,1},{1,0},{2,3},{3,2},{4,5},{5,4},{6,7},{7,6},{8,9},{9,8},{10,11... | collective-permute-start | bytes 393224 | tf_op jit(solution)/shard_map/ppermute | solution.py:131
  36.2 11.8 %collective-permute-start.19 = (bf16[128,512]{1,0:T(8,128)(2,1)S(1)}, bf16[128,512]{1,0:T(8,128)(2,1)S(1)}, u32[]{:S(2)}, u32[]{:S(2)}) collective-permute-start(bf16[128,512]{1,0:T(8,128)(2,1)S(1)} %get-tuple-element.82), channel_id=1, source_target_pairs={{0,2},{1,3},{2,0},{3,1},{4,6},{5,7},{6,4},{7,5},{8,10},{9,11},{10,... | collective-permute-start | bytes 393224 | tf_op jit(solution)/shard_map/ppermute | solution.py:132
  36.2 11.7 %collective-permute-start.18 = (bf16[128,512]{1,0:T(8,128)(2,1)S(1)}, bf16[128,512]{1,0:T(8,128)(2,1)S(1)}, u32[]{:S(2)}, u32[]{:S(2)}) collective-permute-start(bf16[128,512]{1,0:T(8,128)(2,1)S(1)} %get-tuple-element.83), channel_id=1, source_target_pairs={{0,1},{1,0},{2,3},{3,2},{4,5},{5,4},{6,7},{7,6},{8,9},{9,8},{10,11... | collective-permute-start | bytes 393224 | tf_op jit(solution)/shard_map/ppermute | solution.py:131
  36.7 11.3 %collective-permute-start.20 = (bf16[128,512]{1,0:T(8,128)(2,1)S(1)}, bf16[128,512]{1,0:T(8,128)(2,1)S(1)}, u32[]{:S(2)}, u32[]{:S(2)}) collective-permute-start(bf16[128,512]{1,0:T(8,128)(2,1)S(1)} %get-tuple-element.83), channel_id=1, source_target_pairs={{0,2},{1,3},{2,0},{3,1},{4,6},{5,7},{6,4},{7,5},{8,10},{9,11},{10,... | collective-permute-start | bytes 393224 | tf_op jit(solution)/shard_map/ppermute | solution.py:132
  43.9 8.4 %collective-permute-start.21 = (bf16[256,512]{1,0:T(8,128)(2,1)S(1)}, bf16[256,512]{1,0:T(8,128)(2,1)S(1)}, u32[]{:S(2)}, u32[]{:S(2)}) collective-permute-start(bf16[256,512]{1,0:T(8,128)(2,1)S(1)} %collective-permute-done.14.refs_0_), channel_id=1, source_target_pairs={{0,1},{1,0},{2,3},{3,2},{4,5},{5,4},{6,7},{7,6},{8,9},{9,8},{10,11... | collective-permute-start | bytes 786440 | tf_op jit(solution)/shard_map/ppermute | solution.py:136
  43.9 8.3 %collective-permute-start.24 = (bf16[128,512]{1,0:T(8,128)(2,1)S(1)}, bf16[128,512]{1,0:T(8,128)(2,1)S(1)}, u32[]{:S(2)}, u32[]{:S(2)}) collective-permute-start(bf16[128,512]{1,0:T(8,128)(2,1)S(1)} %get-tuple-element.93), channel_id=1, source_target_pairs={{0,2},{1,3},{2,0},{3,1},{4,6},{5,7},{6,4},{7,5},{8,10},{9,11},{10,... | collective-permute-start | bytes 393224 | tf_op jit(solution)/shard_map/ppermute | solution.py:134
  47.9 7.0 %collective-permute-start.15 = (bf16[128,512]{1,0:T(8,128)(2,1)S(1)}, bf16[128,512]{1,0:T(8,128)(2,1)S(1)}, u32[]{:S(2)}, u32[]{:S(2)}) collective-permute-start(bf16[128,512]{1,0:T(8,128)(2,1)S(1)} %get-tuple-element.94), channel_id=1, source_target_pairs={{0,2},{1,3},{2,0},{3,1},{4,6},{5,7},{6,4},{7,5},{8,10},{9,11},{10,... | collective-permute-start | bytes 393224 | tf_op jit(solution)/shard_map/ppermute | solution.py:134
  52.3 2.6 %collective-permute-start.25 = (bf16[128,512]{1,0:T(8,128)(2,1)S(1)}, bf16[128,512]{1,0:T(8,128)(2,1)S(1)}, u32[]{:S(2)}, u32[]{:S(2)}) collective-permute-start(bf16[128,512]{1,0:T(8,128)(2,1)S(1)} %collective-permute-done.24.last_a), channel_id=1, source_target_pairs={{0,1},{1,0},{2,3},{3,2},{4,5},{5,4},{6,7},{7,6},{8,9},{9,8},{10,11... | collective-permute-start | bytes 393224 | tf_op jit(solution)/shard_map/ppermute | solution.py:137
  52.7 2.2 %collective-permute-start.22 = (bf16[128,512]{1,0:T(8,128)(2,1)S(1)}, bf16[128,512]{1,0:T(8,128)(2,1)S(1)}, u32[]{:S(2)}, u32[]{:S(2)}) collective-permute-start(bf16[128,512]{1,0:T(8,128)(2,1)S(1)} %get-tuple-element.88.a), channel_id=1, source_target_pairs={{0,1},{1,0},{2,3},{3,2},{4,5},{5,4},{6,7},{7,6},{8,9},{9,8},{10,11... | collective-permute-start | bytes 393224 | tf_op jit(solution)/shard_map/ppermute | solution.py:137
  53.3 1.6 %collective-permute-start.23 = (bf16[128,512]{1,0:T(8,128)(2,1)S(1)}, bf16[128,512]{1,0:T(8,128)(2,1)S(1)}, u32[]{:S(2)}, u32[]{:S(2)}) collective-permute-start(bf16[128,512]{1,0:T(8,128)(2,1)S(1)} %get-tuple-element.89.b), channel_id=1, source_target_pairs={{0,1},{1,0},{2,3},{3,2},{4,5},{5,4},{6,7},{7,6},{8,9},{9,8},{10,11... | collective-permute-start | bytes 393224 | tf_op jit(solution)/shard_map/ppermute | solution.py:137
  54.9 1.3 %collective-permute-start.16 = (bf16[128,512]{1,0:T(8,128)(2,1)S(1)}, bf16[128,512]{1,0:T(8,128)(2,1)S(1)}, u32[]{:S(2)}, u32[]{:S(2)}) collective-permute-start(bf16[128,512]{1,0:T(8,128)(2,1)S(1)} %collective-permute-done.15.last_b), channel_id=1, source_target_pairs={{0,1},{1,0},{2,3},{3,2},{4,5},{5,4},{6,7},{7,6},{8,9},{9,8},{10,11... | collective-permute-start | bytes 393224 | tf_op jit(solution)/shard_map/ppermute | solution.py:138
